TPU v7x, 32 devices: a whole 2x2x4 slice. The times are simulated.
32 devices in a mesh: groups: 2 (over x), shot: 16 (over z, y, core).
Axes of the slice: x: 2, y: 2, z: 4, core: 2. Of those that a mesh axis runs over, the one named last changes fastest.
Arguments:
- courant_sq: float32 [128, 32, 128], P('groups'), parts along dimension 0, may hold values from 0.05 to 0.2
- wave_now: float32 [512, 32, 128], P(('groups', 'shot')), parts along dimension 0, may hold values from -6 to 6
- wave_before: float32 [512, 32, 128], P(('groups', 'shot')), parts along dimension 0, may hold values from -6 to 6
- wavelet: float32 [32, 8], P(('groups', 'shot')), parts along dimension 0, may hold values from -24 to 24
- source_cell: int32 [32], P(('groups', 'shot')), parts along dimension 0, may hold values from 0 to 65535, as said below
- receiver_cell: int32 [8192], P(('groups', 'shot')), parts along dimension 0, may hold values from 0 to 65535, as said below
- send_order: int32 [8192], P(('groups', 'shot')), parts along dimension 0, may hold values from 0 to 255, as said below
- observed: float32 [512, 128], P(('groups', 'shot')), parts along dimension 0, may hold values from -6 to 6
Outputs:
- gradient_slabs: float32 [128, 32, 128], P(('groups', 'shot')), parts along dimension 0
There are 2 independent parts, one for each index of `groups`. A program takes and returns all parts, laid end to end along the dimension named above; each array names one. Nothing has to cross between parts.
Inputs may be any that keep to these rules, and one draw needn't show every extreme that they name: `source_cell`: a local cell index (x * 32 + y) * 128 + z of a block of 16 planes. `receiver_cell`: a local cell index (x * 32 + y) * 128 + z of a block of 16 planes. `send_order`: each aligned block of 256 entries is a permutation of 0 to 255.
All inputs are finite; a program needn't handle non-finite values.
Results may differ from a plain program's by a relative error of at most 0.00021.
Values sent between devices are 32-bit elements; how exact they have to be, the bound alone decides.
No kernel may reach another device: no remote copies, remote signals or barrier semaphores. Data moves between devices by JAX's collectives and lax.ppermute only.
A program may use at most 64 MiB of HBM per device.

v0:
```python
import jax
import jax.numpy as jnp
from jax import lax
from jax.sharding import PartitionSpec as P

NT = 8
PIECES = 4


stencil_center = -205.0 / 72.0
stencil_weights = (8.0 / 5.0, -1.0 / 5.0, 8.0 / 315.0, -1.0 / 560.0)


def extended_2(cells, sides, width):
    for axis, dim in sides:
        count = lax.axis_size(axis)
        head = lax.slice_in_dim(cells, 0, width, axis=dim)
        tail = lax.slice_in_dim(cells, cells.shape[dim] - width, cells.shape[dim], axis=dim)
        cells = jnp.concatenate(
            [
                lax.ppermute(tail, axis, [(i, (i + 1) % count) for i in range(count)]),
                cells,
                lax.ppermute(head, axis, [((i + 1) % count, i) for i in range(count)]),
            ],
            axis=dim,
        )
    return cells


def shifted_2(value, axis, steps):
    count = lax.axis_size(axis)
    pairs = [(source, (source + steps) % count) for source in range(count)]
    return lax.ppermute(value, axis, pairs)


def shifted(values, offset, axis_pos):
    length = values.shape[axis_pos]
    filler_shape = list(values.shape)
    filler_shape[axis_pos] = abs(offset)
    filler = jnp.zeros(filler_shape, values.dtype)
    if offset > 0:
        return jnp.concatenate(
            [lax.slice_in_dim(values, offset, length, axis=axis_pos), filler], axis_pos
        )
    return jnp.concatenate(
        [filler, lax.slice_in_dim(values, 0, length + offset, axis=axis_pos)], axis_pos
    )


def laplace_rows(extended, start, count_rows):
    center = lax.slice_in_dim(extended, start, start + count_rows, axis=0)
    summed = 3.0 * stencil_center * center
    for distance in range(1, len(stencil_weights) + 1):
        weight = stencil_weights[distance - 1]
        beside_all = lax.slice_in_dim(
            extended, start + distance, start + distance + count_rows, axis=0
        )
        beside_all = beside_all + lax.slice_in_dim(
            extended, start - distance, start - distance + count_rows, axis=0
        )
        beside_all = beside_all + shifted(center, distance, 1) + shifted(center, -distance, 1)
        beside_all = beside_all + shifted(center, distance, 2) + shifted(center, -distance, 2)
        summed = summed + weight * beside_all
    return summed


def cell_tables(cells, rows_total, depth):
    row_of = cells // depth
    col_of = cells % depth
    row_table = (row_of[:, None] == jnp.arange(rows_total, dtype=jnp.int32)[None, :]).astype(
        jnp.float32
    )
    col_table = (col_of[:, None] == jnp.arange(depth, dtype=jnp.int32)[None, :]).astype(jnp.float32)
    return (row_table, col_table)


def inject(wavefield, tables, amounts):
    row_table, col_table = tables
    weighted = row_table * amounts[:, None]
    added = lax.dot_general(
        weighted,
        col_table,
        (((0,), (0,)), ((), ())),
        precision=lax.Precision.HIGHEST,
        preferred_element_type=jnp.float32,
    )
    return wavefield + added.reshape(wavefield.shape)


def extract(wavefield, tables):
    row_table, col_table = tables
    flat_rows = wavefield.reshape(row_table.shape[1], col_table.shape[1])
    picked = jnp.dot(
        row_table, flat_rows, precision=lax.Precision.HIGHEST, preferred_element_type=jnp.float32
    )
    return jnp.sum(picked * col_table, axis=1)


def per_device(
    courant_sq, wave_now, wave_before, wavelet, source_cell, receiver_cell, send_order, observed
):
    device_count = lax.axis_size("shot")
    device_index = lax.axis_index("shot")
    domain_piece = device_index % PIECES
    piece_rows, span_y, span_z = wave_now.shape
    stencil_reach = len(stencil_weights)
    courant_piece = lax.dynamic_slice_in_dim(courant_sq, domain_piece * piece_rows, piece_rows, 0)
    plane_rows = piece_rows * span_y
    source_tables = cell_tables(source_cell, plane_rows, span_z)
    ordered_cells = receiver_cell[send_order]
    receiver_tables = cell_tables(ordered_cells, plane_rows, span_z)

    def single_step(current, previous, tables, amounts):
        extended = extended_2(current, (("shot", 0),), stencil_reach)
        updated = (
            2.0 * current
            - previous
            + courant_piece * laplace_rows(extended, stencil_reach, piece_rows)
        )
        return inject(updated, tables, amounts)

    def advance_all(current, previous, injections):
        produced = []
        for tables, amounts in injections:
            updated = single_step(current, previous, tables, amounts)
            produced.append(updated)
            previous, current = (current, updated)
        return produced

    forward_list = advance_all(
        wave_now,
        wave_before,
        [(source_tables, wavelet[0, step_index : step_index + 1]) for step_index in range(NT)],
    )
    traces = jnp.stack([extract(wavefield, receiver_tables) for wavefield in forward_list])
    receiver_count = receiver_cell.shape[0]
    per_owner = receiver_count // device_count
    packed = (
        traces.reshape(NT, device_count, per_owner)
        .transpose(1, 0, 2)
        .reshape(device_count, NT * per_owner)
    )
    arrived = lax.all_to_all(packed, "shot", split_axis=0, concat_axis=0, tiled=True)
    returned = lax.all_to_all(arrived - observed, "shot", split_axis=0, concat_axis=0, tiled=True)
    misfit = (
        returned.reshape(device_count, NT, per_owner).transpose(1, 0, 2).reshape(NT, receiver_count)
    )
    empty_field = jnp.zeros_like(wave_now)
    adjoint_now = inject(empty_field, receiver_tables, misfit[NT - 1])
    imaging_sum = adjoint_now * forward_list[NT - 1]
    adjoint_list = advance_all(
        adjoint_now,
        empty_field,
        [(receiver_tables, misfit[NT - 1 - adjoint_step]) for adjoint_step in range(1, NT)],
    )
    for position, wavefield in enumerate(adjoint_list):
        imaging_sum = imaging_sum + wavefield * forward_list[NT - 2 - position]
    period_count = device_count // PIECES
    slab_rows = piece_rows // period_count
    period_index = device_index // PIECES
    blocks = imaging_sum.reshape(period_count, slab_rows, span_y, span_z)

    def take_block(block_index):
        return lax.dynamic_index_in_dim(blocks, block_index % period_count, 0, keepdims=False)

    def cycle_step(step_index, carried):
        arrived = shifted_2(carried, "shot", PIECES)
        return arrived + take_block(period_index - 1 - step_index + 2 * period_count)

    start_block = take_block(period_index - 1 + period_count)
    return lax.fori_loop(1, period_count, cycle_step, start_block)


def solution(mesh):
    return jax.shard_map(
        per_device,
        mesh=mesh,
        in_specs=(
            P("groups", None, None),
            P(("groups", "shot"), None, None),
            P(("groups", "shot"), None, None),
            P(("groups", "shot"), None),
            P(("groups", "shot")),
            P(("groups", "shot")),
            P(("groups", "shot")),
            P(("groups", "shot"), None),
        ),
        out_specs=P(("groups", "shot"), None, None),
        check_vma=False,
    )
```

profile of v0, /device:TPU:0, one launch (start us, length us, event | category | flops | bytes accessed | tf_op | source)
XLA Modules:
  0.0 267.8 jit_solution(6011277250517265467)
XLA Ops:
  1.4 5.1 %collective-permute-start.1 = (f32[4,32,128]{2,1,0:T(8,128)S(1)}, f32[4,32,128]{2,1,0:T(8,128)S(1)}, u32[]{:S(2)}, u32[]{:S(2)}) collective-permute-start(f32[4,32,128]{2,1,0:T(8,128)S(1)} %get-tuple-element.404), channel_id=1, source_target_pairs={{1,0},{2,1},{3,2},{4,3},{5,4},{6,5},{7,6},{8,7},{9,8},{10,9},{11,1... | collective-permute-start | bytes 196616 | tf_op jit(solution)/shard_map/ppermute | solution.py:23
  35.2 4.5 %collective-permute-done.4 = f32[4,32,128]{2,1,0:T(8,128)S(1)} collective-permute-done((f32[4,32,128]{2,1,0:T(8,128)S(1)}, f32[4,32,128]{2,1,0:T(8,128)S(1)}, u32[]{:S(2)}, u32[]{:S(2)}) %collective-permute-start.4) | collective-permute-done | bytes 65568 | tf_op jit(solution)/shard_map/ppermute | solution.py:21
  40.3 2.3 fusion.440
  49.2 4.6 %collective-permute-done.6 = f32[4,32,128]{2,1,0:T(8,128)S(1)} collective-permute-done((f32[4,32,128]{2,1,0:T(8,128)S(1)}, f32[4,32,128]{2,1,0:T(8,128)S(1)}, u32[]{:S(2)}, u32[]{:S(2)}) %collective-permute-start.6) | collective-permute-done | bytes 65568 | tf_op jit(solution)/shard_map/ppermute | solution.py:21
  54.4 2.3 fusion.409
  64.0 4.6 %collective-permute-done.8 = f32[4,32,128]{2,1,0:T(8,128)S(1)} collective-permute-done((f32[4,32,128]{2,1,0:T(8,128)S(1)}, f32[4,32,128]{2,1,0:T(8,128)S(1)}, u32[]{:S(2)}, u32[]{:S(2)}) %collective-permute-start.8) | collective-permute-done | bytes 65568 | tf_op jit(solution)/shard_map/ppermute | solution.py:21
  69.2 2.4 fusion.378
  77.1 4.4 %collective-permute-start.9 = (f32[4,32,128]{2,1,0:T(8,128)S(1)}, f32[4,32,128]{2,1,0:T(8,128)S(1)}, u32[]{:S(2)}, u32[]{:S(2)}) collective-permute-start(f32[4,32,128]{2,1,0:T(8,128)S(1)} %get-tuple-element.332), channel_id=1, source_target_pairs={{1,0},{2,1},{3,2},{4,3},{5,4},{6,5},{7,6},{8,7},{9,8},{10,9},{11,1... | collective-permute-start | bytes 196616 | tf_op jit(solution)/shard_map/ppermute | solution.py:23
  84.1 2.5 fusion.347
  92.6 4.5 %collective-permute-start.11 = (f32[4,32,128]{2,1,0:T(8,128)S(1)}, f32[4,32,128]{2,1,0:T(8,128)S(1)}, u32[]{:S(2)}, u32[]{:S(2)}) collective-permute-start(f32[4,32,128]{2,1,0:T(8,128)S(1)} %get-tuple-element.314), channel_id=1, source_target_pairs={{1,0},{2,1},{3,2},{4,3},{5,4},{6,5},{7,6},{8,7},{9,8},{10,9},{11,1... | collective-permute-start | bytes 196616 | tf_op jit(solution)/shard_map/ppermute | solution.py:23
  99.0 4.5 %collective-permute-done.12 = f32[4,32,128]{2,1,0:T(8,128)S(1)} collective-permute-done((f32[4,32,128]{2,1,0:T(8,128)S(1)}, f32[4,32,128]{2,1,0:T(8,128)S(1)}, u32[]{:S(2)}, u32[]{:S(2)}) %collective-permute-start.12) | collective-permute-done | bytes 65568 | tf_op jit(solution)/shard_map/ppermute | solution.py:21
  104.2 2.5 fusion.316
  114.8 4.7 %collective-permute-done.14 = f32[4,32,128]{2,1,0:T(8,128)S(1)} collective-permute-done((f32[4,32,128]{2,1,0:T(8,128)S(1)}, f32[4,32,128]{2,1,0:T(8,128)S(1)}, u32[]{:S(2)}, u32[]{:S(2)}) %collective-permute-start.14) | collective-permute-done | bytes 65568 | tf_op jit(solution)/shard_map/ppermute | solution.py:21
  120.2 2.6 fusion.285
  131.6 4.6 %collective-permute-done.16 = f32[4,32,128]{2,1,0:T(8,128)S(1)} collective-permute-done((f32[4,32,128]{2,1,0:T(8,128)S(1)}, f32[4,32,128]{2,1,0:T(8,128)S(1)}, u32[]{:S(2)}, u32[]{:S(2)}) %collective-permute-start.16) | collective-permute-done | bytes 65568 | tf_op jit(solution)/shard_map/ppermute | solution.py:21
  136.2 2.7 %fusion.254 = f32[16,32,128]{2,1,0:T(8,128)S(1)} fusion(f32[16,32,128]{2,1,0:T(8,128)S(1)} %fusion.285, f32[4,32,128]{2,1,0:T(8,128)S(1)} %collective-permute-done.16, f32[4,32,128]{2,1,0:T(8,128)S(1)} %collective-permute-done.15, f32[16,32,124]{2,1,0:T(8,128)} %get-tuple-element.277, f32[16,32,124]{2,1,0:T(8,128)} %get-tuple-element.276, ...), kind=kLoop, calls=%fused_computation.433 | loop fusion | flops 2818048 | bytes 5171716 | tf_op jit(solution)/shard_map/add | solution.py:87
  141.7 9.0 %all_to_all.21 = f32[16,1,128]{2,1,0:T(1,128)S(1)} all-to-all(f32[16,1,128]{2,1,0:T(1,128)S(1)} %all_to_all.14), channel_id=1, replica_groups=mesh['groups'=2,'shot'=16] {'shot'}, dimensions={0} | all-to-all | bytes 16384 | tf_op jit(solution)/shard_map/all_to_all | solution.py:143
  151.3 3.5 %all-to-all-start.1 = ((f32[16,1,128]{2,1,0:T(1,128)}), f32[16,1,128]{2,1,0:T(1,128)S(1)}, u32[]{:S(2)}, u32[]{:S(2)}) async-start(f32[16,1,128]{2,1,0:T(1,128)} %bitcast.23), calls=%async_computation.1 | async-start | bytes 16384 | tf_op jit(solution)/shard_map/all_to_all | solution.py:144
  154.8 6.3 %all-to-all-done.1 = f32[16,1,128]{2,1,0:T(1,128)S(1)} async-done(((f32[16,1,128]{2,1,0:T(1,128)}), f32[16,1,128]{2,1,0:T(1,128)S(1)}, u32[]{:S(2)}, u32[]{:S(2)}) %all-to-all-start.1) | async-done | bytes 8224 | tf_op jit(solution)/shard_map/all_to_all | solution.py:144
  173.2 2.1 fusion.20
  194.1 2.6 fusion.223
  197.4 4.0 %collective-permute-start.19 = (f32[4,32,128]{2,1,0:T(8,128)S(1)}, f32[4,32,128]{2,1,0:T(8,128)S(1)}, u32[]{:S(2)}, u32[]{:S(2)}) collective-permute-start(f32[4,32,128]{2,1,0:T(8,128)S(1)} %get-tuple-element.242), channel_id=1, source_target_pairs={{1,0},{2,1},{3,2},{4,3},{5,4},{6,5},{7,6},{8,7},{9,8},{10,9},{11,1... | collective-permute-start | bytes 196616 | tf_op jit(solution)/shard_map/ppermute | solution.py:23
  203.3 4.5 %collective-permute-done.20 = f32[4,32,128]{2,1,0:T(8,128)S(1)} collective-permute-done((f32[4,32,128]{2,1,0:T(8,128)S(1)}, f32[4,32,128]{2,1,0:T(8,128)S(1)}, u32[]{:S(2)}, u32[]{:S(2)}) %collective-permute-start.20) | collective-permute-done | bytes 65568 | tf_op jit(solution)/shard_map/ppermute | solution.py:21
  211.1 4.6 %collective-permute-done.22 = f32[4,32,128]{2,1,0:T(8,128)S(1)} collective-permute-done((f32[4,32,128]{2,1,0:T(8,128)S(1)}, f32[4,32,128]{2,1,0:T(8,128)S(1)}, u32[]{:S(2)}, u32[]{:S(2)}) %collective-permute-start.22) | collective-permute-done | bytes 65568 | tf_op jit(solution)/shard_map/ppermute | solution.py:21
  218.9 4.6 %collective-permute-done.24 = f32[4,32,128]{2,1,0:T(8,128)S(1)} collective-permute-done((f32[4,32,128]{2,1,0:T(8,128)S(1)}, f32[4,32,128]{2,1,0:T(8,128)S(1)}, u32[]{:S(2)}, u32[]{:S(2)}) %collective-permute-start.24) | collective-permute-done | bytes 65568 | tf_op jit(solution)/shard_map/ppermute | solution.py:21
  226.8 4.5 %collective-permute-done.26 = f32[4,32,128]{2,1,0:T(8,128)S(1)} collective-permute-done((f32[4,32,128]{2,1,0:T(8,128)S(1)}, f32[4,32,128]{2,1,0:T(8,128)S(1)}, u32[]{:S(2)}, u32[]{:S(2)}) %collective-permute-start.26) | collective-permute-done | bytes 65568 | tf_op jit(solution)/shard_map/ppermute | solution.py:21
  234.6 4.5 %collective-permute-done.28 = f32[4,32,128]{2,1,0:T(8,128)S(1)} collective-permute-done((f32[4,32,128]{2,1,0:T(8,128)S(1)}, f32[4,32,128]{2,1,0:T(8,128)S(1)}, u32[]{:S(2)}, u32[]{:S(2)}) %collective-permute-start.28) | collective-permute-done | bytes 65568 | tf_op jit(solution)/shard_map/ppermute | solution.py:21
  242.4 4.5 %collective-permute-done.30 = f32[4,32,128]{2,1,0:T(8,128)S(1)} collective-permute-done((f32[4,32,128]{2,1,0:T(8,128)S(1)}, f32[4,32,128]{2,1,0:T(8,128)S(1)}, u32[]{:S(2)}, u32[]{:S(2)}) %collective-permute-start.30) | collective-permute-done | bytes 65568 | tf_op jit(solution)/shard_map/ppermute | solution.py:21
  248.0 18.5 %while.15 = (s32[]{:T(128)}, f32[4,32,128]{2,1,0:T(8,128)S(1)}, s32[]{:T(128)}, f32[4,4,32,128]{3,2,1,0:T(8,128)S(1)}, s32[]{:T(128)}, /*index=5*/s32[]{:T(128)}, s32[]{:T(128)}, s32[]{:T(128)}, s32[]{:T(128)}) while((s32[]{:T(128)}, f32[4,32,128]{2,1,0:T(8,128)S(1)}, s32[]{:T(128)}, f32[4,4,32,128]{3,2,1,0:T(8,128)S(1)}, s32[]{:T(128)}, ...), condition=%wide.region_9.10_spmd, body=%wide.region_8.9_spmd.sunk | while | flops 16402 | bytes 459056 | solution.py:171
  248.1 6.1 %collective-permute-done = f32[4,32,128]{2,1,0:T(8,128)S(1)} collective-permute-done((f32[4,32,128]{2,1,0:T(8,128)S(1)}, f32[4,32,128]{2,1,0:T(8,128)S(1)}, u32[]{:S(2)}, u32[]{:S(2)}) %collective-permute-start) | collective-permute-done | bytes 65568 | tf_op jit(solution)/shard_map/while/body/eval_jaxpr/ppermute | solution.py:33
  254.3 6.0 %collective-permute-done = f32[4,32,128]{2,1,0:T(8,128)S(1)} collective-permute-done((f32[4,32,128]{2,1,0:T(8,128)S(1)}, f32[4,32,128]{2,1,0:T(8,128)S(1)}, u32[]{:S(2)}, u32[]{:S(2)}) %collective-permute-start) | collective-permute-done | bytes 65568 | tf_op jit(solution)/shard_map/while/body/eval_jaxpr/ppermute | solution.py:33
  260.5 6.0 %collective-permute-done = f32[4,32,128]{2,1,0:T(8,128)S(1)} collective-permute-done((f32[4,32,128]{2,1,0:T(8,128)S(1)}, f32[4,32,128]{2,1,0:T(8,128)S(1)}, u32[]{:S(2)}, u32[]{:S(2)}) %collective-permute-start) | collective-permute-done | bytes 65568 | tf_op jit(solution)/shard_map/while/body/eval_jaxpr/ppermute | solution.py:33
  (334 shorter events, 134.5 us)
Async XLA Ops:
  0.9 23.8 %collective-permute-start.2 = (f32[4,32,128]{2,1,0:T(8,128)S(1)}, f32[4,32,128]{2,1,0:T(8,128)S(1)}, u32[]{:S(2)}, u32[]{:S(2)}) collective-permute-start(f32[4,32,128]{2,1,0:T(8,128)S(1)} %get-tuple-element.405), channel_id=1, source_target_pairs={{0,1},{1,2},{2,3},{3,4},{4,5},{5,6},{6,7},{7,8},{8,9},{9,10},{10,1... | collective-permute-start | bytes 196616 | tf_op jit(solution)/shard_map/ppermute | solution.py:21
  1.4 23.4 %collective-permute-start.1 = (f32[4,32,128]{2,1,0:T(8,128)S(1)}, f32[4,32,128]{2,1,0:T(8,128)S(1)}, u32[]{:S(2)}, u32[]{:S(2)}) collective-permute-start(f32[4,32,128]{2,1,0:T(8,128)S(1)} %get-tuple-element.404), channel_id=1, source_target_pairs={{1,0},{2,1},{3,2},{4,3},{5,4},{6,5},{7,6},{8,7},{9,8},{10,9},{11,1... | collective-permute-start | bytes 196616 | tf_op jit(solution)/shard_map/ppermute | solution.py:23
  32.5 2.6 collective-permute-start.3
  33.3 6.4 %collective-permute-start.4 = (f32[4,32,128]{2,1,0:T(8,128)S(1)}, f32[4,32,128]{2,1,0:T(8,128)S(1)}, u32[]{:S(2)}, u32[]{:S(2)}) collective-permute-start(f32[4,32,128]{2,1,0:T(8,128)S(1)} %get-tuple-element.387), channel_id=1, source_target_pairs={{0,1},{1,2},{2,3},{3,4},{4,5},{5,6},{6,7},{7,8},{8,9},{9,10},{10,1... | collective-permute-start | bytes 196616 | tf_op jit(solution)/shard_map/ppermute | solution.py:21
  47.2 2.0 collective-permute-start.5
  47.3 6.4 %collective-permute-start.6 = (f32[4,32,128]{2,1,0:T(8,128)S(1)}, f32[4,32,128]{2,1,0:T(8,128)S(1)}, u32[]{:S(2)}, u32[]{:S(2)}) collective-permute-start(f32[4,32,128]{2,1,0:T(8,128)S(1)} %get-tuple-element.369), channel_id=1, source_target_pairs={{0,1},{1,2},{2,3},{3,4},{4,5},{5,6},{6,7},{7,8},{8,9},{9,10},{10,1... | collective-permute-start | bytes 196616 | tf_op jit(solution)/shard_map/ppermute | solution.py:21
  62.0 2.0 collective-permute-start.7
  62.1 6.4 %collective-permute-start.8 = (f32[4,32,128]{2,1,0:T(8,128)S(1)}, f32[4,32,128]{2,1,0:T(8,128)S(1)}, u32[]{:S(2)}, u32[]{:S(2)}) collective-permute-start(f32[4,32,128]{2,1,0:T(8,128)S(1)} %get-tuple-element.351), channel_id=1, source_target_pairs={{0,1},{1,2},{2,3},{3,4},{4,5},{5,6},{6,7},{7,8},{8,9},{9,10},{10,1... | collective-permute-start | bytes 196616 | tf_op jit(solution)/shard_map/ppermute | solution.py:21
  77.0 6.4 %collective-permute-start.10 = (f32[4,32,128]{2,1,0:T(8,128)S(1)}, f32[4,32,128]{2,1,0:T(8,128)S(1)}, u32[]{:S(2)}, u32[]{:S(2)}) collective-permute-start(f32[4,32,128]{2,1,0:T(8,128)S(1)} %get-tuple-element.333), channel_id=1, source_target_pairs={{0,1},{1,2},{2,3},{3,4},{4,5},{5,6},{6,7},{7,8},{8,9},{9,10},{10,1... | collective-permute-start | bytes 196616 | tf_op jit(solution)/shard_map/ppermute | solution.py:21
  77.1 6.4 %collective-permute-start.9 = (f32[4,32,128]{2,1,0:T(8,128)S(1)}, f32[4,32,128]{2,1,0:T(8,128)S(1)}, u32[]{:S(2)}, u32[]{:S(2)}) collective-permute-start(f32[4,32,128]{2,1,0:T(8,128)S(1)} %get-tuple-element.332), channel_id=1, source_target_pairs={{1,0},{2,1},{3,2},{4,3},{5,4},{6,5},{7,6},{8,7},{9,8},{10,9},{11,1... | collective-permute-start | bytes 196616 | tf_op jit(solution)/shard_map/ppermute | solution.py:23
  92.6 6.4 %collective-permute-start.11 = (f32[4,32,128]{2,1,0:T(8,128)S(1)}, f32[4,32,128]{2,1,0:T(8,128)S(1)}, u32[]{:S(2)}, u32[]{:S(2)}) collective-permute-start(f32[4,32,128]{2,1,0:T(8,128)S(1)} %get-tuple-element.314), channel_id=1, source_target_pairs={{1,0},{2,1},{3,2},{4,3},{5,4},{6,5},{7,6},{8,7},{9,8},{10,9},{11,1... | collective-permute-start | bytes 196616 | tf_op jit(solution)/shard_map/ppermute | solution.py:23
  97.1 6.4 %collective-permute-start.12 = (f32[4,32,128]{2,1,0:T(8,128)S(1)}, f32[4,32,128]{2,1,0:T(8,128)S(1)}, u32[]{:S(2)}, u32[]{:S(2)}) collective-permute-start(f32[4,32,128]{2,1,0:T(8,128)S(1)} %get-tuple-element.315), channel_id=1, source_target_pairs={{0,1},{1,2},{2,3},{3,4},{4,5},{5,6},{6,7},{7,8},{8,9},{9,10},{10,1... | collective-permute-start | bytes 196616 | tf_op jit(solution)/shard_map/ppermute | solution.py:21
  112.8 2.0 collective-permute-start.13
  112.9 6.6 %collective-permute-start.14 = (f32[4,32,128]{2,1,0:T(8,128)S(1)}, f32[4,32,128]{2,1,0:T(8,128)S(1)}, u32[]{:S(2)}, u32[]{:S(2)}) collective-permute-start(f32[4,32,128]{2,1,0:T(8,128)S(1)} %get-tuple-element.297), channel_id=1, source_target_pairs={{0,1},{1,2},{2,3},{3,4},{4,5},{5,6},{6,7},{7,8},{8,9},{9,10},{10,1... | collective-permute-start | bytes 196616 | tf_op jit(solution)/shard_map/ppermute | solution.py:21
  129.7 6.4 %collective-permute-start.16 = (f32[4,32,128]{2,1,0:T(8,128)S(1)}, f32[4,32,128]{2,1,0:T(8,128)S(1)}, u32[]{:S(2)}, u32[]{:S(2)}) collective-permute-start(f32[4,32,128]{2,1,0:T(8,128)S(1)} %get-tuple-element.279), channel_id=1, source_target_pairs={{0,1},{1,2},{2,3},{3,4},{4,5},{5,6},{6,7},{7,8},{8,9},{9,10},{10,1... | collective-permute-start | bytes 196616 | tf_op jit(solution)/shard_map/ppermute | solution.py:21
  151.3 9.8 %all-to-all-start.1 = ((f32[16,1,128]{2,1,0:T(1,128)}), f32[16,1,128]{2,1,0:T(1,128)S(1)}, u32[]{:S(2)}, u32[]{:S(2)}) async-start(f32[16,1,128]{2,1,0:T(1,128)} %bitcast.23), calls=%async_computation.1 | async-start | bytes 16384 | tf_op jit(solution)/shard_map/all_to_all | solution.py:144
  171.4 22.7 %collective-permute-start.17 = (f32[4,32,128]{2,1,0:T(8,128)}, f32[4,32,128]{2,1,0:T(8,128)S(1)}, u32[]{:S(2)}, u32[]{:S(2)}) collective-permute-start(f32[4,32,128]{2,1,0:T(8,128)} %bitcast.26), channel_id=1, source_target_pairs={{1,0},{2,1},{3,2},{4,3},{5,4},{6,5},{7,6},{8,7},{9,8},{10,9},{11,1... | collective-permute-start | bytes 196616 | tf_op jit(solution)/shard_map/ppermute | solution.py:23
  171.4 22.7 %collective-permute-start.18 = (f32[4,32,128]{2,1,0:T(8,128)}, f32[4,32,128]{2,1,0:T(8,128)S(1)}, u32[]{:S(2)}, u32[]{:S(2)}) collective-permute-start(f32[4,32,128]{2,1,0:T(8,128)} %bitcast.27), channel_id=1, source_target_pairs={{0,1},{1,2},{2,3},{3,4},{4,5},{5,6},{6,7},{7,8},{8,9},{9,10},{10,1... | collective-permute-start | bytes 196616 | tf_op jit(solution)/shard_map/ppermute | solution.py:21
  197.4 5.9 %collective-permute-start.19 = (f32[4,32,128]{2,1,0:T(8,128)S(1)}, f32[4,32,128]{2,1,0:T(8,128)S(1)}, u32[]{:S(2)}, u32[]{:S(2)}) collective-permute-start(f32[4,32,128]{2,1,0:T(8,128)S(1)} %get-tuple-element.242), channel_id=1, source_target_pairs={{1,0},{2,1},{3,2},{4,3},{5,4},{6,5},{7,6},{8,7},{9,8},{10,9},{11,1... | collective-permute-start | bytes 196616 | tf_op jit(solution)/shard_map/ppermute | solution.py:23
  201.4 6.5 %collective-permute-start.20 = (f32[4,32,128]{2,1,0:T(8,128)S(1)}, f32[4,32,128]{2,1,0:T(8,128)S(1)}, u32[]{:S(2)}, u32[]{:S(2)}) collective-permute-start(f32[4,32,128]{2,1,0:T(8,128)S(1)} %get-tuple-element.243), channel_id=1, source_target_pairs={{0,1},{1,2},{2,3},{3,4},{4,5},{5,6},{6,7},{7,8},{8,9},{9,10},{10,1... | collective-permute-start | bytes 196616 | tf_op jit(solution)/shard_map/ppermute | solution.py:21
  209.2 6.4 %collective-permute-start.22 = (f32[4,32,128]{2,1,0:T(8,128)S(1)}, f32[4,32,128]{2,1,0:T(8,128)S(1)}, u32[]{:S(2)}, u32[]{:S(2)}) collective-permute-start(f32[4,32,128]{2,1,0:T(8,128)S(1)} %get-tuple-element.225), channel_id=1, source_target_pairs={{0,1},{1,2},{2,3},{3,4},{4,5},{5,6},{6,7},{7,8},{8,9},{9,10},{10,1... | collective-permute-start | bytes 196616 | tf_op jit(solution)/shard_map/ppermute | solution.py:21
  217.0 2.0 collective-permute-start.23
  217.0 6.4 %collective-permute-start.24 = (f32[4,32,128]{2,1,0:T(8,128)S(1)}, f32[4,32,128]{2,1,0:T(8,128)S(1)}, u32[]{:S(2)}, u32[]{:S(2)}) collective-permute-start(f32[4,32,128]{2,1,0:T(8,128)S(1)} %get-tuple-element.207), channel_id=1, source_target_pairs={{0,1},{1,2},{2,3},{3,4},{4,5},{5,6},{6,7},{7,8},{8,9},{9,10},{10,1... | collective-permute-start | bytes 196616 | tf_op jit(solution)/shard_map/ppermute | solution.py:21
  224.8 2.0 collective-permute-start.25
  224.9 6.4 %collective-permute-start.26 = (f32[4,32,128]{2,1,0:T(8,128)S(1)}, f32[4,32,128]{2,1,0:T(8,128)S(1)}, u32[]{:S(2)}, u32[]{:S(2)}) collective-permute-start(f32[4,32,128]{2,1,0:T(8,128)S(1)} %get-tuple-element.189), channel_id=1, source_target_pairs={{0,1},{1,2},{2,3},{3,4},{4,5},{5,6},{6,7},{7,8},{8,9},{9,10},{10,1... | collective-permute-start | bytes 196616 | tf_op jit(solution)/shard_map/ppermute | solution.py:21
  232.6 2.0 collective-permute-start.27
  232.7 6.4 %collective-permute-start.28 = (f32[4,32,128]{2,1,0:T(8,128)S(1)}, f32[4,32,128]{2,1,0:T(8,128)S(1)}, u32[]{:S(2)}, u32[]{:S(2)}) collective-permute-start(f32[4,32,128]{2,1,0:T(8,128)S(1)} %get-tuple-element.171), channel_id=1, source_target_pairs={{0,1},{1,2},{2,3},{3,4},{4,5},{5,6},{6,7},{7,8},{8,9},{9,10},{10,1... | collective-permute-start | bytes 196616 | tf_op jit(solution)/shard_map/ppermute | solution.py:21
  240.4 2.1 collective-permute-start.29
  240.5 6.4 %collective-permute-start.30 = (f32[4,32,128]{2,1,0:T(8,128)S(1)}, f32[4,32,128]{2,1,0:T(8,128)S(1)}, u32[]{:S(2)}, u32[]{:S(2)}) collective-permute-start(f32[4,32,128]{2,1,0:T(8,128)S(1)} %get-tuple-element.153), channel_id=1, source_target_pairs={{0,1},{1,2},{2,3},{3,4},{4,5},{5,6},{6,7},{7,8},{8,9},{9,10},{10,1... | collective-permute-start | bytes 196616 | tf_op jit(solution)/shard_map/ppermute | solution.py:21
  248.0 6.2 %collective-permute-start = (f32[4,32,128]{2,1,0:T(8,128)S(1)}, f32[4,32,128]{2,1,0:T(8,128)S(1)}, u32[]{:S(2)}, u32[]{:S(2)}) collective-permute-start(f32[4,32,128]{2,1,0:T(8,128)S(1)} %get-tuple-element.453), channel_id=1, source_target_pairs={{0,4},{1,5},{2,6},{3,7},{4,8},{5,9},{6,10},{7,11},{8,12},{9,13},{1... | collective-permute-start | bytes 196616 | tf_op jit(solution)/shard_map/while/body/eval_jaxpr/ppermute | solution.py:33
  254.3 6.1 %collective-permute-start = (f32[4,32,128]{2,1,0:T(8,128)S(1)}, f32[4,32,128]{2,1,0:T(8,128)S(1)}, u32[]{:S(2)}, u32[]{:S(2)}) collective-permute-start(f32[4,32,128]{2,1,0:T(8,128)S(1)} %get-tuple-element.453), channel_id=1, source_target_pairs={{0,4},{1,5},{2,6},{3,7},{4,8},{5,9},{6,10},{7,11},{8,12},{9,13},{1... | collective-permute-start | bytes 196616 | tf_op jit(solution)/shard_map/while/body/eval_jaxpr/ppermute | solution.py:33
  260.4 6.1 %collective-permute-start = (f32[4,32,128]{2,1,0:T(8,128)S(1)}, f32[4,32,128]{2,1,0:T(8,128)S(1)}, u32[]{:S(2)}, u32[]{:S(2)}) collective-permute-start(f32[4,32,128]{2,1,0:T(8,128)S(1)} %get-tuple-element.453), channel_id=1, source_target_pairs={{0,4},{1,5},{2,6},{3,7},{4,8},{5,9},{6,10},{7,11},{8,12},{9,13},{1... | collective-permute-start | bytes 196616 | tf_op jit(solution)/shard_map/while/body/eval_jaxpr/ppermute | solution.py:33
  (41 other events, 112.5 us)
where the time goes:
time: 269 us; the launch traced here: 268 us
  local copies, waits for them, and re-layouts  88.9 us (33%)
  waiting for transfers between devices  88.1 us (33%)
  other arithmetic  33.2 us (12%)
  starting transfers between devices  28.4 us (11%)
  matrix products  18.3 us (7%)
  blocking collectives  8.98 us (3%)
    ppermute x15, waiting for transfers between devices, extended_2(): lax.ppermute(tail, axis, [(i, (i + 1) % count) for i in range(count)])  55.2 us
    slice x120, local copies, waits for them, and re-layouts, shifted(): lax.slice_in_dim(values, offset, length, axis=axis_pos)  53.9 us
    add x14, other arithmetic, inject(): return wavefield + added.reshape(wavefield.shape)  25.2 us
    ppermute x15, starting transfers between devices, extended_2(): lax.ppermute(head, axis, [((i + 1) % count, i) for i in range(count)])  19.4 us
    ppermute x3, waiting for transfers between devices, shifted_2(): return lax.ppermute(value, axis, pairs)  18.1 us
    dot_general x8, matrix products, inject(): lax.dot_general(weighted, col_table, (((0,), (0,)), ((), ())), precision=...  14.3 us
    mul x16, local copies, waits for them, and re-layouts, inject(): weighted = row_table * amounts[:, None]  12.8 us
    unnamed x80, local copies, waits for them, and re-layouts  10.6 us
  transfers between devices with their start and end apart: 34, of which 23 were waited for; matrix products, arithmetic and copies ran while one was open for 18% of the time, Pallas kernels for 0%

commit v1 on v0

v1 whole, which is shorter than its diff:
```python
import functools

import jax
import jax.numpy as jnp
import numpy as np
from jax import lax
from jax.experimental import pallas as pl
from jax.experimental.pallas import tpu as pltpu
from jax.sharding import PartitionSpec as P

NT = 8
PIECES = 4
RAD = 4
ROUNDS = (4, 4)
SCALE = 5040.0
CENTER = -43050.0
WEIGHTS = (8064.0, -1008.0, 128.0, -9.0)
GROUP = 8
HALO = RAD * (NT - 1)
BF = jnp.bfloat16
F32 = jnp.float32

VMEM = pl.BlockSpec(memory_space=pltpu.VMEM)
SMEM = pl.BlockSpec(memory_space=pltpu.SMEM)


def band(size):
    out = np.zeros((size, size), np.float32)
    for k, weight in enumerate(WEIGHTS, 1):
        out += weight * (np.eye(size, k=k) + np.eye(size, k=-k))
    return out


def matrices(span_y, span_z):
    along_z = np.concatenate([band(span_z)] * 2, axis=0)
    along_y = np.kron(np.eye(GROUP), band(span_y))
    return jnp.asarray(along_z, BF), jnp.asarray(along_y, BF)


def split(values):
    high = values.astype(BF)
    low = (values - high.astype(F32)).astype(BF)
    return high, low


def dot(a, b, dims=(((1,), (0,)), ((), ()))):
    return lax.dot_general(a, b, dims, preferred_element_type=F32)


def advance(cur, old, model, zmat, ymat, first, last, model_shift):
    span_y, span_z = cur.shape[1:]
    zmat, ymat = zmat[...], ymat[...]
    for base in range(first, last, GROUP):
        group = cur[base : base + GROUP].reshape(GROUP * span_y, span_z)
        pair = jnp.concatenate(split(group), axis=1)
        z_part = dot(pair, zmat)
        y_part = dot(ymat, pair)
        for i in range(GROUP):
            x = base + i
            rows = slice(i * span_y, (i + 1) * span_y)
            here = cur[x]
            total = CENTER * here + z_part[rows] + y_part[rows, :span_z] + y_part[rows, span_z:]
            for k, weight in enumerate(WEIGHTS, 1):
                total = total + weight * (cur[x + k] + cur[x - k])
            old[x] = 2.0 * here - old[x] + model[x + model_shift] * total


def add_source(field, pack, step, own, block, halo, rows):
    span_y, span_z = field.shape[1:]
    cell = pack[NT].astype(jnp.int32)
    amount = pack[step]
    plane = own + block * rows + cell // (span_y * span_z)
    y = (cell // span_z) % span_y
    z = cell % span_z

    @pl.when((plane >= own - halo) & (plane < own + rows + halo))
    def _():
        tile = pl.ds(pl.multiple_of((y // 8) * 8, 8), 8)
        sub = lax.broadcasted_iota(jnp.int32, (8, span_z), 0)
        lane = lax.broadcasted_iota(jnp.int32, (8, span_z), 1)
        hit = (sub == y % 8) & (lane == z)
        field[plane, tile, :] = field[plane, tile, :] + jnp.where(hit, amount, 0.0)


def prepare_kernel(courant, cells, order, observed, model_out, pack_out):
    rows = 16
    piece = lax.rem(lax.axis_index("shot"), PIECES)
    period = courant.shape[0]
    window = model_out.shape[0]
    for chunk in range(0, window, RAD):
        source = lax.rem(piece * rows - HALO + chunk + period, period)
        model_out[chunk : chunk + RAD] = courant[pl.ds(source, RAD)] * (1.0 / SCALE)
    count = cells.shape[1]
    wanted = order[...]
    cell = cells[...]
    high = (cell // 256).astype(F32).astype(BF)
    low = (cell % 256).astype(F32).astype(BF)
    which = lax.broadcasted_iota(jnp.int32, (16, count), 0)
    digits = jnp.where(which == 0, high.astype(F32), jnp.where(which == 1, low.astype(F32), 0.0)).astype(BF)
    for j in range(0, count, 256):
        index = lax.broadcasted_iota(jnp.int32, (count, 256), 0)
        chosen = jnp.where(index == wanted[:, j : j + 256], 1.0, 0.0).astype(BF)
        found = dot(digits, chosen)
        ordered = found[0:1] * 256.0 + found[1:2]
        pack_out[j // 128 : j // 128 + 1] = ordered[:, :128]
        pack_out[j // 128 + 1 : j // 128 + 2] = ordered[:, 128:]
    pack_out[count // 128 :] = observed[...]


def cell_row(pack, count):
    parts = [pack[j : j + 1] for j in range(count // 128)]
    return jnp.concatenate(parts, axis=1).astype(jnp.int32)


def pick_tables(cells, table_rows):
    count = cells.shape[1]
    column = jnp.transpose(jnp.broadcast_to(cells.astype(F32), (128, count)))
    column = column.astype(jnp.int32)
    row_of = jnp.concatenate([column // 128] * (table_rows // 128), axis=1)
    lane_of = jnp.concatenate([column % 128] * 2, axis=1)
    lanes = lax.broadcasted_iota(jnp.int32, (count, table_rows), 1)
    rows_table = jnp.where(row_of == lanes, 1.0, 0.0).astype(BF)
    lanes2 = lax.broadcasted_iota(jnp.int32, (count, 256), 1) % 128
    lane_table = jnp.where(lane_of == lanes2, 1.0, 0.0)
    return rows_table, lane_table


def extract(field, step, rows_table, lane_table):
    rows, span_y, span_z = field.shape
    pair = jnp.concatenate(split(field.reshape(rows * span_y, span_z)), axis=1)
    which = lax.broadcasted_iota(jnp.int32, (16, 2 * span_z), 0)
    ones = jnp.where(which == step, 1.0, 0.0).astype(BF)
    out = []
    for j in range(0, rows_table.shape[0], 256):
        found = dot(rows_table[j : j + 256], pair)
        kept = (found * lane_table[j : j + 256]).astype(BF)
        out.append(dot(ones, kept, (((1,), (1,)), ((), ()))))
    return jnp.concatenate(out, axis=1)


def forward_round(
    index, refs_in, zmat, ymat, model, pack_left, pack_own, pack_right, fields, buf_a, buf_b
):
    steps = ROUNDS[index]
    done = sum(ROUNDS[:index])
    rows = 16
    own = RAD * steps
    cur, old = buf_a, buf_b
    wide, narrow = RAD * steps, RAD * (steps - 1)
    if index == 0:
        now, before, now_l, now_r, before_l, before_r = refs_in
        cur[own : own + rows] = now[...]
        old[own : own + rows] = before[...]
        cur[own - wide : own] = now_l[...]
        cur[own + rows : own + rows + wide] = now_r[...]
        if narrow:
            old[own - narrow : own] = before_l[...]
            old[own + rows : own + rows + narrow] = before_r[...]
    else:
        earlier, known, got_l, got_r = refs_in
        cur[own : own + rows] = earlier[earlier.shape[0] - 1]
        old[own : own + rows] = earlier[earlier.shape[0] - 2]
        cur[own - wide : own] = got_l[0:wide]
        cur[own + rows : own + rows + wide] = got_r[0:wide]
        if narrow:
            old[own - RAD : own] = known[0]
            old[own + rows : own + rows + RAD] = known[1]
        if narrow > RAD:
            old[own - narrow : own - RAD] = got_l[wide:]
            old[own + rows + RAD : own + rows + narrow] = got_r[wide:]
    for step in range(steps):
        halo = RAD * (steps - 1 - step)
        advance(cur, old, model, zmat, ymat, own - halo, own + rows + halo, HALO - own)
        for block, pack in ((-1, pack_left), (0, pack_own), (1, pack_right)):
            if halo or block == 0:
                add_source(old, pack, done + step, own, block, halo, rows)
        fields[step] = old[own : own + rows]
        cur, old = old, cur
    return cur, old, own


def send_shapes(index):
    steps = ROUNDS[index]
    return RAD * steps + RAD * max(steps - 2, 0)


def forward_kernel(index, *refs):
    take = 6 if index == 0 else 4
    refs_in, refs = refs[:take], refs[take:]
    zmat, ymat, model, pack_left, pack_own, pack_right, fields, known, send_l, send_r, buf_a, buf_b = refs
    cur, old, own = forward_round(
        index, refs_in, zmat, ymat, model, pack_left, pack_own, pack_right, fields, buf_a, buf_b
    )
    rows = 16
    known[0] = old[own - RAD : own]
    known[1] = old[own + rows : own + rows + RAD]
    wide = RAD * ROUNDS[index + 1]
    inner = wide - RAD
    send_l[0:wide] = cur[own : own + wide]
    send_r[0:wide] = cur[own + rows - wide : own + rows]
    if inner > RAD:
        send_l[wide:] = old[own + RAD : own + inner]
        send_r[wide:] = old[own + rows - inner : own + rows - RAD]


def tables_kernel(count, *refs):
    (pack, *fields), (rows_out, lanes_out, traces) = refs[:-3], refs[-3:]
    rows_table, lane_table = pick_tables(cell_row(pack, count), rows_out.shape[1])
    rows_out[...] = rows_table
    lanes_out[...] = lane_table
    total = jnp.zeros((16, count), F32)
    step = 0
    for group in fields:
        for i in range(group.shape[0]):
            total = total + extract(group[i], step, rows_table, lane_table)
            step += 1
    traces[...] = total


def last_kernel(index, *refs):
    take = 6 if index == 0 else 4
    refs_in, refs = refs[:take], refs[take:]
    zmat, ymat, model, pack_left, pack_own, pack_right = refs[:6]
    rows_table, lane_table, traces, observed = refs[6:10]
    fields, adj, buf_a, buf_b = refs[10:]
    forward_round(index, refs_in, zmat, ymat, model, pack_left, pack_own, pack_right, fields, buf_a, buf_b)
    total = traces[...]
    done = sum(ROUNDS[:index])
    rows_table = rows_table[...]
    lane_table = lane_table[...]
    for step in range(ROUNDS[index]):
        total = total + extract(fields[step], done + step, rows_table, lane_table)
    adj[...] = total[0:NT] - observed[...]


def inject_tables_kernel(count, packs, rows_out, lanes_out):
    me = lax.axis_index("shot")
    devices = packs.shape[0]
    for block in range(5):
        cells = cell_row(packs.at[lax.rem(me + block - 2 + devices, devices)], count)
        sub = lax.broadcasted_iota(jnp.int32, (rows_out.shape[1], count), 0)
        rows_out[block] = jnp.where(sub == cells // 128, 1.0, 0.0).astype(BF)
        lanes_out[block : block + 1] = cells % 128


def adjoint_kernel(field_groups, slabs, count, *refs):
    fields = []
    for ref in refs[:field_groups]:
        fields += [ref.at[i] for i in range(ref.shape[0])]
    refs = refs[field_groups:]
    zmat, ymat, model, rows_table, lanes, *adjs = refs[:10]
    outs = refs[10 : 10 + slabs]
    buf_a, buf_b, image = refs[10 + slabs :]
    rows = 16
    own = HALO
    span_y, span_z = buf_a.shape[1:]

    def inject(field, number):
        halo = RAD * (NT - number)
        step = NT - number
        for block in range(-2, 3):
            begin = own + block * rows
            first = max(begin, own - halo)
            last = min(begin + rows, own + rows + halo)
            if first >= last:
                continue
            amounts = adjs[block + 2][step : step + 1]
            high = amounts.astype(BF).astype(F32)
            low = amounts - high
            sub = lax.broadcasted_iota(jnp.int32, (span_z, count), 0)
            hit = sub == lanes[block + 2 : block + 3]
            both = jnp.concatenate(
                [jnp.where(hit, high, 0.0).astype(BF), jnp.where(hit, low, 0.0).astype(BF)], axis=0
            )
            table = rows_table[block + 2, (first - begin) * span_y : (last - begin) * span_y, :]
            added = dot(table, both, (((1,), (1,)), ((), ())))
            added = (added[:, :span_z] + added[:, span_z:]).reshape(last - first, span_y, span_z)
            if number == 1:
                field[first:last] = added
            else:
                field[first:last] = field[first:last] + added

    cur, old = buf_a, buf_b
    inject(cur, 1)
    old[...] = jnp.zeros(old.shape, F32)
    image[...] = cur[own : own + rows] * fields[NT - 1][...]
    for number in range(2, NT + 1):
        halo = RAD * (NT - number)
        advance(cur, old, model, zmat, ymat, own - halo, own + rows + halo, 0)
        inject(old, number)
        image[...] = image[...] + old[own : own + rows] * fields[NT - number][...]
        cur, old = old, cur
    mine = lax.axis_index("shot") // PIECES
    thick = rows // slabs
    for i in range(slabs):
        outs[i][...] = image[pl.ds(lax.rem(mine + i, slabs) * thick, thick)]


def call(kernel, outs, ins, specs=None, scratch=(), cost=(1e6, 1e6), name=None):
    return pl.pallas_call(
        kernel,
        out_shape=outs,
        in_specs=specs or [VMEM] * len(ins),
        out_specs=jax.tree.map(lambda _: VMEM, outs),
        scratch_shapes=list(scratch),
        compiler_params=pltpu.CompilerParams(vmem_limit_bytes=48 * 1024 * 1024),
        cost_estimate=pl.CostEstimate(flops=int(cost[0]), bytes_accessed=int(cost[1]), transcendentals=0),
        name=name,
    )(*ins)


def shifted(value, steps):
    count = lax.axis_size("shot")
    return lax.ppermute(value, "shot", [(i, (i + steps) % count) for i in range(count)])


def per_device(
    courant_sq, wave_now, wave_before, wavelet, source_cell, receiver_cell, send_order, observed
):
    devices = lax.axis_size("shot")
    me = lax.axis_index("shot")
    rows, span_y, span_z = wave_now.shape
    count = receiver_cell.shape[0]
    per_owner = count // devices
    table_rows = rows * span_y
    plane = (span_y, span_z)
    zmat, ymat = matrices(span_y, span_z)

    wide = RAD * ROUNDS[0]
    narrow = wide - RAD
    pack_own = jnp.concatenate([wavelet.reshape(-1), source_cell.astype(F32)])
    pack_left, pack_right = shifted(pack_own, 1), shifted(pack_own, -1)
    now_l, now_r = shifted(wave_now[rows - wide :], 1), shifted(wave_now[:wide], -1)
    before_l, before_r = shifted(wave_before[rows - narrow :], 1), shifted(wave_before[:narrow], -1)

    model, pack = call(
        prepare_kernel,
        (
            jax.ShapeDtypeStruct((rows + 2 * HALO,) + plane, F32),
            jax.ShapeDtypeStruct((count // 128 + devices, 128), F32),
        ),
        (courant_sq, receiver_cell.reshape(1, count), send_order.reshape(1, count), observed),
        name="prepare",
    )
    packs = lax.all_gather(pack, "shot", axis=0, tiled=False)

    common = (zmat, ymat, model, pack_left, pack_own, pack_right)
    common_specs = [VMEM] * 3 + [SMEM] * 3
    field_list = []
    ins = (wave_now, wave_before, now_l, now_r, before_l, before_r)
    for index in range(len(ROUNDS) - 1):
        window = rows + 2 * RAD * ROUNDS[index]
        sent = send_shapes(index + 1)
        fields, known, send_l, send_r = call(
            functools.partial(forward_kernel, index),
            (
                jax.ShapeDtypeStruct((ROUNDS[index], rows) + plane, F32),
                jax.ShapeDtypeStruct((2, RAD) + plane, F32),
                jax.ShapeDtypeStruct((sent,) + plane, F32),
                jax.ShapeDtypeStruct((sent,) + plane, F32),
            ),
            ins + common,
            specs=[VMEM] * len(ins) + common_specs,
            scratch=[pltpu.VMEM((window,) + plane, F32)] * 2,
            name="forward",
        )
        field_list.append(fields)
        ins = (fields, known, shifted(send_r, 1), shifted(send_l, -1))

    rows_table, lane_table, traces = call(
        functools.partial(tables_kernel, count),
        (
            jax.ShapeDtypeStruct((count, table_rows), BF),
            jax.ShapeDtypeStruct((count, 256), F32),
            jax.ShapeDtypeStruct((16, count), F32),
        ),
        (pack, *field_list),
        name="traces",
    )
    mine = lax.dynamic_index_in_dim(packs[:, count // 128 :], me, 1, keepdims=False)
    target = mine.reshape(devices, NT, per_owner).transpose(1, 0, 2).reshape(NT, count)
    inject_rows, inject_lanes = call(
        functools.partial(inject_tables_kernel, count),
        (
            jax.ShapeDtypeStruct((5, table_rows, count), BF),
            jax.ShapeDtypeStruct((5, count), jnp.int32),
        ),
        (packs,),
        name="inject_tables",
    )

    index = len(ROUNDS) - 1
    window = rows + 2 * RAD * ROUNDS[index]
    fields, adj = call(
        functools.partial(last_kernel, index),
        (
            jax.ShapeDtypeStruct((ROUNDS[index], rows) + plane, F32),
            jax.ShapeDtypeStruct((NT, count), F32),
        ),
        ins + common + (rows_table, lane_table, traces, target),
        specs=[VMEM] * len(ins) + common_specs + [VMEM] * 4,
        scratch=[pltpu.VMEM((window,) + plane, F32)] * 2,
        name="forward_last",
    )
    field_list.append(fields)

    adjs = [shifted(adj, 2), shifted(adj, 1), adj, shifted(adj, -1), shifted(adj, -2)]
    slabs = devices // PIECES
    thick = rows // slabs
    parts = call(
        functools.partial(adjoint_kernel, len(field_list), slabs, count),
        tuple(jax.ShapeDtypeStruct((thick,) + plane, F32) for _ in range(slabs)),
        (*field_list, zmat, ymat, model, inject_rows, inject_lanes, *adjs),
        scratch=[pltpu.VMEM((rows + 2 * HALO,) + plane, F32)] * 2 + [pltpu.VMEM((rows,) + plane, F32)],
        name="adjoint",
    )
    total = parts[0]
    for i in range(1, slabs):
        total = total + shifted(parts[i], i * PIECES)
    return total


def solution(mesh):
    return jax.shard_map(
        per_device,
        mesh=mesh,
        in_specs=(
            P("groups", None, None),
            P(("groups", "shot"), None, None),
            P(("groups", "shot"), None, None),
            P(("groups", "shot"), None),
            P(("groups", "shot")),
            P(("groups", "shot")),
            P(("groups", "shot")),
            P(("groups", "shot"), None),
        ),
        out_specs=P(("groups", "shot"), None, None),
        check_vma=False,
    )
```

time: 269 us -> 88 us (0.33)
  local copies, waits for them, and re-layouts: 88.9 us -> 12.8 us
  waiting for transfers between devices: 88.1 us -> 14.9 us
  other arithmetic: 33.2 us -> 1.38 us
  matrix products: 18.3 us -> 0 us
  Pallas kernels: 0 us -> 14.4 us
  blocking collectives: 8.98 us -> 21.6 us
  starting transfers between devices: 28.4 us -> 21.7 us
    ppermute x33 -> x15, waiting for transfers between devices: 81.9 us -> 14.9 us  [shifted(): lax.ppermute(value, 'shot', [(i, (i + steps) % count) for i in range(coun...]
    slice x137 -> x2, local copies, waits for them, and re-layouts: 57.1 us -> 1.72 us  [the longest x1 1.05 us: per_device(): wave_before[:narrow]]
    add x18 -> x1, other arithmetic: 26.3 us -> 0.65 us  [per_device(): total = total + shifted(parts[i], i * PIECES)]
    all_gather x0 -> x1, blocking collectives: none -> 21.6 us  [per_device(): packs = lax.all_gather(pack, 'shot', axis=0, tiled=False)]
    dot_general x16 -> x0, matrix products: 18.3 us -> none  [the longest x8 14.3 us: inject(): lax.dot_general(weighted, col_table, (((0,), (0,)), ((), ())), precision=...]
    pallas_call x0 -> x6, Pallas kernels: none -> 14.4 us  [call(): pl.pallas_call(kernel, out_shape=outs, in_specs=specs or [VMEM] * len(ins...]
    mul x16 -> x0, local copies, waits for them, and re-layouts: 12.8 us -> none  [inject(): weighted = row_table * amounts[:, None]]
    all_to_all x1 -> x0, blocking collectives: 8.98 us -> none  [per_device(): lax.all_to_all(packed, 'shot', split_axis=0, concat_axis=0, tiled=True)]
  transfers between devices with their start and end apart: 34 -> 15, of which waited for: 23 -> 6; matrix products, arithmetic and copies ran while one was open for 18% -> 9% of each run, Pallas kernels for 0% -> 2%
where the time goes in v1:
time: 88 us; the launch traced here: 87.5 us
  starting transfers between devices  21.7 us (25%)
  blocking collectives  21.6 us (25%)
  waiting for transfers between devices  14.9 us (17%)
  Pallas kernels  14.4 us (16%)
  local copies, waits for them, and re-layouts  12.8 us (15%)
  other arithmetic  1.38 us (2%)
    ppermute x15, starting transfers between devices, shifted(): lax.ppermute(value, 'shot', [(i, (i + steps) % count) for i in range(coun...  21.7 us
    all_gather x1, blocking collectives, per_device(): packs = lax.all_gather(pack, 'shot', axis=0, tiled=False)  21.6 us
    ppermute x15, waiting for transfers between devices, shifted(): lax.ppermute(value, 'shot', [(i, (i + steps) % count) for i in range(coun...  14.9 us
    pallas_call x6, Pallas kernels, call(): pl.pallas_call(kernel, out_shape=outs, in_specs=specs or [VMEM] * len(ins...  14.4 us
    unnamed x26, local copies, waits for them, and re-layouts  5.27 us
    reshape x2, local copies, waits for them, and re-layouts, per_device(): mine.reshape(devices, NT, per_owner).transpose(1, 0, 2).reshape(NT, count)  2.93 us
  transfers between devices with their start and end apart: 15, of which 6 were waited for; matrix products, arithmetic and copies ran while one was open for 9% of the time, Pallas kernels for 2%

profile of v1, /device:TPU:0, one launch (start us, length us, event | category | flops | bytes accessed | tf_op | source)
XLA Modules:
  0.0 87.5 jit_solution(17967642864594338839)
XLA Ops:
  0.5 5.1 %collective-permute-start.1 = (f32[16,32,128]{2,1,0:T(8,128)}, f32[16,32,128]{2,1,0:T(8,128)S(1)}, u32[]{:S(2)}, u32[]{:S(2)}) collective-permute-start(f32[16,32,128]{2,1,0:T(8,128)} %refs_0_.1), channel_id=1, source_target_pairs={{0,15},{1,0},{2,1},{3,2},{4,3},{5,4},{6,5},{7,6},{8,7},{9,8},{10,9... | collective-permute-start | bytes 786440 | tf_op jit(solution)/shard_map/ppermute | solution.py:314
  5.6 1.0 %fusion = (f32[12,32,128]{2,1,0:T(8,128)S(1)}, f32[12,32,128]{2,1,0:T(8,128)S(1)}) fusion(f32[16,32,128]{2,1,0:T(8,128)} %refs_1_.1), kind=kLoop, calls=%fused_computation.3 | loop fusion | bytes 786432 | tf_op jit(solution)/shard_map/slice | solution.py:334
  6.6 0.7 collective-permute-start.3
  8.0 0.7 pad_maximum_fusion.refs_10_.refs_8_
  8.7 4.4 %collective-permute-start.5 = (f32[9]{0:T(128)S(1)}, f32[9]{0:T(128)S(1)}, u32[]{:S(2)}, u32[]{:S(2)}) collective-permute-start(f32[9]{0:T(128)S(1)} %pad_maximum_fusion.refs_10_.refs_8_), channel_id=1, source_target_pairs={{0,15},{1,0},{2,1},{3,2},{4,3},{5,4},{6,5},{7,6},{8,7},{9,8},{10,9... | collective-permute-start | bytes 116 | tf_op jit(solution)/shard_map/ppermute | solution.py:314
  13.2 1.2 %copy-done.2 = f32[64,32,128]{2,1,0:T(8,128)S(1)} copy-done((f32[64,32,128]{2,1,0:T(8,128)S(1)}, f32[64,32,128]{2,1,0:T(8,128)}, u32[]{:S(2)}) %copy-start.2) | copy-done | bytes 1048600
  14.4 0.7 copy-done.6
  15.1 0.7 copy-done.11
  15.8 0.7 copy-done.12
  16.8 5.6 %collective-permute-done.4.refs_9_.refs_7_ = f32[9]{0:T(128)S(1)} collective-permute-done((f32[9]{0:T(128)S(1)}, f32[9]{0:T(128)S(1)}, u32[]{:S(2)}, u32[]{:S(2)}) %collective-permute-start.4) | collective-permute-done | bytes 68 | tf_op jit(solution)/shard_map/ppermute | solution.py:314
  22.5 3.8 %forward.1 = (f32[4,16,32,128]{3,2,1,0:T(8,128)S(1)}, f32[2,4,32,128]{3,2,1,0:T(8,128)S(1)}, f32[24,32,128]{2,1,0:T(8,128)}, f32[24,32,128]{2,1,0:T(8,128)}) custom-call(f32[16,32,128]{2,1,0:T(8,128)S(1)} %copy-done.4, f32[16,32,128]{2,1,0:T(8,128)S(1)} %copy-done, f32[16,32,128]{2,1,0:T(8,128)S(1)} %collective-permute-done.refs_2_, ...), custom_call_target="tpu_custom_call" | custom-call | flops 1000000 | bytes 1000000 | tf_op jit(solution)/shard_map/forward/pallas_call | solution.py:300
  26.3 4.4 %collective-permute-start.7 = (f32[24,32,128]{2,1,0:T(8,128)}, f32[24,32,128]{2,1,0:T(8,128)S(1)}, u32[]{:S(2)}, u32[]{:S(2)}) collective-permute-start(f32[24,32,128]{2,1,0:T(8,128)} %get-tuple-element.26), channel_id=1, source_target_pairs={{0,15},{1,0},{2,1},{3,2},{4,3},{5,4},{6,5},{7,6},{8,7},{9,8},{10,9... | collective-permute-start | bytes 1179656 | tf_op jit(solution)/shard_map/ppermute | solution.py:314
  30.8 21.6 %all-gather.1.packs = f32[16,18,128]{2,1,0:T(8,128)S(1)} all-gather(f32[1,18,128]{2,1,0:T(8,128)S(1)} %bitcast.5), channel_id=2, replica_groups=mesh['groups'=2,'shot'=16] {'shot'}, dimensions={0}, use_global_device_ids=true | all-gather | bytes 156672 | tf_op jit(solution)/shard_map/all_gather | solution.py:345
  52.3 0.7 slice.12
  53.0 1.5 %dynamic-slice_reduce_fusion = f32[16,128]{1,0:T(8,128)} fusion(f32[16,16,128]{2,1,0:T(8,128)} %slice.12, s32[]{:T(128)S(6)} %select_n.4), kind=kLoop, calls=%fused_computation.1 | loop fusion | bytes 16388 | tf_op jit(solution)/shard_map/jit(dynamic_index_in_dim)/dynamic_slice | solution.py:380
  54.4 1.4 %reshape.19 = f32[16,8,16]{2,1,0:T(8,128)} reshape(f32[16,128]{1,0:T(8,128)} %dynamic-slice_reduce_fusion) | data formatting | bytes 16384 | tf_op jit(solution)/shard_map/reshape | solution.py:381
  55.8 1.5 %copy.12 = f32[8,16,16]{2,1,0:T(8,128)} copy(f32[8,16,16]{2,0,1:T(8,128)} %bitcast.8) | data formatting | bytes 16384 | tf_op jit(solution)/shard_map/transpose | solution.py:381
  57.3 1.5 %reshape.20.refs_13_ = f32[8,256]{1,0:T(8,128)} reshape(f32[8,16,16]{2,1,0:T(8,128)} %copy.12) | data formatting | bytes 16384 | tf_op jit(solution)/shard_map/reshape | solution.py:381
  58.8 0.8 traces.1
  59.7 0.7 copy-done.5
  60.4 0.7 copy-done.8
  61.7 3.7 %forward_last.1 = (f32[4,16,32,128]{3,2,1,0:T(8,128)S(1)}, f32[8,256]{1,0:T(8,128)S(1)}) custom-call(f32[4,16,32,128]{3,2,1,0:T(8,128)S(1)} %get-tuple-element.23.refs_1_.refs_0_, f32[2,4,32,128]{3,2,1,0:T(8,128)S(1)} %get-tuple-element.24.refs_1_, f32[24,32,128]{2,1,0:T(8,128)S(1)} %collective-permute-done.6.refs_2_, ...), custom_call_target="tpu_custom_call" | custom-call | flops 1000000 | bytes 1000000 | tf_op jit(solution)/shard_map/forward_last/pallas_call | solution.py:300
  65.9 2.0 %collective-permute-start.8 = (f32[8,256]{1,0:T(8,128)S(1)}, f32[8,256]{1,0:T(8,128)S(1)}, u32[]{:S(2)}, u32[]{:S(2)}) collective-permute-start(f32[8,256]{1,0:T(8,128)S(1)} %get-tuple-element.34.refs_9_), channel_id=1, source_target_pairs={{0,2},{1,3},{2,4},{3,5},{4,6},{5,7},{6,8},{7,9},{8,10},{9,11},{10,... | collective-permute-start | bytes 24584 | tf_op jit(solution)/shard_map/ppermute | solution.py:314
  68.3 0.8 collective-permute-done.11.refs_11_
  69.1 2.2 %collective-permute-done.9.refs_8_ = f32[8,256]{1,0:T(8,128)S(1)} collective-permute-done((f32[8,256]{1,0:T(8,128)S(1)}, f32[8,256]{1,0:T(8,128)S(1)}, u32[]{:S(2)}, u32[]{:S(2)}) %collective-permute-start.9) | collective-permute-done | bytes 8224 | tf_op jit(solution)/shard_map/ppermute | solution.py:314
  71.3 1.0 %collective-permute-done.8.refs_7_ = f32[8,256]{1,0:T(8,128)S(1)} collective-permute-done((f32[8,256]{1,0:T(8,128)S(1)}, f32[8,256]{1,0:T(8,128)S(1)}, u32[]{:S(2)}, u32[]{:S(2)}) %collective-permute-start.8) | collective-permute-done | bytes 8224 | tf_op jit(solution)/shard_map/ppermute | solution.py:314
  72.3 5.5 %adjoint.1 = (f32[4,32,128]{2,1,0:T(8,128)S(1)}, f32[4,32,128]{2,1,0:T(8,128)S(1)}, f32[4,32,128]{2,1,0:T(8,128)S(1)}, f32[4,32,128]{2,1,0:T(8,128)S(1)}) custom-call(f32[4,16,32,128]{3,2,1,0:T(8,128)S(1)} %get-tuple-element.23.refs_1_.refs_0_, f32[4,16,32,128]{3,2,1,0:T(8,128)S(1)} %get-tuple-element.31.refs_1_, bf16[256,128]{1,0:T(8,128)(2,1)S(1)} %copy-done.3, ...), custom_call_target="tpu_custom_call" | custom-call | flops 1000000 | bytes 1000000 | tf_op jit(solution)/shard_map/adjoint/pallas_call | solution.py:300
  77.8 1.0 %collective-permute-start.12 = (f32[4,32,128]{2,1,0:T(8,128)S(1)}, f32[4,32,128]{2,1,0:T(8,128)S(1)}, u32[]{:S(2)}, u32[]{:S(2)}) collective-permute-start(f32[4,32,128]{2,1,0:T(8,128)S(1)} %get-tuple-element.36), channel_id=1, source_target_pairs={{0,4},{1,5},{2,6},{3,7},{4,8},{5,9},{6,10},{7,11},{8,12},{9,13},{1... | collective-permute-start | bytes 196616 | tf_op jit(solution)/shard_map/ppermute | solution.py:314
  78.8 2.9 %collective-permute-start.14 = (f32[4,32,128]{2,1,0:T(8,128)S(1)}, f32[4,32,128]{2,1,0:T(8,128)S(1)}, u32[]{:S(2)}, u32[]{:S(2)}) collective-permute-start(f32[4,32,128]{2,1,0:T(8,128)S(1)} %get-tuple-element.38), channel_id=1, source_target_pairs={{0,12},{1,13},{2,14},{3,15},{4,0},{5,1},{6,2},{7,3},{8,4},{9,5},{1... | collective-permute-start | bytes 196616 | tf_op jit(solution)/shard_map/ppermute | solution.py:314
  81.7 3.0 %collective-permute-done.12 = f32[4,32,128]{2,1,0:T(8,128)S(1)} collective-permute-done((f32[4,32,128]{2,1,0:T(8,128)S(1)}, f32[4,32,128]{2,1,0:T(8,128)S(1)}, u32[]{:S(2)}, u32[]{:S(2)}) %collective-permute-start.12) | collective-permute-done | bytes 65568 | tf_op jit(solution)/shard_map/ppermute | solution.py:314
  84.6 2.2 %collective-permute-done.13 = f32[4,32,128]{2,1,0:T(8,128)S(1)} collective-permute-done((f32[4,32,128]{2,1,0:T(8,128)S(1)}, f32[4,32,128]{2,1,0:T(8,128)S(1)}, u32[]{:S(2)}, u32[]{:S(2)}) %collective-permute-start.13) | collective-permute-done | bytes 65568 | tf_op jit(solution)/shard_map/ppermute | solution.py:314
  86.9 0.6 add_add_fusion
  (39 shorter events, 2.3 us)
Async XLA Ops:
  0.0 22.4 %copy-start.1 = (bf16[256,256]{1,0:T(8,128)(2,1)S(1)}, bf16[256,256]{1,0:T(8,128)(2,1)}, u32[]{:S(2)}) copy-start(bf16[256,256]{1,0:T(8,128)(2,1)} %constant.15.clone.refs_7_.refs_5_.refs_3_) | copy-start | bytes 393220
  0.0 22.4 %copy-start.3 = (bf16[256,128]{1,0:T(8,128)(2,1)S(1)}, bf16[256,128]{1,0:T(8,128)(2,1)}, u32[]{:S(2)}) copy-start(bf16[256,128]{1,0:T(8,128)(2,1)} %constant.14.clone.refs_6_.refs_4_.refs_2_) | copy-start | bytes 196612
  0.0 22.5 %copy-start.4 = (f32[16,32,128]{2,1,0:T(8,128)S(1)}, f32[16,32,128]{2,1,0:T(8,128)}, u32[]{:S(2)}) copy-start(f32[16,32,128]{2,1,0:T(8,128)} %refs_0_.1) | copy-start | bytes 786436
  0.0 22.5 %copy-start = (f32[16,32,128]{2,1,0:T(8,128)S(1)}, f32[16,32,128]{2,1,0:T(8,128)}, u32[]{:S(2)}) copy-start(f32[16,32,128]{2,1,0:T(8,128)} %refs_1_.1) | copy-start | bytes 786436
  0.0 22.4 %collective-permute-start = (f32[16,32,128]{2,1,0:T(8,128)}, f32[16,32,128]{2,1,0:T(8,128)S(1)}, u32[]{:S(2)}, u32[]{:S(2)}) collective-permute-start(f32[16,32,128]{2,1,0:T(8,128)} %refs_0_.1), channel_id=1, source_target_pairs={{0,1},{1,2},{2,3},{3,4},{4,5},{5,6},{6,7},{7,8},{8,9},{9,10},{10,1... | collective-permute-start | bytes 786440 | tf_op jit(solution)/shard_map/ppermute | solution.py:314
  0.5 21.9 %collective-permute-start.1 = (f32[16,32,128]{2,1,0:T(8,128)}, f32[16,32,128]{2,1,0:T(8,128)S(1)}, u32[]{:S(2)}, u32[]{:S(2)}) collective-permute-start(f32[16,32,128]{2,1,0:T(8,128)} %refs_0_.1), channel_id=1, source_target_pairs={{0,15},{1,0},{2,1},{3,2},{4,3},{5,4},{6,5},{7,6},{8,7},{9,8},{10,9... | collective-permute-start | bytes 786440 | tf_op jit(solution)/shard_map/ppermute | solution.py:314
  6.6 15.8 %collective-permute-start.3 = (f32[12,32,128]{2,1,0:T(8,128)S(1)}, f32[12,32,128]{2,1,0:T(8,128)S(1)}, u32[]{:S(2)}, u32[]{:S(2)}) collective-permute-start(f32[12,32,128]{2,1,0:T(8,128)S(1)} %get-tuple-element.39), channel_id=1, source_target_pairs={{0,15},{1,0},{2,1},{3,2},{4,3},{5,4},{6,5},{7,6},{8,7},{9,8},{10,9... | collective-permute-start | bytes 589832 | tf_op jit(solution)/shard_map/ppermute | solution.py:314
  7.4 15.1 %collective-permute-start.2 = (f32[12,32,128]{2,1,0:T(8,128)S(1)}, f32[12,32,128]{2,1,0:T(8,128)S(1)}, u32[]{:S(2)}, u32[]{:S(2)}) collective-permute-start(f32[12,32,128]{2,1,0:T(8,128)S(1)} %get-tuple-element.40), channel_id=1, source_target_pairs={{0,1},{1,2},{2,3},{3,4},{4,5},{5,6},{6,7},{7,8},{8,9},{9,10},{10,1... | collective-permute-start | bytes 589832 | tf_op jit(solution)/shard_map/ppermute | solution.py:314
  8.7 8.0 %collective-permute-start.5 = (f32[9]{0:T(128)S(1)}, f32[9]{0:T(128)S(1)}, u32[]{:S(2)}, u32[]{:S(2)}) collective-permute-start(f32[9]{0:T(128)S(1)} %pad_maximum_fusion.refs_10_.refs_8_), channel_id=1, source_target_pairs={{0,15},{1,0},{2,1},{3,2},{4,3},{5,4},{6,5},{7,6},{8,7},{9,8},{10,9... | collective-permute-start | bytes 116 | tf_op jit(solution)/shard_map/ppermute | solution.py:314
  13.2 1.2 %copy-start.2 = (f32[64,32,128]{2,1,0:T(8,128)S(1)}, f32[64,32,128]{2,1,0:T(8,128)}, u32[]{:S(2)}) copy-start(f32[64,32,128]{2,1,0:T(8,128)} %courant.1) | copy-start | bytes 3145732
  14.4 0.7 copy-start.6
  15.1 0.7 copy-start.11
  15.8 0.7 copy-start.12
  16.7 9.6 %copy-start.7 = (f32[9]{0:T(128)}, f32[9]{0:T(128)S(1)}, u32[]{:S(2)}) copy-start(f32[9]{0:T(128)S(1)} %collective-permute-done.5.refs_11_.refs_9_) | copy-start | bytes 112
  16.7 5.7 %collective-permute-start.4 = (f32[9]{0:T(128)S(1)}, f32[9]{0:T(128)S(1)}, u32[]{:S(2)}, u32[]{:S(2)}) collective-permute-start(f32[9]{0:T(128)S(1)} %pad_maximum_fusion.refs_10_.refs_8_), channel_id=1, source_target_pairs={{0,1},{1,2},{2,3},{3,4},{4,5},{5,6},{6,7},{7,8},{8,9},{9,10},{10,1... | collective-permute-start | bytes 116 | tf_op jit(solution)/shard_map/ppermute | solution.py:314
  22.4 3.9 %copy-start.9 = (f32[9]{0:T(128)}, f32[9]{0:T(128)S(1)}, u32[]{:S(2)}) copy-start(f32[9]{0:T(128)S(1)} %collective-permute-done.4.refs_9_.refs_7_) | copy-start | bytes 112
  26.3 33.4 %collective-permute-start.6 = (f32[24,32,128]{2,1,0:T(8,128)}, f32[24,32,128]{2,1,0:T(8,128)S(1)}, u32[]{:S(2)}, u32[]{:S(2)}) collective-permute-start(f32[24,32,128]{2,1,0:T(8,128)} %get-tuple-element.25), channel_id=1, source_target_pairs={{0,1},{1,2},{2,3},{3,4},{4,5},{5,6},{6,7},{7,8},{8,9},{9,10},{10,1... | collective-permute-start | bytes 1179656 | tf_op jit(solution)/shard_map/ppermute | solution.py:314
  26.3 33.4 %collective-permute-start.7 = (f32[24,32,128]{2,1,0:T(8,128)}, f32[24,32,128]{2,1,0:T(8,128)S(1)}, u32[]{:S(2)}, u32[]{:S(2)}) collective-permute-start(f32[24,32,128]{2,1,0:T(8,128)} %get-tuple-element.26), channel_id=1, source_target_pairs={{0,15},{1,0},{2,1},{3,2},{4,3},{5,4},{6,5},{7,6},{8,7},{9,8},{10,9... | collective-permute-start | bytes 1179656 | tf_op jit(solution)/shard_map/ppermute | solution.py:314
  59.7 0.7 copy-start.5
  60.4 0.7 copy-start.8
  61.1 0.6 copy-start.10
  65.4 3.7 %collective-permute-start.11 = (f32[8,256]{1,0:T(8,128)S(1)}, f32[8,256]{1,0:T(8,128)S(1)}, u32[]{:S(2)}, u32[]{:S(2)}) collective-permute-start(f32[8,256]{1,0:T(8,128)S(1)} %get-tuple-element.34.refs_9_), channel_id=1, source_target_pairs={{0,14},{1,15},{2,0},{3,1},{4,2},{5,3},{6,4},{7,5},{8,6},{9,7},{10,... | collective-permute-start | bytes 24584 | tf_op jit(solution)/shard_map/ppermute | solution.py:314
  65.4 3.7 %collective-permute-start.10 = (f32[8,256]{1,0:T(8,128)S(1)}, f32[8,256]{1,0:T(8,128)S(1)}, u32[]{:S(2)}, u32[]{:S(2)}) collective-permute-start(f32[8,256]{1,0:T(8,128)S(1)} %get-tuple-element.34.refs_9_), channel_id=1, source_target_pairs={{0,15},{1,0},{2,1},{3,2},{4,3},{5,4},{6,5},{7,6},{8,7},{9,8},{10,9... | collective-permute-start | bytes 24584 | tf_op jit(solution)/shard_map/ppermute | solution.py:314
  65.4 5.8 %collective-permute-start.9 = (f32[8,256]{1,0:T(8,128)S(1)}, f32[8,256]{1,0:T(8,128)S(1)}, u32[]{:S(2)}, u32[]{:S(2)}) collective-permute-start(f32[8,256]{1,0:T(8,128)S(1)} %get-tuple-element.34.refs_9_), channel_id=1, source_target_pairs={{0,1},{1,2},{2,3},{3,4},{4,5},{5,6},{6,7},{7,8},{8,9},{9,10},{10,1... | collective-permute-start | bytes 24584 | tf_op jit(solution)/shard_map/ppermute | solution.py:314
  65.9 6.3 %collective-permute-start.8 = (f32[8,256]{1,0:T(8,128)S(1)}, f32[8,256]{1,0:T(8,128)S(1)}, u32[]{:S(2)}, u32[]{:S(2)}) collective-permute-start(f32[8,256]{1,0:T(8,128)S(1)} %get-tuple-element.34.refs_9_), channel_id=1, source_target_pairs={{0,2},{1,3},{2,4},{3,5},{4,6},{5,7},{6,8},{7,9},{8,10},{9,11},{10,... | collective-permute-start | bytes 24584 | tf_op jit(solution)/shard_map/ppermute | solution.py:314
  77.8 6.8 %collective-permute-start.12 = (f32[4,32,128]{2,1,0:T(8,128)S(1)}, f32[4,32,128]{2,1,0:T(8,128)S(1)}, u32[]{:S(2)}, u32[]{:S(2)}) collective-permute-start(f32[4,32,128]{2,1,0:T(8,128)S(1)} %get-tuple-element.36), channel_id=1, source_target_pairs={{0,4},{1,5},{2,6},{3,7},{4,8},{5,9},{6,10},{7,11},{8,12},{9,13},{1... | collective-permute-start | bytes 196616 | tf_op jit(solution)/shard_map/ppermute | solution.py:314
  78.8 8.1 %collective-permute-start.13 = (f32[4,32,128]{2,1,0:T(8,128)S(1)}, f32[4,32,128]{2,1,0:T(8,128)S(1)}, u32[]{:S(2)}, u32[]{:S(2)}) collective-permute-start(f32[4,32,128]{2,1,0:T(8,128)S(1)} %get-tuple-element.37), channel_id=1, source_target_pairs={{0,8},{1,9},{2,10},{3,11},{4,12},{5,13},{6,14},{7,15},{8,0},{9,1},... | collective-permute-start | bytes 196616 | tf_op jit(solution)/shard_map/ppermute | solution.py:314
  78.8 8.1 %collective-permute-start.14 = (f32[4,32,128]{2,1,0:T(8,128)S(1)}, f32[4,32,128]{2,1,0:T(8,128)S(1)}, u32[]{:S(2)}, u32[]{:S(2)}) collective-permute-start(f32[4,32,128]{2,1,0:T(8,128)S(1)} %get-tuple-element.38), channel_id=1, source_target_pairs={{0,12},{1,13},{2,14},{3,15},{4,0},{5,1},{6,2},{7,3},{8,4},{9,5},{1... | collective-permute-start | bytes 196616 | tf_op jit(solution)/shard_map/ppermute | solution.py:314

commit v2 on v1

--- a/solution.py
+++ b/solution.py
@@ -65,10 +65,8 @@
             old[x] = 2.0 * here - old[x] + model[x + model_shift] * total
 
 
-def add_source(field, pack, step, own, block, halo, rows):
+def add_source(field, pack, cell, step, own, block, halo, rows):
     span_y, span_z = field.shape[1:]
-    cell = pack[NT].astype(jnp.int32)
-    amount = pack[step]
     plane = own + block * rows + cell // (span_y * span_z)
     y = (cell // span_z) % span_y
     z = cell % span_z
@@ -79,10 +77,25 @@
         sub = lax.broadcasted_iota(jnp.int32, (8, span_z), 0)
         lane = lax.broadcasted_iota(jnp.int32, (8, span_z), 1)
         hit = (sub == y % 8) & (lane == z)
-        field[plane, tile, :] = field[plane, tile, :] + jnp.where(hit, amount, 0.0)
-
-
-def prepare_kernel(courant, cells, order, observed, model_out, pack_out):
+        field[plane, tile, :] = field[plane, tile, :] + jnp.where(hit, pack[step : step + 1], 0.0)
+
+
+def message_kernel(before, wavelet, source, left_out, right_out, pack_out):
+    rows, span_y, span_z = before.shape
+    which = lax.broadcasted_iota(jnp.int32, (16, span_z), 0)
+    pack = jnp.where(which >= NT, source[0].astype(F32), 0.0)
+    for step in range(NT):
+        pack = jnp.where(which == step, wavelet[0, step], pack)
+    pack_out[...] = pack
+    narrow = RAD * (ROUNDS[0] - 1)
+    size = narrow * span_y
+    left_out[:size] = before[:narrow].reshape(size, span_z)
+    right_out[:size] = before[rows - narrow :].reshape(size, span_z)
+    left_out[size:] = pack
+    right_out[size:] = pack
+
+
+def prepare_kernel(courant, cells, order, observed, pack, model_out, cells_out, observed_out):
     rows = 16
     piece = lax.rem(lax.axis_index("shot"), PIECES)
     period = courant.shape[0]
@@ -93,23 +106,15 @@
     count = cells.shape[1]
     wanted = order[...]
     cell = cells[...]
-    high = (cell // 256).astype(F32).astype(BF)
-    low = (cell % 256).astype(F32).astype(BF)
     which = lax.broadcasted_iota(jnp.int32, (16, count), 0)
-    digits = jnp.where(which == 0, high.astype(F32), jnp.where(which == 1, low.astype(F32), 0.0)).astype(BF)
+    digits = jnp.where(which == 0, cell // 256, jnp.where(which == 1, cell % 256, 0)).astype(F32).astype(BF)
     for j in range(0, count, 256):
         index = lax.broadcasted_iota(jnp.int32, (count, 256), 0)
         chosen = jnp.where(index == wanted[:, j : j + 256], 1.0, 0.0).astype(BF)
         found = dot(digits, chosen)
         ordered = found[0:1] * 256.0 + found[1:2]
-        pack_out[j // 128 : j // 128 + 1] = ordered[:, :128]
-        pack_out[j // 128 + 1 : j // 128 + 2] = ordered[:, 128:]
-    pack_out[count // 128 :] = observed[...]
-
-
-def cell_row(pack, count):
-    parts = [pack[j : j + 1] for j in range(count // 128)]
-    return jnp.concatenate(parts, axis=1).astype(jnp.int32)
+        cells_out[:, j : j + 256] = jnp.broadcast_to(ordered, (8, 256))
+    observed_out[...] = observed[...] + 0.0 * pack[0:1, :]
 
 
 def pick_tables(cells, table_rows):
@@ -139,7 +144,7 @@
 
 
 def forward_round(
-    index, refs_in, zmat, ymat, model, pack_left, pack_own, pack_right, fields, buf_a, buf_b
+    index, refs_in, zmat, ymat, model, packs, fields, buf_a, buf_b
 ):
     steps = ROUNDS[index]
     done = sum(ROUNDS[:index])
@@ -154,8 +159,9 @@
         cur[own - wide : own] = now_l[...]
         cur[own + rows : own + rows + wide] = now_r[...]
         if narrow:
-            old[own - narrow : own] = before_l[...]
-            old[own + rows : own + rows + narrow] = before_r[...]
+            size = narrow * cur.shape[1]
+            old[own - narrow : own] = before_l[:size].reshape((narrow,) + cur.shape[1:])
+            old[own + rows : own + rows + narrow] = before_r[:size].reshape((narrow,) + cur.shape[1:])
     else:
         earlier, known, got_l, got_r = refs_in
         cur[own : own + rows] = earlier[earlier.shape[0] - 1]
@@ -168,12 +174,14 @@
         if narrow > RAD:
             old[own - narrow : own - RAD] = got_l[wide:]
             old[own + rows + RAD : own + rows + narrow] = got_r[wide:]
+    cells = [jnp.max(packs[block, NT : 2 * NT]).astype(jnp.int32) for block in range(3)]
     for step in range(steps):
         halo = RAD * (steps - 1 - step)
         advance(cur, old, model, zmat, ymat, own - halo, own + rows + halo, HALO - own)
-        for block, pack in ((-1, pack_left), (0, pack_own), (1, pack_right)):
+        for block in (-1, 0, 1):
             if halo or block == 0:
-                add_source(old, pack, done + step, own, block, halo, rows)
+                pack = packs.at[block + 1]
+                add_source(old, pack, cells[block + 1], done + step, own, block, halo, rows)
         fields[step] = old[own : own + rows]
         cur, old = old, cur
     return cur, old, own
@@ -184,13 +192,22 @@
     return RAD * steps + RAD * max(steps - 2, 0)
 
 
+def gather_packs(pack_own, before_l, before_r, packs):
+    packs[0] = before_l[before_l.shape[0] - 16 :]
+    packs[1] = pack_own[...]
+    packs[2] = before_r[before_r.shape[0] - 16 :]
+
+
 def forward_kernel(index, *refs):
     take = 6 if index == 0 else 4
     refs_in, refs = refs[:take], refs[take:]
-    zmat, ymat, model, pack_left, pack_own, pack_right, fields, known, send_l, send_r, buf_a, buf_b = refs
-    cur, old, own = forward_round(
-        index, refs_in, zmat, ymat, model, pack_left, pack_own, pack_right, fields, buf_a, buf_b
-    )
+    zmat, ymat, model, pack, fields, known, send_l, send_r = refs[:8]
+    if index == 0:
+        packs, buf_a, buf_b = refs[8:]
+        gather_packs(pack, refs_in[4], refs_in[5], packs)
+    else:
+        packs, (buf_a, buf_b) = pack, refs[8:]
+    cur, old, own = forward_round(index, refs_in, zmat, ymat, model, packs, fields, buf_a, buf_b)
     rows = 16
     known[0] = old[own - RAD : own]
     known[1] = old[own + rows : own + rows + RAD]
@@ -203,9 +220,35 @@
         send_r[wide:] = old[own + rows - inner : own + rows - RAD]
 
 
+def split_exactly(values):
+    high = values.astype(BF)
+    rest = values - high.astype(F32)
+    middle = rest.astype(BF)
+    return high, middle, (rest - middle.astype(F32)).astype(BF)
+
+
+def in_send_order(observed, count):
+    owners = observed.shape[0]
+    per_owner = count // owners
+    slot = lax.broadcasted_iota(jnp.int32, (owners, count), 1)
+    owner = lax.broadcasted_iota(jnp.int32, (owners, count), 0)
+    owned = jnp.where(slot // per_owner == owner, 1.0, 0.0).astype(BF)
+    spread = jnp.zeros((NT * per_owner, count), F32)
+    for part in split_exactly(observed):
+        spread = spread + dot(part, owned, (((0,), (0,)), ((), ())))
+    line = lax.broadcasted_iota(jnp.int32, (per_owner, count), 0)
+    slot = lax.broadcasted_iota(jnp.int32, (per_owner, count), 1)
+    hit = slot % per_owner == line
+    out = []
+    for step in range(NT):
+        part = spread[step * per_owner : (step + 1) * per_owner]
+        out.append(jnp.sum(jnp.where(hit, part, 0.0), axis=0, keepdims=True))
+    return jnp.concatenate(out, axis=0)
+
+
 def tables_kernel(count, *refs):
-    (pack, *fields), (rows_out, lanes_out, traces) = refs[:-3], refs[-3:]
-    rows_table, lane_table = pick_tables(cell_row(pack, count), rows_out.shape[1])
+    (cells, observed, *fields), (rows_out, lanes_out, traces) = refs[:-3], refs[-3:]
+    rows_table, lane_table = pick_tables(cells[0:1].astype(jnp.int32), rows_out.shape[1])
     rows_out[...] = rows_table
     lanes_out[...] = lane_table
     total = jnp.zeros((16, count), F32)
@@ -214,33 +257,23 @@
         for i in range(group.shape[0]):
             total = total + extract(group[i], step, rows_table, lane_table)
             step += 1
-    traces[...] = total
+    traces[...] = total[:NT] - in_send_order(observed[...], count)
 
 
 def last_kernel(index, *refs):
     take = 6 if index == 0 else 4
     refs_in, refs = refs[:take], refs[take:]
-    zmat, ymat, model, pack_left, pack_own, pack_right = refs[:6]
-    rows_table, lane_table, traces, observed = refs[6:10]
-    fields, adj, buf_a, buf_b = refs[10:]
-    forward_round(index, refs_in, zmat, ymat, model, pack_left, pack_own, pack_right, fields, buf_a, buf_b)
-    total = traces[...]
+    zmat, ymat, model, packs, cells, rows_table, lane_table, traces = refs[:8]
+    fields, adj, buf_a, buf_b = refs[8:]
+    forward_round(index, refs_in, zmat, ymat, model, packs, fields, buf_a, buf_b)
     done = sum(ROUNDS[:index])
     rows_table = rows_table[...]
     lane_table = lane_table[...]
-    for step in range(ROUNDS[index]):
+    total = extract(fields[0], done, rows_table, lane_table)
+    for step in range(1, ROUNDS[index]):
         total = total + extract(fields[step], done + step, rows_table, lane_table)
-    adj[...] = total[0:NT] - observed[...]
-
-
-def inject_tables_kernel(count, packs, rows_out, lanes_out):
-    me = lax.axis_index("shot")
-    devices = packs.shape[0]
-    for block in range(5):
-        cells = cell_row(packs.at[lax.rem(me + block - 2 + devices, devices)], count)
-        sub = lax.broadcasted_iota(jnp.int32, (rows_out.shape[1], count), 0)
-        rows_out[block] = jnp.where(sub == cells // 128, 1.0, 0.0).astype(BF)
-        lanes_out[block : block + 1] = cells % 128
+    adj[0:NT] = total[0:NT] + traces[...]
+    adj[NT:] = cells[...]
 
 
 def adjoint_kernel(field_groups, slabs, count, *refs):
@@ -248,12 +281,19 @@
     for ref in refs[:field_groups]:
         fields += [ref.at[i] for i in range(ref.shape[0])]
     refs = refs[field_groups:]
-    zmat, ymat, model, rows_table, lanes, *adjs = refs[:10]
-    outs = refs[10 : 10 + slabs]
-    buf_a, buf_b, image = refs[10 + slabs :]
+    zmat, ymat, model, *adjs = refs[:8]
+    outs = refs[8 : 8 + slabs]
+    buf_a, buf_b, image, rows_table = refs[8 + slabs :]
     rows = 16
     own = HALO
     span_y, span_z = buf_a.shape[1:]
+    table_rows = rows * span_y
+    lanes = []
+    for block in range(5):
+        cells = adjs[block][NT : NT + 1].astype(jnp.int32)
+        sub = lax.broadcasted_iota(jnp.int32, (table_rows, count), 0)
+        rows_table[block] = jnp.where(sub == cells // span_z, 1.0, 0.0).astype(BF)
+        lanes.append(cells % span_z)
 
     def inject(field, number):
         halo = RAD * (NT - number)
@@ -268,7 +308,7 @@
             high = amounts.astype(BF).astype(F32)
             low = amounts - high
             sub = lax.broadcasted_iota(jnp.int32, (span_z, count), 0)
-            hit = sub == lanes[block + 2 : block + 3]
+            hit = sub == lanes[block + 2]
             both = jnp.concatenate(
                 [jnp.where(hit, high, 0.0).astype(BF), jnp.where(hit, low, 0.0).astype(BF)], axis=0
             )
@@ -318,53 +358,59 @@
     courant_sq, wave_now, wave_before, wavelet, source_cell, receiver_cell, send_order, observed
 ):
     devices = lax.axis_size("shot")
-    me = lax.axis_index("shot")
     rows, span_y, span_z = wave_now.shape
     count = receiver_cell.shape[0]
-    per_owner = count // devices
     table_rows = rows * span_y
     plane = (span_y, span_z)
     zmat, ymat = matrices(span_y, span_z)
 
     wide = RAD * ROUNDS[0]
     narrow = wide - RAD
-    pack_own = jnp.concatenate([wavelet.reshape(-1), source_cell.astype(F32)])
-    pack_left, pack_right = shifted(pack_own, 1), shifted(pack_own, -1)
     now_l, now_r = shifted(wave_now[rows - wide :], 1), shifted(wave_now[:wide], -1)
-    before_l, before_r = shifted(wave_before[rows - narrow :], 1), shifted(wave_before[:narrow], -1)
-
-    model, pack = call(
+    message = jax.ShapeDtypeStruct((narrow * span_y + 16, span_z), F32)
+    to_left, to_right, pack = call(
+        message_kernel,
+        (message, message, jax.ShapeDtypeStruct((16, span_z), F32)),
+        (wave_before, wavelet, source_cell),
+        specs=[VMEM, SMEM, SMEM],
+        name="message",
+    )
+    before_l, before_r = shifted(to_right, 1), shifted(to_left, -1)
+
+    model, cells, observed = call(
         prepare_kernel,
         (
             jax.ShapeDtypeStruct((rows + 2 * HALO,) + plane, F32),
-            jax.ShapeDtypeStruct((count // 128 + devices, 128), F32),
+            jax.ShapeDtypeStruct((8, count), F32),
+            jax.ShapeDtypeStruct(observed.shape, F32),
         ),
-        (courant_sq, receiver_cell.reshape(1, count), send_order.reshape(1, count), observed),
+        (courant_sq, receiver_cell.reshape(1, count), send_order.reshape(1, count), observed, pack),
         name="prepare",
     )
-    packs = lax.all_gather(pack, "shot", axis=0, tiled=False)
-
-    common = (zmat, ymat, model, pack_left, pack_own, pack_right)
-    common_specs = [VMEM] * 3 + [SMEM] * 3
+    recorded = lax.all_to_all(observed, "shot", split_axis=0, concat_axis=0, tiled=True)
+
+    common = (zmat, ymat, model)
     field_list = []
     ins = (wave_now, wave_before, now_l, now_r, before_l, before_r)
     for index in range(len(ROUNDS) - 1):
         window = rows + 2 * RAD * ROUNDS[index]
         sent = send_shapes(index + 1)
-        fields, known, send_l, send_r = call(
+        packs = (jax.ShapeDtypeStruct((3, 16, span_z), F32),) if index == 0 else ()
+        fields, known, send_l, send_r, *made = call(
             functools.partial(forward_kernel, index),
             (
                 jax.ShapeDtypeStruct((ROUNDS[index], rows) + plane, F32),
                 jax.ShapeDtypeStruct((2, RAD) + plane, F32),
                 jax.ShapeDtypeStruct((sent,) + plane, F32),
                 jax.ShapeDtypeStruct((sent,) + plane, F32),
-            ),
-            ins + common,
-            specs=[VMEM] * len(ins) + common_specs,
+            )
+            + packs,
+            ins + common + (pack,),
             scratch=[pltpu.VMEM((window,) + plane, F32)] * 2,
             name="forward",
         )
         field_list.append(fields)
+        pack = made[0] if made else pack
         ins = (fields, known, shifted(send_r, 1), shifted(send_l, -1))
 
     rows_table, lane_table, traces = call(
@@ -372,33 +418,20 @@
         (
             jax.ShapeDtypeStruct((count, table_rows), BF),
             jax.ShapeDtypeStruct((count, 256), F32),
-            jax.ShapeDtypeStruct((16, count), F32),
+            jax.ShapeDtypeStruct((NT, count), F32),
         ),
-        (pack, *field_list),
+        (cells, recorded, *field_list),
         name="traces",
     )
-    mine = lax.dynamic_index_in_dim(packs[:, count // 128 :], me, 1, keepdims=False)
-    target = mine.reshape(devices, NT, per_owner).transpose(1, 0, 2).reshape(NT, count)
-    inject_rows, inject_lanes = call(
-        functools.partial(inject_tables_kernel, count),
-        (
-            jax.ShapeDtypeStruct((5, table_rows, count), BF),
-            jax.ShapeDtypeStruct((5, count), jnp.int32),
-        ),
-        (packs,),
-        name="inject_tables",
-    )
-
     index = len(ROUNDS) - 1
     window = rows + 2 * RAD * ROUNDS[index]
     fields, adj = call(
         functools.partial(last_kernel, index),
         (
             jax.ShapeDtypeStruct((ROUNDS[index], rows) + plane, F32),
-            jax.ShapeDtypeStruct((NT, count), F32),
+            jax.ShapeDtypeStruct((2 * NT, count), F32),
         ),
-        ins + common + (rows_table, lane_table, traces, target),
-        specs=[VMEM] * len(ins) + common_specs + [VMEM] * 4,
+        ins + common + (pack, cells, rows_table, lane_table, traces),
         scratch=[pltpu.VMEM((window,) + plane, F32)] * 2,
         name="forward_last",
     )
@@ -410,8 +443,9 @@
     parts = call(
         functools.partial(adjoint_kernel, len(field_list), slabs, count),
         tuple(jax.ShapeDtypeStruct((thick,) + plane, F32) for _ in range(slabs)),
-        (*field_list, zmat, ymat, model, inject_rows, inject_lanes, *adjs),
-        scratch=[pltpu.VMEM((rows + 2 * HALO,) + plane, F32)] * 2 + [pltpu.VMEM((rows,) + plane, F32)],
+        (*field_list, zmat, ymat, model, *adjs),
+        scratch=[pltpu.VMEM((rows + 2 * HALO,) + plane, F32)] * 2
+        + [pltpu.VMEM((rows,) + plane, F32), pltpu.VMEM((5, table_rows, count), BF)],
         name="adjoint",
     )
     total = parts[0]

time: 88 us -> 62 us (0.70)
  blocking collectives: 21.6 us -> 8.97 us
  local copies, waits for them, and re-layouts: 12.8 us -> 5.62 us
  waiting for transfers between devices: 14.9 us -> 10.5 us
    all_gather x1 -> x0, blocking collectives: 21.6 us -> none  [per_device(): packs = lax.all_gather(pack, 'shot', axis=0, tiled=False)]
    all_to_all x0 -> x1, blocking collectives: none -> 8.97 us  [per_device(): lax.all_to_all(observed, 'shot', split_axis=0, concat_axis=0, tiled=True)]
    ppermute x15 -> x13, waiting for transfers between devices: 14.9 us -> 10.5 us  [shifted(): lax.ppermute(value, 'shot', [(i, (i + steps) % count) for i in range(coun...]
    reshape x2 -> x0, local copies, waits for them, and re-layouts: 2.93 us -> none  [per_device(): mine.reshape(devices, NT, per_owner).transpose(1, 0, 2).reshape(NT, count)]
    slice x2 -> x0, local copies, waits for them, and re-layouts: 1.72 us -> none  [the longest x1 1.05 us: per_device(): wave_before[:narrow]]
    transpose x1 -> x0, local copies, waits for them, and re-layouts: 1.47 us -> none  [per_device(): mine.reshape(devices, NT, per_owner).transpose(1, 0, 2).reshape(NT, count)]
    dynamic_slice x1 -> x0, local copies, waits for them, and re-layouts: 1.46 us -> none  [per_device(): lax.dynamic_index_in_dim(packs[:, count // 128:], me, 1, keepdims=False)]
    ppermute x15 -> x13, starting transfers between devices: 21.7 us -> 21.3 us  [shifted(): lax.ppermute(value, 'shot', [(i, (i + steps) % count) for i in range(coun...]
  transfers between devices with their start and end apart: 15 -> 13, of which waited for: 6 -> 5; matrix products, arithmetic and copies ran while one was open for 9% -> 0% of each run, Pallas kernels for 2% -> 3%
where the time goes in v2:
time: 62 us; the launch traced here: 61.7 us
  starting transfers between devices  21.3 us (34%)
  Pallas kernels  13.9 us (22%)
  waiting for transfers between devices  10.5 us (17%)
  blocking collectives  8.97 us (14%)
  local copies, waits for them, and re-layouts  5.62 us (9%)
  between operations  0.76 us (1%)
  other arithmetic  0.65 us (1%)
    ppermute x13, starting transfers between devices, shifted(): lax.ppermute(value, 'shot', [(i, (i + steps) % count) for i in range(coun...  21.3 us
    pallas_call x6, Pallas kernels, call(): pl.pallas_call(kernel, out_shape=outs, in_specs=specs or [VMEM] * len(ins...  13.9 us
    ppermute x13, waiting for transfers between devices, shifted(): lax.ppermute(value, 'shot', [(i, (i + steps) % count) for i in range(coun...  10.5 us
    all_to_all x1, blocking collectives, per_device(): lax.all_to_all(observed, 'shot', split_axis=0, concat_axis=0, tiled=True)  8.97 us
    unnamed x20, local copies, waits for them, and re-layouts  5.62 us
  transfers between devices with their start and end apart: 13, of which 5 were waited for; matrix products, arithmetic and copies ran while one was open for 0% of the time, Pallas kernels for 3%

profile of v2, /device:TPU:0, one launch (start us, length us, event | category | flops | bytes accessed | tf_op | source)
XLA Modules:
  0.0 61.7 jit_solution(16234298327066814705)
XLA Ops:
  0.0 0.5 collective-permute-start
  0.5 5.0 %collective-permute-start.1 = (f32[16,32,128]{2,1,0:T(8,128)}, f32[16,32,128]{2,1,0:T(8,128)S(1)}, u32[]{:S(2)}, u32[]{:S(2)}) collective-permute-start(f32[16,32,128]{2,1,0:T(8,128)} %refs_0_.1), channel_id=1, source_target_pairs={{0,15},{1,0},{2,1},{3,2},{4,3},{5,4},{6,5},{7,6},{8,7},{9,8},{10,9... | collective-permute-start | bytes 786440 | tf_op jit(solution)/shard_map/ppermute | solution.py:354
  6.2 0.9 %copy-done.2 = f32[16,32,128]{2,1,0:T(8,128)S(1)} copy-done((f32[16,32,128]{2,1,0:T(8,128)S(1)}, f32[16,32,128]{2,1,0:T(8,128)}, u32[]{:S(2)}) %copy-start.2) | copy-done | bytes 262168
  7.1 0.7 %copy-done.9 = f32[1,8]{1,0:T(1,128)S(1)} copy-done((f32[1,8]{1,0:T(1,128)S(1)}, f32[1,8]{1,0:T(1,128)}, u32[]{:S(2)}) %copy-start.9) | copy-done | bytes 56
  7.8 0.6 message.1
  8.3 0.1 collective-permute-start.2
  8.4 4.4 %collective-permute-start.3 = (f32[400,128]{1,0:T(8,128)S(1)}, f32[400,128]{1,0:T(8,128)S(1)}, u32[]{:S(2)}, u32[]{:S(2)}) collective-permute-start(f32[400,128]{1,0:T(8,128)S(1)} %get-tuple-element.26), channel_id=1, source_target_pairs={{0,15},{1,0},{2,1},{3,2},{4,3},{5,4},{6,5},{7,6},{8,7},{9,8},{10,9... | collective-permute-start | bytes 614408 | tf_op jit(solution)/shard_map/ppermute | solution.py:354
  12.8 1.2 %copy-done.1 = f32[64,32,128]{2,1,0:T(8,128)S(1)} copy-done((f32[64,32,128]{2,1,0:T(8,128)S(1)}, f32[64,32,128]{2,1,0:T(8,128)}, u32[]{:S(2)}) %copy-start.1) | copy-done | bytes 1048600
  14.1 0.7 %copy-done.6 = f32[16,128]{1,0:T(8,128)S(1)} copy-done((f32[16,128]{1,0:T(8,128)S(1)}, f32[16,128]{1,0:T(8,128)}, u32[]{:S(2)}) %copy-start.6) | copy-done | bytes 8216
  14.8 0.7 %copy-done.7 = s32[256]{0:T(256)S(1)} copy-done((s32[256]{0:T(256)S(1)}, s32[256]{0:T(256)}, u32[]{:S(2)}) %copy-start.7) | copy-done | bytes 1048
  15.4 0.7 %copy-done.8 = s32[256]{0:T(256)S(1)} copy-done((s32[256]{0:T(256)S(1)}, s32[256]{0:T(256)}, u32[]{:S(2)}) %copy-start.8) | copy-done | bytes 1048
  16.1 0.2 prepare.1
  16.4 0.7 %copy-done.3 = f32[16,32,128]{2,1,0:T(8,128)S(1)} copy-done((f32[16,32,128]{2,1,0:T(8,128)S(1)}, f32[16,32,128]{2,1,0:T(8,128)}, u32[]{:S(2)}) %copy-start.3) | copy-done | bytes 262168
  17.1 0.1 copy-done.5
  17.1 2.6 %forward.1 = (f32[4,16,32,128]{3,2,1,0:T(8,128)S(1)}, f32[2,4,32,128]{3,2,1,0:T(8,128)S(1)}, f32[24,32,128]{2,1,0:T(8,128)S(1)}, f32[24,32,128]{2,1,0:T(8,128)S(1)}, f32[3,16,128]{2,1,0:T(8,128)S(1)}) custom-call(f32[16,32,128]{2,1,0:T(8,128)S(1)} %copy-done.5, f32[16,32,128]{2,1,0:T(8,128)S(1)} %copy-done.3, ...), custom_call_target="tpu_custom_call" | custom-call | flops 1000000 | bytes 1000000 | tf_op jit(solution)/shard_map/forward/pallas_call | solution.py:340
  19.8 4.4 %collective-permute-start.5 = (f32[24,32,128]{2,1,0:T(8,128)S(1)}, f32[24,32,128]{2,1,0:T(8,128)S(1)}, u32[]{:S(2)}, u32[]{:S(2)}) collective-permute-start(f32[24,32,128]{2,1,0:T(8,128)S(1)} %get-tuple-element.32), channel_id=1, source_target_pairs={{0,15},{1,0},{2,1},{3,2},{4,3},{5,4},{6,5},{7,6},{8,7},{9,8},{10,9... | collective-permute-start | bytes 1179656 | tf_op jit(solution)/shard_map/ppermute | solution.py:354
  24.2 9.0 %all_to_all.11 = f32[16,1,128]{2,1,0:T(1,128)S(1)} all-to-all(f32[16,1,128]{2,1,0:T(1,128)S(1)} %bitcast.7), channel_id=1, replica_groups=mesh['groups'=2,'shot'=16] {'shot'}, dimensions={0} | all-to-all | bytes 16384 | tf_op jit(solution)/shard_map/all_to_all | solution.py:390
  33.2 0.8 %traces.1 = (bf16[256,512]{1,0:T(8,128)(2,1)S(1)}, f32[256,256]{1,0:T(8,128)S(1)}, f32[8,256]{1,0:T(8,128)S(1)}) custom-call(f32[8,256]{1,0:T(8,128)S(1)} %get-tuple-element.34.refs_0_.refs_8_, f32[16,128]{1,0:T(8,128)S(1)} %bitcast.6, f32[4,16,32,128]{3,2,1,0:T(8,128)S(1)} %get-tuple-element.29.refs_2_.refs_0_), custom_call_target="tpu_custom_call" | custom-call | flops 1000000 | bytes 1000000 | tf_op jit(solution)/shard_map/traces/pallas_call | solution.py:340
  34.1 3.6 %forward_last.1 = (f32[4,16,32,128]{3,2,1,0:T(8,128)S(1)}, f32[16,256]{1,0:T(8,128)S(1)}) custom-call(f32[4,16,32,128]{3,2,1,0:T(8,128)S(1)} %get-tuple-element.29.refs_2_.refs_0_, f32[2,4,32,128]{3,2,1,0:T(8,128)S(1)} %get-tuple-element.30.refs_1_, f32[24,32,128]{2,1,0:T(8,128)S(1)} %collective-permute-done.4.refs_2_, ...), custom_call_target="tpu_custom_call" | custom-call | flops 1000000 | bytes 1000000 | tf_op jit(solution)/shard_map/forward_last/pallas_call | solution.py:340
  37.6 1.7 %collective-permute-start.9 = (f32[16,256]{1,0:T(8,128)S(1)}, f32[16,256]{1,0:T(8,128)S(1)}, u32[]{:S(2)}, u32[]{:S(2)}) collective-permute-start(f32[16,256]{1,0:T(8,128)S(1)} %get-tuple-element.40.refs_7_), channel_id=1, source_target_pairs={{0,14},{1,15},{2,0},{3,1},{4,2},{5,3},{6,4},{7,5},{8,6},{9,7},{10,... | collective-permute-start | bytes 49160 | tf_op jit(solution)/shard_map/ppermute | solution.py:354
  39.3 0.5 collective-permute-start.7
  39.8 0.8 %collective-permute-start.6 = (f32[16,256]{1,0:T(8,128)S(1)}, f32[16,256]{1,0:T(8,128)S(1)}, u32[]{:S(2)}, u32[]{:S(2)}) collective-permute-start(f32[16,256]{1,0:T(8,128)S(1)} %get-tuple-element.40.refs_7_), channel_id=1, source_target_pairs={{0,2},{1,3},{2,4},{3,5},{4,6},{5,7},{6,8},{7,9},{8,10},{9,11},{10,... | collective-permute-start | bytes 49160 | tf_op jit(solution)/shard_map/ppermute | solution.py:354
  40.6 0.8 %collective-permute-done.9.refs_9_ = f32[16,256]{1,0:T(8,128)S(1)} collective-permute-done((f32[16,256]{1,0:T(8,128)S(1)}, f32[16,256]{1,0:T(8,128)S(1)}, u32[]{:S(2)}, u32[]{:S(2)}) %collective-permute-start.9) | collective-permute-done | bytes 16416 | tf_op jit(solution)/shard_map/ppermute | solution.py:354
  41.4 3.8 %collective-permute-done.7.refs_6_ = f32[16,256]{1,0:T(8,128)S(1)} collective-permute-done((f32[16,256]{1,0:T(8,128)S(1)}, f32[16,256]{1,0:T(8,128)S(1)}, u32[]{:S(2)}, u32[]{:S(2)}) %collective-permute-start.7) | collective-permute-done | bytes 16416 | tf_op jit(solution)/shard_map/ppermute | solution.py:354
  45.2 1.2 %collective-permute-done.6.refs_5_ = f32[16,256]{1,0:T(8,128)S(1)} collective-permute-done((f32[16,256]{1,0:T(8,128)S(1)}, f32[16,256]{1,0:T(8,128)S(1)}, u32[]{:S(2)}, u32[]{:S(2)}) %collective-permute-start.6) | collective-permute-done | bytes 16416 | tf_op jit(solution)/shard_map/ppermute | solution.py:354
  46.3 6.1 %adjoint.1 = (f32[4,32,128]{2,1,0:T(8,128)S(1)}, f32[4,32,128]{2,1,0:T(8,128)S(1)}, f32[4,32,128]{2,1,0:T(8,128)S(1)}, f32[4,32,128]{2,1,0:T(8,128)S(1)}) custom-call(f32[4,16,32,128]{3,2,1,0:T(8,128)S(1)} %get-tuple-element.29.refs_2_.refs_0_, f32[4,16,32,128]{3,2,1,0:T(8,128)S(1)} %get-tuple-element.39.refs_1_, bf16[256,128]{1,0:T(8,128)(2,1)S(1)} %copy-done.4, ...), custom_call_target="tpu_custom_call" | custom-call | flops 1000000 | bytes 1000000 | tf_op jit(solution)/shard_map/adjoint/pallas_call | solution.py:340
  52.4 0.1 collective-permute-start.10
  52.5 0.1 collective-permute-start.11
  52.6 3.7 %collective-permute-start.12 = (f32[4,32,128]{2,1,0:T(8,128)S(1)}, f32[4,32,128]{2,1,0:T(8,128)S(1)}, u32[]{:S(2)}, u32[]{:S(2)}) collective-permute-start(f32[4,32,128]{2,1,0:T(8,128)S(1)} %get-tuple-element.44), channel_id=1, source_target_pairs={{0,12},{1,13},{2,14},{3,15},{4,0},{5,1},{6,2},{7,3},{8,4},{9,5},{1... | collective-permute-start | bytes 196616 | tf_op jit(solution)/shard_map/ppermute | solution.py:354
  56.3 3.0 %collective-permute-done.10 = f32[4,32,128]{2,1,0:T(8,128)S(1)} collective-permute-done((f32[4,32,128]{2,1,0:T(8,128)S(1)}, f32[4,32,128]{2,1,0:T(8,128)S(1)}, u32[]{:S(2)}, u32[]{:S(2)}) %collective-permute-start.10) | collective-permute-done | bytes 65568 | tf_op jit(solution)/shard_map/ppermute | solution.py:354
  59.2 1.8 %collective-permute-done.11 = f32[4,32,128]{2,1,0:T(8,128)S(1)} collective-permute-done((f32[4,32,128]{2,1,0:T(8,128)S(1)}, f32[4,32,128]{2,1,0:T(8,128)S(1)}, u32[]{:S(2)}, u32[]{:S(2)}) %collective-permute-start.11) | collective-permute-done | bytes 65568 | tf_op jit(solution)/shard_map/ppermute | solution.py:354
  61.0 0.6 %add_add_fusion = f32[4,32,128]{2,1,0:T(8,128)} fusion(f32[4,32,128]{2,1,0:T(8,128)S(1)} %collective-permute-done.12, f32[4,32,128]{2,1,0:T(8,128)S(1)} %collective-permute-done.11, f32[4,32,128]{2,1,0:T(8,128)S(1)} %get-tuple-element.41, f32[4,32,128]{2,1,0:T(8,128)S(1)} %collective-permute-done.10), kind=kLoop, calls=%fused_computation | loop fusion | flops 49152 | bytes 327680 | tf_op jit(solution)/shard_map/add | solution.py:453
  (22 shorter events, 0.1 us)
Async XLA Ops:
  0.0 16.4 %copy-start = (bf16[256,256]{1,0:T(8,128)(2,1)S(1)}, bf16[256,256]{1,0:T(8,128)(2,1)}, u32[]{:S(2)}) copy-start(bf16[256,256]{1,0:T(8,128)(2,1)} %constant.5.clone.refs_7_.refs_5_.refs_3_) | copy-start | bytes 393220
  0.0 16.4 %collective-permute-start = (f32[16,32,128]{2,1,0:T(8,128)}, f32[16,32,128]{2,1,0:T(8,128)S(1)}, u32[]{:S(2)}, u32[]{:S(2)}) collective-permute-start(f32[16,32,128]{2,1,0:T(8,128)} %refs_0_.1), channel_id=1, source_target_pairs={{0,1},{1,2},{2,3},{3,4},{4,5},{5,6},{6,7},{7,8},{8,9},{9,10},{10,1... | collective-permute-start | bytes 786440 | tf_op jit(solution)/shard_map/ppermute | solution.py:354
  0.5 15.9 %collective-permute-start.1 = (f32[16,32,128]{2,1,0:T(8,128)}, f32[16,32,128]{2,1,0:T(8,128)S(1)}, u32[]{:S(2)}, u32[]{:S(2)}) collective-permute-start(f32[16,32,128]{2,1,0:T(8,128)} %refs_0_.1), channel_id=1, source_target_pairs={{0,15},{1,0},{2,1},{3,2},{4,3},{5,4},{6,5},{7,6},{8,7},{9,8},{10,9... | collective-permute-start | bytes 786440 | tf_op jit(solution)/shard_map/ppermute | solution.py:354
  6.1 1.0 %copy-start.2 = (f32[16,32,128]{2,1,0:T(8,128)S(1)}, f32[16,32,128]{2,1,0:T(8,128)}, u32[]{:S(2)}) copy-start(f32[16,32,128]{2,1,0:T(8,128)} %refs_1_.1) | copy-start | bytes 786436
  7.1 0.7 %copy-start.9 = (f32[1,8]{1,0:T(1,128)S(1)}, f32[1,8]{1,0:T(1,128)}, u32[]{:S(2)}) copy-start(f32[1,8]{1,0:T(1,128)} %wavelet.1) | copy-start | bytes 100
  7.8 8.6 %copy-start.4 = (bf16[256,128]{1,0:T(8,128)(2,1)S(1)}, bf16[256,128]{1,0:T(8,128)(2,1)}, u32[]{:S(2)}) copy-start(bf16[256,128]{1,0:T(8,128)(2,1)} %constant.4.clone.refs_6_.refs_4_.refs_2_) | copy-start | bytes 196612
  8.3 8.0 %collective-permute-start.2 = (f32[400,128]{1,0:T(8,128)S(1)}, f32[400,128]{1,0:T(8,128)S(1)}, u32[]{:S(2)}, u32[]{:S(2)}) collective-permute-start(f32[400,128]{1,0:T(8,128)S(1)} %get-tuple-element.25), channel_id=1, source_target_pairs={{0,1},{1,2},{2,3},{3,4},{4,5},{5,6},{6,7},{7,8},{8,9},{9,10},{10,1... | collective-permute-start | bytes 614408 | tf_op jit(solution)/shard_map/ppermute | solution.py:354
  8.4 8.0 %collective-permute-start.3 = (f32[400,128]{1,0:T(8,128)S(1)}, f32[400,128]{1,0:T(8,128)S(1)}, u32[]{:S(2)}, u32[]{:S(2)}) collective-permute-start(f32[400,128]{1,0:T(8,128)S(1)} %get-tuple-element.26), channel_id=1, source_target_pairs={{0,15},{1,0},{2,1},{3,2},{4,3},{5,4},{6,5},{7,6},{8,7},{9,8},{10,9... | collective-permute-start | bytes 614408 | tf_op jit(solution)/shard_map/ppermute | solution.py:354
  12.8 1.2 %copy-start.1 = (f32[64,32,128]{2,1,0:T(8,128)S(1)}, f32[64,32,128]{2,1,0:T(8,128)}, u32[]{:S(2)}) copy-start(f32[64,32,128]{2,1,0:T(8,128)} %courant.1) | copy-start | bytes 3145732
  14.1 0.7 %copy-start.6 = (f32[16,128]{1,0:T(8,128)S(1)}, f32[16,128]{1,0:T(8,128)}, u32[]{:S(2)}) copy-start(f32[16,128]{1,0:T(8,128)} %observed.1) | copy-start | bytes 24580
  14.8 0.7 %copy-start.7 = (s32[256]{0:T(256)S(1)}, s32[256]{0:T(256)}, u32[]{:S(2)}) copy-start(s32[256]{0:T(256)} %param.15) | copy-start | bytes 3076
  15.4 0.7 %copy-start.8 = (s32[256]{0:T(256)S(1)}, s32[256]{0:T(256)}, u32[]{:S(2)}) copy-start(s32[256]{0:T(256)} %param.16) | copy-start | bytes 3076
  16.1 0.9 %copy-start.3 = (f32[16,32,128]{2,1,0:T(8,128)S(1)}, f32[16,32,128]{2,1,0:T(8,128)}, u32[]{:S(2)}) copy-start(f32[16,32,128]{2,1,0:T(8,128)} %refs_1_.1) | copy-start | bytes 786436
  16.1 1.0 %copy-start.5 = (f32[16,32,128]{2,1,0:T(8,128)S(1)}, f32[16,32,128]{2,1,0:T(8,128)}, u32[]{:S(2)}) copy-start(f32[16,32,128]{2,1,0:T(8,128)} %refs_0_.1) | copy-start | bytes 786436
  19.8 14.3 %collective-permute-start.4 = (f32[24,32,128]{2,1,0:T(8,128)S(1)}, f32[24,32,128]{2,1,0:T(8,128)S(1)}, u32[]{:S(2)}, u32[]{:S(2)}) collective-permute-start(f32[24,32,128]{2,1,0:T(8,128)S(1)} %get-tuple-element.31), channel_id=1, source_target_pairs={{0,1},{1,2},{2,3},{3,4},{4,5},{5,6},{6,7},{7,8},{8,9},{9,10},{10,1... | collective-permute-start | bytes 1179656 | tf_op jit(solution)/shard_map/ppermute | solution.py:354
  19.8 14.2 %collective-permute-start.5 = (f32[24,32,128]{2,1,0:T(8,128)S(1)}, f32[24,32,128]{2,1,0:T(8,128)S(1)}, u32[]{:S(2)}, u32[]{:S(2)}) collective-permute-start(f32[24,32,128]{2,1,0:T(8,128)S(1)} %get-tuple-element.32), channel_id=1, source_target_pairs={{0,15},{1,0},{2,1},{3,2},{4,3},{5,4},{6,5},{7,6},{8,7},{9,8},{10,9... | collective-permute-start | bytes 1179656 | tf_op jit(solution)/shard_map/ppermute | solution.py:354
  37.6 3.7 %collective-permute-start.9 = (f32[16,256]{1,0:T(8,128)S(1)}, f32[16,256]{1,0:T(8,128)S(1)}, u32[]{:S(2)}, u32[]{:S(2)}) collective-permute-start(f32[16,256]{1,0:T(8,128)S(1)} %get-tuple-element.40.refs_7_), channel_id=1, source_target_pairs={{0,14},{1,15},{2,0},{3,1},{4,2},{5,3},{6,4},{7,5},{8,6},{9,7},{10,... | collective-permute-start | bytes 49160 | tf_op jit(solution)/shard_map/ppermute | solution.py:354
  39.3 2.1 %collective-permute-start.8 = (f32[16,256]{1,0:T(8,128)S(1)}, f32[16,256]{1,0:T(8,128)S(1)}, u32[]{:S(2)}, u32[]{:S(2)}) collective-permute-start(f32[16,256]{1,0:T(8,128)S(1)} %get-tuple-element.40.refs_7_), channel_id=1, source_target_pairs={{0,15},{1,0},{2,1},{3,2},{4,3},{5,4},{6,5},{7,6},{8,7},{9,8},{10,9... | collective-permute-start | bytes 49160 | tf_op jit(solution)/shard_map/ppermute | solution.py:354
  39.3 5.9 %collective-permute-start.7 = (f32[16,256]{1,0:T(8,128)S(1)}, f32[16,256]{1,0:T(8,128)S(1)}, u32[]{:S(2)}, u32[]{:S(2)}) collective-permute-start(f32[16,256]{1,0:T(8,128)S(1)} %get-tuple-element.40.refs_7_), channel_id=1, source_target_pairs={{0,1},{1,2},{2,3},{3,4},{4,5},{5,6},{6,7},{7,8},{8,9},{9,10},{10,1... | collective-permute-start | bytes 49160 | tf_op jit(solution)/shard_map/ppermute | solution.py:354
  39.8 6.5 %collective-permute-start.6 = (f32[16,256]{1,0:T(8,128)S(1)}, f32[16,256]{1,0:T(8,128)S(1)}, u32[]{:S(2)}, u32[]{:S(2)}) collective-permute-start(f32[16,256]{1,0:T(8,128)S(1)} %get-tuple-element.40.refs_7_), channel_id=1, source_target_pairs={{0,2},{1,3},{2,4},{3,5},{4,6},{5,7},{6,8},{7,9},{8,10},{9,11},{10,... | collective-permute-start | bytes 49160 | tf_op jit(solution)/shard_map/ppermute | solution.py:354
  52.4 6.8 %collective-permute-start.10 = (f32[4,32,128]{2,1,0:T(8,128)S(1)}, f32[4,32,128]{2,1,0:T(8,128)S(1)}, u32[]{:S(2)}, u32[]{:S(2)}) collective-permute-start(f32[4,32,128]{2,1,0:T(8,128)S(1)} %get-tuple-element.42), channel_id=1, source_target_pairs={{0,4},{1,5},{2,6},{3,7},{4,8},{5,9},{6,10},{7,11},{8,12},{9,13},{1... | collective-permute-start | bytes 196616 | tf_op jit(solution)/shard_map/ppermute | solution.py:354
  52.5 8.5 %collective-permute-start.11 = (f32[4,32,128]{2,1,0:T(8,128)S(1)}, f32[4,32,128]{2,1,0:T(8,128)S(1)}, u32[]{:S(2)}, u32[]{:S(2)}) collective-permute-start(f32[4,32,128]{2,1,0:T(8,128)S(1)} %get-tuple-element.43), channel_id=1, source_target_pairs={{0,8},{1,9},{2,10},{3,11},{4,12},{5,13},{6,14},{7,15},{8,0},{9,1},... | collective-permute-start | bytes 196616 | tf_op jit(solution)/shard_map/ppermute | solution.py:354
  52.6 8.5 %collective-permute-start.12 = (f32[4,32,128]{2,1,0:T(8,128)S(1)}, f32[4,32,128]{2,1,0:T(8,128)S(1)}, u32[]{:S(2)}, u32[]{:S(2)}) collective-permute-start(f32[4,32,128]{2,1,0:T(8,128)S(1)} %get-tuple-element.44), channel_id=1, source_target_pairs={{0,12},{1,13},{2,14},{3,15},{4,0},{5,1},{6,2},{7,3},{8,4},{9,5},{1... | collective-permute-start | bytes 196616 | tf_op jit(solution)/shard_map/ppermute | solution.py:354

commit v3 on v2

--- a/solution.py
+++ b/solution.py
@@ -80,7 +80,11 @@
         field[plane, tile, :] = field[plane, tile, :] + jnp.where(hit, pack[step : step + 1], 0.0)
 
 
-def message_kernel(before, wavelet, source, left_out, right_out, pack_out):
+def parity():
+    return lax.rem(lax.axis_index("shot"), 2)
+
+
+def message_kernel(before, wavelet, source, outer_out, mate_out, pack_out):
     rows, span_y, span_z = before.shape
     which = lax.broadcasted_iota(jnp.int32, (16, span_z), 0)
     pack = jnp.where(which >= NT, source[0].astype(F32), 0.0)
@@ -89,10 +93,11 @@
     pack_out[...] = pack
     narrow = RAD * (ROUNDS[0] - 1)
     size = narrow * span_y
-    left_out[:size] = before[:narrow].reshape(size, span_z)
-    right_out[:size] = before[rows - narrow :].reshape(size, span_z)
-    left_out[size:] = pack
-    right_out[size:] = pack
+    odd = parity()
+    outer_out[:size] = before[pl.ds(odd * (rows - narrow), narrow)].reshape(size, span_z)
+    mate_out[:size] = before[pl.ds((1 - odd) * (rows - narrow), narrow)].reshape(size, span_z)
+    outer_out[size:] = pack
+    mate_out[size:] = pack
 
 
 def prepare_kernel(courant, cells, order, observed, pack, model_out, cells_out, observed_out):
@@ -152,28 +157,33 @@
     own = RAD * steps
     cur, old = buf_a, buf_b
     wide, narrow = RAD * steps, RAD * (steps - 1)
+    odd = parity()
+    shape = cur.shape[1:]
+    low, high = own - wide, own + rows
+    cur_outer = jnp.where(odd == 0, low, high)
+    cur_mate = jnp.where(odd == 0, high, low)
     if index == 0:
-        now, before, now_l, now_r, before_l, before_r = refs_in
+        now, before, now_outer, now_mate, before_outer, before_mate = refs_in
         cur[own : own + rows] = now[...]
         old[own : own + rows] = before[...]
-        cur[own - wide : own] = now_l[...]
-        cur[own + rows : own + rows + wide] = now_r[...]
-        if narrow:
-            size = narrow * cur.shape[1]
-            old[own - narrow : own] = before_l[:size].reshape((narrow,) + cur.shape[1:])
-            old[own + rows : own + rows + narrow] = before_r[:size].reshape((narrow,) + cur.shape[1:])
+        cur[pl.ds(cur_outer, wide)] = now_outer[...]
+        cur[pl.ds(cur_mate, wide)] = now_mate[...]
+        size = narrow * shape[0]
+        low = own - narrow
+        old[pl.ds(jnp.where(odd == 0, low, high), narrow)] = before_outer[:size].reshape((narrow,) + shape)
+        old[pl.ds(jnp.where(odd == 0, high, low), narrow)] = before_mate[:size].reshape((narrow,) + shape)
     else:
-        earlier, known, got_l, got_r = refs_in
+        earlier, known, got_outer, got_mate = refs_in
         cur[own : own + rows] = earlier[earlier.shape[0] - 1]
         old[own : own + rows] = earlier[earlier.shape[0] - 2]
-        cur[own - wide : own] = got_l[0:wide]
-        cur[own + rows : own + rows + wide] = got_r[0:wide]
-        if narrow:
-            old[own - RAD : own] = known[0]
-            old[own + rows : own + rows + RAD] = known[1]
-        if narrow > RAD:
-            old[own - narrow : own - RAD] = got_l[wide:]
-            old[own + rows + RAD : own + rows + narrow] = got_r[wide:]
+        cur[pl.ds(cur_outer, wide)] = got_outer[0:wide]
+        cur[pl.ds(cur_mate, wide)] = got_mate[0:wide]
+        old[own - RAD : own] = known[0]
+        old[own + rows : own + rows + RAD] = known[1]
+        low, high = own - narrow, own + rows + RAD
+        more = narrow - RAD
+        old[pl.ds(jnp.where(odd == 0, low, high), more)] = got_outer[wide:]
+        old[pl.ds(jnp.where(odd == 0, high, low), more)] = got_mate[wide:]
     cells = [jnp.max(packs[block, NT : 2 * NT]).astype(jnp.int32) for block in range(3)]
     for step in range(steps):
         halo = RAD * (steps - 1 - step)
@@ -187,37 +197,28 @@
     return cur, old, own
 
 
-def send_shapes(index):
-    steps = ROUNDS[index]
-    return RAD * steps + RAD * max(steps - 2, 0)
-
-
-def gather_packs(pack_own, before_l, before_r, packs):
-    packs[0] = before_l[before_l.shape[0] - 16 :]
+def gather_packs(pack_own, outer, mate, packs):
+    odd = parity()
+    packs[2 * odd] = outer[outer.shape[0] - 16 :]
     packs[1] = pack_own[...]
-    packs[2] = before_r[before_r.shape[0] - 16 :]
+    packs[2 - 2 * odd] = mate[mate.shape[0] - 16 :]
 
 
 def forward_kernel(index, *refs):
     take = 6 if index == 0 else 4
     refs_in, refs = refs[:take], refs[take:]
-    zmat, ymat, model, pack, fields, known, send_l, send_r = refs[:8]
+    zmat, ymat, model, pack, fields, known, send = refs[:7]
     if index == 0:
-        packs, buf_a, buf_b = refs[8:]
+        packs, buf_a, buf_b = refs[7:]
         gather_packs(pack, refs_in[4], refs_in[5], packs)
     else:
-        packs, (buf_a, buf_b) = pack, refs[8:]
+        packs, (buf_a, buf_b) = pack, refs[7:]
     cur, old, own = forward_round(index, refs_in, zmat, ymat, model, packs, fields, buf_a, buf_b)
     rows = 16
     known[0] = old[own - RAD : own]
     known[1] = old[own + rows : own + rows + RAD]
-    wide = RAD * ROUNDS[index + 1]
-    inner = wide - RAD
-    send_l[0:wide] = cur[own : own + wide]
-    send_r[0:wide] = cur[own + rows - wide : own + rows]
-    if inner > RAD:
-        send_l[wide:] = old[own + RAD : own + inner]
-        send_r[wide:] = old[own + rows - inner : own + rows - RAD]
+    send[0:rows] = cur[own : own + rows]
+    send[rows:] = old[own + RAD : own + rows - RAD]
 
 
 def split_exactly(values):
@@ -281,16 +282,23 @@
     for ref in refs[:field_groups]:
         fields += [ref.at[i] for i in range(ref.shape[0])]
     refs = refs[field_groups:]
-    zmat, ymat, model, *adjs = refs[:8]
+    zmat, ymat, model, adj, outer, mate, even_pair, odd_pair = refs[:8]
     outs = refs[8 : 8 + slabs]
-    buf_a, buf_b, image, rows_table = refs[8 + slabs :]
+    buf_a, buf_b, image, rows_table, adjs = refs[8 + slabs :]
+    odd = parity()
+    odd_chip = lax.rem(lax.axis_index("shot") // 2, 2)
+    adjs[2] = adj[...]
+    adjs[1 + 2 * odd] = outer[...]
+    adjs[3 - 2 * odd] = mate[...]
+    adjs[4 - 4 * odd_chip] = even_pair[...]
+    adjs[4 * odd_chip] = odd_pair[...]
     rows = 16
     own = HALO
     span_y, span_z = buf_a.shape[1:]
     table_rows = rows * span_y
     lanes = []
     for block in range(5):
-        cells = adjs[block][NT : NT + 1].astype(jnp.int32)
+        cells = adjs[block, NT : NT + 1].astype(jnp.int32)
         sub = lax.broadcasted_iota(jnp.int32, (table_rows, count), 0)
         rows_table[block] = jnp.where(sub == cells // span_z, 1.0, 0.0).astype(BF)
         lanes.append(cells % span_z)
@@ -304,7 +312,7 @@
             last = min(begin + rows, own + rows + halo)
             if first >= last:
                 continue
-            amounts = adjs[block + 2][step : step + 1]
+            amounts = adjs[block + 2, step : step + 1]
             high = amounts.astype(BF).astype(F32)
             low = amounts - high
             sub = lax.broadcasted_iota(jnp.int32, (span_z, count), 0)
@@ -333,7 +341,7 @@
     mine = lax.axis_index("shot") // PIECES
     thick = rows // slabs
     for i in range(slabs):
-        outs[i][...] = image[pl.ds(lax.rem(mine + i, slabs) * thick, thick)]
+        outs[i][...] = image[pl.ds((mine ^ i) * thick, thick)]
 
 
 def call(kernel, outs, ins, specs=None, scratch=(), cost=(1e6, 1e6), name=None):
@@ -349,9 +357,25 @@
     )(*ins)
 
 
-def shifted(value, steps):
+def swapped(value, partner):
     count = lax.axis_size("shot")
-    return lax.ppermute(value, "shot", [(i, (i + steps) % count) for i in range(count)])
+    return lax.ppermute(value, "shot", [(d, partner(d) % count) for d in range(count)])
+
+
+def with_mate(value):
+    return swapped(value, lambda d: d ^ 1)
+
+
+def with_outer(value):
+    return swapped(value, lambda d: d + 1 if d % 2 else d - 1)
+
+
+def with_even_pair(value):
+    return swapped(value, lambda d: d ^ 2)
+
+
+def with_odd_pair(value):
+    return swapped(value, lambda d: d + 2 if d % 4 >= 2 else d - 2)
 
 
 def per_device(
@@ -364,18 +388,17 @@
     plane = (span_y, span_z)
     zmat, ymat = matrices(span_y, span_z)
 
-    wide = RAD * ROUNDS[0]
-    narrow = wide - RAD
-    now_l, now_r = shifted(wave_now[rows - wide :], 1), shifted(wave_now[:wide], -1)
+    narrow = RAD * (ROUNDS[0] - 1)
+    now_outer, now_mate = with_outer(wave_now), with_mate(wave_now)
     message = jax.ShapeDtypeStruct((narrow * span_y + 16, span_z), F32)
-    to_left, to_right, pack = call(
+    to_outer, to_mate, pack = call(
         message_kernel,
         (message, message, jax.ShapeDtypeStruct((16, span_z), F32)),
         (wave_before, wavelet, source_cell),
         specs=[VMEM, SMEM, SMEM],
         name="message",
     )
-    before_l, before_r = shifted(to_right, 1), shifted(to_left, -1)
+    before_outer, before_mate = with_outer(to_outer), with_mate(to_mate)
 
     model, cells, observed = call(
         prepare_kernel,
@@ -391,17 +414,16 @@
 
     common = (zmat, ymat, model)
     field_list = []
-    ins = (wave_now, wave_before, now_l, now_r, before_l, before_r)
+    ins = (wave_now, wave_before, now_outer, now_mate, before_outer, before_mate)
     for index in range(len(ROUNDS) - 1):
         window = rows + 2 * RAD * ROUNDS[index]
-        sent = send_shapes(index + 1)
+        sent = 2 * rows - 2 * RAD
         packs = (jax.ShapeDtypeStruct((3, 16, span_z), F32),) if index == 0 else ()
-        fields, known, send_l, send_r, *made = call(
+        fields, known, send, *made = call(
             functools.partial(forward_kernel, index),
             (
                 jax.ShapeDtypeStruct((ROUNDS[index], rows) + plane, F32),
                 jax.ShapeDtypeStruct((2, RAD) + plane, F32),
-                jax.ShapeDtypeStruct((sent,) + plane, F32),
                 jax.ShapeDtypeStruct((sent,) + plane, F32),
             )
             + packs,
@@ -411,7 +433,7 @@
         )
         field_list.append(fields)
         pack = made[0] if made else pack
-        ins = (fields, known, shifted(send_r, 1), shifted(send_l, -1))
+        ins = (fields, known, with_outer(send), with_mate(send))
 
     rows_table, lane_table, traces = call(
         functools.partial(tables_kernel, count),
@@ -437,7 +459,7 @@
     )
     field_list.append(fields)
 
-    adjs = [shifted(adj, 2), shifted(adj, 1), adj, shifted(adj, -1), shifted(adj, -2)]
+    adjs = [adj, with_outer(adj), with_mate(adj), with_even_pair(adj), with_odd_pair(adj)]
     slabs = devices // PIECES
     thick = rows // slabs
     parts = call(
@@ -445,12 +467,13 @@
         tuple(jax.ShapeDtypeStruct((thick,) + plane, F32) for _ in range(slabs)),
         (*field_list, zmat, ymat, model, *adjs),
         scratch=[pltpu.VMEM((rows + 2 * HALO,) + plane, F32)] * 2
-        + [pltpu.VMEM((rows,) + plane, F32), pltpu.VMEM((5, table_rows, count), BF)],
+        + [pltpu.VMEM((rows,) + plane, F32), pltpu.VMEM((5, table_rows, count), BF)]
+        + [pltpu.VMEM((5, 2 * NT, count), F32)],
         name="adjoint",
     )
     total = parts[0]
     for i in range(1, slabs):
-        total = total + shifted(parts[i], i * PIECES)
+        total = total + swapped(parts[i], lambda d: d ^ (i * PIECES))
     return total
 
 

time: 62 us -> 59.2 us (0.955)
  starting transfers between devices: 21.3 us -> 18.6 us
  local copies, waits for them, and re-layouts: 5.62 us -> 4.89 us
    ppermute x13, starting transfers between devices: 21.3 us -> 18.6 us  [swapped(): lax.ppermute(value, 'shot', [(d, partner(d) % count) for d in range(count)])]
    unnamed x20, local copies, waits for them, and re-layouts: 5.62 us -> 4.89 us
where the time goes in v3:
time: 59.2 us; the launch traced here: 58.9 us
  starting transfers between devices  18.6 us (31%)
  Pallas kernels  14.3 us (24%)
  waiting for transfers between devices  10.5 us (18%)
  blocking collectives  9.14 us (15%)
  local copies, waits for them, and re-layouts  4.89 us (8%)
  between operations  0.75 us (1%)
  other arithmetic  0.65 us (1%)
    ppermute x13, starting transfers between devices, swapped(): lax.ppermute(value, 'shot', [(d, partner(d) % count) for d in range(count)])  18.6 us
    pallas_call x6, Pallas kernels, call(): pl.pallas_call(kernel, out_shape=outs, in_specs=specs or [VMEM] * len(ins...  14.3 us
    ppermute x13, waiting for transfers between devices, swapped(): lax.ppermute(value, 'shot', [(d, partner(d) % count) for d in range(count)])  10.5 us
    all_to_all x1, blocking collectives, per_device(): lax.all_to_all(observed, 'shot', split_axis=0, concat_axis=0, tiled=True)  9.14 us
    unnamed x20, local copies, waits for them, and re-layouts  4.89 us
  transfers between devices with their start and end apart: 13, of which 5 were waited for; matrix products, arithmetic and copies ran while one was open for 0% of the time, Pallas kernels for 3%

profile of v3, /device:TPU:0, one launch (start us, length us, event | category | flops | bytes accessed | tf_op | source)
XLA Modules:
  0.0 58.9 jit_solution(15153203517618271292)
XLA Ops:
  0.0 5.4 %collective-permute-start = (f32[16,32,128]{2,1,0:T(8,128)}, f32[16,32,128]{2,1,0:T(8,128)S(1)}, u32[]{:S(2)}, u32[]{:S(2)}) collective-permute-start(f32[16,32,128]{2,1,0:T(8,128)} %refs_0_.1), channel_id=1, source_target_pairs={{0,15},{1,2},{2,1},{3,4},{4,3},{5,6},{6,5},{7,8},{8,7},{9,10},{10,... | collective-permute-start | bytes 786440 | tf_op jit(solution)/shard_map/ppermute | solution.py:362
  5.4 0.0 collective-permute-start.1
  6.1 0.0 copy-start.2
  6.1 0.9 %copy-done.2 = f32[16,32,128]{2,1,0:T(8,128)S(1)} copy-done((f32[16,32,128]{2,1,0:T(8,128)S(1)}, f32[16,32,128]{2,1,0:T(8,128)}, u32[]{:S(2)}) %copy-start.2) | copy-done | bytes 262168
  7.1 0.7 %copy-done.9 = f32[1,8]{1,0:T(1,128)S(1)} copy-done((f32[1,8]{1,0:T(1,128)S(1)}, f32[1,8]{1,0:T(1,128)}, u32[]{:S(2)}) %copy-start.9) | copy-done | bytes 56
  7.7 0.6 message.1
  8.3 0.8 %collective-permute-start.2 = (f32[400,128]{1,0:T(8,128)S(1)}, f32[400,128]{1,0:T(8,128)S(1)}, u32[]{:S(2)}, u32[]{:S(2)}) collective-permute-start(f32[400,128]{1,0:T(8,128)S(1)} %get-tuple-element.24), channel_id=1, source_target_pairs={{0,15},{1,2},{2,1},{3,4},{4,3},{5,6},{6,5},{7,8},{8,7},{9,10},{10,... | collective-permute-start | bytes 614408 | tf_op jit(solution)/shard_map/ppermute | solution.py:362
  9.1 1.2 %copy-done.1 = f32[64,32,128]{2,1,0:T(8,128)S(1)} copy-done((f32[64,32,128]{2,1,0:T(8,128)S(1)}, f32[64,32,128]{2,1,0:T(8,128)}, u32[]{:S(2)}) %copy-start.1) | copy-done | bytes 1048600
  10.3 0.7 %copy-done.6 = f32[16,128]{1,0:T(8,128)S(1)} copy-done((f32[16,128]{1,0:T(8,128)S(1)}, f32[16,128]{1,0:T(8,128)}, u32[]{:S(2)}) %copy-start.6) | copy-done | bytes 8216
  11.0 0.7 %copy-done.7 = s32[256]{0:T(256)S(1)} copy-done((s32[256]{0:T(256)S(1)}, s32[256]{0:T(256)}, u32[]{:S(2)}) %copy-start.7) | copy-done | bytes 1048
  11.7 0.7 %copy-done.8 = s32[256]{0:T(256)S(1)} copy-done((s32[256]{0:T(256)S(1)}, s32[256]{0:T(256)}, u32[]{:S(2)}) %copy-start.8) | copy-done | bytes 1048
  12.4 0.2 prepare.1
  12.6 3.7 %collective-permute-done.2.refs_4_ = f32[400,128]{1,0:T(8,128)S(1)} collective-permute-done((f32[400,128]{1,0:T(8,128)S(1)}, f32[400,128]{1,0:T(8,128)S(1)}, u32[]{:S(2)}, u32[]{:S(2)}) %collective-permute-start.2) | collective-permute-done | bytes 204832 | tf_op jit(solution)/shard_map/ppermute | solution.py:362
  16.4 0.0 collective-permute-done.refs_2_
  16.4 0.0 collective-permute-done.1.refs_3_
  16.4 2.7 %forward.1 = (f32[4,16,32,128]{3,2,1,0:T(8,128)S(1)}, f32[2,4,32,128]{3,2,1,0:T(8,128)S(1)}, f32[24,32,128]{2,1,0:T(8,128)S(1)}, f32[3,16,128]{2,1,0:T(8,128)S(1)}) custom-call(f32[16,32,128]{2,1,0:T(8,128)S(1)} %copy-done.5, f32[16,32,128]{2,1,0:T(8,128)S(1)} %copy-done.3, f32[16,32,128]{2,1,0:T(8,128)S(1)} %collective-permute-done.refs_2_, ...), custom_call_target="tpu_custom_call" | custom-call | flops 1000000 | bytes 1000000 | tf_op jit(solution)/shard_map/forward/pallas_call | solution.py:348
  19.1 0.1 collective-permute-start.5
  19.2 3.0 %collective-permute-start.4 = (f32[24,32,128]{2,1,0:T(8,128)S(1)}, f32[24,32,128]{2,1,0:T(8,128)S(1)}, u32[]{:S(2)}, u32[]{:S(2)}) collective-permute-start(f32[24,32,128]{2,1,0:T(8,128)S(1)} %get-tuple-element.30), channel_id=1, source_target_pairs={{0,15},{1,2},{2,1},{3,4},{4,3},{5,6},{6,5},{7,8},{8,7},{9,10},{10,... | collective-permute-start | bytes 1179656 | tf_op jit(solution)/shard_map/ppermute | solution.py:362
  22.2 9.1 %all_to_all.11 = f32[16,1,128]{2,1,0:T(1,128)S(1)} all-to-all(f32[16,1,128]{2,1,0:T(1,128)S(1)} %bitcast.7), channel_id=1, replica_groups=mesh['groups'=2,'shot'=16] {'shot'}, dimensions={0} | all-to-all | bytes 16384 | tf_op jit(solution)/shard_map/all_to_all | solution.py:413
  31.3 0.8 %traces.1 = (bf16[256,512]{1,0:T(8,128)(2,1)S(1)}, f32[256,256]{1,0:T(8,128)S(1)}, f32[8,256]{1,0:T(8,128)S(1)}) custom-call(f32[8,256]{1,0:T(8,128)S(1)} %get-tuple-element.32.refs_0_.refs_8_, f32[16,128]{1,0:T(8,128)S(1)} %bitcast.6, f32[4,16,32,128]{3,2,1,0:T(8,128)S(1)} %get-tuple-element.28.refs_2_.refs_0_), custom_call_target="tpu_custom_call" | custom-call | flops 1000000 | bytes 1000000 | tf_op jit(solution)/shard_map/traces/pallas_call | solution.py:348
  32.2 3.8 %forward_last.1 = (f32[4,16,32,128]{3,2,1,0:T(8,128)S(1)}, f32[16,256]{1,0:T(8,128)S(1)}) custom-call(f32[4,16,32,128]{3,2,1,0:T(8,128)S(1)} %get-tuple-element.28.refs_2_.refs_0_, f32[2,4,32,128]{3,2,1,0:T(8,128)S(1)} %get-tuple-element.29.refs_1_, f32[24,32,128]{2,1,0:T(8,128)S(1)} %collective-permute-done.4.refs_2_, ...), custom_call_target="tpu_custom_call" | custom-call | flops 1000000 | bytes 1000000 | tf_op jit(solution)/shard_map/forward_last/pallas_call | solution.py:348
  36.0 2.4 %collective-permute-start.9 = (f32[16,256]{1,0:T(8,128)S(1)}, f32[16,256]{1,0:T(8,128)S(1)}, u32[]{:S(2)}, u32[]{:S(2)}) collective-permute-start(f32[16,256]{1,0:T(8,128)S(1)} %get-tuple-element.38.refs_5_), channel_id=1, source_target_pairs={{0,14},{1,15},{2,4},{3,5},{4,2},{5,3},{6,8},{7,9},{8,6},{9,7},{10,... | collective-permute-start | bytes 49160 | tf_op jit(solution)/shard_map/ppermute | solution.py:362
  38.5 2.4 %collective-permute-start.6 = (f32[16,256]{1,0:T(8,128)S(1)}, f32[16,256]{1,0:T(8,128)S(1)}, u32[]{:S(2)}, u32[]{:S(2)}) collective-permute-start(f32[16,256]{1,0:T(8,128)S(1)} %get-tuple-element.38.refs_5_), channel_id=1, source_target_pairs={{0,15},{1,2},{2,1},{3,4},{4,3},{5,6},{6,5},{7,8},{8,7},{9,10},{10,... | collective-permute-start | bytes 49160 | tf_op jit(solution)/shard_map/ppermute | solution.py:362
  40.9 1.7 %collective-permute-done.9.refs_9_ = f32[16,256]{1,0:T(8,128)S(1)} collective-permute-done((f32[16,256]{1,0:T(8,128)S(1)}, f32[16,256]{1,0:T(8,128)S(1)}, u32[]{:S(2)}, u32[]{:S(2)}) %collective-permute-start.9) | collective-permute-done | bytes 16416 | tf_op jit(solution)/shard_map/ppermute | solution.py:362
  42.6 1.8 %collective-permute-done.6.refs_6_ = f32[16,256]{1,0:T(8,128)S(1)} collective-permute-done((f32[16,256]{1,0:T(8,128)S(1)}, f32[16,256]{1,0:T(8,128)S(1)}, u32[]{:S(2)}, u32[]{:S(2)}) %collective-permute-start.6) | collective-permute-done | bytes 16416 | tf_op jit(solution)/shard_map/ppermute | solution.py:362
  44.3 6.1 %adjoint.1 = (f32[4,32,128]{2,1,0:T(8,128)S(1)}, f32[4,32,128]{2,1,0:T(8,128)S(1)}, f32[4,32,128]{2,1,0:T(8,128)S(1)}, f32[4,32,128]{2,1,0:T(8,128)S(1)}) custom-call(f32[4,16,32,128]{3,2,1,0:T(8,128)S(1)} %get-tuple-element.28.refs_2_.refs_0_, f32[4,16,32,128]{3,2,1,0:T(8,128)S(1)} %get-tuple-element.37.refs_1_, bf16[256,128]{1,0:T(8,128)(2,1)S(1)} %copy-done.4, ...), custom_call_target="tpu_custom_call" | custom-call | flops 1000000 | bytes 1000000 | tf_op jit(solution)/shard_map/adjoint/pallas_call | solution.py:348
  50.4 0.1 collective-permute-start.10
  50.5 1.6 %collective-permute-start.11 = (f32[4,32,128]{2,1,0:T(8,128)S(1)}, f32[4,32,128]{2,1,0:T(8,128)S(1)}, u32[]{:S(2)}, u32[]{:S(2)}) collective-permute-start(f32[4,32,128]{2,1,0:T(8,128)S(1)} %get-tuple-element.41), channel_id=1, source_target_pairs={{0,8},{1,9},{2,10},{3,11},{4,12},{5,13},{6,14},{7,15},{8,0},{9,1},... | collective-permute-start | bytes 196616 | tf_op jit(solution)/shard_map/ppermute | solution.py:362
  52.1 2.8 %collective-permute-start.12 = (f32[4,32,128]{2,1,0:T(8,128)S(1)}, f32[4,32,128]{2,1,0:T(8,128)S(1)}, u32[]{:S(2)}, u32[]{:S(2)}) collective-permute-start(f32[4,32,128]{2,1,0:T(8,128)S(1)} %get-tuple-element.42), channel_id=1, source_target_pairs={{0,12},{1,13},{2,14},{3,15},{4,8},{5,9},{6,10},{7,11},{8,4},{9,5},... | collective-permute-start | bytes 196616 | tf_op jit(solution)/shard_map/ppermute | solution.py:362
  54.9 0.9 %collective-permute-done.11 = f32[4,32,128]{2,1,0:T(8,128)S(1)} collective-permute-done((f32[4,32,128]{2,1,0:T(8,128)S(1)}, f32[4,32,128]{2,1,0:T(8,128)S(1)}, u32[]{:S(2)}, u32[]{:S(2)}) %collective-permute-start.11) | collective-permute-done | bytes 65568 | tf_op jit(solution)/shard_map/ppermute | solution.py:362
  55.7 2.5 %collective-permute-done.12 = f32[4,32,128]{2,1,0:T(8,128)S(1)} collective-permute-done((f32[4,32,128]{2,1,0:T(8,128)S(1)}, f32[4,32,128]{2,1,0:T(8,128)S(1)}, u32[]{:S(2)}, u32[]{:S(2)}) %collective-permute-start.12) | collective-permute-done | bytes 65568 | tf_op jit(solution)/shard_map/ppermute | solution.py:362
  58.2 0.6 %add_add_fusion = f32[4,32,128]{2,1,0:T(8,128)} fusion(f32[4,32,128]{2,1,0:T(8,128)S(1)} %collective-permute-done.12, f32[4,32,128]{2,1,0:T(8,128)S(1)} %collective-permute-done.11, f32[4,32,128]{2,1,0:T(8,128)S(1)} %get-tuple-element.39, f32[4,32,128]{2,1,0:T(8,128)S(1)} %collective-permute-done.10), kind=kLoop, calls=%fused_computation | loop fusion | flops 49152 | bytes 327680 | tf_op jit(solution)/shard_map/add | solution.py:476
  (22 shorter events, 0.0 us)
Async XLA Ops:
  0.0 16.4 %copy-start = (bf16[256,256]{1,0:T(8,128)(2,1)S(1)}, bf16[256,256]{1,0:T(8,128)(2,1)}, u32[]{:S(2)}) copy-start(bf16[256,256]{1,0:T(8,128)(2,1)} %constant.5.clone.refs_7_.refs_5_.refs_3_) | copy-start | bytes 393220
  0.0 16.4 %collective-permute-start = (f32[16,32,128]{2,1,0:T(8,128)}, f32[16,32,128]{2,1,0:T(8,128)S(1)}, u32[]{:S(2)}, u32[]{:S(2)}) collective-permute-start(f32[16,32,128]{2,1,0:T(8,128)} %refs_0_.1), channel_id=1, source_target_pairs={{0,15},{1,2},{2,1},{3,4},{4,3},{5,6},{6,5},{7,8},{8,7},{9,10},{10,... | collective-permute-start | bytes 786440 | tf_op jit(solution)/shard_map/ppermute | solution.py:362
  5.4 10.9 %collective-permute-start.1 = (f32[16,32,128]{2,1,0:T(8,128)}, f32[16,32,128]{2,1,0:T(8,128)S(1)}, u32[]{:S(2)}, u32[]{:S(2)}) collective-permute-start(f32[16,32,128]{2,1,0:T(8,128)} %refs_0_.1), channel_id=1, source_target_pairs={{0,1},{1,0},{2,3},{3,2},{4,5},{5,4},{6,7},{7,6},{8,9},{9,8},{10,11... | collective-permute-start | bytes 786440 | tf_op jit(solution)/shard_map/ppermute | solution.py:362
  6.1 1.0 %copy-start.2 = (f32[16,32,128]{2,1,0:T(8,128)S(1)}, f32[16,32,128]{2,1,0:T(8,128)}, u32[]{:S(2)}) copy-start(f32[16,32,128]{2,1,0:T(8,128)} %refs_1_.1) | copy-start | bytes 786436
  7.1 0.7 %copy-start.9 = (f32[1,8]{1,0:T(1,128)S(1)}, f32[1,8]{1,0:T(1,128)}, u32[]{:S(2)}) copy-start(f32[1,8]{1,0:T(1,128)} %wavelet.1) | copy-start | bytes 100
  7.7 8.7 %copy-start.4 = (bf16[256,128]{1,0:T(8,128)(2,1)S(1)}, bf16[256,128]{1,0:T(8,128)(2,1)}, u32[]{:S(2)}) copy-start(bf16[256,128]{1,0:T(8,128)(2,1)} %constant.4.clone.refs_6_.refs_4_.refs_2_) | copy-start | bytes 196612
  8.3 8.1 %collective-permute-start.2 = (f32[400,128]{1,0:T(8,128)S(1)}, f32[400,128]{1,0:T(8,128)S(1)}, u32[]{:S(2)}, u32[]{:S(2)}) collective-permute-start(f32[400,128]{1,0:T(8,128)S(1)} %get-tuple-element.24), channel_id=1, source_target_pairs={{0,15},{1,2},{2,1},{3,4},{4,3},{5,6},{6,5},{7,8},{8,7},{9,10},{10,... | collective-permute-start | bytes 614408 | tf_op jit(solution)/shard_map/ppermute | solution.py:362
  9.1 7.3 %collective-permute-start.3 = (f32[400,128]{1,0:T(8,128)S(1)}, f32[400,128]{1,0:T(8,128)S(1)}, u32[]{:S(2)}, u32[]{:S(2)}) collective-permute-start(f32[400,128]{1,0:T(8,128)S(1)} %get-tuple-element.25), channel_id=1, source_target_pairs={{0,1},{1,0},{2,3},{3,2},{4,5},{5,4},{6,7},{7,6},{8,9},{9,8},{10,11... | collective-permute-start | bytes 614408 | tf_op jit(solution)/shard_map/ppermute | solution.py:362
  9.1 1.2 %copy-start.1 = (f32[64,32,128]{2,1,0:T(8,128)S(1)}, f32[64,32,128]{2,1,0:T(8,128)}, u32[]{:S(2)}) copy-start(f32[64,32,128]{2,1,0:T(8,128)} %courant.1) | copy-start | bytes 3145732
  10.3 0.7 %copy-start.6 = (f32[16,128]{1,0:T(8,128)S(1)}, f32[16,128]{1,0:T(8,128)}, u32[]{:S(2)}) copy-start(f32[16,128]{1,0:T(8,128)} %observed.1) | copy-start | bytes 24580
  11.0 0.7 %copy-start.7 = (s32[256]{0:T(256)S(1)}, s32[256]{0:T(256)}, u32[]{:S(2)}) copy-start(s32[256]{0:T(256)} %param.15) | copy-start | bytes 3076
  11.7 0.7 %copy-start.8 = (s32[256]{0:T(256)S(1)}, s32[256]{0:T(256)}, u32[]{:S(2)}) copy-start(s32[256]{0:T(256)} %param.16) | copy-start | bytes 3076
  12.4 4.0 %copy-start.3 = (f32[16,32,128]{2,1,0:T(8,128)S(1)}, f32[16,32,128]{2,1,0:T(8,128)}, u32[]{:S(2)}) copy-start(f32[16,32,128]{2,1,0:T(8,128)} %refs_1_.1) | copy-start | bytes 786436
  12.4 4.0 %copy-start.5 = (f32[16,32,128]{2,1,0:T(8,128)S(1)}, f32[16,32,128]{2,1,0:T(8,128)}, u32[]{:S(2)}) copy-start(f32[16,32,128]{2,1,0:T(8,128)} %refs_0_.1) | copy-start | bytes 786436
  19.1 13.1 %collective-permute-start.5 = (f32[24,32,128]{2,1,0:T(8,128)S(1)}, f32[24,32,128]{2,1,0:T(8,128)S(1)}, u32[]{:S(2)}, u32[]{:S(2)}) collective-permute-start(f32[24,32,128]{2,1,0:T(8,128)S(1)} %get-tuple-element.30), channel_id=1, source_target_pairs={{0,1},{1,0},{2,3},{3,2},{4,5},{5,4},{6,7},{7,6},{8,9},{9,8},{10,11... | collective-permute-start | bytes 1179656 | tf_op jit(solution)/shard_map/ppermute | solution.py:362
  19.2 13.0 %collective-permute-start.4 = (f32[24,32,128]{2,1,0:T(8,128)S(1)}, f32[24,32,128]{2,1,0:T(8,128)S(1)}, u32[]{:S(2)}, u32[]{:S(2)}) collective-permute-start(f32[24,32,128]{2,1,0:T(8,128)S(1)} %get-tuple-element.30), channel_id=1, source_target_pairs={{0,15},{1,2},{2,1},{3,4},{4,3},{5,6},{6,5},{7,8},{8,7},{9,10},{10,... | collective-permute-start | bytes 1179656 | tf_op jit(solution)/shard_map/ppermute | solution.py:362
  36.0 6.5 %collective-permute-start.9 = (f32[16,256]{1,0:T(8,128)S(1)}, f32[16,256]{1,0:T(8,128)S(1)}, u32[]{:S(2)}, u32[]{:S(2)}) collective-permute-start(f32[16,256]{1,0:T(8,128)S(1)} %get-tuple-element.38.refs_5_), channel_id=1, source_target_pairs={{0,14},{1,15},{2,4},{3,5},{4,2},{5,3},{6,8},{7,9},{8,6},{9,7},{10,... | collective-permute-start | bytes 49160 | tf_op jit(solution)/shard_map/ppermute | solution.py:362
  38.5 4.1 %collective-permute-start.8 = (f32[16,256]{1,0:T(8,128)S(1)}, f32[16,256]{1,0:T(8,128)S(1)}, u32[]{:S(2)}, u32[]{:S(2)}) collective-permute-start(f32[16,256]{1,0:T(8,128)S(1)} %get-tuple-element.38.refs_5_), channel_id=1, source_target_pairs={{0,2},{1,3},{2,0},{3,1},{4,6},{5,7},{6,4},{7,5},{8,10},{9,11},{10,... | collective-permute-start | bytes 49160 | tf_op jit(solution)/shard_map/ppermute | solution.py:362
  38.5 4.1 %collective-permute-start.7 = (f32[16,256]{1,0:T(8,128)S(1)}, f32[16,256]{1,0:T(8,128)S(1)}, u32[]{:S(2)}, u32[]{:S(2)}) collective-permute-start(f32[16,256]{1,0:T(8,128)S(1)} %get-tuple-element.38.refs_5_), channel_id=1, source_target_pairs={{0,1},{1,0},{2,3},{3,2},{4,5},{5,4},{6,7},{7,6},{8,9},{9,8},{10,11... | collective-permute-start | bytes 49160 | tf_op jit(solution)/shard_map/ppermute | solution.py:362
  38.5 5.9 %collective-permute-start.6 = (f32[16,256]{1,0:T(8,128)S(1)}, f32[16,256]{1,0:T(8,128)S(1)}, u32[]{:S(2)}, u32[]{:S(2)}) collective-permute-start(f32[16,256]{1,0:T(8,128)S(1)} %get-tuple-element.38.refs_5_), channel_id=1, source_target_pairs={{0,15},{1,2},{2,1},{3,4},{4,3},{5,6},{6,5},{7,8},{8,7},{9,10},{10,... | collective-permute-start | bytes 49160 | tf_op jit(solution)/shard_map/ppermute | solution.py:362
  50.4 4.5 %collective-permute-start.10 = (f32[4,32,128]{2,1,0:T(8,128)S(1)}, f32[4,32,128]{2,1,0:T(8,128)S(1)}, u32[]{:S(2)}, u32[]{:S(2)}) collective-permute-start(f32[4,32,128]{2,1,0:T(8,128)S(1)} %get-tuple-element.40), channel_id=1, source_target_pairs={{0,4},{1,5},{2,6},{3,7},{4,0},{5,1},{6,2},{7,3},{8,12},{9,13},{10,... | collective-permute-start | bytes 196616 | tf_op jit(solution)/shard_map/ppermute | solution.py:362
  50.5 5.2 %collective-permute-start.11 = (f32[4,32,128]{2,1,0:T(8,128)S(1)}, f32[4,32,128]{2,1,0:T(8,128)S(1)}, u32[]{:S(2)}, u32[]{:S(2)}) collective-permute-start(f32[4,32,128]{2,1,0:T(8,128)S(1)} %get-tuple-element.41), channel_id=1, source_target_pairs={{0,8},{1,9},{2,10},{3,11},{4,12},{5,13},{6,14},{7,15},{8,0},{9,1},... | collective-permute-start | bytes 196616 | tf_op jit(solution)/shard_map/ppermute | solution.py:362
  52.1 6.1 %collective-permute-start.12 = (f32[4,32,128]{2,1,0:T(8,128)S(1)}, f32[4,32,128]{2,1,0:T(8,128)S(1)}, u32[]{:S(2)}, u32[]{:S(2)}) collective-permute-start(f32[4,32,128]{2,1,0:T(8,128)S(1)} %get-tuple-element.42), channel_id=1, source_target_pairs={{0,12},{1,13},{2,14},{3,15},{4,8},{5,9},{6,10},{7,11},{8,4},{9,5},... | collective-permute-start | bytes 196616 | tf_op jit(solution)/shard_map/ppermute | solution.py:362

commit v4 on v3

--- a/solution.py
+++ b/solution.py
@@ -33,8 +33,12 @@
 
 def matrices(span_y, span_z):
     along_z = np.concatenate([band(span_z)] * 2, axis=0)
-    along_y = np.kron(np.eye(GROUP), band(span_y))
-    return jnp.asarray(along_z, BF), jnp.asarray(along_y, BF)
+    tiles = span_y // 8
+    along_y = band(span_y).reshape(tiles, 8, tiles, 8)
+    full = np.zeros((tiles, GROUP, 8, tiles, GROUP, 8), np.float32)
+    for i in range(GROUP):
+        full[:, i, :, :, i, :] = along_y
+    return jnp.asarray(along_z, BF), jnp.asarray(full.reshape(GROUP * span_y, GROUP * span_y), BF)
 
 
 def split(values):
@@ -51,18 +55,23 @@
     span_y, span_z = cur.shape[1:]
     zmat, ymat = zmat[...], ymat[...]
     for base in range(first, last, GROUP):
-        group = cur[base : base + GROUP].reshape(GROUP * span_y, span_z)
+        columns = [slice(j, j + 8) for j in range(0, span_y, 8)]
+        order = [(i, column) for column in columns for i in range(GROUP)]
+        group = jnp.concatenate([cur[base + i, column] for i, column in order], axis=0)
         pair = jnp.concatenate(split(group), axis=1)
         z_part = dot(pair, zmat)
         y_part = dot(ymat, pair)
-        for i in range(GROUP):
-            x = base + i
-            rows = slice(i * span_y, (i + 1) * span_y)
-            here = cur[x]
-            total = CENTER * here + z_part[rows] + y_part[rows, :span_z] + y_part[rows, span_z:]
-            for k, weight in enumerate(WEIGHTS, 1):
-                total = total + weight * (cur[x + k] + cur[x - k])
-            old[x] = 2.0 * here - old[x] + model[x + model_shift] * total
+        for j, column in enumerate(columns):
+            tiles = [cur[base - RAD + q, column] for q in range(GROUP + 2 * RAD)]
+            for i in range(GROUP):
+                x = base + i
+                at = (j * GROUP + i) * 8
+                rows = slice(at, at + 8)
+                here = tiles[i + RAD]
+                total = z_part[rows] + (y_part[rows, :span_z] + y_part[rows, span_z:]) + CENTER * here
+                for k, weight in enumerate(WEIGHTS, 1):
+                    total = total + weight * (tiles[i + RAD + k] + tiles[i + RAD - k])
+                old[x, column] = (here + here - old[x, column]) + model[x + model_shift, column] * total
 
 
 def add_source(field, pack, cell, step, own, block, halo, rows):
@@ -71,13 +80,13 @@
     y = (cell // span_z) % span_y
     z = cell % span_z
 
-    @pl.when((plane >= own - halo) & (plane < own + rows + halo))
-    def _():
-        tile = pl.ds(pl.multiple_of((y // 8) * 8, 8), 8)
-        sub = lax.broadcasted_iota(jnp.int32, (8, span_z), 0)
-        lane = lax.broadcasted_iota(jnp.int32, (8, span_z), 1)
-        hit = (sub == y % 8) & (lane == z)
-        field[plane, tile, :] = field[plane, tile, :] + jnp.where(hit, pack[step : step + 1], 0.0)
+    inside = (plane >= own - halo) & (plane < own + rows + halo)
+    plane = jnp.where(inside, plane, own)
+    tile = pl.ds(pl.multiple_of((y // 8) * 8, 8), 8)
+    sub = lax.broadcasted_iota(jnp.int32, (8, span_z), 0)
+    lane = lax.broadcasted_iota(jnp.int32, (8, span_z), 1)
+    hit = (sub == jnp.where(inside, y % 8, 8)) & (lane == z)
+    field[plane, tile, :] = field[plane, tile, :] + jnp.where(hit, pack[step : step + 1], 0.0)
 
 
 def parity():
@@ -277,17 +286,40 @@
     adj[NT:] = cells[...]
 
 
-def adjoint_kernel(field_groups, slabs, count, *refs):
+def source_planes(rows_table, lanes, amounts, span_z):
+    high = amounts.astype(BF).astype(F32)
+    low = amounts - high
+    sub = lax.broadcasted_iota(jnp.int32, (span_z, lanes.shape[1]), 0)
+    hit = sub == lanes
+    both = jnp.concatenate([jnp.where(hit, high, 0.0).astype(BF), jnp.where(hit, low, 0.0).astype(BF)], axis=0)
+    added = dot(rows_table, both, (((1,), (1,)), ((), ())))
+    return added[:, :span_z] + added[:, span_z:]
+
+
+def injection_table(cells, table_rows, span_z):
+    sub = lax.broadcasted_iota(jnp.int32, (table_rows, cells.shape[1]), 0)
+    return jnp.where(sub == cells // span_z, 1.0, 0.0).astype(BF)
+
+
+def own_sources_kernel(adj, out):
+    rows, span_y, span_z = out.shape[1:]
+    cells = adj[NT : NT + 1].astype(jnp.int32)
+    table = injection_table(cells, rows * span_y, span_z)
+    for step in range(NT):
+        added = source_planes(table, cells % span_z, adj[step : step + 1], span_z)
+        out[step] = added.reshape(rows, span_y, span_z)
+
+
+def adjoint_kernel(field_groups, slabs, *refs):
     fields = []
     for ref in refs[:field_groups]:
         fields += [ref.at[i] for i in range(ref.shape[0])]
     refs = refs[field_groups:]
-    zmat, ymat, model, adj, outer, mate, even_pair, odd_pair = refs[:8]
+    zmat, ymat, model, sources, outer, mate, even_pair, odd_pair = refs[:8]
     outs = refs[8 : 8 + slabs]
     buf_a, buf_b, image, rows_table, adjs = refs[8 + slabs :]
     odd = parity()
     odd_chip = lax.rem(lax.axis_index("shot") // 2, 2)
-    adjs[2] = adj[...]
     adjs[1 + 2 * odd] = outer[...]
     adjs[3 - 2 * odd] = mate[...]
     adjs[4 - 4 * odd_chip] = even_pair[...]
@@ -296,12 +328,11 @@
     own = HALO
     span_y, span_z = buf_a.shape[1:]
     table_rows = rows * span_y
-    lanes = []
-    for block in range(5):
-        cells = adjs[block, NT : NT + 1].astype(jnp.int32)
-        sub = lax.broadcasted_iota(jnp.int32, (table_rows, count), 0)
-        rows_table[block] = jnp.where(sub == cells // span_z, 1.0, 0.0).astype(BF)
-        lanes.append(cells % span_z)
+    lanes = {}
+    for block in (-2, -1, 1, 2):
+        cells = adjs[block + 2, NT : NT + 1].astype(jnp.int32)
+        rows_table[block + 2] = injection_table(cells, table_rows, span_z)
+        lanes[block] = cells % span_z
 
     def inject(field, number):
         halo = RAD * (NT - number)
@@ -312,17 +343,12 @@
             last = min(begin + rows, own + rows + halo)
             if first >= last:
                 continue
-            amounts = adjs[block + 2, step : step + 1]
-            high = amounts.astype(BF).astype(F32)
-            low = amounts - high
-            sub = lax.broadcasted_iota(jnp.int32, (span_z, count), 0)
-            hit = sub == lanes[block + 2]
-            both = jnp.concatenate(
-                [jnp.where(hit, high, 0.0).astype(BF), jnp.where(hit, low, 0.0).astype(BF)], axis=0
-            )
-            table = rows_table[block + 2, (first - begin) * span_y : (last - begin) * span_y, :]
-            added = dot(table, both, (((1,), (1,)), ((), ())))
-            added = (added[:, :span_z] + added[:, span_z:]).reshape(last - first, span_y, span_z)
+            if block:
+                table = rows_table[block + 2, (first - begin) * span_y : (last - begin) * span_y, :]
+                added = source_planes(table, lanes[block], adjs[block + 2, step : step + 1], span_z)
+                added = added.reshape(last - first, span_y, span_z)
+            else:
+                added = sources[step]
             if number == 1:
                 field[first:last] = added
             else:
@@ -459,11 +485,14 @@
     )
     field_list.append(fields)
 
-    adjs = [adj, with_outer(adj), with_mate(adj), with_even_pair(adj), with_odd_pair(adj)]
+    sources = call(
+        own_sources_kernel, jax.ShapeDtypeStruct((NT, rows) + plane, F32), (adj,), name="own_sources"
+    )
+    adjs = [sources, with_outer(adj), with_mate(adj), with_even_pair(adj), with_odd_pair(adj)]
     slabs = devices // PIECES
     thick = rows // slabs
     parts = call(
-        functools.partial(adjoint_kernel, len(field_list), slabs, count),
+        functools.partial(adjoint_kernel, len(field_list), slabs),
         tuple(jax.ShapeDtypeStruct((thick,) + plane, F32) for _ in range(slabs)),
         (*field_list, zmat, ymat, model, *adjs),
         scratch=[pltpu.VMEM((rows + 2 * HALO,) + plane, F32)] * 2

time: 59.2 us -> 62.5 us (1.056)
  local copies, waits for them, and re-layouts: 4.89 us -> 8.52 us
  waiting for transfers between devices: 10.5 us -> 9.85 us
    unnamed x20, local copies, waits for them, and re-layouts: 4.89 us -> 8.52 us
    ppermute x13, waiting for transfers between devices: 10.5 us -> 9.85 us  [swapped(): lax.ppermute(value, 'shot', [(d, partner(d) % count) for d in range(count)])]
    pallas_call x6 -> x7, Pallas kernels: 14.3 us -> 14.6 us  [call(): pl.pallas_call(kernel, out_shape=outs, in_specs=specs or [VMEM] * len(ins...]
  transfers between devices with their start and end apart: 13 -> 13, of which waited for: 5 -> 5; matrix products, arithmetic and copies ran while one was open for 0% -> 0% of each run, Pallas kernels for 3% -> 4%
where the time goes in v4:
time: 62.5 us; the launch traced here: 62.1 us
  starting transfers between devices  18.5 us (30%)
  Pallas kernels  14.6 us (23%)
  waiting for transfers between devices  9.85 us (16%)
  blocking collectives  9.19 us (15%)
  local copies, waits for them, and re-layouts  8.52 us (14%)
  between operations  0.75 us (1%)
  other arithmetic  0.65 us (1%)
    ppermute x13, starting transfers between devices, swapped(): lax.ppermute(value, 'shot', [(d, partner(d) % count) for d in range(count)])  18.5 us
    pallas_call x7, Pallas kernels, call(): pl.pallas_call(kernel, out_shape=outs, in_specs=specs or [VMEM] * len(ins...  14.6 us
    ppermute x13, waiting for transfers between devices, swapped(): lax.ppermute(value, 'shot', [(d, partner(d) % count) for d in range(count)])  9.85 us
    all_to_all x1, blocking collectives, per_device(): lax.all_to_all(observed, 'shot', split_axis=0, concat_axis=0, tiled=True)  9.19 us
    unnamed x20, local copies, waits for them, and re-layouts  8.52 us
  transfers between devices with their start and end apart: 13, of which 5 were waited for; matrix products, arithmetic and copies ran while one was open for 0% of the time, Pallas kernels for 4%

profile of v4, /device:TPU:0, one launch (start us, length us, event | category | flops | bytes accessed | tf_op | source)
XLA Modules:
  0.0 62.1 jit_solution(10949630597770165041)
XLA Ops:
  0.0 5.4 %collective-permute-start = (f32[16,32,128]{2,1,0:T(8,128)}, f32[16,32,128]{2,1,0:T(8,128)S(1)}, u32[]{:S(2)}, u32[]{:S(2)}) collective-permute-start(f32[16,32,128]{2,1,0:T(8,128)} %refs_0_.1), channel_id=1, source_target_pairs={{0,15},{1,2},{2,1},{3,4},{4,3},{5,6},{6,5},{7,8},{8,7},{9,10},{10,... | collective-permute-start | bytes 786440 | tf_op jit(solution)/shard_map/ppermute | solution.py:388
  6.1 0.9 %copy-done.2 = f32[16,32,128]{2,1,0:T(8,128)S(1)} copy-done((f32[16,32,128]{2,1,0:T(8,128)S(1)}, f32[16,32,128]{2,1,0:T(8,128)}, u32[]{:S(2)}) %copy-start.2) | copy-done | bytes 262168
  7.1 0.7 %copy-done.9 = f32[1,8]{1,0:T(1,128)S(1)} copy-done((f32[1,8]{1,0:T(1,128)S(1)}, f32[1,8]{1,0:T(1,128)}, u32[]{:S(2)}) %copy-start.9) | copy-done | bytes 56
  7.7 0.6 message.1
  8.3 0.7 %collective-permute-start.2 = (f32[400,128]{1,0:T(8,128)S(1)}, f32[400,128]{1,0:T(8,128)S(1)}, u32[]{:S(2)}, u32[]{:S(2)}) collective-permute-start(f32[400,128]{1,0:T(8,128)S(1)} %get-tuple-element.24), channel_id=1, source_target_pairs={{0,15},{1,2},{2,1},{3,4},{4,3},{5,6},{6,5},{7,8},{8,7},{9,10},{10,... | collective-permute-start | bytes 614408 | tf_op jit(solution)/shard_map/ppermute | solution.py:388
  9.0 1.2 %copy-done.1 = f32[64,32,128]{2,1,0:T(8,128)S(1)} copy-done((f32[64,32,128]{2,1,0:T(8,128)S(1)}, f32[64,32,128]{2,1,0:T(8,128)}, u32[]{:S(2)}) %copy-start.1) | copy-done | bytes 1048600
  10.3 0.7 %copy-done.6 = f32[16,128]{1,0:T(8,128)S(1)} copy-done((f32[16,128]{1,0:T(8,128)S(1)}, f32[16,128]{1,0:T(8,128)}, u32[]{:S(2)}) %copy-start.6) | copy-done | bytes 8216
  11.0 0.7 %copy-done.7 = s32[256]{0:T(256)S(1)} copy-done((s32[256]{0:T(256)S(1)}, s32[256]{0:T(256)}, u32[]{:S(2)}) %copy-start.7) | copy-done | bytes 1048
  11.6 0.7 %copy-done.8 = s32[256]{0:T(256)S(1)} copy-done((s32[256]{0:T(256)S(1)}, s32[256]{0:T(256)}, u32[]{:S(2)}) %copy-start.8) | copy-done | bytes 1048
  12.3 0.2 prepare.1
  12.6 3.8 %collective-permute-done.2.refs_4_ = f32[400,128]{1,0:T(8,128)S(1)} collective-permute-done((f32[400,128]{1,0:T(8,128)S(1)}, f32[400,128]{1,0:T(8,128)S(1)}, u32[]{:S(2)}, u32[]{:S(2)}) %collective-permute-start.2) | collective-permute-done | bytes 204832 | tf_op jit(solution)/shard_map/ppermute | solution.py:388
  16.4 0.9 %copy-done = bf16[256,256]{1,0:T(8,128)(2,1)S(1)} copy-done((bf16[256,256]{1,0:T(8,128)(2,1)S(1)}, bf16[256,256]{1,0:T(8,128)(2,1)}, u32[]{:S(2)}) %copy-start) | copy-done | bytes 131096
  17.3 0.9 %copy-done.3 = f32[16,32,128]{2,1,0:T(8,128)S(1)} copy-done((f32[16,32,128]{2,1,0:T(8,128)S(1)}, f32[16,32,128]{2,1,0:T(8,128)}, u32[]{:S(2)}) %copy-start.3) | copy-done | bytes 262168
  18.2 0.8 %copy-done.4 = bf16[256,128]{1,0:T(8,128)(2,1)S(1)} copy-done((bf16[256,128]{1,0:T(8,128)(2,1)S(1)}, bf16[256,128]{1,0:T(8,128)(2,1)}, u32[]{:S(2)}) %copy-start.4) | copy-done | bytes 65560
  19.1 0.9 %copy-done.5 = f32[16,32,128]{2,1,0:T(8,128)S(1)} copy-done((f32[16,32,128]{2,1,0:T(8,128)S(1)}, f32[16,32,128]{2,1,0:T(8,128)}, u32[]{:S(2)}) %copy-start.5) | copy-done | bytes 262168
  20.0 2.9 %forward.1 = (f32[4,16,32,128]{3,2,1,0:T(8,128)S(1)}, f32[2,4,32,128]{3,2,1,0:T(8,128)S(1)}, f32[24,32,128]{2,1,0:T(8,128)S(1)}, f32[3,16,128]{2,1,0:T(8,128)S(1)}) custom-call(f32[16,32,128]{2,1,0:T(8,128)S(1)} %copy-done.5, f32[16,32,128]{2,1,0:T(8,128)S(1)} %copy-done.3, f32[16,32,128]{2,1,0:T(8,128)S(1)} %collective-permute-done.refs_2_, ...), custom_call_target="tpu_custom_call" | custom-call | flops 1000000 | bytes 1000000 | tf_op jit(solution)/shard_map/forward/pallas_call | solution.py:374
  22.9 0.1 collective-permute-start.5
  23.0 3.0 %collective-permute-start.4 = (f32[24,32,128]{2,1,0:T(8,128)S(1)}, f32[24,32,128]{2,1,0:T(8,128)S(1)}, u32[]{:S(2)}, u32[]{:S(2)}) collective-permute-start(f32[24,32,128]{2,1,0:T(8,128)S(1)} %get-tuple-element.30), channel_id=1, source_target_pairs={{0,15},{1,2},{2,1},{3,4},{4,3},{5,6},{6,5},{7,8},{8,7},{9,10},{10,... | collective-permute-start | bytes 1179656 | tf_op jit(solution)/shard_map/ppermute | solution.py:388
  25.9 9.2 %all_to_all.11 = f32[16,1,128]{2,1,0:T(1,128)S(1)} all-to-all(f32[16,1,128]{2,1,0:T(1,128)S(1)} %bitcast.7), channel_id=1, replica_groups=mesh['groups'=2,'shot'=16] {'shot'}, dimensions={0} | all-to-all | bytes 16384 | tf_op jit(solution)/shard_map/all_to_all | solution.py:439
  35.1 0.8 %traces.1 = (bf16[256,512]{1,0:T(8,128)(2,1)S(1)}, f32[256,256]{1,0:T(8,128)S(1)}, f32[8,256]{1,0:T(8,128)S(1)}) custom-call(f32[8,256]{1,0:T(8,128)S(1)} %get-tuple-element.32.refs_0_.refs_8_, f32[16,128]{1,0:T(8,128)S(1)} %bitcast.6, f32[4,16,32,128]{3,2,1,0:T(8,128)S(1)} %get-tuple-element.28.refs_2_.refs_0_), custom_call_target="tpu_custom_call" | custom-call | flops 1000000 | bytes 1000000 | tf_op jit(solution)/shard_map/traces/pallas_call | solution.py:374
  36.0 3.7 %forward_last.1 = (f32[4,16,32,128]{3,2,1,0:T(8,128)S(1)}, f32[16,256]{1,0:T(8,128)S(1)}) custom-call(f32[4,16,32,128]{3,2,1,0:T(8,128)S(1)} %get-tuple-element.28.refs_2_.refs_0_, f32[2,4,32,128]{3,2,1,0:T(8,128)S(1)} %get-tuple-element.29.refs_1_, f32[24,32,128]{2,1,0:T(8,128)S(1)} %collective-permute-done.4.refs_2_, ...), custom_call_target="tpu_custom_call" | custom-call | flops 1000000 | bytes 1000000 | tf_op jit(solution)/shard_map/forward_last/pallas_call | solution.py:374
  39.7 2.3 %collective-permute-start.9 = (f32[16,256]{1,0:T(8,128)S(1)}, f32[16,256]{1,0:T(8,128)S(1)}, u32[]{:S(2)}, u32[]{:S(2)}) collective-permute-start(f32[16,256]{1,0:T(8,128)S(1)} %get-tuple-element.38.adj), channel_id=1, source_target_pairs={{0,14},{1,15},{2,4},{3,5},{4,2},{5,3},{6,8},{7,9},{8,6},{9,7},{10,... | collective-permute-start | bytes 49160 | tf_op jit(solution)/shard_map/ppermute | solution.py:388
  42.0 2.5 %collective-permute-start.6 = (f32[16,256]{1,0:T(8,128)S(1)}, f32[16,256]{1,0:T(8,128)S(1)}, u32[]{:S(2)}, u32[]{:S(2)}) collective-permute-start(f32[16,256]{1,0:T(8,128)S(1)} %get-tuple-element.38.adj), channel_id=1, source_target_pairs={{0,15},{1,2},{2,1},{3,4},{4,3},{5,6},{6,5},{7,8},{8,7},{9,10},{10,... | collective-permute-start | bytes 49160 | tf_op jit(solution)/shard_map/ppermute | solution.py:388
  44.5 0.8 %own_sources.1.refs_5_ = f32[8,16,32,128]{3,2,1,0:T(8,128)S(1)} custom-call(f32[16,256]{1,0:T(8,128)S(1)} %get-tuple-element.38.adj), custom_call_target="tpu_custom_call" | custom-call | flops 1000000 | bytes 1000000 | tf_op jit(solution)/shard_map/own_sources/pallas_call | solution.py:374
  45.3 0.8 %collective-permute-done.9.refs_9_ = f32[16,256]{1,0:T(8,128)S(1)} collective-permute-done((f32[16,256]{1,0:T(8,128)S(1)}, f32[16,256]{1,0:T(8,128)S(1)}, u32[]{:S(2)}, u32[]{:S(2)}) %collective-permute-start.9) | collective-permute-done | bytes 16416 | tf_op jit(solution)/shard_map/ppermute | solution.py:388
  46.2 1.8 %collective-permute-done.6.refs_6_ = f32[16,256]{1,0:T(8,128)S(1)} collective-permute-done((f32[16,256]{1,0:T(8,128)S(1)}, f32[16,256]{1,0:T(8,128)S(1)}, u32[]{:S(2)}, u32[]{:S(2)}) %collective-permute-start.6) | collective-permute-done | bytes 16416 | tf_op jit(solution)/shard_map/ppermute | solution.py:388
  47.9 5.6 %adjoint.1 = (f32[4,32,128]{2,1,0:T(8,128)S(1)}, f32[4,32,128]{2,1,0:T(8,128)S(1)}, f32[4,32,128]{2,1,0:T(8,128)S(1)}, f32[4,32,128]{2,1,0:T(8,128)S(1)}) custom-call(f32[4,16,32,128]{3,2,1,0:T(8,128)S(1)} %get-tuple-element.28.refs_2_.refs_0_, f32[4,16,32,128]{3,2,1,0:T(8,128)S(1)} %get-tuple-element.37.refs_1_, bf16[256,128]{1,0:T(8,128)(2,1)S(1)} %copy-done.4, ...), custom_call_target="tpu_custom_call" | custom-call | flops 1000000 | bytes 1000000 | tf_op jit(solution)/shard_map/adjoint/pallas_call | solution.py:374
  53.6 1.7 %collective-permute-start.11 = (f32[4,32,128]{2,1,0:T(8,128)S(1)}, f32[4,32,128]{2,1,0:T(8,128)S(1)}, u32[]{:S(2)}, u32[]{:S(2)}) collective-permute-start(f32[4,32,128]{2,1,0:T(8,128)S(1)} %get-tuple-element.41), channel_id=1, source_target_pairs={{0,8},{1,9},{2,10},{3,11},{4,12},{5,13},{6,14},{7,15},{8,0},{9,1},... | collective-permute-start | bytes 196616 | tf_op jit(solution)/shard_map/ppermute | solution.py:388
  55.3 2.7 %collective-permute-start.12 = (f32[4,32,128]{2,1,0:T(8,128)S(1)}, f32[4,32,128]{2,1,0:T(8,128)S(1)}, u32[]{:S(2)}, u32[]{:S(2)}) collective-permute-start(f32[4,32,128]{2,1,0:T(8,128)S(1)} %get-tuple-element.42), channel_id=1, source_target_pairs={{0,12},{1,13},{2,14},{3,15},{4,8},{5,9},{6,10},{7,11},{8,4},{9,5},... | collective-permute-start | bytes 196616 | tf_op jit(solution)/shard_map/ppermute | solution.py:388
  58.0 0.9 %collective-permute-done.11 = f32[4,32,128]{2,1,0:T(8,128)S(1)} collective-permute-done((f32[4,32,128]{2,1,0:T(8,128)S(1)}, f32[4,32,128]{2,1,0:T(8,128)S(1)}, u32[]{:S(2)}, u32[]{:S(2)}) %collective-permute-start.11) | collective-permute-done | bytes 65568 | tf_op jit(solution)/shard_map/ppermute | solution.py:388
  58.8 2.6 %collective-permute-done.12 = f32[4,32,128]{2,1,0:T(8,128)S(1)} collective-permute-done((f32[4,32,128]{2,1,0:T(8,128)S(1)}, f32[4,32,128]{2,1,0:T(8,128)S(1)}, u32[]{:S(2)}, u32[]{:S(2)}) %collective-permute-start.12) | collective-permute-done | bytes 65568 | tf_op jit(solution)/shard_map/ppermute | solution.py:388
  61.4 0.6 %add_add_fusion = f32[4,32,128]{2,1,0:T(8,128)} fusion(f32[4,32,128]{2,1,0:T(8,128)S(1)} %collective-permute-done.12, f32[4,32,128]{2,1,0:T(8,128)S(1)} %collective-permute-done.11, f32[4,32,128]{2,1,0:T(8,128)S(1)} %get-tuple-element.39, f32[4,32,128]{2,1,0:T(8,128)S(1)} %collective-permute-done.10), kind=kLoop, calls=%fused_computation | loop fusion | flops 49152 | bytes 327680 | tf_op jit(solution)/shard_map/add | solution.py:505
  (23 shorter events, 0.1 us)
Async XLA Ops:
  0.0 16.4 %collective-permute-start = (f32[16,32,128]{2,1,0:T(8,128)}, f32[16,32,128]{2,1,0:T(8,128)S(1)}, u32[]{:S(2)}, u32[]{:S(2)}) collective-permute-start(f32[16,32,128]{2,1,0:T(8,128)} %refs_0_.1), channel_id=1, source_target_pairs={{0,15},{1,2},{2,1},{3,4},{4,3},{5,6},{6,5},{7,8},{8,7},{9,10},{10,... | collective-permute-start | bytes 786440 | tf_op jit(solution)/shard_map/ppermute | solution.py:388
  5.4 10.9 %collective-permute-start.1 = (f32[16,32,128]{2,1,0:T(8,128)}, f32[16,32,128]{2,1,0:T(8,128)S(1)}, u32[]{:S(2)}, u32[]{:S(2)}) collective-permute-start(f32[16,32,128]{2,1,0:T(8,128)} %refs_0_.1), channel_id=1, source_target_pairs={{0,1},{1,0},{2,3},{3,2},{4,5},{5,4},{6,7},{7,6},{8,9},{9,8},{10,11... | collective-permute-start | bytes 786440 | tf_op jit(solution)/shard_map/ppermute | solution.py:388
  6.1 1.0 %copy-start.2 = (f32[16,32,128]{2,1,0:T(8,128)S(1)}, f32[16,32,128]{2,1,0:T(8,128)}, u32[]{:S(2)}) copy-start(f32[16,32,128]{2,1,0:T(8,128)} %refs_1_.1) | copy-start | bytes 786436
  7.1 0.7 %copy-start.9 = (f32[1,8]{1,0:T(1,128)S(1)}, f32[1,8]{1,0:T(1,128)}, u32[]{:S(2)}) copy-start(f32[1,8]{1,0:T(1,128)} %wavelet.1) | copy-start | bytes 100
  8.3 8.1 %collective-permute-start.2 = (f32[400,128]{1,0:T(8,128)S(1)}, f32[400,128]{1,0:T(8,128)S(1)}, u32[]{:S(2)}, u32[]{:S(2)}) collective-permute-start(f32[400,128]{1,0:T(8,128)S(1)} %get-tuple-element.24), channel_id=1, source_target_pairs={{0,15},{1,2},{2,1},{3,4},{4,3},{5,6},{6,5},{7,8},{8,7},{9,10},{10,... | collective-permute-start | bytes 614408 | tf_op jit(solution)/shard_map/ppermute | solution.py:388
  9.0 7.3 %collective-permute-start.3 = (f32[400,128]{1,0:T(8,128)S(1)}, f32[400,128]{1,0:T(8,128)S(1)}, u32[]{:S(2)}, u32[]{:S(2)}) collective-permute-start(f32[400,128]{1,0:T(8,128)S(1)} %get-tuple-element.25), channel_id=1, source_target_pairs={{0,1},{1,0},{2,3},{3,2},{4,5},{5,4},{6,7},{7,6},{8,9},{9,8},{10,11... | collective-permute-start | bytes 614408 | tf_op jit(solution)/shard_map/ppermute | solution.py:388
  9.0 1.2 %copy-start.1 = (f32[64,32,128]{2,1,0:T(8,128)S(1)}, f32[64,32,128]{2,1,0:T(8,128)}, u32[]{:S(2)}) copy-start(f32[64,32,128]{2,1,0:T(8,128)} %courant.1) | copy-start | bytes 3145732
  10.3 0.7 %copy-start.6 = (f32[16,128]{1,0:T(8,128)S(1)}, f32[16,128]{1,0:T(8,128)}, u32[]{:S(2)}) copy-start(f32[16,128]{1,0:T(8,128)} %observed.1) | copy-start | bytes 24580
  11.0 0.7 %copy-start.7 = (s32[256]{0:T(256)S(1)}, s32[256]{0:T(256)}, u32[]{:S(2)}) copy-start(s32[256]{0:T(256)} %param.15) | copy-start | bytes 3076
  11.6 0.7 %copy-start.8 = (s32[256]{0:T(256)S(1)}, s32[256]{0:T(256)}, u32[]{:S(2)}) copy-start(s32[256]{0:T(256)} %param.16) | copy-start | bytes 3076
  16.4 0.9 %copy-start = (bf16[256,256]{1,0:T(8,128)(2,1)S(1)}, bf16[256,256]{1,0:T(8,128)(2,1)}, u32[]{:S(2)}) copy-start(bf16[256,256]{1,0:T(8,128)(2,1)} %constant.5.clone.refs_7_.refs_5_.refs_3_) | copy-start | bytes 393220
  17.3 0.9 %copy-start.3 = (f32[16,32,128]{2,1,0:T(8,128)S(1)}, f32[16,32,128]{2,1,0:T(8,128)}, u32[]{:S(2)}) copy-start(f32[16,32,128]{2,1,0:T(8,128)} %refs_1_.1) | copy-start | bytes 786436
  18.2 0.8 %copy-start.4 = (bf16[256,128]{1,0:T(8,128)(2,1)S(1)}, bf16[256,128]{1,0:T(8,128)(2,1)}, u32[]{:S(2)}) copy-start(bf16[256,128]{1,0:T(8,128)(2,1)} %constant.4.clone.refs_6_.refs_4_.refs_2_) | copy-start | bytes 196612
  19.1 0.9 %copy-start.5 = (f32[16,32,128]{2,1,0:T(8,128)S(1)}, f32[16,32,128]{2,1,0:T(8,128)}, u32[]{:S(2)}) copy-start(f32[16,32,128]{2,1,0:T(8,128)} %refs_0_.1) | copy-start | bytes 786436
  22.9 13.1 %collective-permute-start.5 = (f32[24,32,128]{2,1,0:T(8,128)S(1)}, f32[24,32,128]{2,1,0:T(8,128)S(1)}, u32[]{:S(2)}, u32[]{:S(2)}) collective-permute-start(f32[24,32,128]{2,1,0:T(8,128)S(1)} %get-tuple-element.30), channel_id=1, source_target_pairs={{0,1},{1,0},{2,3},{3,2},{4,5},{5,4},{6,7},{7,6},{8,9},{9,8},{10,11... | collective-permute-start | bytes 1179656 | tf_op jit(solution)/shard_map/ppermute | solution.py:388
  23.0 13.0 %collective-permute-start.4 = (f32[24,32,128]{2,1,0:T(8,128)S(1)}, f32[24,32,128]{2,1,0:T(8,128)S(1)}, u32[]{:S(2)}, u32[]{:S(2)}) collective-permute-start(f32[24,32,128]{2,1,0:T(8,128)S(1)} %get-tuple-element.30), channel_id=1, source_target_pairs={{0,15},{1,2},{2,1},{3,4},{4,3},{5,6},{6,5},{7,8},{8,7},{9,10},{10,... | collective-permute-start | bytes 1179656 | tf_op jit(solution)/shard_map/ppermute | solution.py:388
  39.7 6.4 %collective-permute-start.9 = (f32[16,256]{1,0:T(8,128)S(1)}, f32[16,256]{1,0:T(8,128)S(1)}, u32[]{:S(2)}, u32[]{:S(2)}) collective-permute-start(f32[16,256]{1,0:T(8,128)S(1)} %get-tuple-element.38.adj), channel_id=1, source_target_pairs={{0,14},{1,15},{2,4},{3,5},{4,2},{5,3},{6,8},{7,9},{8,6},{9,7},{10,... | collective-permute-start | bytes 49160 | tf_op jit(solution)/shard_map/ppermute | solution.py:388
  42.0 4.1 %collective-permute-start.8 = (f32[16,256]{1,0:T(8,128)S(1)}, f32[16,256]{1,0:T(8,128)S(1)}, u32[]{:S(2)}, u32[]{:S(2)}) collective-permute-start(f32[16,256]{1,0:T(8,128)S(1)} %get-tuple-element.38.adj), channel_id=1, source_target_pairs={{0,2},{1,3},{2,0},{3,1},{4,6},{5,7},{6,4},{7,5},{8,10},{9,11},{10,... | collective-permute-start | bytes 49160 | tf_op jit(solution)/shard_map/ppermute | solution.py:388
  42.0 4.1 %collective-permute-start.7 = (f32[16,256]{1,0:T(8,128)S(1)}, f32[16,256]{1,0:T(8,128)S(1)}, u32[]{:S(2)}, u32[]{:S(2)}) collective-permute-start(f32[16,256]{1,0:T(8,128)S(1)} %get-tuple-element.38.adj), channel_id=1, source_target_pairs={{0,1},{1,0},{2,3},{3,2},{4,5},{5,4},{6,7},{7,6},{8,9},{9,8},{10,11... | collective-permute-start | bytes 49160 | tf_op jit(solution)/shard_map/ppermute | solution.py:388
  42.0 5.9 %collective-permute-start.6 = (f32[16,256]{1,0:T(8,128)S(1)}, f32[16,256]{1,0:T(8,128)S(1)}, u32[]{:S(2)}, u32[]{:S(2)}) collective-permute-start(f32[16,256]{1,0:T(8,128)S(1)} %get-tuple-element.38.adj), channel_id=1, source_target_pairs={{0,15},{1,2},{2,1},{3,4},{4,3},{5,6},{6,5},{7,8},{8,7},{9,10},{10,... | collective-permute-start | bytes 49160 | tf_op jit(solution)/shard_map/ppermute | solution.py:388
  53.5 4.5 %collective-permute-start.10 = (f32[4,32,128]{2,1,0:T(8,128)S(1)}, f32[4,32,128]{2,1,0:T(8,128)S(1)}, u32[]{:S(2)}, u32[]{:S(2)}) collective-permute-start(f32[4,32,128]{2,1,0:T(8,128)S(1)} %get-tuple-element.40), channel_id=1, source_target_pairs={{0,4},{1,5},{2,6},{3,7},{4,0},{5,1},{6,2},{7,3},{8,12},{9,13},{10,... | collective-permute-start | bytes 196616 | tf_op jit(solution)/shard_map/ppermute | solution.py:388
  53.6 5.2 %collective-permute-start.11 = (f32[4,32,128]{2,1,0:T(8,128)S(1)}, f32[4,32,128]{2,1,0:T(8,128)S(1)}, u32[]{:S(2)}, u32[]{:S(2)}) collective-permute-start(f32[4,32,128]{2,1,0:T(8,128)S(1)} %get-tuple-element.41), channel_id=1, source_target_pairs={{0,8},{1,9},{2,10},{3,11},{4,12},{5,13},{6,14},{7,15},{8,0},{9,1},... | collective-permute-start | bytes 196616 | tf_op jit(solution)/shard_map/ppermute | solution.py:388
  55.3 6.1 %collective-permute-start.12 = (f32[4,32,128]{2,1,0:T(8,128)S(1)}, f32[4,32,128]{2,1,0:T(8,128)S(1)}, u32[]{:S(2)}, u32[]{:S(2)}) collective-permute-start(f32[4,32,128]{2,1,0:T(8,128)S(1)} %get-tuple-element.42), channel_id=1, source_target_pairs={{0,12},{1,13},{2,14},{3,15},{4,8},{5,9},{6,10},{7,11},{8,4},{9,5},... | collective-permute-start | bytes 196616 | tf_op jit(solution)/shard_map/ppermute | solution.py:388

commit v5 on v4

--- a/solution.py
+++ b/solution.py
@@ -2,7 +2,6 @@
 
 import jax
 import jax.numpy as jnp
-import numpy as np
 from jax import lax
 from jax.experimental import pallas as pl
 from jax.experimental.pallas import tpu as pltpu
@@ -13,7 +12,8 @@
 RAD = 4
 ROUNDS = (4, 4)
 SCALE = 5040.0
-CENTER = -43050.0
+CENTER_Y = -43008.0
+CENTER_Z = -42.0
 WEIGHTS = (8064.0, -1008.0, 128.0, -9.0)
 GROUP = 8
 HALO = RAD * (NT - 1)
@@ -24,21 +24,25 @@
 SMEM = pl.BlockSpec(memory_space=pltpu.SMEM)
 
 
-def band(size):
-    out = np.zeros((size, size), np.float32)
+def band(distance, center):
+    out = jnp.where(distance == 0, center, 0.0)
     for k, weight in enumerate(WEIGHTS, 1):
-        out += weight * (np.eye(size, k=k) + np.eye(size, k=-k))
+        out = jnp.where(jnp.abs(distance) == k, weight, out)
     return out
 
 
-def matrices(span_y, span_z):
-    along_z = np.concatenate([band(span_z)] * 2, axis=0)
-    tiles = span_y // 8
-    along_y = band(span_y).reshape(tiles, 8, tiles, 8)
-    full = np.zeros((tiles, GROUP, 8, tiles, GROUP, 8), np.float32)
-    for i in range(GROUP):
-        full[:, i, :, :, i, :] = along_y
-    return jnp.asarray(along_z, BF), jnp.asarray(full.reshape(GROUP * span_y, GROUP * span_y), BF)
+def build_bands(span_y, span_z, rows_out, fixed_out):
+    size = GROUP * span_y
+    row = lax.broadcasted_iota(jnp.int32, (size, size), 0)
+    col = lax.broadcasted_iota(jnp.int32, (size, size), 1)
+    tile = 8 * GROUP
+    y_row = row // tile * 8 + row % 8
+    y_col = col // tile * 8 + col % 8
+    same = (row // 8) % GROUP == (col // 8) % GROUP
+    rows_out[...] = jnp.where(same, band(y_row - y_col, CENTER_Y), 0.0).astype(BF)
+    z = lax.broadcasted_iota(jnp.int32, (2 * span_z, 2 * span_z), 0) % span_z
+    to = lax.broadcasted_iota(jnp.int32, (2 * span_z, 2 * span_z), 1)
+    fixed_out[...] = jnp.where(to < span_z, band(z - to, CENTER_Z), 0.0).astype(BF)
 
 
 def split(values):
@@ -59,8 +63,9 @@
         order = [(i, column) for column in columns for i in range(GROUP)]
         group = jnp.concatenate([cur[base + i, column] for i, column in order], axis=0)
         pair = jnp.concatenate(split(group), axis=1)
-        z_part = dot(pair, zmat)
-        y_part = dot(ymat, pair)
+        left = jnp.concatenate([ymat, pair], axis=1)
+        right = jnp.concatenate([pair, zmat], axis=0)
+        part = dot(left, right)
         for j, column in enumerate(columns):
             tiles = [cur[base - RAD + q, column] for q in range(GROUP + 2 * RAD)]
             for i in range(GROUP):
@@ -68,7 +73,7 @@
                 at = (j * GROUP + i) * 8
                 rows = slice(at, at + 8)
                 here = tiles[i + RAD]
-                total = z_part[rows] + (y_part[rows, :span_z] + y_part[rows, span_z:]) + CENTER * here
+                total = part[rows, :span_z] + part[rows, span_z:]
                 for k, weight in enumerate(WEIGHTS, 1):
                     total = total + weight * (tiles[i + RAD + k] + tiles[i + RAD - k])
                 old[x, column] = (here + here - old[x, column]) + model[x + model_shift, column] * total
@@ -93,13 +98,14 @@
     return lax.rem(lax.axis_index("shot"), 2)
 
 
-def message_kernel(before, wavelet, source, outer_out, mate_out, pack_out):
+def message_kernel(before, wavelet, source, outer_out, mate_out, pack_out, before_out):
     rows, span_y, span_z = before.shape
     which = lax.broadcasted_iota(jnp.int32, (16, span_z), 0)
     pack = jnp.where(which >= NT, source[0].astype(F32), 0.0)
     for step in range(NT):
         pack = jnp.where(which == step, wavelet[0, step], pack)
     pack_out[...] = pack
+    before_out[...] = before[...]
     narrow = RAD * (ROUNDS[0] - 1)
     size = narrow * span_y
     odd = parity()
@@ -109,8 +115,12 @@
     mate_out[size:] = pack
 
 
-def prepare_kernel(courant, cells, order, observed, pack, model_out, cells_out, observed_out):
-    rows = 16
+def prepare_kernel(
+    courant, cells, order, observed, pack, now, model_out, cells_out, observed_out, now_out, ymat_out, zmat_out
+):
+    rows, span_y, span_z = now.shape
+    now_out[...] = now[...]
+    build_bands(span_y, span_z, ymat_out, zmat_out)
     piece = lax.rem(lax.axis_index("shot"), PIECES)
     period = courant.shape[0]
     window = model_out.shape[0]
@@ -310,26 +320,32 @@
         out[step] = added.reshape(rows, span_y, span_z)
 
 
+def pair_kernel(adj, mate, out):
+    odd = parity()
+    out[odd] = adj[...]
+    out[1 - odd] = mate[...]
+
+
 def adjoint_kernel(field_groups, slabs, *refs):
     fields = []
     for ref in refs[:field_groups]:
         fields += [ref.at[i] for i in range(ref.shape[0])]
     refs = refs[field_groups:]
-    zmat, ymat, model, sources, outer, mate, even_pair, odd_pair = refs[:8]
-    outs = refs[8 : 8 + slabs]
-    buf_a, buf_b, image, rows_table, adjs = refs[8 + slabs :]
+    zmat, ymat, model, sources, own_pair, even_pair, odd_pair = refs[:7]
+    outs = refs[7 : 7 + slabs]
+    buf_a, buf_b, image, rows_table, adjs, near = refs[7 + slabs :]
     odd = parity()
     odd_chip = lax.rem(lax.axis_index("shot") // 2, 2)
-    adjs[1 + 2 * odd] = outer[...]
-    adjs[3 - 2 * odd] = mate[...]
-    adjs[4 - 4 * odd_chip] = even_pair[...]
-    adjs[4 * odd_chip] = odd_pair[...]
+    near[2:4] = own_pair[...]
+    near[pl.ds(4 - 4 * odd_chip, 2)] = even_pair[...]
+    near[pl.ds(4 * odd_chip, 2)] = odd_pair[...]
     rows = 16
     own = HALO
     span_y, span_z = buf_a.shape[1:]
     table_rows = rows * span_y
     lanes = {}
     for block in (-2, -1, 1, 2):
+        adjs[block + 2] = near[2 + odd + block]
         cells = adjs[block + 2, NT : NT + 1].astype(jnp.int32)
         rows_table[block + 2] = injection_table(cells, table_rows, span_z)
         lanes[block] = cells % span_z
@@ -412,35 +428,37 @@
     count = receiver_cell.shape[0]
     table_rows = rows * span_y
     plane = (span_y, span_z)
-    zmat, ymat = matrices(span_y, span_z)
 
     narrow = RAD * (ROUNDS[0] - 1)
     now_outer, now_mate = with_outer(wave_now), with_mate(wave_now)
     message = jax.ShapeDtypeStruct((narrow * span_y + 16, span_z), F32)
-    to_outer, to_mate, pack = call(
+    to_outer, to_mate, pack, before = call(
         message_kernel,
-        (message, message, jax.ShapeDtypeStruct((16, span_z), F32)),
+        (message, message, jax.ShapeDtypeStruct((16, span_z), F32), jax.ShapeDtypeStruct(wave_before.shape, F32)),
         (wave_before, wavelet, source_cell),
         specs=[VMEM, SMEM, SMEM],
         name="message",
     )
     before_outer, before_mate = with_outer(to_outer), with_mate(to_mate)
 
-    model, cells, observed = call(
+    model, cells, observed, now, ymat, zmat = call(
         prepare_kernel,
         (
             jax.ShapeDtypeStruct((rows + 2 * HALO,) + plane, F32),
             jax.ShapeDtypeStruct((8, count), F32),
             jax.ShapeDtypeStruct(observed.shape, F32),
+            jax.ShapeDtypeStruct(wave_now.shape, F32),
+            jax.ShapeDtypeStruct((GROUP * span_y, GROUP * span_y), BF),
+            jax.ShapeDtypeStruct((2 * span_z, 2 * span_z), BF),
         ),
-        (courant_sq, receiver_cell.reshape(1, count), send_order.reshape(1, count), observed, pack),
+        (courant_sq, receiver_cell.reshape(1, count), send_order.reshape(1, count), observed, pack, wave_now),
         name="prepare",
     )
     recorded = lax.all_to_all(observed, "shot", split_axis=0, concat_axis=0, tiled=True)
 
     common = (zmat, ymat, model)
     field_list = []
-    ins = (wave_now, wave_before, now_outer, now_mate, before_outer, before_mate)
+    ins = (now, before, now_outer, now_mate, before_outer, before_mate)
     for index in range(len(ROUNDS) - 1):
         window = rows + 2 * RAD * ROUNDS[index]
         sent = 2 * rows - 2 * RAD
@@ -488,7 +506,10 @@
     sources = call(
         own_sources_kernel, jax.ShapeDtypeStruct((NT, rows) + plane, F32), (adj,), name="own_sources"
     )
-    adjs = [sources, with_outer(adj), with_mate(adj), with_even_pair(adj), with_odd_pair(adj)]
+    pair = call(
+        pair_kernel, jax.ShapeDtypeStruct((2, 2 * NT, count), F32), (adj, with_mate(adj)), name="pair"
+    )
+    adjs = [sources, pair, with_even_pair(pair), with_odd_pair(pair)]
     slabs = devices // PIECES
     thick = rows // slabs
     parts = call(
@@ -497,7 +518,7 @@
         (*field_list, zmat, ymat, model, *adjs),
         scratch=[pltpu.VMEM((rows + 2 * HALO,) + plane, F32)] * 2
         + [pltpu.VMEM((rows,) + plane, F32), pltpu.VMEM((5, table_rows, count), BF)]
-        + [pltpu.VMEM((5, 2 * NT, count), F32)],
+        + [pltpu.VMEM((5, 2 * NT, count), F32), pltpu.VMEM((6, 2 * NT, count), F32)],
         name="adjoint",
     )
     total = parts[0]

time: 62.5 us -> 58.6 us (0.938)
  local copies, waits for them, and re-layouts: 8.52 us -> 5.82 us
  starting transfers between devices: 18.5 us -> 16 us
  waiting for transfers between devices: 9.85 us -> 10.8 us
    unnamed x20 -> x14, local copies, waits for them, and re-layouts: 8.52 us -> 5.82 us
    ppermute x13 -> x12, starting transfers between devices: 18.5 us -> 16 us  [swapped(): lax.ppermute(value, 'shot', [(d, partner(d) % count) for d in range(count)])]
    ppermute x13 -> x12, waiting for transfers between devices: 9.85 us -> 10.8 us  [swapped(): lax.ppermute(value, 'shot', [(d, partner(d) % count) for d in range(count)])]
    pallas_call x7 -> x8, Pallas kernels: 14.6 us -> 14.9 us  [call(): pl.pallas_call(kernel, out_shape=outs, in_specs=specs or [VMEM] * len(ins...]
  transfers between devices with their start and end apart: 13 -> 12, of which waited for: 5 -> 4; matrix products, arithmetic and copies ran while one was open for 0% -> 0% of each run, Pallas kernels for 4% -> 5%
where the time goes in v5:
time: 58.6 us; the launch traced here: 58.2 us
  starting transfers between devices  16 us (27%)
  Pallas kernels  14.9 us (25%)
  waiting for transfers between devices  10.8 us (18%)
  blocking collectives  9.24 us (16%)
  local copies, waits for them, and re-layouts  5.82 us (10%)
  between operations  0.76 us (1%)
  other arithmetic  0.65 us (1%)
    ppermute x12, starting transfers between devices, swapped(): lax.ppermute(value, 'shot', [(d, partner(d) % count) for d in range(count)])  16 us
    pallas_call x8, Pallas kernels, call(): pl.pallas_call(kernel, out_shape=outs, in_specs=specs or [VMEM] * len(ins...  14.9 us
    ppermute x12, waiting for transfers between devices, swapped(): lax.ppermute(value, 'shot', [(d, partner(d) % count) for d in range(count)])  10.8 us
    all_to_all x1, blocking collectives, per_device(): lax.all_to_all(observed, 'shot', split_axis=0, concat_axis=0, tiled=True)  9.24 us
    unnamed x14, local copies, waits for them, and re-layouts  5.82 us
  transfers between devices with their start and end apart: 12, of which 4 were waited for; matrix products, arithmetic and copies ran while one was open for 0% of the time, Pallas kernels for 5%

profile of v5, /device:TPU:0, one launch (start us, length us, event | category | flops | bytes accessed | tf_op | source)
XLA Modules:
  0.0 58.2 jit_solution(16553972855545449950)
XLA Ops:
  0.0 0.5 collective-permute-start.1
  0.5 5.7 %collective-permute-start = (f32[16,32,128]{2,1,0:T(8,128)}, f32[16,32,128]{2,1,0:T(8,128)S(1)}, u32[]{:S(2)}, u32[]{:S(2)}) collective-permute-start(f32[16,32,128]{2,1,0:T(8,128)} %now.1), channel_id=1, source_target_pairs={{0,15},{1,2},{2,1},{3,4},{4,3},{5,6},{6,5},{7,8},{8,7},{9,10},{10,... | collective-permute-start | bytes 786440 | tf_op jit(solution)/shard_map/ppermute | solution.py:404
  6.8 0.9 %copy-done.1 = f32[16,32,128]{2,1,0:T(8,128)S(1)} copy-done((f32[16,32,128]{2,1,0:T(8,128)S(1)}, f32[16,32,128]{2,1,0:T(8,128)}, u32[]{:S(2)}) %copy-start.1) | copy-done | bytes 262168
  7.7 0.7 %copy-done.6 = f32[1,8]{1,0:T(1,128)S(1)} copy-done((f32[1,8]{1,0:T(1,128)S(1)}, f32[1,8]{1,0:T(1,128)}, u32[]{:S(2)}) %copy-start.6) | copy-done | bytes 56
  8.4 0.6 %message.1 = (f32[400,128]{1,0:T(8,128)S(1)}, f32[400,128]{1,0:T(8,128)S(1)}, f32[16,128]{1,0:T(8,128)S(1)}, f32[16,32,128]{2,1,0:T(8,128)S(1)}) custom-call(f32[16,32,128]{2,1,0:T(8,128)S(1)} %copy-done.1, f32[1,8]{1,0:T(1,128)S(1)} %copy-done.6, s32[1]{0:T(128)S(6)} %copy.10.source), custom_call_target="tpu_custom_call" | custom-call | flops 1000000 | bytes 1000000 | tf_op jit(solution)/shard_map/message/pallas_call | solution.py:390
  9.0 0.1 collective-permute-start.2
  9.1 0.1 collective-permute-start.3
  9.1 0.0 copy-start
  9.1 1.2 %copy-done = f32[64,32,128]{2,1,0:T(8,128)S(1)} copy-done((f32[64,32,128]{2,1,0:T(8,128)S(1)}, f32[64,32,128]{2,1,0:T(8,128)}, u32[]{:S(2)}) %copy-start) | copy-done | bytes 1048600
  10.4 0.9 %copy-done.2 = f32[16,32,128]{2,1,0:T(8,128)S(1)} copy-done((f32[16,32,128]{2,1,0:T(8,128)S(1)}, f32[16,32,128]{2,1,0:T(8,128)}, u32[]{:S(2)}) %copy-start.2) | copy-done | bytes 262168
  11.3 0.7 %copy-done.3 = f32[16,128]{1,0:T(8,128)S(1)} copy-done((f32[16,128]{1,0:T(8,128)S(1)}, f32[16,128]{1,0:T(8,128)}, u32[]{:S(2)}) %copy-start.3) | copy-done | bytes 8216
  12.0 0.7 %copy-done.4 = s32[256]{0:T(256)S(1)} copy-done((s32[256]{0:T(256)S(1)}, s32[256]{0:T(256)}, u32[]{:S(2)}) %copy-start.4) | copy-done | bytes 1048
  12.7 0.7 %copy-done.5 = s32[256]{0:T(256)S(1)} copy-done((s32[256]{0:T(256)S(1)}, s32[256]{0:T(256)}, u32[]{:S(2)}) %copy-start.5) | copy-done | bytes 1048
  13.4 0.6 prepare.1
  13.9 3.0 %collective-permute-done.2.refs_4_ = f32[400,128]{1,0:T(8,128)S(1)} collective-permute-done((f32[400,128]{1,0:T(8,128)S(1)}, f32[400,128]{1,0:T(8,128)S(1)}, u32[]{:S(2)}, u32[]{:S(2)}) %collective-permute-start.2) | collective-permute-done | bytes 204832 | tf_op jit(solution)/shard_map/ppermute | solution.py:404
  16.9 2.9 %forward.1 = (f32[4,16,32,128]{3,2,1,0:T(8,128)S(1)}, f32[2,4,32,128]{3,2,1,0:T(8,128)S(1)}, f32[24,32,128]{2,1,0:T(8,128)S(1)}, f32[3,16,128]{2,1,0:T(8,128)S(1)}) custom-call(f32[16,32,128]{2,1,0:T(8,128)S(1)} %get-tuple-element.29.refs_0_, f32[16,32,128]{2,1,0:T(8,128)S(1)} %get-tuple-element.30.refs_1_, f32[16,32,128]{2,1,0:T(8,128)S(1)} %collective-permute-done.refs_2_, ...), custom_call_target="tpu_custom_call" | custom-call | flops 1000000 | bytes 1000000 | tf_op jit(solution)/shard_map/forward/pallas_call | solution.py:390
  19.9 0.1 collective-permute-start.5
  20.0 2.9 %collective-permute-start.4 = (f32[24,32,128]{2,1,0:T(8,128)S(1)}, f32[24,32,128]{2,1,0:T(8,128)S(1)}, u32[]{:S(2)}, u32[]{:S(2)}) collective-permute-start(f32[24,32,128]{2,1,0:T(8,128)S(1)} %get-tuple-element.38), channel_id=1, source_target_pairs={{0,15},{1,2},{2,1},{3,4},{4,3},{5,6},{6,5},{7,8},{8,7},{9,10},{10,... | collective-permute-start | bytes 1179656 | tf_op jit(solution)/shard_map/ppermute | solution.py:404
  22.9 9.2 %all_to_all.11 = f32[16,1,128]{2,1,0:T(1,128)S(1)} all-to-all(f32[16,1,128]{2,1,0:T(1,128)S(1)} %bitcast.7), channel_id=1, replica_groups=mesh['groups'=2,'shot'=16] {'shot'}, dimensions={0} | all-to-all | bytes 16384 | tf_op jit(solution)/shard_map/all_to_all | solution.py:457
  32.1 0.8 %traces.1 = (bf16[256,512]{1,0:T(8,128)(2,1)S(1)}, f32[256,256]{1,0:T(8,128)S(1)}, f32[8,256]{1,0:T(8,128)S(1)}) custom-call(f32[8,256]{1,0:T(8,128)S(1)} %get-tuple-element.40.refs_0_.refs_8_, f32[16,128]{1,0:T(8,128)S(1)} %bitcast.6, f32[4,16,32,128]{3,2,1,0:T(8,128)S(1)} %get-tuple-element.36.refs_2_.refs_0_), custom_call_target="tpu_custom_call" | custom-call | flops 1000000 | bytes 1000000 | tf_op jit(solution)/shard_map/traces/pallas_call | solution.py:390
  33.0 3.9 %forward_last.1 = (f32[4,16,32,128]{3,2,1,0:T(8,128)S(1)}, f32[16,256]{1,0:T(8,128)S(1)}) custom-call(f32[4,16,32,128]{3,2,1,0:T(8,128)S(1)} %get-tuple-element.36.refs_2_.refs_0_, f32[2,4,32,128]{3,2,1,0:T(8,128)S(1)} %get-tuple-element.37.refs_1_, f32[24,32,128]{2,1,0:T(8,128)S(1)} %collective-permute-done.4.refs_2_, ...), custom_call_target="tpu_custom_call" | custom-call | flops 1000000 | bytes 1000000 | tf_op jit(solution)/shard_map/forward_last/pallas_call | solution.py:390
  36.8 0.1 collective-permute-start.6
  36.9 1.1 %collective-permute-done.6.mate = f32[16,256]{1,0:T(8,128)S(1)} collective-permute-done((f32[16,256]{1,0:T(8,128)S(1)}, f32[16,256]{1,0:T(8,128)S(1)}, u32[]{:S(2)}, u32[]{:S(2)}) %collective-permute-start.6) | collective-permute-done | bytes 16416 | tf_op jit(solution)/shard_map/ppermute | solution.py:404
  38.0 2.3 %collective-permute-start.8 = (f32[2,16,256]{2,1,0:T(8,128)S(1)}, f32[2,16,256]{2,1,0:T(8,128)S(1)}, u32[]{:S(2)}, u32[]{:S(2)}) collective-permute-start(f32[2,16,256]{2,1,0:T(8,128)S(1)} %pair.1.refs_6_), channel_id=1, source_target_pairs={{0,14},{1,15},{2,4},{3,5},{4,2},{5,3},{6,8},{7,9},{8,6},{9,7},{10,... | collective-permute-start | bytes 98312 | tf_op jit(solution)/shard_map/ppermute | solution.py:404
  40.3 0.8 %own_sources.1.refs_5_ = f32[8,16,32,128]{3,2,1,0:T(8,128)S(1)} custom-call(f32[16,256]{1,0:T(8,128)S(1)} %get-tuple-element.46.adj), custom_call_target="tpu_custom_call" | custom-call | flops 1000000 | bytes 1000000 | tf_op jit(solution)/shard_map/own_sources/pallas_call | solution.py:390
  41.1 3.6 %collective-permute-done.8.refs_8_ = f32[2,16,256]{2,1,0:T(8,128)S(1)} collective-permute-done((f32[2,16,256]{2,1,0:T(8,128)S(1)}, f32[2,16,256]{2,1,0:T(8,128)S(1)}, u32[]{:S(2)}, u32[]{:S(2)}) %collective-permute-start.8) | collective-permute-done | bytes 32800 | tf_op jit(solution)/shard_map/ppermute | solution.py:404
  44.7 5.3 %adjoint.1 = (f32[4,32,128]{2,1,0:T(8,128)S(1)}, f32[4,32,128]{2,1,0:T(8,128)S(1)}, f32[4,32,128]{2,1,0:T(8,128)S(1)}, f32[4,32,128]{2,1,0:T(8,128)S(1)}) custom-call(f32[4,16,32,128]{3,2,1,0:T(8,128)S(1)} %get-tuple-element.36.refs_2_.refs_0_, f32[4,16,32,128]{3,2,1,0:T(8,128)S(1)} %get-tuple-element.45.refs_1_, ...), custom_call_target="tpu_custom_call" | custom-call | flops 1000000 | bytes 1000000 | tf_op jit(solution)/shard_map/adjoint/pallas_call | solution.py:390
  50.0 0.1 collective-permute-start.9
  50.1 1.1 %collective-permute-start.10 = (f32[4,32,128]{2,1,0:T(8,128)S(1)}, f32[4,32,128]{2,1,0:T(8,128)S(1)}, u32[]{:S(2)}, u32[]{:S(2)}) collective-permute-start(f32[4,32,128]{2,1,0:T(8,128)S(1)} %get-tuple-element.49), channel_id=1, source_target_pairs={{0,8},{1,9},{2,10},{3,11},{4,12},{5,13},{6,14},{7,15},{8,0},{9,1},... | collective-permute-start | bytes 196616 | tf_op jit(solution)/shard_map/ppermute | solution.py:404
  51.2 3.3 %collective-permute-start.11 = (f32[4,32,128]{2,1,0:T(8,128)S(1)}, f32[4,32,128]{2,1,0:T(8,128)S(1)}, u32[]{:S(2)}, u32[]{:S(2)}) collective-permute-start(f32[4,32,128]{2,1,0:T(8,128)S(1)} %get-tuple-element.50), channel_id=1, source_target_pairs={{0,12},{1,13},{2,14},{3,15},{4,8},{5,9},{6,10},{7,11},{8,4},{9,5},... | collective-permute-start | bytes 196616 | tf_op jit(solution)/shard_map/ppermute | solution.py:404
  54.5 3.1 %collective-permute-done.10 = f32[4,32,128]{2,1,0:T(8,128)S(1)} collective-permute-done((f32[4,32,128]{2,1,0:T(8,128)S(1)}, f32[4,32,128]{2,1,0:T(8,128)S(1)}, u32[]{:S(2)}, u32[]{:S(2)}) %collective-permute-start.10) | collective-permute-done | bytes 65568 | tf_op jit(solution)/shard_map/ppermute | solution.py:404
  57.6 0.6 %add_add_fusion = f32[4,32,128]{2,1,0:T(8,128)} fusion(f32[4,32,128]{2,1,0:T(8,128)S(1)} %collective-permute-done.11, f32[4,32,128]{2,1,0:T(8,128)S(1)} %collective-permute-done.10, f32[4,32,128]{2,1,0:T(8,128)S(1)} %get-tuple-element.47, f32[4,32,128]{2,1,0:T(8,128)S(1)} %collective-permute-done.9), kind=kLoop, calls=%fused_computation | loop fusion | flops 49152 | bytes 327680 | tf_op jit(solution)/shard_map/add | solution.py:526
  (16 shorter events, 0.0 us)
Async XLA Ops:
  0.0 16.9 %collective-permute-start.1 = (f32[16,32,128]{2,1,0:T(8,128)}, f32[16,32,128]{2,1,0:T(8,128)S(1)}, u32[]{:S(2)}, u32[]{:S(2)}) collective-permute-start(f32[16,32,128]{2,1,0:T(8,128)} %now.1), channel_id=1, source_target_pairs={{0,1},{1,0},{2,3},{3,2},{4,5},{5,4},{6,7},{7,6},{8,9},{9,8},{10,11... | collective-permute-start | bytes 786440 | tf_op jit(solution)/shard_map/ppermute | solution.py:404
  0.5 16.5 %collective-permute-start = (f32[16,32,128]{2,1,0:T(8,128)}, f32[16,32,128]{2,1,0:T(8,128)S(1)}, u32[]{:S(2)}, u32[]{:S(2)}) collective-permute-start(f32[16,32,128]{2,1,0:T(8,128)} %now.1), channel_id=1, source_target_pairs={{0,15},{1,2},{2,1},{3,4},{4,3},{5,6},{6,5},{7,8},{8,7},{9,10},{10,... | collective-permute-start | bytes 786440 | tf_op jit(solution)/shard_map/ppermute | solution.py:404
  6.8 1.0 %copy-start.1 = (f32[16,32,128]{2,1,0:T(8,128)S(1)}, f32[16,32,128]{2,1,0:T(8,128)}, u32[]{:S(2)}) copy-start(f32[16,32,128]{2,1,0:T(8,128)} %before.1) | copy-start | bytes 786436
  7.7 0.7 %copy-start.6 = (f32[1,8]{1,0:T(1,128)S(1)}, f32[1,8]{1,0:T(1,128)}, u32[]{:S(2)}) copy-start(f32[1,8]{1,0:T(1,128)} %wavelet.1) | copy-start | bytes 100
  9.0 7.9 %collective-permute-start.2 = (f32[400,128]{1,0:T(8,128)S(1)}, f32[400,128]{1,0:T(8,128)S(1)}, u32[]{:S(2)}, u32[]{:S(2)}) collective-permute-start(f32[400,128]{1,0:T(8,128)S(1)} %get-tuple-element.31), channel_id=1, source_target_pairs={{0,15},{1,2},{2,1},{3,4},{4,3},{5,6},{6,5},{7,8},{8,7},{9,10},{10,... | collective-permute-start | bytes 614408 | tf_op jit(solution)/shard_map/ppermute | solution.py:404
  9.1 7.9 %collective-permute-start.3 = (f32[400,128]{1,0:T(8,128)S(1)}, f32[400,128]{1,0:T(8,128)S(1)}, u32[]{:S(2)}, u32[]{:S(2)}) collective-permute-start(f32[400,128]{1,0:T(8,128)S(1)} %get-tuple-element.32), channel_id=1, source_target_pairs={{0,1},{1,0},{2,3},{3,2},{4,5},{5,4},{6,7},{7,6},{8,9},{9,8},{10,11... | collective-permute-start | bytes 614408 | tf_op jit(solution)/shard_map/ppermute | solution.py:404
  9.1 1.2 %copy-start = (f32[64,32,128]{2,1,0:T(8,128)S(1)}, f32[64,32,128]{2,1,0:T(8,128)}, u32[]{:S(2)}) copy-start(f32[64,32,128]{2,1,0:T(8,128)} %courant.1) | copy-start | bytes 3145732
  10.4 0.9 %copy-start.2 = (f32[16,32,128]{2,1,0:T(8,128)S(1)}, f32[16,32,128]{2,1,0:T(8,128)}, u32[]{:S(2)}) copy-start(f32[16,32,128]{2,1,0:T(8,128)} %now.1) | copy-start | bytes 786436
  11.3 0.7 %copy-start.3 = (f32[16,128]{1,0:T(8,128)S(1)}, f32[16,128]{1,0:T(8,128)}, u32[]{:S(2)}) copy-start(f32[16,128]{1,0:T(8,128)} %observed.1) | copy-start | bytes 24580
  12.0 0.7 %copy-start.4 = (s32[256]{0:T(256)S(1)}, s32[256]{0:T(256)}, u32[]{:S(2)}) copy-start(s32[256]{0:T(256)} %param.13) | copy-start | bytes 3076
  12.7 0.7 %copy-start.5 = (s32[256]{0:T(256)S(1)}, s32[256]{0:T(256)}, u32[]{:S(2)}) copy-start(s32[256]{0:T(256)} %param.14) | copy-start | bytes 3076
  19.9 13.1 %collective-permute-start.5 = (f32[24,32,128]{2,1,0:T(8,128)S(1)}, f32[24,32,128]{2,1,0:T(8,128)S(1)}, u32[]{:S(2)}, u32[]{:S(2)}) collective-permute-start(f32[24,32,128]{2,1,0:T(8,128)S(1)} %get-tuple-element.38), channel_id=1, source_target_pairs={{0,1},{1,0},{2,3},{3,2},{4,5},{5,4},{6,7},{7,6},{8,9},{9,8},{10,11... | collective-permute-start | bytes 1179656 | tf_op jit(solution)/shard_map/ppermute | solution.py:404
  20.0 13.0 %collective-permute-start.4 = (f32[24,32,128]{2,1,0:T(8,128)S(1)}, f32[24,32,128]{2,1,0:T(8,128)S(1)}, u32[]{:S(2)}, u32[]{:S(2)}) collective-permute-start(f32[24,32,128]{2,1,0:T(8,128)S(1)} %get-tuple-element.38), channel_id=1, source_target_pairs={{0,15},{1,2},{2,1},{3,4},{4,3},{5,6},{6,5},{7,8},{8,7},{9,10},{10,... | collective-permute-start | bytes 1179656 | tf_op jit(solution)/shard_map/ppermute | solution.py:404
  36.8 1.2 %collective-permute-start.6 = (f32[16,256]{1,0:T(8,128)S(1)}, f32[16,256]{1,0:T(8,128)S(1)}, u32[]{:S(2)}, u32[]{:S(2)}) collective-permute-start(f32[16,256]{1,0:T(8,128)S(1)} %get-tuple-element.46.adj), channel_id=1, source_target_pairs={{0,1},{1,0},{2,3},{3,2},{4,5},{5,4},{6,7},{7,6},{8,9},{9,8},{10,11... | collective-permute-start | bytes 49160 | tf_op jit(solution)/shard_map/ppermute | solution.py:404
  38.0 6.6 %collective-permute-start.8 = (f32[2,16,256]{2,1,0:T(8,128)S(1)}, f32[2,16,256]{2,1,0:T(8,128)S(1)}, u32[]{:S(2)}, u32[]{:S(2)}) collective-permute-start(f32[2,16,256]{2,1,0:T(8,128)S(1)} %pair.1.refs_6_), channel_id=1, source_target_pairs={{0,14},{1,15},{2,4},{3,5},{4,2},{5,3},{6,8},{7,9},{8,6},{9,7},{10,... | collective-permute-start | bytes 98312 | tf_op jit(solution)/shard_map/ppermute | solution.py:404
  40.3 4.3 %collective-permute-start.7 = (f32[2,16,256]{2,1,0:T(8,128)S(1)}, f32[2,16,256]{2,1,0:T(8,128)S(1)}, u32[]{:S(2)}, u32[]{:S(2)}) collective-permute-start(f32[2,16,256]{2,1,0:T(8,128)S(1)} %pair.1.refs_6_), channel_id=1, source_target_pairs={{0,2},{1,3},{2,0},{3,1},{4,6},{5,7},{6,4},{7,5},{8,10},{9,11},{10,... | collective-permute-start | bytes 98312 | tf_op jit(solution)/shard_map/ppermute | solution.py:404
  50.0 4.5 %collective-permute-start.9 = (f32[4,32,128]{2,1,0:T(8,128)S(1)}, f32[4,32,128]{2,1,0:T(8,128)S(1)}, u32[]{:S(2)}, u32[]{:S(2)}) collective-permute-start(f32[4,32,128]{2,1,0:T(8,128)S(1)} %get-tuple-element.48), channel_id=1, source_target_pairs={{0,4},{1,5},{2,6},{3,7},{4,0},{5,1},{6,2},{7,3},{8,12},{9,13},{10,... | collective-permute-start | bytes 196616 | tf_op jit(solution)/shard_map/ppermute | solution.py:404
  50.1 7.5 %collective-permute-start.10 = (f32[4,32,128]{2,1,0:T(8,128)S(1)}, f32[4,32,128]{2,1,0:T(8,128)S(1)}, u32[]{:S(2)}, u32[]{:S(2)}) collective-permute-start(f32[4,32,128]{2,1,0:T(8,128)S(1)} %get-tuple-element.49), channel_id=1, source_target_pairs={{0,8},{1,9},{2,10},{3,11},{4,12},{5,13},{6,14},{7,15},{8,0},{9,1},... | collective-permute-start | bytes 196616 | tf_op jit(solution)/shard_map/ppermute | solution.py:404
  51.2 6.4 %collective-permute-start.11 = (f32[4,32,128]{2,1,0:T(8,128)S(1)}, f32[4,32,128]{2,1,0:T(8,128)S(1)}, u32[]{:S(2)}, u32[]{:S(2)}) collective-permute-start(f32[4,32,128]{2,1,0:T(8,128)S(1)} %get-tuple-element.50), channel_id=1, source_target_pairs={{0,12},{1,13},{2,14},{3,15},{4,8},{5,9},{6,10},{7,11},{8,4},{9,5},... | collective-permute-start | bytes 196616 | tf_op jit(solution)/shard_map/ppermute | solution.py:404

commit v6 on v5

--- a/solution.py
+++ b/solution.py
@@ -98,28 +98,29 @@
     return lax.rem(lax.axis_index("shot"), 2)
 
 
-def message_kernel(before, wavelet, source, outer_out, mate_out, pack_out, before_out):
+def message_kernel(now, before, wavelet, source, outer_out, mate_out, pack_out, now_out, before_out):
     rows, span_y, span_z = before.shape
     which = lax.broadcasted_iota(jnp.int32, (16, span_z), 0)
     pack = jnp.where(which >= NT, source[0].astype(F32), 0.0)
     for step in range(NT):
         pack = jnp.where(which == step, wavelet[0, step], pack)
     pack_out[...] = pack
+    narrow = RAD * (ROUNDS[0] - 1)
+    wide = rows * span_y
+    size = wide + narrow * span_y
+    odd = parity()
+    field = now[...]
+    now_out[...] = field
     before_out[...] = before[...]
-    narrow = RAD * (ROUNDS[0] - 1)
-    size = narrow * span_y
-    odd = parity()
-    outer_out[:size] = before[pl.ds(odd * (rows - narrow), narrow)].reshape(size, span_z)
-    mate_out[:size] = before[pl.ds((1 - odd) * (rows - narrow), narrow)].reshape(size, span_z)
-    outer_out[size:] = pack
-    mate_out[size:] = pack
-
-
-def prepare_kernel(
-    courant, cells, order, observed, pack, now, model_out, cells_out, observed_out, now_out, ymat_out, zmat_out
-):
-    rows, span_y, span_z = now.shape
-    now_out[...] = now[...]
+    for out, side in ((outer_out, odd), (mate_out, 1 - odd)):
+        out[:wide] = field.reshape(wide, span_z)
+        out[wide:size] = before[pl.ds(side * (rows - narrow), narrow)].reshape(size - wide, span_z)
+        out[size:] = pack
+
+
+def prepare_kernel(courant, cells, order, observed, pack, model_out, cells_out, ymat_out, zmat_out, *parts_out):
+    rows = 16
+    span_y, span_z = courant.shape[1:]
     build_bands(span_y, span_z, ymat_out, zmat_out)
     piece = lax.rem(lax.axis_index("shot"), PIECES)
     period = courant.shape[0]
@@ -138,7 +139,20 @@
         found = dot(digits, chosen)
         ordered = found[0:1] * 256.0 + found[1:2]
         cells_out[:, j : j + 256] = jnp.broadcast_to(ordered, (8, 256))
-    observed_out[...] = observed[...] + 0.0 * pack[0:1, :]
+    period = lax.axis_index("shot") // PIECES
+    for i, out in enumerate(parts_out):
+        out[...] = observed[pl.ds((period ^ i) * PIECES, PIECES)]
+
+
+def middle_kernel(*refs):
+    half = len(refs) - PIECES - 1
+    (pack, *parts), (pack_out, *outs) = refs[:half], refs[half:]
+    pack_out[...] = pack[...]
+    period = lax.axis_index("shot") // PIECES
+    piece = lax.rem(lax.axis_index("shot"), PIECES)
+    for i, part in enumerate(parts):
+        for j, out in enumerate(outs):
+            out[period ^ i] = part[piece ^ j]
 
 
 def pick_tables(cells, table_rows):
@@ -182,15 +196,16 @@
     cur_outer = jnp.where(odd == 0, low, high)
     cur_mate = jnp.where(odd == 0, high, low)
     if index == 0:
-        now, before, now_outer, now_mate, before_outer, before_mate = refs_in
+        now, before, got_outer, got_mate = refs_in
+        edge = wide * shape[0]
         cur[own : own + rows] = now[...]
         old[own : own + rows] = before[...]
-        cur[pl.ds(cur_outer, wide)] = now_outer[...]
-        cur[pl.ds(cur_mate, wide)] = now_mate[...]
-        size = narrow * shape[0]
+        cur[pl.ds(cur_outer, wide)] = got_outer[:edge].reshape((wide,) + shape)
+        cur[pl.ds(cur_mate, wide)] = got_mate[:edge].reshape((wide,) + shape)
+        size = edge + narrow * shape[0]
         low = own - narrow
-        old[pl.ds(jnp.where(odd == 0, low, high), narrow)] = before_outer[:size].reshape((narrow,) + shape)
-        old[pl.ds(jnp.where(odd == 0, high, low), narrow)] = before_mate[:size].reshape((narrow,) + shape)
+        old[pl.ds(jnp.where(odd == 0, low, high), narrow)] = got_outer[edge:size].reshape((narrow,) + shape)
+        old[pl.ds(jnp.where(odd == 0, high, low), narrow)] = got_mate[edge:size].reshape((narrow,) + shape)
     else:
         earlier, known, got_outer, got_mate = refs_in
         cur[own : own + rows] = earlier[earlier.shape[0] - 1]
@@ -224,12 +239,11 @@
 
 
 def forward_kernel(index, *refs):
-    take = 6 if index == 0 else 4
-    refs_in, refs = refs[:take], refs[take:]
+    refs_in, refs = refs[:4], refs[4:]
     zmat, ymat, model, pack, fields, known, send = refs[:7]
     if index == 0:
         packs, buf_a, buf_b = refs[7:]
-        gather_packs(pack, refs_in[4], refs_in[5], packs)
+        gather_packs(pack, refs_in[2], refs_in[3], packs)
     else:
         packs, (buf_a, buf_b) = pack, refs[7:]
     cur, old, own = forward_round(index, refs_in, zmat, ymat, model, packs, fields, buf_a, buf_b)
@@ -267,7 +281,12 @@
 
 
 def tables_kernel(count, *refs):
-    (cells, observed, *fields), (rows_out, lanes_out, traces) = refs[:-3], refs[-3:]
+    (cells, *refs), (rows_out, lanes_out, traces, observed) = refs[:-4], refs[-4:]
+    groups, fields = refs[:PIECES], refs[PIECES:]
+    piece = lax.rem(lax.axis_index("shot"), PIECES)
+    for j, group in enumerate(groups):
+        for period in range(group.shape[0]):
+            observed[pl.ds(period * PIECES + (piece ^ j), 1)] = group[period]
     rows_table, lane_table = pick_tables(cells[0:1].astype(jnp.int32), rows_out.shape[1])
     rows_out[...] = rows_table
     lanes_out[...] = lane_table
@@ -281,8 +300,7 @@
 
 
 def last_kernel(index, *refs):
-    take = 6 if index == 0 else 4
-    refs_in, refs = refs[:take], refs[take:]
+    refs_in, refs = refs[:4], refs[4:]
     zmat, ymat, model, packs, cells, rows_table, lane_table, traces = refs[:8]
     fields, adj, buf_a, buf_b = refs[8:]
     forward_round(index, refs_in, zmat, ymat, model, packs, fields, buf_a, buf_b)
@@ -430,35 +448,55 @@
     plane = (span_y, span_z)
 
     narrow = RAD * (ROUNDS[0] - 1)
-    now_outer, now_mate = with_outer(wave_now), with_mate(wave_now)
-    message = jax.ShapeDtypeStruct((narrow * span_y + 16, span_z), F32)
-    to_outer, to_mate, pack, before = call(
+    message = jax.ShapeDtypeStruct(((rows + narrow) * span_y + 16, span_z), F32)
+    to_outer, to_mate, pack, now, before = call(
         message_kernel,
-        (message, message, jax.ShapeDtypeStruct((16, span_z), F32), jax.ShapeDtypeStruct(wave_before.shape, F32)),
-        (wave_before, wavelet, source_cell),
-        specs=[VMEM, SMEM, SMEM],
+        (
+            message,
+            message,
+            jax.ShapeDtypeStruct((16, span_z), F32),
+            jax.ShapeDtypeStruct(wave_now.shape, F32),
+            jax.ShapeDtypeStruct(wave_before.shape, F32),
+        ),
+        (wave_now, wave_before, wavelet, source_cell),
+        specs=[VMEM, VMEM, SMEM, SMEM],
         name="message",
     )
-    before_outer, before_mate = with_outer(to_outer), with_mate(to_mate)
-
-    model, cells, observed, now, ymat, zmat = call(
+    got_outer, got_mate = with_outer(to_outer), with_mate(to_mate)
+
+    slabs = devices // PIECES
+    part = jax.ShapeDtypeStruct((PIECES, 1, observed.shape[1]), F32)
+    model, cells, ymat, zmat, *parts = call(
         prepare_kernel,
         (
             jax.ShapeDtypeStruct((rows + 2 * HALO,) + plane, F32),
             jax.ShapeDtypeStruct((8, count), F32),
-            jax.ShapeDtypeStruct(observed.shape, F32),
-            jax.ShapeDtypeStruct(wave_now.shape, F32),
             jax.ShapeDtypeStruct((GROUP * span_y, GROUP * span_y), BF),
             jax.ShapeDtypeStruct((2 * span_z, 2 * span_z), BF),
+        )
+        + (part,) * slabs,
+        (
+            courant_sq,
+            receiver_cell.reshape(1, count),
+            send_order.reshape(1, count),
+            observed.reshape(devices, 1, observed.shape[1]),
+            pack,
         ),
-        (courant_sq, receiver_cell.reshape(1, count), send_order.reshape(1, count), observed, pack, wave_now),
         name="prepare",
     )
-    recorded = lax.all_to_all(observed, "shot", split_axis=0, concat_axis=0, tiled=True)
+    parts[1:] = [swapped(parts[i], lambda d: d ^ (i * PIECES)) for i in range(1, slabs)]
+    pack, *groups = call(
+        middle_kernel,
+        (jax.ShapeDtypeStruct(pack.shape, F32),)
+        + (jax.ShapeDtypeStruct((slabs, 1, observed.shape[1]), F32),) * PIECES,
+        (pack, *parts),
+        name="middle",
+    )
+    groups = [groups[0]] + [swapped(groups[j], lambda d: d ^ j) for j in range(1, PIECES)]
 
     common = (zmat, ymat, model)
     field_list = []
-    ins = (now, before, now_outer, now_mate, before_outer, before_mate)
+    ins = (now, before, got_outer, got_mate)
     for index in range(len(ROUNDS) - 1):
         window = rows + 2 * RAD * ROUNDS[index]
         sent = 2 * rows - 2 * RAD
@@ -486,7 +524,8 @@
             jax.ShapeDtypeStruct((count, 256), F32),
             jax.ShapeDtypeStruct((NT, count), F32),
         ),
-        (cells, recorded, *field_list),
+        (cells, *groups, *field_list),
+        scratch=[pltpu.VMEM(observed.shape, F32)],
         name="traces",
     )
     index = len(ROUNDS) - 1
@@ -510,7 +549,6 @@
         pair_kernel, jax.ShapeDtypeStruct((2, 2 * NT, count), F32), (adj, with_mate(adj)), name="pair"
     )
     adjs = [sources, pair, with_even_pair(pair), with_odd_pair(pair)]
-    slabs = devices // PIECES
     thick = rows // slabs
     parts = call(
         functools.partial(adjoint_kernel, len(field_list), slabs),

time: 58.6 us -> 61.8 us (1.055)
  blocking collectives: 9.24 us -> 0 us
  waiting for transfers between devices: 10.8 us -> 18.8 us
  starting transfers between devices: 16 us -> 20.8 us
    all_to_all x1 -> x0, blocking collectives: 9.24 us -> none  [per_device(): lax.all_to_all(observed, 'shot', split_axis=0, concat_axis=0, tiled=True)]
    ppermute x12 -> x16, waiting for transfers between devices: 10.8 us -> 18.8 us  [swapped(): lax.ppermute(value, 'shot', [(d, partner(d) % count) for d in range(count)])]
    ppermute x12 -> x16, starting transfers between devices: 16 us -> 20.8 us  [swapped(): lax.ppermute(value, 'shot', [(d, partner(d) % count) for d in range(count)])]
    pallas_call x8 -> x9, Pallas kernels: 14.9 us -> 14.7 us  [call(): pl.pallas_call(kernel, out_shape=outs, in_specs=specs or [VMEM] * len(ins...]
  transfers between devices with their start and end apart: 12 -> 16, of which waited for: 4 -> 6; matrix products, arithmetic and copies ran while one was open for 0% -> 0% of each run, Pallas kernels for 5% -> 4%
where the time goes in v6:
time: 61.8 us; the launch traced here: 61.5 us
  starting transfers between devices  20.8 us (34%)
  waiting for transfers between devices  18.8 us (30%)
  Pallas kernels  14.7 us (24%)
  local copies, waits for them, and re-layouts  5.83 us (9%)
  between operations  0.76 us (1%)
  other arithmetic  0.65 us (1%)
    ppermute x16, starting transfers between devices, swapped(): lax.ppermute(value, 'shot', [(d, partner(d) % count) for d in range(count)])  20.8 us
    ppermute x16, waiting for transfers between devices, swapped(): lax.ppermute(value, 'shot', [(d, partner(d) % count) for d in range(count)])  18.8 us
    pallas_call x9, Pallas kernels, call(): pl.pallas_call(kernel, out_shape=outs, in_specs=specs or [VMEM] * len(ins...  14.7 us
    unnamed x14, local copies, waits for them, and re-layouts  5.83 us
  transfers between devices with their start and end apart: 16, of which 6 were waited for; matrix products, arithmetic and copies ran while one was open for 0% of the time, Pallas kernels for 4%

profile of v6, /device:TPU:0, one launch (start us, length us, event | category | flops | bytes accessed | tf_op | source)
XLA Modules:
  0.0 61.5 jit_solution(8710062455739007965)
XLA Ops:
  0.7 0.9 %copy-done.1 = f32[16,32,128]{2,1,0:T(8,128)S(1)} copy-done((f32[16,32,128]{2,1,0:T(8,128)S(1)}, f32[16,32,128]{2,1,0:T(8,128)}, u32[]{:S(2)}) %copy-start.1) | copy-done | bytes 262168
  1.6 0.9 %copy-done.2 = f32[16,32,128]{2,1,0:T(8,128)S(1)} copy-done((f32[16,32,128]{2,1,0:T(8,128)S(1)}, f32[16,32,128]{2,1,0:T(8,128)}, u32[]{:S(2)}) %copy-start.2) | copy-done | bytes 262168
  2.6 0.7 %copy-done.6 = f32[1,8]{1,0:T(1,128)S(1)} copy-done((f32[1,8]{1,0:T(1,128)S(1)}, f32[1,8]{1,0:T(1,128)}, u32[]{:S(2)}) %copy-start.6) | copy-done | bytes 56
  3.2 0.6 %message.1 = (f32[912,128]{1,0:T(8,128)S(1)}, f32[912,128]{1,0:T(8,128)S(1)}, f32[16,128]{1,0:T(8,128)S(1)}, f32[16,32,128]{2,1,0:T(8,128)S(1)}, f32[16,32,128]{2,1,0:T(8,128)S(1)}) custom-call(f32[16,32,128]{2,1,0:T(8,128)S(1)} %copy-done.1, f32[16,32,128]{2,1,0:T(8,128)S(1)} %copy-done.2, f32[1,8]{1,0:T(1,128)S(1)} %copy-done.6, s32[1]{0:T(128)S(6)} %copy.9.source), custom_call_target="tpu_custom_call" | custom-call | flops 1000000 | bytes 1000000 | tf_op jit(solution)/shard_map/message/pallas_call | solution.py:408
  3.9 5.5 %collective-permute-start = (f32[912,128]{1,0:T(8,128)S(1)}, f32[912,128]{1,0:T(8,128)S(1)}, u32[]{:S(2)}, u32[]{:S(2)}) collective-permute-start(f32[912,128]{1,0:T(8,128)S(1)} %get-tuple-element.38), channel_id=1, source_target_pairs={{0,15},{1,2},{2,1},{3,4},{4,3},{5,6},{6,5},{7,8},{8,7},{9,10},{10,... | collective-permute-start | bytes 1400840 | tf_op jit(solution)/shard_map/ppermute | solution.py:422
  9.4 1.2 %copy-done = f32[64,32,128]{2,1,0:T(8,128)S(1)} copy-done((f32[64,32,128]{2,1,0:T(8,128)S(1)}, f32[64,32,128]{2,1,0:T(8,128)}, u32[]{:S(2)}) %copy-start) | copy-done | bytes 1048600
  10.6 0.7 %copy-done.3 = f32[16,128]{1,0:T(8,128)S(1)} copy-done((f32[16,128]{1,0:T(8,128)S(1)}, f32[16,128]{1,0:T(8,128)}, u32[]{:S(2)}) %copy-start.3) | copy-done | bytes 8216
  11.3 0.7 %copy-done.4 = s32[256]{0:T(256)S(1)} copy-done((s32[256]{0:T(256)S(1)}, s32[256]{0:T(256)}, u32[]{:S(2)}) %copy-start.4) | copy-done | bytes 1048
  12.0 0.7 %copy-done.5 = s32[256]{0:T(256)S(1)} copy-done((s32[256]{0:T(256)S(1)}, s32[256]{0:T(256)}, u32[]{:S(2)}) %copy-start.5) | copy-done | bytes 1048
  12.6 0.6 prepare.1
  13.2 1.8 %collective-permute-start.3 = (f32[4,1,128]{2,1,0:T(1,128)S(1)}, f32[4,1,128]{2,1,0:T(1,128)S(1)}, u32[]{:S(2)}, u32[]{:S(2)}) collective-permute-start(f32[4,1,128]{2,1,0:T(1,128)S(1)} %get-tuple-element.46), channel_id=1, source_target_pairs={{0,8},{1,9},{2,10},{3,11},{4,12},{5,13},{6,14},{7,15},{8,0},{9,1},... | collective-permute-start | bytes 6152 | tf_op jit(solution)/shard_map/ppermute | solution.py:422
  15.0 2.6 %collective-permute-start.4 = (f32[4,1,128]{2,1,0:T(1,128)S(1)}, f32[4,1,128]{2,1,0:T(1,128)S(1)}, u32[]{:S(2)}, u32[]{:S(2)}) collective-permute-start(f32[4,1,128]{2,1,0:T(1,128)S(1)} %get-tuple-element.47), channel_id=1, source_target_pairs={{0,12},{1,13},{2,14},{3,15},{4,8},{5,9},{6,10},{7,11},{8,4},{9,5},... | collective-permute-start | bytes 6152 | tf_op jit(solution)/shard_map/ppermute | solution.py:422
  17.6 0.1 collective-permute-done.3.refs_3_
  17.7 2.7 %collective-permute-done.4.refs_4_ = f32[4,1,128]{2,1,0:T(1,128)S(1)} collective-permute-done((f32[4,1,128]{2,1,0:T(1,128)S(1)}, f32[4,1,128]{2,1,0:T(1,128)S(1)}, u32[]{:S(2)}, u32[]{:S(2)}) %collective-permute-start.4) | collective-permute-done | bytes 2080 | tf_op jit(solution)/shard_map/ppermute | solution.py:422
  20.4 2.9 %forward.1 = (f32[4,16,32,128]{3,2,1,0:T(8,128)S(1)}, f32[2,4,32,128]{3,2,1,0:T(8,128)S(1)}, f32[24,32,128]{2,1,0:T(8,128)S(1)}, f32[3,16,128]{2,1,0:T(8,128)S(1)}) custom-call(f32[16,32,128]{2,1,0:T(8,128)S(1)} %get-tuple-element.36.refs_0_, f32[16,32,128]{2,1,0:T(8,128)S(1)} %get-tuple-element.37.refs_1_, f32[912,128]{1,0:T(8,128)S(1)} %collective-permute-done.refs_2_, ...), custom_call_target="tpu_custom_call" | custom-call | flops 1000000 | bytes 1000000 | tf_op jit(solution)/shard_map/forward/pallas_call | solution.py:408
  23.3 0.1 collective-permute-start.6
  23.4 2.6 %collective-permute-start.5 = (f32[24,32,128]{2,1,0:T(8,128)S(1)}, f32[24,32,128]{2,1,0:T(8,128)S(1)}, u32[]{:S(2)}, u32[]{:S(2)}) collective-permute-start(f32[24,32,128]{2,1,0:T(8,128)S(1)} %get-tuple-element.51), channel_id=1, source_target_pairs={{0,15},{1,2},{2,1},{3,4},{4,3},{5,6},{6,5},{7,8},{8,7},{9,10},{10,... | collective-permute-start | bytes 1179656 | tf_op jit(solution)/shard_map/ppermute | solution.py:422
  26.0 1.9 %collective-permute-start.9 = (f32[4,1,128]{2,1,0:T(1,128)S(1)}, f32[4,1,128]{2,1,0:T(1,128)S(1)}, u32[]{:S(2)}, u32[]{:S(2)}) collective-permute-start(f32[4,1,128]{2,1,0:T(1,128)S(1)} %get-tuple-element.57), channel_id=1, source_target_pairs={{0,3},{1,2},{2,1},{3,0},{4,7},{5,6},{6,5},{7,4},{8,11},{9,10},{10,... | collective-permute-start | bytes 6152 | tf_op jit(solution)/shard_map/ppermute | solution.py:422
  27.8 7.7 %collective-permute-done.8.refs_3_ = f32[4,1,128]{2,1,0:T(1,128)S(1)} collective-permute-done((f32[4,1,128]{2,1,0:T(1,128)S(1)}, f32[4,1,128]{2,1,0:T(1,128)S(1)}, u32[]{:S(2)}, u32[]{:S(2)}) %collective-permute-start.8) | collective-permute-done | bytes 2080 | tf_op jit(solution)/shard_map/ppermute | solution.py:422
  35.6 0.8 %traces.1 = (bf16[256,512]{1,0:T(8,128)(2,1)S(1)}, f32[256,256]{1,0:T(8,128)S(1)}, f32[8,256]{1,0:T(8,128)S(1)}) custom-call(f32[8,256]{1,0:T(8,128)S(1)} %get-tuple-element.53.refs_0_.refs_8_, f32[4,1,128]{2,1,0:T(1,128)S(1)} %get-tuple-element.54.refs_1_, f32[4,1,128]{2,1,0:T(1,128)S(1)} %collective-permute-done.7.refs_2_, ...), custom_call_target="tpu_custom_call" | custom-call | flops 1000000 | bytes 1000000 | tf_op jit(solution)/shard_map/traces/pallas_call | solution.py:408
  36.4 3.8 %forward_last.1 = (f32[4,16,32,128]{3,2,1,0:T(8,128)S(1)}, f32[16,256]{1,0:T(8,128)S(1)}) custom-call(f32[4,16,32,128]{3,2,1,0:T(8,128)S(1)} %get-tuple-element.49.refs_5_.refs_0_, f32[2,4,32,128]{3,2,1,0:T(8,128)S(1)} %get-tuple-element.50.refs_1_, f32[24,32,128]{2,1,0:T(8,128)S(1)} %collective-permute-done.5.refs_2_, ...), custom_call_target="tpu_custom_call" | custom-call | flops 1000000 | bytes 1000000 | tf_op jit(solution)/shard_map/forward_last/pallas_call | solution.py:408
  40.2 0.1 collective-permute-start.10
  40.4 1.1 %collective-permute-done.10.mate = f32[16,256]{1,0:T(8,128)S(1)} collective-permute-done((f32[16,256]{1,0:T(8,128)S(1)}, f32[16,256]{1,0:T(8,128)S(1)}, u32[]{:S(2)}, u32[]{:S(2)}) %collective-permute-start.10) | collective-permute-done | bytes 16416 | tf_op jit(solution)/shard_map/ppermute | solution.py:422
  41.4 1.9 %collective-permute-start.12 = (f32[2,16,256]{2,1,0:T(8,128)S(1)}, f32[2,16,256]{2,1,0:T(8,128)S(1)}, u32[]{:S(2)}, u32[]{:S(2)}) collective-permute-start(f32[2,16,256]{2,1,0:T(8,128)S(1)} %pair.1.refs_6_), channel_id=1, source_target_pairs={{0,14},{1,15},{2,4},{3,5},{4,2},{5,3},{6,8},{7,9},{8,6},{9,7},{10,... | collective-permute-start | bytes 98312 | tf_op jit(solution)/shard_map/ppermute | solution.py:422
  43.3 0.8 %own_sources.1.refs_5_ = f32[8,16,32,128]{3,2,1,0:T(8,128)S(1)} custom-call(f32[16,256]{1,0:T(8,128)S(1)} %get-tuple-element.62.adj), custom_call_target="tpu_custom_call" | custom-call | flops 1000000 | bytes 1000000 | tf_op jit(solution)/shard_map/own_sources/pallas_call | solution.py:408
  44.1 4.0 %collective-permute-done.12.refs_8_ = f32[2,16,256]{2,1,0:T(8,128)S(1)} collective-permute-done((f32[2,16,256]{2,1,0:T(8,128)S(1)}, f32[2,16,256]{2,1,0:T(8,128)S(1)}, u32[]{:S(2)}, u32[]{:S(2)}) %collective-permute-start.12) | collective-permute-done | bytes 32800 | tf_op jit(solution)/shard_map/ppermute | solution.py:422
  48.1 5.2 %adjoint.1 = (f32[4,32,128]{2,1,0:T(8,128)S(1)}, f32[4,32,128]{2,1,0:T(8,128)S(1)}, f32[4,32,128]{2,1,0:T(8,128)S(1)}, f32[4,32,128]{2,1,0:T(8,128)S(1)}) custom-call(f32[4,16,32,128]{3,2,1,0:T(8,128)S(1)} %get-tuple-element.49.refs_5_.refs_0_, f32[4,16,32,128]{3,2,1,0:T(8,128)S(1)} %get-tuple-element.61.refs_1_, ...), custom_call_target="tpu_custom_call" | custom-call | flops 1000000 | bytes 1000000 | tf_op jit(solution)/shard_map/adjoint/pallas_call | solution.py:408
  53.2 0.1 collective-permute-start.13
  53.3 1.5 %collective-permute-start.14 = (f32[4,32,128]{2,1,0:T(8,128)S(1)}, f32[4,32,128]{2,1,0:T(8,128)S(1)}, u32[]{:S(2)}, u32[]{:S(2)}) collective-permute-start(f32[4,32,128]{2,1,0:T(8,128)S(1)} %get-tuple-element.65), channel_id=1, source_target_pairs={{0,8},{1,9},{2,10},{3,11},{4,12},{5,13},{6,14},{7,15},{8,0},{9,1},... | collective-permute-start | bytes 196616 | tf_op jit(solution)/shard_map/ppermute | solution.py:422
  54.8 2.9 %collective-permute-start.15 = (f32[4,32,128]{2,1,0:T(8,128)S(1)}, f32[4,32,128]{2,1,0:T(8,128)S(1)}, u32[]{:S(2)}, u32[]{:S(2)}) collective-permute-start(f32[4,32,128]{2,1,0:T(8,128)S(1)} %get-tuple-element.66), channel_id=1, source_target_pairs={{0,12},{1,13},{2,14},{3,15},{4,8},{5,9},{6,10},{7,11},{8,4},{9,5},... | collective-permute-start | bytes 196616 | tf_op jit(solution)/shard_map/ppermute | solution.py:422
  57.7 3.2 %collective-permute-done.14 = f32[4,32,128]{2,1,0:T(8,128)S(1)} collective-permute-done((f32[4,32,128]{2,1,0:T(8,128)S(1)}, f32[4,32,128]{2,1,0:T(8,128)S(1)}, u32[]{:S(2)}, u32[]{:S(2)}) %collective-permute-start.14) | collective-permute-done | bytes 65568 | tf_op jit(solution)/shard_map/ppermute | solution.py:422
  60.9 0.6 %add_add_fusion = f32[4,32,128]{2,1,0:T(8,128)} fusion(f32[4,32,128]{2,1,0:T(8,128)S(1)} %collective-permute-done.15, f32[4,32,128]{2,1,0:T(8,128)S(1)} %collective-permute-done.14, f32[4,32,128]{2,1,0:T(8,128)S(1)} %get-tuple-element.63, f32[4,32,128]{2,1,0:T(8,128)S(1)} %collective-permute-done.13), kind=kLoop, calls=%fused_computation | loop fusion | flops 49152 | bytes 327680 | tf_op jit(solution)/shard_map/add | solution.py:564
  (24 shorter events, 0.1 us)
Async XLA Ops:
  0.7 1.0 %copy-start.1 = (f32[16,32,128]{2,1,0:T(8,128)S(1)}, f32[16,32,128]{2,1,0:T(8,128)}, u32[]{:S(2)}) copy-start(f32[16,32,128]{2,1,0:T(8,128)} %now.1) | copy-start | bytes 786436
  1.6 0.9 %copy-start.2 = (f32[16,32,128]{2,1,0:T(8,128)S(1)}, f32[16,32,128]{2,1,0:T(8,128)}, u32[]{:S(2)}) copy-start(f32[16,32,128]{2,1,0:T(8,128)} %before.1) | copy-start | bytes 786436
  2.6 0.7 %copy-start.6 = (f32[1,8]{1,0:T(1,128)S(1)}, f32[1,8]{1,0:T(1,128)}, u32[]{:S(2)}) copy-start(f32[1,8]{1,0:T(1,128)} %wavelet.1) | copy-start | bytes 100
  3.9 16.6 %collective-permute-start = (f32[912,128]{1,0:T(8,128)S(1)}, f32[912,128]{1,0:T(8,128)S(1)}, u32[]{:S(2)}, u32[]{:S(2)}) collective-permute-start(f32[912,128]{1,0:T(8,128)S(1)} %get-tuple-element.38), channel_id=1, source_target_pairs={{0,15},{1,2},{2,1},{3,4},{4,3},{5,6},{6,5},{7,8},{8,7},{9,10},{10,... | collective-permute-start | bytes 1400840 | tf_op jit(solution)/shard_map/ppermute | solution.py:422
  9.4 11.1 %collective-permute-start.1 = (f32[912,128]{1,0:T(8,128)S(1)}, f32[912,128]{1,0:T(8,128)S(1)}, u32[]{:S(2)}, u32[]{:S(2)}) collective-permute-start(f32[912,128]{1,0:T(8,128)S(1)} %get-tuple-element.39), channel_id=1, source_target_pairs={{0,1},{1,0},{2,3},{3,2},{4,5},{5,4},{6,7},{7,6},{8,9},{9,8},{10,11... | collective-permute-start | bytes 1400840 | tf_op jit(solution)/shard_map/ppermute | solution.py:422
  9.4 1.2 %copy-start = (f32[64,32,128]{2,1,0:T(8,128)S(1)}, f32[64,32,128]{2,1,0:T(8,128)}, u32[]{:S(2)}) copy-start(f32[64,32,128]{2,1,0:T(8,128)} %courant.1) | copy-start | bytes 3145732
  10.6 0.7 %copy-start.3 = (f32[16,128]{1,0:T(8,128)S(1)}, f32[16,128]{1,0:T(8,128)}, u32[]{:S(2)}) copy-start(f32[16,128]{1,0:T(8,128)} %param.15) | copy-start | bytes 24580
  11.3 0.7 %copy-start.4 = (s32[256]{0:T(256)S(1)}, s32[256]{0:T(256)}, u32[]{:S(2)}) copy-start(s32[256]{0:T(256)} %param.13) | copy-start | bytes 3076
  12.0 0.7 %copy-start.5 = (s32[256]{0:T(256)S(1)}, s32[256]{0:T(256)}, u32[]{:S(2)}) copy-start(s32[256]{0:T(256)} %param.14) | copy-start | bytes 3076
  13.2 4.4 %collective-permute-start.2 = (f32[4,1,128]{2,1,0:T(1,128)S(1)}, f32[4,1,128]{2,1,0:T(1,128)S(1)}, u32[]{:S(2)}, u32[]{:S(2)}) collective-permute-start(f32[4,1,128]{2,1,0:T(1,128)S(1)} %get-tuple-element.45), channel_id=1, source_target_pairs={{0,4},{1,5},{2,6},{3,7},{4,0},{5,1},{6,2},{7,3},{8,12},{9,13},{10,... | collective-permute-start | bytes 6152 | tf_op jit(solution)/shard_map/ppermute | solution.py:422
  13.2 4.5 %collective-permute-start.3 = (f32[4,1,128]{2,1,0:T(1,128)S(1)}, f32[4,1,128]{2,1,0:T(1,128)S(1)}, u32[]{:S(2)}, u32[]{:S(2)}) collective-permute-start(f32[4,1,128]{2,1,0:T(1,128)S(1)} %get-tuple-element.46), channel_id=1, source_target_pairs={{0,8},{1,9},{2,10},{3,11},{4,12},{5,13},{6,14},{7,15},{8,0},{9,1},... | collective-permute-start | bytes 6152 | tf_op jit(solution)/shard_map/ppermute | solution.py:422
  15.0 5.4 %collective-permute-start.4 = (f32[4,1,128]{2,1,0:T(1,128)S(1)}, f32[4,1,128]{2,1,0:T(1,128)S(1)}, u32[]{:S(2)}, u32[]{:S(2)}) collective-permute-start(f32[4,1,128]{2,1,0:T(1,128)S(1)} %get-tuple-element.47), channel_id=1, source_target_pairs={{0,12},{1,13},{2,14},{3,15},{4,8},{5,9},{6,10},{7,11},{8,4},{9,5},... | collective-permute-start | bytes 6152 | tf_op jit(solution)/shard_map/ppermute | solution.py:422
  23.3 13.1 %collective-permute-start.6 = (f32[24,32,128]{2,1,0:T(8,128)S(1)}, f32[24,32,128]{2,1,0:T(8,128)S(1)}, u32[]{:S(2)}, u32[]{:S(2)}) collective-permute-start(f32[24,32,128]{2,1,0:T(8,128)S(1)} %get-tuple-element.51), channel_id=1, source_target_pairs={{0,1},{1,0},{2,3},{3,2},{4,5},{5,4},{6,7},{7,6},{8,9},{9,8},{10,11... | collective-permute-start | bytes 1179656 | tf_op jit(solution)/shard_map/ppermute | solution.py:422
  23.4 13.0 %collective-permute-start.5 = (f32[24,32,128]{2,1,0:T(8,128)S(1)}, f32[24,32,128]{2,1,0:T(8,128)S(1)}, u32[]{:S(2)}, u32[]{:S(2)}) collective-permute-start(f32[24,32,128]{2,1,0:T(8,128)S(1)} %get-tuple-element.51), channel_id=1, source_target_pairs={{0,15},{1,2},{2,1},{3,4},{4,3},{5,6},{6,5},{7,8},{8,7},{9,10},{10,... | collective-permute-start | bytes 1179656 | tf_op jit(solution)/shard_map/ppermute | solution.py:422
  26.0 1.9 %collective-permute-start.7 = (f32[4,1,128]{2,1,0:T(1,128)S(1)}, f32[4,1,128]{2,1,0:T(1,128)S(1)}, u32[]{:S(2)}, u32[]{:S(2)}) collective-permute-start(f32[4,1,128]{2,1,0:T(1,128)S(1)} %get-tuple-element.55), channel_id=1, source_target_pairs={{0,1},{1,0},{2,3},{3,2},{4,5},{5,4},{6,7},{7,6},{8,9},{9,8},{10,11... | collective-permute-start | bytes 6152 | tf_op jit(solution)/shard_map/ppermute | solution.py:422
  26.0 9.6 %collective-permute-start.8 = (f32[4,1,128]{2,1,0:T(1,128)S(1)}, f32[4,1,128]{2,1,0:T(1,128)S(1)}, u32[]{:S(2)}, u32[]{:S(2)}) collective-permute-start(f32[4,1,128]{2,1,0:T(1,128)S(1)} %get-tuple-element.56), channel_id=1, source_target_pairs={{0,2},{1,3},{2,0},{3,1},{4,6},{5,7},{6,4},{7,5},{8,10},{9,11},{10,... | collective-permute-start | bytes 6152 | tf_op jit(solution)/shard_map/ppermute | solution.py:422
  26.0 9.6 %collective-permute-start.9 = (f32[4,1,128]{2,1,0:T(1,128)S(1)}, f32[4,1,128]{2,1,0:T(1,128)S(1)}, u32[]{:S(2)}, u32[]{:S(2)}) collective-permute-start(f32[4,1,128]{2,1,0:T(1,128)S(1)} %get-tuple-element.57), channel_id=1, source_target_pairs={{0,3},{1,2},{2,1},{3,0},{4,7},{5,6},{6,5},{7,4},{8,11},{9,10},{10,... | collective-permute-start | bytes 6152 | tf_op jit(solution)/shard_map/ppermute | solution.py:422
  40.2 1.2 %collective-permute-start.10 = (f32[16,256]{1,0:T(8,128)S(1)}, f32[16,256]{1,0:T(8,128)S(1)}, u32[]{:S(2)}, u32[]{:S(2)}) collective-permute-start(f32[16,256]{1,0:T(8,128)S(1)} %get-tuple-element.62.adj), channel_id=1, source_target_pairs={{0,1},{1,0},{2,3},{3,2},{4,5},{5,4},{6,7},{7,6},{8,9},{9,8},{10,11... | collective-permute-start | bytes 49160 | tf_op jit(solution)/shard_map/ppermute | solution.py:422
  41.4 6.6 %collective-permute-start.12 = (f32[2,16,256]{2,1,0:T(8,128)S(1)}, f32[2,16,256]{2,1,0:T(8,128)S(1)}, u32[]{:S(2)}, u32[]{:S(2)}) collective-permute-start(f32[2,16,256]{2,1,0:T(8,128)S(1)} %pair.1.refs_6_), channel_id=1, source_target_pairs={{0,14},{1,15},{2,4},{3,5},{4,2},{5,3},{6,8},{7,9},{8,6},{9,7},{10,... | collective-permute-start | bytes 98312 | tf_op jit(solution)/shard_map/ppermute | solution.py:422
  43.3 4.7 %collective-permute-start.11 = (f32[2,16,256]{2,1,0:T(8,128)S(1)}, f32[2,16,256]{2,1,0:T(8,128)S(1)}, u32[]{:S(2)}, u32[]{:S(2)}) collective-permute-start(f32[2,16,256]{2,1,0:T(8,128)S(1)} %pair.1.refs_6_), channel_id=1, source_target_pairs={{0,2},{1,3},{2,0},{3,1},{4,6},{5,7},{6,4},{7,5},{8,10},{9,11},{10,... | collective-permute-start | bytes 98312 | tf_op jit(solution)/shard_map/ppermute | solution.py:422
  53.2 4.5 %collective-permute-start.13 = (f32[4,32,128]{2,1,0:T(8,128)S(1)}, f32[4,32,128]{2,1,0:T(8,128)S(1)}, u32[]{:S(2)}, u32[]{:S(2)}) collective-permute-start(f32[4,32,128]{2,1,0:T(8,128)S(1)} %get-tuple-element.64), channel_id=1, source_target_pairs={{0,4},{1,5},{2,6},{3,7},{4,0},{5,1},{6,2},{7,3},{8,12},{9,13},{10,... | collective-permute-start | bytes 196616 | tf_op jit(solution)/shard_map/ppermute | solution.py:422
  53.3 7.6 %collective-permute-start.14 = (f32[4,32,128]{2,1,0:T(8,128)S(1)}, f32[4,32,128]{2,1,0:T(8,128)S(1)}, u32[]{:S(2)}, u32[]{:S(2)}) collective-permute-start(f32[4,32,128]{2,1,0:T(8,128)S(1)} %get-tuple-element.65), channel_id=1, source_target_pairs={{0,8},{1,9},{2,10},{3,11},{4,12},{5,13},{6,14},{7,15},{8,0},{9,1},... | collective-permute-start | bytes 196616 | tf_op jit(solution)/shard_map/ppermute | solution.py:422
  54.8 6.1 %collective-permute-start.15 = (f32[4,32,128]{2,1,0:T(8,128)S(1)}, f32[4,32,128]{2,1,0:T(8,128)S(1)}, u32[]{:S(2)}, u32[]{:S(2)}) collective-permute-start(f32[4,32,128]{2,1,0:T(8,128)S(1)} %get-tuple-element.66), channel_id=1, source_target_pairs={{0,12},{1,13},{2,14},{3,15},{4,8},{5,9},{6,10},{7,11},{8,4},{9,5},... | collective-permute-start | bytes 196616 | tf_op jit(solution)/shard_map/ppermute | solution.py:422

commit v7 on v5

--- a/solution.py
+++ b/solution.py
@@ -168,7 +168,7 @@
 
 
 def forward_round(
-    index, refs_in, zmat, ymat, model, packs, fields, buf_a, buf_b
+    index, refs_in, zmat, ymat, model, packs, fields, buf_a, buf_b, after_step=None
 ):
     steps = ROUNDS[index]
     done = sum(ROUNDS[:index])
@@ -212,6 +212,8 @@
                 pack = packs.at[block + 1]
                 add_source(old, pack, cells[block + 1], done + step, own, block, halo, rows)
         fields[step] = old[own : own + rows]
+        if after_step:
+            after_step(step, old[own : own + rows])
         cur, old = old, cur
     return cur, old, own
 
@@ -285,25 +287,29 @@
     refs_in, refs = refs[:take], refs[take:]
     zmat, ymat, model, packs, cells, rows_table, lane_table, traces = refs[:8]
     fields, adj, buf_a, buf_b = refs[8:]
-    forward_round(index, refs_in, zmat, ymat, model, packs, fields, buf_a, buf_b)
     done = sum(ROUNDS[:index])
-    rows_table = rows_table[...]
-    lane_table = lane_table[...]
-    total = extract(fields[0], done, rows_table, lane_table)
-    for step in range(1, ROUNDS[index]):
-        total = total + extract(fields[step], done + step, rows_table, lane_table)
-    adj[0:NT] = total[0:NT] + traces[...]
+    total = [traces[...]]
+
+    def pick(step, field):
+        total[0] = total[0] + extract(field, done + step, rows_table[...], lane_table[...])[:NT]
+
+    forward_round(index, refs_in, zmat, ymat, model, packs, fields, buf_a, buf_b, pick)
+    adj[0:NT] = total[0]
     adj[NT:] = cells[...]
 
 
-def source_planes(rows_table, lanes, amounts, span_z):
-    high = amounts.astype(BF).astype(F32)
-    low = amounts - high
-    sub = lax.broadcasted_iota(jnp.int32, (span_z, lanes.shape[1]), 0)
-    hit = sub == lanes
-    both = jnp.concatenate([jnp.where(hit, high, 0.0).astype(BF), jnp.where(hit, low, 0.0).astype(BF)], axis=0)
+def source_planes(rows_table, lane_table, amounts, span_z):
+    tiles = split(jnp.broadcast_to(amounts, (16, amounts.shape[1])))
+    both = jnp.concatenate(
+        [lane_table[z : z + 16] * tile for tile in tiles for z in range(0, span_z, 16)], axis=0
+    )
     added = dot(rows_table, both, (((1,), (1,)), ((), ())))
     return added[:, :span_z] + added[:, span_z:]
+
+
+def injection_lanes(cells, span_z):
+    sub = lax.broadcasted_iota(jnp.int32, (span_z, cells.shape[1]), 0)
+    return jnp.where(sub == cells % span_z, 1.0, 0.0).astype(BF)
 
 
 def injection_table(cells, table_rows, span_z):
@@ -315,8 +321,9 @@
     rows, span_y, span_z = out.shape[1:]
     cells = adj[NT : NT + 1].astype(jnp.int32)
     table = injection_table(cells, rows * span_y, span_z)
+    lanes = injection_lanes(cells, span_z)
     for step in range(NT):
-        added = source_planes(table, cells % span_z, adj[step : step + 1], span_z)
+        added = source_planes(table, lanes, adj[step : step + 1], span_z)
         out[step] = added.reshape(rows, span_y, span_z)
 
 
@@ -348,7 +355,7 @@
         adjs[block + 2] = near[2 + odd + block]
         cells = adjs[block + 2, NT : NT + 1].astype(jnp.int32)
         rows_table[block + 2] = injection_table(cells, table_rows, span_z)
-        lanes[block] = cells % span_z
+        lanes[block] = injection_lanes(cells, span_z)
 
     def inject(field, number):
         halo = RAD * (NT - number)

time: 58.6 us -> 58.3 us (level)
  no operation moved by 1% of the time
where the time goes in v7:
time: 58.3 us; the launch traced here: 58 us
  starting transfers between devices  16 us (27%)
  Pallas kernels  14.7 us (25%)
  waiting for transfers between devices  10.8 us (19%)
  blocking collectives  9.24 us (16%)
  local copies, waits for them, and re-layouts  5.82 us (10%)
  between operations  0.76 us (1%)
  other arithmetic  0.65 us (1%)
    ppermute x12, starting transfers between devices, swapped(): lax.ppermute(value, 'shot', [(d, partner(d) % count) for d in range(count)])  16 us
    pallas_call x8, Pallas kernels, call(): pl.pallas_call(kernel, out_shape=outs, in_specs=specs or [VMEM] * len(ins...  14.7 us
    ppermute x12, waiting for transfers between devices, swapped(): lax.ppermute(value, 'shot', [(d, partner(d) % count) for d in range(count)])  10.8 us
    all_to_all x1, blocking collectives, per_device(): lax.all_to_all(observed, 'shot', split_axis=0, concat_axis=0, tiled=True)  9.24 us
    unnamed x14, local copies, waits for them, and re-layouts  5.82 us
  transfers between devices with their start and end apart: 12, of which 4 were waited for; matrix products, arithmetic and copies ran while one was open for 0% of the time, Pallas kernels for 5%

profile of v7, /device:TPU:0, one launch (start us, length us, event | category | flops | bytes accessed | tf_op | source)
XLA Modules:
  0.0 58.0 jit_solution(434730327789284653)
XLA Ops:
  0.0 0.5 collective-permute-start.1
  0.5 5.7 %collective-permute-start = (f32[16,32,128]{2,1,0:T(8,128)}, f32[16,32,128]{2,1,0:T(8,128)S(1)}, u32[]{:S(2)}, u32[]{:S(2)}) collective-permute-start(f32[16,32,128]{2,1,0:T(8,128)} %now.1), channel_id=1, source_target_pairs={{0,15},{1,2},{2,1},{3,4},{4,3},{5,6},{6,5},{7,8},{8,7},{9,10},{10,... | collective-permute-start | bytes 786440 | tf_op jit(solution)/shard_map/ppermute | solution.py:411
  6.8 0.9 %copy-done.1 = f32[16,32,128]{2,1,0:T(8,128)S(1)} copy-done((f32[16,32,128]{2,1,0:T(8,128)S(1)}, f32[16,32,128]{2,1,0:T(8,128)}, u32[]{:S(2)}) %copy-start.1) | copy-done | bytes 262168
  7.7 0.7 %copy-done.6 = f32[1,8]{1,0:T(1,128)S(1)} copy-done((f32[1,8]{1,0:T(1,128)S(1)}, f32[1,8]{1,0:T(1,128)}, u32[]{:S(2)}) %copy-start.6) | copy-done | bytes 56
  8.4 0.6 %message.1 = (f32[400,128]{1,0:T(8,128)S(1)}, f32[400,128]{1,0:T(8,128)S(1)}, f32[16,128]{1,0:T(8,128)S(1)}, f32[16,32,128]{2,1,0:T(8,128)S(1)}) custom-call(f32[16,32,128]{2,1,0:T(8,128)S(1)} %copy-done.1, f32[1,8]{1,0:T(1,128)S(1)} %copy-done.6, s32[1]{0:T(128)S(6)} %copy.10.source), custom_call_target="tpu_custom_call" | custom-call | flops 1000000 | bytes 1000000 | tf_op jit(solution)/shard_map/message/pallas_call | solution.py:397
  9.0 0.1 collective-permute-start.2
  9.1 0.1 collective-permute-start.3
  9.1 0.0 copy-start
  9.1 1.2 %copy-done = f32[64,32,128]{2,1,0:T(8,128)S(1)} copy-done((f32[64,32,128]{2,1,0:T(8,128)S(1)}, f32[64,32,128]{2,1,0:T(8,128)}, u32[]{:S(2)}) %copy-start) | copy-done | bytes 1048600
  10.4 0.9 %copy-done.2 = f32[16,32,128]{2,1,0:T(8,128)S(1)} copy-done((f32[16,32,128]{2,1,0:T(8,128)S(1)}, f32[16,32,128]{2,1,0:T(8,128)}, u32[]{:S(2)}) %copy-start.2) | copy-done | bytes 262168
  11.3 0.7 %copy-done.3 = f32[16,128]{1,0:T(8,128)S(1)} copy-done((f32[16,128]{1,0:T(8,128)S(1)}, f32[16,128]{1,0:T(8,128)}, u32[]{:S(2)}) %copy-start.3) | copy-done | bytes 8216
  12.0 0.7 %copy-done.4 = s32[256]{0:T(256)S(1)} copy-done((s32[256]{0:T(256)S(1)}, s32[256]{0:T(256)}, u32[]{:S(2)}) %copy-start.4) | copy-done | bytes 1048
  12.7 0.7 %copy-done.5 = s32[256]{0:T(256)S(1)} copy-done((s32[256]{0:T(256)S(1)}, s32[256]{0:T(256)}, u32[]{:S(2)}) %copy-start.5) | copy-done | bytes 1048
  13.4 0.6 prepare.1
  13.9 3.0 %collective-permute-done.2.refs_4_ = f32[400,128]{1,0:T(8,128)S(1)} collective-permute-done((f32[400,128]{1,0:T(8,128)S(1)}, f32[400,128]{1,0:T(8,128)S(1)}, u32[]{:S(2)}, u32[]{:S(2)}) %collective-permute-start.2) | collective-permute-done | bytes 204832 | tf_op jit(solution)/shard_map/ppermute | solution.py:411
  16.9 2.9 %forward.1 = (f32[4,16,32,128]{3,2,1,0:T(8,128)S(1)}, f32[2,4,32,128]{3,2,1,0:T(8,128)S(1)}, f32[24,32,128]{2,1,0:T(8,128)S(1)}, f32[3,16,128]{2,1,0:T(8,128)S(1)}) custom-call(f32[16,32,128]{2,1,0:T(8,128)S(1)} %get-tuple-element.29.refs_0_, f32[16,32,128]{2,1,0:T(8,128)S(1)} %get-tuple-element.30.refs_1_, f32[16,32,128]{2,1,0:T(8,128)S(1)} %collective-permute-done.refs_2_, ...), custom_call_target="tpu_custom_call" | custom-call | flops 1000000 | bytes 1000000 | tf_op jit(solution)/shard_map/forward/pallas_call | solution.py:397
  19.9 0.1 collective-permute-start.5
  20.0 2.9 %collective-permute-start.4 = (f32[24,32,128]{2,1,0:T(8,128)S(1)}, f32[24,32,128]{2,1,0:T(8,128)S(1)}, u32[]{:S(2)}, u32[]{:S(2)}) collective-permute-start(f32[24,32,128]{2,1,0:T(8,128)S(1)} %get-tuple-element.38), channel_id=1, source_target_pairs={{0,15},{1,2},{2,1},{3,4},{4,3},{5,6},{6,5},{7,8},{8,7},{9,10},{10,... | collective-permute-start | bytes 1179656 | tf_op jit(solution)/shard_map/ppermute | solution.py:411
  22.9 9.2 %all_to_all.11 = f32[16,1,128]{2,1,0:T(1,128)S(1)} all-to-all(f32[16,1,128]{2,1,0:T(1,128)S(1)} %bitcast.7), channel_id=1, replica_groups=mesh['groups'=2,'shot'=16] {'shot'}, dimensions={0} | all-to-all | bytes 16384 | tf_op jit(solution)/shard_map/all_to_all | solution.py:464
  32.1 0.8 %traces.1 = (bf16[256,512]{1,0:T(8,128)(2,1)S(1)}, f32[256,256]{1,0:T(8,128)S(1)}, f32[8,256]{1,0:T(8,128)S(1)}) custom-call(f32[8,256]{1,0:T(8,128)S(1)} %get-tuple-element.40.refs_0_.refs_8_, f32[16,128]{1,0:T(8,128)S(1)} %bitcast.6, f32[4,16,32,128]{3,2,1,0:T(8,128)S(1)} %get-tuple-element.36.refs_2_.refs_0_), custom_call_target="tpu_custom_call" | custom-call | flops 1000000 | bytes 1000000 | tf_op jit(solution)/shard_map/traces/pallas_call | solution.py:397
  33.0 3.7 %forward_last.1 = (f32[4,16,32,128]{3,2,1,0:T(8,128)S(1)}, f32[16,256]{1,0:T(8,128)S(1)}) custom-call(f32[4,16,32,128]{3,2,1,0:T(8,128)S(1)} %get-tuple-element.36.refs_2_.refs_0_, f32[2,4,32,128]{3,2,1,0:T(8,128)S(1)} %get-tuple-element.37.refs_1_, f32[24,32,128]{2,1,0:T(8,128)S(1)} %collective-permute-done.4.refs_2_, ...), custom_call_target="tpu_custom_call" | custom-call | flops 1000000 | bytes 1000000 | tf_op jit(solution)/shard_map/forward_last/pallas_call | solution.py:397
  36.6 0.1 collective-permute-start.6
  36.7 1.1 %collective-permute-done.6.mate = f32[16,256]{1,0:T(8,128)S(1)} collective-permute-done((f32[16,256]{1,0:T(8,128)S(1)}, f32[16,256]{1,0:T(8,128)S(1)}, u32[]{:S(2)}, u32[]{:S(2)}) %collective-permute-start.6) | collective-permute-done | bytes 16416 | tf_op jit(solution)/shard_map/ppermute | solution.py:411
  37.8 2.3 %collective-permute-start.8 = (f32[2,16,256]{2,1,0:T(8,128)S(1)}, f32[2,16,256]{2,1,0:T(8,128)S(1)}, u32[]{:S(2)}, u32[]{:S(2)}) collective-permute-start(f32[2,16,256]{2,1,0:T(8,128)S(1)} %pair.1.refs_6_), channel_id=1, source_target_pairs={{0,14},{1,15},{2,4},{3,5},{4,2},{5,3},{6,8},{7,9},{8,6},{9,7},{10,... | collective-permute-start | bytes 98312 | tf_op jit(solution)/shard_map/ppermute | solution.py:411
  40.1 0.7 %own_sources.1.refs_5_ = f32[8,16,32,128]{3,2,1,0:T(8,128)S(1)} custom-call(f32[16,256]{1,0:T(8,128)S(1)} %get-tuple-element.46.adj), custom_call_target="tpu_custom_call" | custom-call | flops 1000000 | bytes 1000000 | tf_op jit(solution)/shard_map/own_sources/pallas_call | solution.py:397
  40.8 3.6 %collective-permute-done.8.refs_8_ = f32[2,16,256]{2,1,0:T(8,128)S(1)} collective-permute-done((f32[2,16,256]{2,1,0:T(8,128)S(1)}, f32[2,16,256]{2,1,0:T(8,128)S(1)}, u32[]{:S(2)}, u32[]{:S(2)}) %collective-permute-start.8) | collective-permute-done | bytes 32800 | tf_op jit(solution)/shard_map/ppermute | solution.py:411
  44.4 5.3 %adjoint.1 = (f32[4,32,128]{2,1,0:T(8,128)S(1)}, f32[4,32,128]{2,1,0:T(8,128)S(1)}, f32[4,32,128]{2,1,0:T(8,128)S(1)}, f32[4,32,128]{2,1,0:T(8,128)S(1)}) custom-call(f32[4,16,32,128]{3,2,1,0:T(8,128)S(1)} %get-tuple-element.36.refs_2_.refs_0_, f32[4,16,32,128]{3,2,1,0:T(8,128)S(1)} %get-tuple-element.45.refs_1_, ...), custom_call_target="tpu_custom_call" | custom-call | flops 1000000 | bytes 1000000 | tf_op jit(solution)/shard_map/adjoint/pallas_call | solution.py:397
  49.8 0.1 collective-permute-start.9
  49.9 1.1 %collective-permute-start.10 = (f32[4,32,128]{2,1,0:T(8,128)S(1)}, f32[4,32,128]{2,1,0:T(8,128)S(1)}, u32[]{:S(2)}, u32[]{:S(2)}) collective-permute-start(f32[4,32,128]{2,1,0:T(8,128)S(1)} %get-tuple-element.49), channel_id=1, source_target_pairs={{0,8},{1,9},{2,10},{3,11},{4,12},{5,13},{6,14},{7,15},{8,0},{9,1},... | collective-permute-start | bytes 196616 | tf_op jit(solution)/shard_map/ppermute | solution.py:411
  51.0 3.3 %collective-permute-start.11 = (f32[4,32,128]{2,1,0:T(8,128)S(1)}, f32[4,32,128]{2,1,0:T(8,128)S(1)}, u32[]{:S(2)}, u32[]{:S(2)}) collective-permute-start(f32[4,32,128]{2,1,0:T(8,128)S(1)} %get-tuple-element.50), channel_id=1, source_target_pairs={{0,12},{1,13},{2,14},{3,15},{4,8},{5,9},{6,10},{7,11},{8,4},{9,5},... | collective-permute-start | bytes 196616 | tf_op jit(solution)/shard_map/ppermute | solution.py:411
  54.2 3.1 %collective-permute-done.10 = f32[4,32,128]{2,1,0:T(8,128)S(1)} collective-permute-done((f32[4,32,128]{2,1,0:T(8,128)S(1)}, f32[4,32,128]{2,1,0:T(8,128)S(1)}, u32[]{:S(2)}, u32[]{:S(2)}) %collective-permute-start.10) | collective-permute-done | bytes 65568 | tf_op jit(solution)/shard_map/ppermute | solution.py:411
  57.3 0.6 %add_add_fusion = f32[4,32,128]{2,1,0:T(8,128)} fusion(f32[4,32,128]{2,1,0:T(8,128)S(1)} %collective-permute-done.11, f32[4,32,128]{2,1,0:T(8,128)S(1)} %collective-permute-done.10, f32[4,32,128]{2,1,0:T(8,128)S(1)} %get-tuple-element.47, f32[4,32,128]{2,1,0:T(8,128)S(1)} %collective-permute-done.9), kind=kLoop, calls=%fused_computation | loop fusion | flops 49152 | bytes 327680 | tf_op jit(solution)/shard_map/add | solution.py:533
  (16 shorter events, 0.0 us)
Async XLA Ops:
  0.0 16.9 %collective-permute-start.1 = (f32[16,32,128]{2,1,0:T(8,128)}, f32[16,32,128]{2,1,0:T(8,128)S(1)}, u32[]{:S(2)}, u32[]{:S(2)}) collective-permute-start(f32[16,32,128]{2,1,0:T(8,128)} %now.1), channel_id=1, source_target_pairs={{0,1},{1,0},{2,3},{3,2},{4,5},{5,4},{6,7},{7,6},{8,9},{9,8},{10,11... | collective-permute-start | bytes 786440 | tf_op jit(solution)/shard_map/ppermute | solution.py:411
  0.5 16.5 %collective-permute-start = (f32[16,32,128]{2,1,0:T(8,128)}, f32[16,32,128]{2,1,0:T(8,128)S(1)}, u32[]{:S(2)}, u32[]{:S(2)}) collective-permute-start(f32[16,32,128]{2,1,0:T(8,128)} %now.1), channel_id=1, source_target_pairs={{0,15},{1,2},{2,1},{3,4},{4,3},{5,6},{6,5},{7,8},{8,7},{9,10},{10,... | collective-permute-start | bytes 786440 | tf_op jit(solution)/shard_map/ppermute | solution.py:411
  6.8 1.0 %copy-start.1 = (f32[16,32,128]{2,1,0:T(8,128)S(1)}, f32[16,32,128]{2,1,0:T(8,128)}, u32[]{:S(2)}) copy-start(f32[16,32,128]{2,1,0:T(8,128)} %before.1) | copy-start | bytes 786436
  7.7 0.7 %copy-start.6 = (f32[1,8]{1,0:T(1,128)S(1)}, f32[1,8]{1,0:T(1,128)}, u32[]{:S(2)}) copy-start(f32[1,8]{1,0:T(1,128)} %wavelet.1) | copy-start | bytes 100
  9.0 7.9 %collective-permute-start.2 = (f32[400,128]{1,0:T(8,128)S(1)}, f32[400,128]{1,0:T(8,128)S(1)}, u32[]{:S(2)}, u32[]{:S(2)}) collective-permute-start(f32[400,128]{1,0:T(8,128)S(1)} %get-tuple-element.31), channel_id=1, source_target_pairs={{0,15},{1,2},{2,1},{3,4},{4,3},{5,6},{6,5},{7,8},{8,7},{9,10},{10,... | collective-permute-start | bytes 614408 | tf_op jit(solution)/shard_map/ppermute | solution.py:411
  9.1 7.9 %collective-permute-start.3 = (f32[400,128]{1,0:T(8,128)S(1)}, f32[400,128]{1,0:T(8,128)S(1)}, u32[]{:S(2)}, u32[]{:S(2)}) collective-permute-start(f32[400,128]{1,0:T(8,128)S(1)} %get-tuple-element.32), channel_id=1, source_target_pairs={{0,1},{1,0},{2,3},{3,2},{4,5},{5,4},{6,7},{7,6},{8,9},{9,8},{10,11... | collective-permute-start | bytes 614408 | tf_op jit(solution)/shard_map/ppermute | solution.py:411
  9.1 1.2 %copy-start = (f32[64,32,128]{2,1,0:T(8,128)S(1)}, f32[64,32,128]{2,1,0:T(8,128)}, u32[]{:S(2)}) copy-start(f32[64,32,128]{2,1,0:T(8,128)} %courant.1) | copy-start | bytes 3145732
  10.4 0.9 %copy-start.2 = (f32[16,32,128]{2,1,0:T(8,128)S(1)}, f32[16,32,128]{2,1,0:T(8,128)}, u32[]{:S(2)}) copy-start(f32[16,32,128]{2,1,0:T(8,128)} %now.1) | copy-start | bytes 786436
  11.3 0.7 %copy-start.3 = (f32[16,128]{1,0:T(8,128)S(1)}, f32[16,128]{1,0:T(8,128)}, u32[]{:S(2)}) copy-start(f32[16,128]{1,0:T(8,128)} %observed.1) | copy-start | bytes 24580
  12.0 0.7 %copy-start.4 = (s32[256]{0:T(256)S(1)}, s32[256]{0:T(256)}, u32[]{:S(2)}) copy-start(s32[256]{0:T(256)} %param.13) | copy-start | bytes 3076
  12.7 0.7 %copy-start.5 = (s32[256]{0:T(256)S(1)}, s32[256]{0:T(256)}, u32[]{:S(2)}) copy-start(s32[256]{0:T(256)} %param.14) | copy-start | bytes 3076
  19.9 13.1 %collective-permute-start.5 = (f32[24,32,128]{2,1,0:T(8,128)S(1)}, f32[24,32,128]{2,1,0:T(8,128)S(1)}, u32[]{:S(2)}, u32[]{:S(2)}) collective-permute-start(f32[24,32,128]{2,1,0:T(8,128)S(1)} %get-tuple-element.38), channel_id=1, source_target_pairs={{0,1},{1,0},{2,3},{3,2},{4,5},{5,4},{6,7},{7,6},{8,9},{9,8},{10,11... | collective-permute-start | bytes 1179656 | tf_op jit(solution)/shard_map/ppermute | solution.py:411
  20.0 13.0 %collective-permute-start.4 = (f32[24,32,128]{2,1,0:T(8,128)S(1)}, f32[24,32,128]{2,1,0:T(8,128)S(1)}, u32[]{:S(2)}, u32[]{:S(2)}) collective-permute-start(f32[24,32,128]{2,1,0:T(8,128)S(1)} %get-tuple-element.38), channel_id=1, source_target_pairs={{0,15},{1,2},{2,1},{3,4},{4,3},{5,6},{6,5},{7,8},{8,7},{9,10},{10,... | collective-permute-start | bytes 1179656 | tf_op jit(solution)/shard_map/ppermute | solution.py:411
  36.6 1.2 %collective-permute-start.6 = (f32[16,256]{1,0:T(8,128)S(1)}, f32[16,256]{1,0:T(8,128)S(1)}, u32[]{:S(2)}, u32[]{:S(2)}) collective-permute-start(f32[16,256]{1,0:T(8,128)S(1)} %get-tuple-element.46.adj), channel_id=1, source_target_pairs={{0,1},{1,0},{2,3},{3,2},{4,5},{5,4},{6,7},{7,6},{8,9},{9,8},{10,11... | collective-permute-start | bytes 49160 | tf_op jit(solution)/shard_map/ppermute | solution.py:411
  37.8 6.6 %collective-permute-start.8 = (f32[2,16,256]{2,1,0:T(8,128)S(1)}, f32[2,16,256]{2,1,0:T(8,128)S(1)}, u32[]{:S(2)}, u32[]{:S(2)}) collective-permute-start(f32[2,16,256]{2,1,0:T(8,128)S(1)} %pair.1.refs_6_), channel_id=1, source_target_pairs={{0,14},{1,15},{2,4},{3,5},{4,2},{5,3},{6,8},{7,9},{8,6},{9,7},{10,... | collective-permute-start | bytes 98312 | tf_op jit(solution)/shard_map/ppermute | solution.py:411
  40.1 4.4 %collective-permute-start.7 = (f32[2,16,256]{2,1,0:T(8,128)S(1)}, f32[2,16,256]{2,1,0:T(8,128)S(1)}, u32[]{:S(2)}, u32[]{:S(2)}) collective-permute-start(f32[2,16,256]{2,1,0:T(8,128)S(1)} %pair.1.refs_6_), channel_id=1, source_target_pairs={{0,2},{1,3},{2,0},{3,1},{4,6},{5,7},{6,4},{7,5},{8,10},{9,11},{10,... | collective-permute-start | bytes 98312 | tf_op jit(solution)/shard_map/ppermute | solution.py:411
  49.8 4.5 %collective-permute-start.9 = (f32[4,32,128]{2,1,0:T(8,128)S(1)}, f32[4,32,128]{2,1,0:T(8,128)S(1)}, u32[]{:S(2)}, u32[]{:S(2)}) collective-permute-start(f32[4,32,128]{2,1,0:T(8,128)S(1)} %get-tuple-element.48), channel_id=1, source_target_pairs={{0,4},{1,5},{2,6},{3,7},{4,0},{5,1},{6,2},{7,3},{8,12},{9,13},{10,... | collective-permute-start | bytes 196616 | tf_op jit(solution)/shard_map/ppermute | solution.py:411
  49.9 7.5 %collective-permute-start.10 = (f32[4,32,128]{2,1,0:T(8,128)S(1)}, f32[4,32,128]{2,1,0:T(8,128)S(1)}, u32[]{:S(2)}, u32[]{:S(2)}) collective-permute-start(f32[4,32,128]{2,1,0:T(8,128)S(1)} %get-tuple-element.49), channel_id=1, source_target_pairs={{0,8},{1,9},{2,10},{3,11},{4,12},{5,13},{6,14},{7,15},{8,0},{9,1},... | collective-permute-start | bytes 196616 | tf_op jit(solution)/shard_map/ppermute | solution.py:411
  51.0 6.4 %collective-permute-start.11 = (f32[4,32,128]{2,1,0:T(8,128)S(1)}, f32[4,32,128]{2,1,0:T(8,128)S(1)}, u32[]{:S(2)}, u32[]{:S(2)}) collective-permute-start(f32[4,32,128]{2,1,0:T(8,128)S(1)} %get-tuple-element.50), channel_id=1, source_target_pairs={{0,12},{1,13},{2,14},{3,15},{4,8},{5,9},{6,10},{7,11},{8,4},{9,5},... | collective-permute-start | bytes 196616 | tf_op jit(solution)/shard_map/ppermute | solution.py:411

commit v8 on v7

--- a/solution.py
+++ b/solution.py
@@ -55,7 +55,7 @@
     return lax.dot_general(a, b, dims, preferred_element_type=F32)
 
 
-def advance(cur, old, model, zmat, ymat, first, last, model_shift):
+def advance(cur, old, model, zmat, ymat, first, last, model_shift, extra, keep):
     span_y, span_z = cur.shape[1:]
     zmat, ymat = zmat[...], ymat[...]
     for base in range(first, last, GROUP):
@@ -76,22 +76,19 @@
                 total = part[rows, :span_z] + part[rows, span_z:]
                 for k, weight in enumerate(WEIGHTS, 1):
                     total = total + weight * (tiles[i + RAD + k] + tiles[i + RAD - k])
-                old[x, column] = (here + here - old[x, column]) + model[x + model_shift, column] * total
-
-
-def add_source(field, pack, cell, step, own, block, halo, rows):
-    span_y, span_z = field.shape[1:]
-    plane = own + block * rows + cell // (span_y * span_z)
+                tile = (here + here - old[x, column]) + model[x + model_shift, column] * total + extra(x, column)
+                old[x, column] = tile
+                keep(x, column, tile)
+
+
+def mark_source(mask, cell, block, rows):
+    span_y, span_z = mask.shape[1:]
+    plane = (1 + block) * rows + cell // (span_y * span_z)
     y = (cell // span_z) % span_y
-    z = cell % span_z
-
-    inside = (plane >= own - halo) & (plane < own + rows + halo)
-    plane = jnp.where(inside, plane, own)
     tile = pl.ds(pl.multiple_of((y // 8) * 8, 8), 8)
     sub = lax.broadcasted_iota(jnp.int32, (8, span_z), 0)
     lane = lax.broadcasted_iota(jnp.int32, (8, span_z), 1)
-    hit = (sub == jnp.where(inside, y % 8, 8)) & (lane == z)
-    field[plane, tile, :] = field[plane, tile, :] + jnp.where(hit, pack[step : step + 1], 0.0)
+    mask[plane, tile, :] = jnp.where((sub == y % 8) & (lane == cell % span_z), 1.0, 0.0)
 
 
 def parity():
@@ -168,7 +165,7 @@
 
 
 def forward_round(
-    index, refs_in, zmat, ymat, model, packs, fields, buf_a, buf_b, after_step=None
+    index, refs_in, zmat, ymat, model, packs, fields, buf_a, buf_b, mask, after_step=None
 ):
     steps = ROUNDS[index]
     done = sum(ROUNDS[:index])
@@ -203,15 +200,22 @@
         more = narrow - RAD
         old[pl.ds(jnp.where(odd == 0, low, high), more)] = got_outer[wide:]
         old[pl.ds(jnp.where(odd == 0, high, low), more)] = got_mate[wide:]
-    cells = [jnp.max(packs[block, NT : 2 * NT]).astype(jnp.int32) for block in range(3)]
+    mask[...] = jnp.zeros(mask.shape, F32)
+    for block in (-1, 0, 1):
+        mark_source(mask, jnp.max(packs[block + 1, NT : 2 * NT]).astype(jnp.int32), block, rows)
     for step in range(steps):
         halo = RAD * (steps - 1 - step)
-        advance(cur, old, model, zmat, ymat, own - halo, own + rows + halo, HALO - own)
-        for block in (-1, 0, 1):
-            if halo or block == 0:
-                pack = packs.at[block + 1]
-                add_source(old, pack, cells[block + 1], done + step, own, block, halo, rows)
-        fields[step] = old[own : own + rows]
+        amounts = [jnp.broadcast_to(packs[i, done + step : done + step + 1], (8, shape[1])) for i in range(3)]
+
+        def extra(x, column):
+            place = x - own + rows
+            return mask[place, column] * amounts[place // rows]
+
+        def keep(x, column, tile):
+            if own <= x < own + rows:
+                fields[step, x - own, column] = tile
+
+        advance(cur, old, model, zmat, ymat, own - halo, own + rows + halo, HALO - own, extra, keep)
         if after_step:
             after_step(step, old[own : own + rows])
         cur, old = old, cur
@@ -230,11 +234,11 @@
     refs_in, refs = refs[:take], refs[take:]
     zmat, ymat, model, pack, fields, known, send = refs[:7]
     if index == 0:
-        packs, buf_a, buf_b = refs[7:]
+        packs, buf_a, buf_b, mask = refs[7:]
         gather_packs(pack, refs_in[4], refs_in[5], packs)
     else:
-        packs, (buf_a, buf_b) = pack, refs[7:]
-    cur, old, own = forward_round(index, refs_in, zmat, ymat, model, packs, fields, buf_a, buf_b)
+        packs, (buf_a, buf_b, mask) = pack, refs[7:]
+    cur, old, own = forward_round(index, refs_in, zmat, ymat, model, packs, fields, buf_a, buf_b, mask)
     rows = 16
     known[0] = old[own - RAD : own]
     known[1] = old[own + rows : own + rows + RAD]
@@ -286,14 +290,14 @@
     take = 6 if index == 0 else 4
     refs_in, refs = refs[:take], refs[take:]
     zmat, ymat, model, packs, cells, rows_table, lane_table, traces = refs[:8]
-    fields, adj, buf_a, buf_b = refs[8:]
+    fields, adj, buf_a, buf_b, mask = refs[8:]
     done = sum(ROUNDS[:index])
     total = [traces[...]]
 
     def pick(step, field):
         total[0] = total[0] + extract(field, done + step, rows_table[...], lane_table[...])[:NT]
 
-    forward_round(index, refs_in, zmat, ymat, model, packs, fields, buf_a, buf_b, pick)
+    forward_round(index, refs_in, zmat, ymat, model, packs, fields, buf_a, buf_b, mask, pick)
     adj[0:NT] = total[0]
     adj[NT:] = cells[...]
 
@@ -340,7 +344,7 @@
     refs = refs[field_groups:]
     zmat, ymat, model, sources, own_pair, even_pair, odd_pair = refs[:7]
     outs = refs[7 : 7 + slabs]
-    buf_a, buf_b, image, rows_table, adjs, near = refs[7 + slabs :]
+    buf_a, buf_b, planes, image, rows_table, adjs, near = refs[7 + slabs :]
     odd = parity()
     odd_chip = lax.rem(lax.axis_index("shot") // 2, 2)
     near[2:4] = own_pair[...]
@@ -357,35 +361,37 @@
         rows_table[block + 2] = injection_table(cells, table_rows, span_z)
         lanes[block] = injection_lanes(cells, span_z)
 
-    def inject(field, number):
+    def place_sources(number, out):
         halo = RAD * (NT - number)
         step = NT - number
-        for block in range(-2, 3):
+        for block in (-2, -1, 1, 2):
             begin = own + block * rows
             first = max(begin, own - halo)
             last = min(begin + rows, own + rows + halo)
             if first >= last:
                 continue
-            if block:
-                table = rows_table[block + 2, (first - begin) * span_y : (last - begin) * span_y, :]
-                added = source_planes(table, lanes[block], adjs[block + 2, step : step + 1], span_z)
-                added = added.reshape(last - first, span_y, span_z)
-            else:
-                added = sources[step]
-            if number == 1:
-                field[first:last] = added
-            else:
-                field[first:last] = field[first:last] + added
+            table = rows_table[block + 2, (first - begin) * span_y : (last - begin) * span_y, :]
+            added = source_planes(table, lanes[block], adjs[block + 2, step : step + 1], span_z)
+            out[first:last] = added.reshape(last - first, span_y, span_z)
 
     cur, old = buf_a, buf_b
-    inject(cur, 1)
+    place_sources(1, cur)
+    cur[own : own + rows] = sources[NT - 1]
     old[...] = jnp.zeros(old.shape, F32)
-    image[...] = cur[own : own + rows] * fields[NT - 1][...]
+    image[...] = sources[NT - 1] * fields[NT - 1][...]
     for number in range(2, NT + 1):
         halo = RAD * (NT - number)
-        advance(cur, old, model, zmat, ymat, own - halo, own + rows + halo, 0)
-        inject(old, number)
-        image[...] = image[...] + old[own : own + rows] * fields[NT - number][...]
+        step = NT - number
+        place_sources(number, planes)
+
+        def extra(x, column):
+            return sources[step, x - own, column] if own <= x < own + rows else planes[x, column]
+
+        def keep(x, column, tile):
+            if own <= x < own + rows:
+                image[x - own, column] = image[x - own, column] + tile * fields[step][x - own, column]
+
+        advance(cur, old, model, zmat, ymat, own - halo, own + rows + halo, 0, extra, keep)
         cur, old = old, cur
     mine = lax.axis_index("shot") // PIECES
     thick = rows // slabs
@@ -479,7 +485,7 @@
             )
             + packs,
             ins + common + (pack,),
-            scratch=[pltpu.VMEM((window,) + plane, F32)] * 2,
+            scratch=[pltpu.VMEM((window,) + plane, F32)] * 2 + [pltpu.VMEM((3 * rows,) + plane, F32)],
             name="forward",
         )
         field_list.append(fields)
@@ -505,7 +511,7 @@
             jax.ShapeDtypeStruct((2 * NT, count), F32),
         ),
         ins + common + (pack, cells, rows_table, lane_table, traces),
-        scratch=[pltpu.VMEM((window,) + plane, F32)] * 2,
+        scratch=[pltpu.VMEM((window,) + plane, F32)] * 2 + [pltpu.VMEM((3 * rows,) + plane, F32)],
         name="forward_last",
     )
     field_list.append(fields)
@@ -523,7 +529,7 @@
         functools.partial(adjoint_kernel, len(field_list), slabs),
         tuple(jax.ShapeDtypeStruct((thick,) + plane, F32) for _ in range(slabs)),
         (*field_list, zmat, ymat, model, *adjs),
-        scratch=[pltpu.VMEM((rows + 2 * HALO,) + plane, F32)] * 2
+        scratch=[pltpu.VMEM((rows + 2 * HALO,) + plane, F32)] * 3
         + [pltpu.VMEM((rows,) + plane, F32), pltpu.VMEM((5, table_rows, count), BF)]
         + [pltpu.VMEM((5, 2 * NT, count), F32), pltpu.VMEM((6, 2 * NT, count), F32)],
         name="adjoint",

time: 58.3 us -> 57.2 us (0.981)
  Pallas kernels: 14.7 us -> 13.5 us
    pallas_call x8, Pallas kernels: 14.7 us -> 13.5 us  [call(): pl.pallas_call(kernel, out_shape=outs, in_specs=specs or [VMEM] * len(ins...]
where the time goes in v8:
time: 57.2 us; the launch traced here: 56.8 us
  starting transfers between devices  16 us (28%)
  Pallas kernels  13.5 us (24%)
  waiting for transfers between devices  10.8 us (19%)
  blocking collectives  9.23 us (16%)
  local copies, waits for them, and re-layouts  5.82 us (10%)
  between operations  0.76 us (1%)
  other arithmetic  0.65 us (1%)
    ppermute x12, starting transfers between devices, swapped(): lax.ppermute(value, 'shot', [(d, partner(d) % count) for d in range(count)])  16 us
    pallas_call x8, Pallas kernels, call(): pl.pallas_call(kernel, out_shape=outs, in_specs=specs or [VMEM] * len(ins...  13.5 us
    ppermute x12, waiting for transfers between devices, swapped(): lax.ppermute(value, 'shot', [(d, partner(d) % count) for d in range(count)])  10.8 us
    all_to_all x1, blocking collectives, per_device(): lax.all_to_all(observed, 'shot', split_axis=0, concat_axis=0, tiled=True)  9.23 us
    unnamed x14, local copies, waits for them, and re-layouts  5.82 us
  transfers between devices with their start and end apart: 12, of which 4 were waited for; matrix products, arithmetic and copies ran while one was open for 0% of the time, Pallas kernels for 5%

profile of v8, /device:TPU:0, one launch (start us, length us, event | category | flops | bytes accessed | tf_op | source)
XLA Modules:
  0.0 56.8 jit_solution(5312377134647914011)
XLA Ops:
  0.0 0.5 collective-permute-start.1
  0.5 5.7 %collective-permute-start = (f32[16,32,128]{2,1,0:T(8,128)}, f32[16,32,128]{2,1,0:T(8,128)S(1)}, u32[]{:S(2)}, u32[]{:S(2)}) collective-permute-start(f32[16,32,128]{2,1,0:T(8,128)} %now.1), channel_id=1, source_target_pairs={{0,15},{1,2},{2,1},{3,4},{4,3},{5,6},{6,5},{7,8},{8,7},{9,10},{10,... | collective-permute-start | bytes 786440 | tf_op jit(solution)/shard_map/ppermute | solution.py:417
  6.8 0.9 %copy-done.1 = f32[16,32,128]{2,1,0:T(8,128)S(1)} copy-done((f32[16,32,128]{2,1,0:T(8,128)S(1)}, f32[16,32,128]{2,1,0:T(8,128)}, u32[]{:S(2)}) %copy-start.1) | copy-done | bytes 262168
  7.7 0.7 %copy-done.6 = f32[1,8]{1,0:T(1,128)S(1)} copy-done((f32[1,8]{1,0:T(1,128)S(1)}, f32[1,8]{1,0:T(1,128)}, u32[]{:S(2)}) %copy-start.6) | copy-done | bytes 56
  8.4 0.6 %message.1 = (f32[400,128]{1,0:T(8,128)S(1)}, f32[400,128]{1,0:T(8,128)S(1)}, f32[16,128]{1,0:T(8,128)S(1)}, f32[16,32,128]{2,1,0:T(8,128)S(1)}) custom-call(f32[16,32,128]{2,1,0:T(8,128)S(1)} %copy-done.1, f32[1,8]{1,0:T(1,128)S(1)} %copy-done.6, s32[1]{0:T(128)S(6)} %copy.10.source), custom_call_target="tpu_custom_call" | custom-call | flops 1000000 | bytes 1000000 | tf_op jit(solution)/shard_map/message/pallas_call | solution.py:403
  9.0 0.1 collective-permute-start.2
  9.1 0.1 collective-permute-start.3
  9.1 0.0 copy-start
  9.1 1.2 %copy-done = f32[64,32,128]{2,1,0:T(8,128)S(1)} copy-done((f32[64,32,128]{2,1,0:T(8,128)S(1)}, f32[64,32,128]{2,1,0:T(8,128)}, u32[]{:S(2)}) %copy-start) | copy-done | bytes 1048600
  10.4 0.9 %copy-done.2 = f32[16,32,128]{2,1,0:T(8,128)S(1)} copy-done((f32[16,32,128]{2,1,0:T(8,128)S(1)}, f32[16,32,128]{2,1,0:T(8,128)}, u32[]{:S(2)}) %copy-start.2) | copy-done | bytes 262168
  11.3 0.7 %copy-done.3 = f32[16,128]{1,0:T(8,128)S(1)} copy-done((f32[16,128]{1,0:T(8,128)S(1)}, f32[16,128]{1,0:T(8,128)}, u32[]{:S(2)}) %copy-start.3) | copy-done | bytes 8216
  12.0 0.7 %copy-done.4 = s32[256]{0:T(256)S(1)} copy-done((s32[256]{0:T(256)S(1)}, s32[256]{0:T(256)}, u32[]{:S(2)}) %copy-start.4) | copy-done | bytes 1048
  12.7 0.7 %copy-done.5 = s32[256]{0:T(256)S(1)} copy-done((s32[256]{0:T(256)S(1)}, s32[256]{0:T(256)}, u32[]{:S(2)}) %copy-start.5) | copy-done | bytes 1048
  13.4 0.6 prepare.1
  13.9 3.0 %collective-permute-done.2.refs_4_ = f32[400,128]{1,0:T(8,128)S(1)} collective-permute-done((f32[400,128]{1,0:T(8,128)S(1)}, f32[400,128]{1,0:T(8,128)S(1)}, u32[]{:S(2)}, u32[]{:S(2)}) %collective-permute-start.2) | collective-permute-done | bytes 204832 | tf_op jit(solution)/shard_map/ppermute | solution.py:417
  16.9 2.3 %forward.1 = (f32[4,16,32,128]{3,2,1,0:T(8,128)S(1)}, f32[2,4,32,128]{3,2,1,0:T(8,128)S(1)}, f32[24,32,128]{2,1,0:T(8,128)S(1)}, f32[3,16,128]{2,1,0:T(8,128)S(1)}) custom-call(f32[16,32,128]{2,1,0:T(8,128)S(1)} %get-tuple-element.29.refs_0_, f32[16,32,128]{2,1,0:T(8,128)S(1)} %get-tuple-element.30.refs_1_, f32[16,32,128]{2,1,0:T(8,128)S(1)} %collective-permute-done.refs_2_, ...), custom_call_target="tpu_custom_call" | custom-call | flops 1000000 | bytes 1000000 | tf_op jit(solution)/shard_map/forward/pallas_call | solution.py:403
  19.2 0.1 collective-permute-start.5
  19.3 2.9 %collective-permute-start.4 = (f32[24,32,128]{2,1,0:T(8,128)S(1)}, f32[24,32,128]{2,1,0:T(8,128)S(1)}, u32[]{:S(2)}, u32[]{:S(2)}) collective-permute-start(f32[24,32,128]{2,1,0:T(8,128)S(1)} %get-tuple-element.38), channel_id=1, source_target_pairs={{0,15},{1,2},{2,1},{3,4},{4,3},{5,6},{6,5},{7,8},{8,7},{9,10},{10,... | collective-permute-start | bytes 1179656 | tf_op jit(solution)/shard_map/ppermute | solution.py:417
  22.2 9.2 %all_to_all.11 = f32[16,1,128]{2,1,0:T(1,128)S(1)} all-to-all(f32[16,1,128]{2,1,0:T(1,128)S(1)} %bitcast.7), channel_id=1, replica_groups=mesh['groups'=2,'shot'=16] {'shot'}, dimensions={0} | all-to-all | bytes 16384 | tf_op jit(solution)/shard_map/all_to_all | solution.py:470
  31.4 0.8 %traces.1 = (bf16[256,512]{1,0:T(8,128)(2,1)S(1)}, f32[256,256]{1,0:T(8,128)S(1)}, f32[8,256]{1,0:T(8,128)S(1)}) custom-call(f32[8,256]{1,0:T(8,128)S(1)} %get-tuple-element.40.refs_0_.refs_8_, f32[16,128]{1,0:T(8,128)S(1)} %bitcast.6, f32[4,16,32,128]{3,2,1,0:T(8,128)S(1)} %get-tuple-element.36.refs_2_.refs_0_), custom_call_target="tpu_custom_call" | custom-call | flops 1000000 | bytes 1000000 | tf_op jit(solution)/shard_map/traces/pallas_call | solution.py:403
  32.3 3.3 %forward_last.1 = (f32[4,16,32,128]{3,2,1,0:T(8,128)S(1)}, f32[16,256]{1,0:T(8,128)S(1)}) custom-call(f32[4,16,32,128]{3,2,1,0:T(8,128)S(1)} %get-tuple-element.36.refs_2_.refs_0_, f32[2,4,32,128]{3,2,1,0:T(8,128)S(1)} %get-tuple-element.37.refs_1_, f32[24,32,128]{2,1,0:T(8,128)S(1)} %collective-permute-done.4.refs_2_, ...), custom_call_target="tpu_custom_call" | custom-call | flops 1000000 | bytes 1000000 | tf_op jit(solution)/shard_map/forward_last/pallas_call | solution.py:403
  35.6 0.1 collective-permute-start.6
  35.6 1.1 %collective-permute-done.6.mate = f32[16,256]{1,0:T(8,128)S(1)} collective-permute-done((f32[16,256]{1,0:T(8,128)S(1)}, f32[16,256]{1,0:T(8,128)S(1)}, u32[]{:S(2)}, u32[]{:S(2)}) %collective-permute-start.6) | collective-permute-done | bytes 16416 | tf_op jit(solution)/shard_map/ppermute | solution.py:417
  36.8 2.3 %collective-permute-start.8 = (f32[2,16,256]{2,1,0:T(8,128)S(1)}, f32[2,16,256]{2,1,0:T(8,128)S(1)}, u32[]{:S(2)}, u32[]{:S(2)}) collective-permute-start(f32[2,16,256]{2,1,0:T(8,128)S(1)} %pair.1.refs_6_), channel_id=1, source_target_pairs={{0,14},{1,15},{2,4},{3,5},{4,2},{5,3},{6,8},{7,9},{8,6},{9,7},{10,... | collective-permute-start | bytes 98312 | tf_op jit(solution)/shard_map/ppermute | solution.py:417
  39.0 0.8 %own_sources.1.refs_5_ = f32[8,16,32,128]{3,2,1,0:T(8,128)S(1)} custom-call(f32[16,256]{1,0:T(8,128)S(1)} %get-tuple-element.46.adj), custom_call_target="tpu_custom_call" | custom-call | flops 1000000 | bytes 1000000 | tf_op jit(solution)/shard_map/own_sources/pallas_call | solution.py:403
  39.8 3.6 %collective-permute-done.8.refs_8_ = f32[2,16,256]{2,1,0:T(8,128)S(1)} collective-permute-done((f32[2,16,256]{2,1,0:T(8,128)S(1)}, f32[2,16,256]{2,1,0:T(8,128)S(1)}, u32[]{:S(2)}, u32[]{:S(2)}) %collective-permute-start.8) | collective-permute-done | bytes 32800 | tf_op jit(solution)/shard_map/ppermute | solution.py:417
  43.4 5.2 %adjoint.1 = (f32[4,32,128]{2,1,0:T(8,128)S(1)}, f32[4,32,128]{2,1,0:T(8,128)S(1)}, f32[4,32,128]{2,1,0:T(8,128)S(1)}, f32[4,32,128]{2,1,0:T(8,128)S(1)}) custom-call(f32[4,16,32,128]{3,2,1,0:T(8,128)S(1)} %get-tuple-element.36.refs_2_.refs_0_, f32[4,16,32,128]{3,2,1,0:T(8,128)S(1)} %get-tuple-element.45.refs_1_, ...), custom_call_target="tpu_custom_call" | custom-call | flops 1000000 | bytes 1000000 | tf_op jit(solution)/shard_map/adjoint/pallas_call | solution.py:403
  48.6 0.1 collective-permute-start.9
  48.7 1.1 %collective-permute-start.10 = (f32[4,32,128]{2,1,0:T(8,128)S(1)}, f32[4,32,128]{2,1,0:T(8,128)S(1)}, u32[]{:S(2)}, u32[]{:S(2)}) collective-permute-start(f32[4,32,128]{2,1,0:T(8,128)S(1)} %get-tuple-element.49), channel_id=1, source_target_pairs={{0,8},{1,9},{2,10},{3,11},{4,12},{5,13},{6,14},{7,15},{8,0},{9,1},... | collective-permute-start | bytes 196616 | tf_op jit(solution)/shard_map/ppermute | solution.py:417
  49.8 3.3 %collective-permute-start.11 = (f32[4,32,128]{2,1,0:T(8,128)S(1)}, f32[4,32,128]{2,1,0:T(8,128)S(1)}, u32[]{:S(2)}, u32[]{:S(2)}) collective-permute-start(f32[4,32,128]{2,1,0:T(8,128)S(1)} %get-tuple-element.50), channel_id=1, source_target_pairs={{0,12},{1,13},{2,14},{3,15},{4,8},{5,9},{6,10},{7,11},{8,4},{9,5},... | collective-permute-start | bytes 196616 | tf_op jit(solution)/shard_map/ppermute | solution.py:417
  53.1 3.1 %collective-permute-done.10 = f32[4,32,128]{2,1,0:T(8,128)S(1)} collective-permute-done((f32[4,32,128]{2,1,0:T(8,128)S(1)}, f32[4,32,128]{2,1,0:T(8,128)S(1)}, u32[]{:S(2)}, u32[]{:S(2)}) %collective-permute-start.10) | collective-permute-done | bytes 65568 | tf_op jit(solution)/shard_map/ppermute | solution.py:417
  56.2 0.6 %add_add_fusion = f32[4,32,128]{2,1,0:T(8,128)} fusion(f32[4,32,128]{2,1,0:T(8,128)S(1)} %collective-permute-done.11, f32[4,32,128]{2,1,0:T(8,128)S(1)} %collective-permute-done.10, f32[4,32,128]{2,1,0:T(8,128)S(1)} %get-tuple-element.47, f32[4,32,128]{2,1,0:T(8,128)S(1)} %collective-permute-done.9), kind=kLoop, calls=%fused_computation | loop fusion | flops 49152 | bytes 327680 | tf_op jit(solution)/shard_map/add | solution.py:539
  (16 shorter events, 0.0 us)
Async XLA Ops:
  0.0 16.9 %collective-permute-start.1 = (f32[16,32,128]{2,1,0:T(8,128)}, f32[16,32,128]{2,1,0:T(8,128)S(1)}, u32[]{:S(2)}, u32[]{:S(2)}) collective-permute-start(f32[16,32,128]{2,1,0:T(8,128)} %now.1), channel_id=1, source_target_pairs={{0,1},{1,0},{2,3},{3,2},{4,5},{5,4},{6,7},{7,6},{8,9},{9,8},{10,11... | collective-permute-start | bytes 786440 | tf_op jit(solution)/shard_map/ppermute | solution.py:417
  0.5 16.5 %collective-permute-start = (f32[16,32,128]{2,1,0:T(8,128)}, f32[16,32,128]{2,1,0:T(8,128)S(1)}, u32[]{:S(2)}, u32[]{:S(2)}) collective-permute-start(f32[16,32,128]{2,1,0:T(8,128)} %now.1), channel_id=1, source_target_pairs={{0,15},{1,2},{2,1},{3,4},{4,3},{5,6},{6,5},{7,8},{8,7},{9,10},{10,... | collective-permute-start | bytes 786440 | tf_op jit(solution)/shard_map/ppermute | solution.py:417
  6.8 1.0 %copy-start.1 = (f32[16,32,128]{2,1,0:T(8,128)S(1)}, f32[16,32,128]{2,1,0:T(8,128)}, u32[]{:S(2)}) copy-start(f32[16,32,128]{2,1,0:T(8,128)} %before.1) | copy-start | bytes 786436
  7.7 0.7 %copy-start.6 = (f32[1,8]{1,0:T(1,128)S(1)}, f32[1,8]{1,0:T(1,128)}, u32[]{:S(2)}) copy-start(f32[1,8]{1,0:T(1,128)} %wavelet.1) | copy-start | bytes 100
  9.0 7.9 %collective-permute-start.2 = (f32[400,128]{1,0:T(8,128)S(1)}, f32[400,128]{1,0:T(8,128)S(1)}, u32[]{:S(2)}, u32[]{:S(2)}) collective-permute-start(f32[400,128]{1,0:T(8,128)S(1)} %get-tuple-element.31), channel_id=1, source_target_pairs={{0,15},{1,2},{2,1},{3,4},{4,3},{5,6},{6,5},{7,8},{8,7},{9,10},{10,... | collective-permute-start | bytes 614408 | tf_op jit(solution)/shard_map/ppermute | solution.py:417
  9.1 7.9 %collective-permute-start.3 = (f32[400,128]{1,0:T(8,128)S(1)}, f32[400,128]{1,0:T(8,128)S(1)}, u32[]{:S(2)}, u32[]{:S(2)}) collective-permute-start(f32[400,128]{1,0:T(8,128)S(1)} %get-tuple-element.32), channel_id=1, source_target_pairs={{0,1},{1,0},{2,3},{3,2},{4,5},{5,4},{6,7},{7,6},{8,9},{9,8},{10,11... | collective-permute-start | bytes 614408 | tf_op jit(solution)/shard_map/ppermute | solution.py:417
  9.1 1.2 %copy-start = (f32[64,32,128]{2,1,0:T(8,128)S(1)}, f32[64,32,128]{2,1,0:T(8,128)}, u32[]{:S(2)}) copy-start(f32[64,32,128]{2,1,0:T(8,128)} %courant.1) | copy-start | bytes 3145732
  10.4 0.9 %copy-start.2 = (f32[16,32,128]{2,1,0:T(8,128)S(1)}, f32[16,32,128]{2,1,0:T(8,128)}, u32[]{:S(2)}) copy-start(f32[16,32,128]{2,1,0:T(8,128)} %now.1) | copy-start | bytes 786436
  11.3 0.7 %copy-start.3 = (f32[16,128]{1,0:T(8,128)S(1)}, f32[16,128]{1,0:T(8,128)}, u32[]{:S(2)}) copy-start(f32[16,128]{1,0:T(8,128)} %observed.1) | copy-start | bytes 24580
  12.0 0.7 %copy-start.4 = (s32[256]{0:T(256)S(1)}, s32[256]{0:T(256)}, u32[]{:S(2)}) copy-start(s32[256]{0:T(256)} %param.13) | copy-start | bytes 3076
  12.7 0.7 %copy-start.5 = (s32[256]{0:T(256)S(1)}, s32[256]{0:T(256)}, u32[]{:S(2)}) copy-start(s32[256]{0:T(256)} %param.14) | copy-start | bytes 3076
  19.2 13.1 %collective-permute-start.5 = (f32[24,32,128]{2,1,0:T(8,128)S(1)}, f32[24,32,128]{2,1,0:T(8,128)S(1)}, u32[]{:S(2)}, u32[]{:S(2)}) collective-permute-start(f32[24,32,128]{2,1,0:T(8,128)S(1)} %get-tuple-element.38), channel_id=1, source_target_pairs={{0,1},{1,0},{2,3},{3,2},{4,5},{5,4},{6,7},{7,6},{8,9},{9,8},{10,11... | collective-permute-start | bytes 1179656 | tf_op jit(solution)/shard_map/ppermute | solution.py:417
  19.3 13.0 %collective-permute-start.4 = (f32[24,32,128]{2,1,0:T(8,128)S(1)}, f32[24,32,128]{2,1,0:T(8,128)S(1)}, u32[]{:S(2)}, u32[]{:S(2)}) collective-permute-start(f32[24,32,128]{2,1,0:T(8,128)S(1)} %get-tuple-element.38), channel_id=1, source_target_pairs={{0,15},{1,2},{2,1},{3,4},{4,3},{5,6},{6,5},{7,8},{8,7},{9,10},{10,... | collective-permute-start | bytes 1179656 | tf_op jit(solution)/shard_map/ppermute | solution.py:417
  35.6 1.2 %collective-permute-start.6 = (f32[16,256]{1,0:T(8,128)S(1)}, f32[16,256]{1,0:T(8,128)S(1)}, u32[]{:S(2)}, u32[]{:S(2)}) collective-permute-start(f32[16,256]{1,0:T(8,128)S(1)} %get-tuple-element.46.adj), channel_id=1, source_target_pairs={{0,1},{1,0},{2,3},{3,2},{4,5},{5,4},{6,7},{7,6},{8,9},{9,8},{10,11... | collective-permute-start | bytes 49160 | tf_op jit(solution)/shard_map/ppermute | solution.py:417
  36.8 6.6 %collective-permute-start.8 = (f32[2,16,256]{2,1,0:T(8,128)S(1)}, f32[2,16,256]{2,1,0:T(8,128)S(1)}, u32[]{:S(2)}, u32[]{:S(2)}) collective-permute-start(f32[2,16,256]{2,1,0:T(8,128)S(1)} %pair.1.refs_6_), channel_id=1, source_target_pairs={{0,14},{1,15},{2,4},{3,5},{4,2},{5,3},{6,8},{7,9},{8,6},{9,7},{10,... | collective-permute-start | bytes 98312 | tf_op jit(solution)/shard_map/ppermute | solution.py:417
  39.0 4.3 %collective-permute-start.7 = (f32[2,16,256]{2,1,0:T(8,128)S(1)}, f32[2,16,256]{2,1,0:T(8,128)S(1)}, u32[]{:S(2)}, u32[]{:S(2)}) collective-permute-start(f32[2,16,256]{2,1,0:T(8,128)S(1)} %pair.1.refs_6_), channel_id=1, source_target_pairs={{0,2},{1,3},{2,0},{3,1},{4,6},{5,7},{6,4},{7,5},{8,10},{9,11},{10,... | collective-permute-start | bytes 98312 | tf_op jit(solution)/shard_map/ppermute | solution.py:417
  48.6 4.5 %collective-permute-start.9 = (f32[4,32,128]{2,1,0:T(8,128)S(1)}, f32[4,32,128]{2,1,0:T(8,128)S(1)}, u32[]{:S(2)}, u32[]{:S(2)}) collective-permute-start(f32[4,32,128]{2,1,0:T(8,128)S(1)} %get-tuple-element.48), channel_id=1, source_target_pairs={{0,4},{1,5},{2,6},{3,7},{4,0},{5,1},{6,2},{7,3},{8,12},{9,13},{10,... | collective-permute-start | bytes 196616 | tf_op jit(solution)/shard_map/ppermute | solution.py:417
  48.7 7.5 %collective-permute-start.10 = (f32[4,32,128]{2,1,0:T(8,128)S(1)}, f32[4,32,128]{2,1,0:T(8,128)S(1)}, u32[]{:S(2)}, u32[]{:S(2)}) collective-permute-start(f32[4,32,128]{2,1,0:T(8,128)S(1)} %get-tuple-element.49), channel_id=1, source_target_pairs={{0,8},{1,9},{2,10},{3,11},{4,12},{5,13},{6,14},{7,15},{8,0},{9,1},... | collective-permute-start | bytes 196616 | tf_op jit(solution)/shard_map/ppermute | solution.py:417
  49.8 6.4 %collective-permute-start.11 = (f32[4,32,128]{2,1,0:T(8,128)S(1)}, f32[4,32,128]{2,1,0:T(8,128)S(1)}, u32[]{:S(2)}, u32[]{:S(2)}) collective-permute-start(f32[4,32,128]{2,1,0:T(8,128)S(1)} %get-tuple-element.50), channel_id=1, source_target_pairs={{0,12},{1,13},{2,14},{3,15},{4,8},{5,9},{6,10},{7,11},{8,4},{9,5},... | collective-permute-start | bytes 196616 | tf_op jit(solution)/shard_map/ppermute | solution.py:417

commit v9 on v8

--- a/solution.py
+++ b/solution.py
@@ -38,8 +38,10 @@
     tile = 8 * GROUP
     y_row = row // tile * 8 + row % 8
     y_col = col // tile * 8 + col % 8
-    same = (row // 8) % GROUP == (col // 8) % GROUP
-    rows_out[...] = jnp.where(same, band(y_row - y_col, CENTER_Y), 0.0).astype(BF)
+    x_far = (row // 8) % GROUP - (col // 8) % GROUP
+    y_far = y_row - y_col
+    across = jnp.where(y_far == 0, band(x_far, 0.0), 0.0)
+    rows_out[...] = jnp.where(x_far == 0, band(y_far, CENTER_Y), across).astype(BF)
     z = lax.broadcasted_iota(jnp.int32, (2 * span_z, 2 * span_z), 0) % span_z
     to = lax.broadcasted_iota(jnp.int32, (2 * span_z, 2 * span_z), 1)
     fixed_out[...] = jnp.where(to < span_z, band(z - to, CENTER_Z), 0.0).astype(BF)
@@ -75,7 +77,10 @@
                 here = tiles[i + RAD]
                 total = part[rows, :span_z] + part[rows, span_z:]
                 for k, weight in enumerate(WEIGHTS, 1):
-                    total = total + weight * (tiles[i + RAD + k] + tiles[i + RAD - k])
+                    if i + k >= GROUP:
+                        total = total + weight * tiles[i + RAD + k]
+                    if i < k:
+                        total = total + weight * tiles[i + RAD - k]
                 tile = (here + here - old[x, column]) + model[x + model_shift, column] * total + extra(x, column)
                 old[x, column] = tile
                 keep(x, column, tile)

time: 57.2 us -> 55.9 us (0.977)
  Pallas kernels: 13.5 us -> 12.3 us
    pallas_call x8, Pallas kernels: 13.5 us -> 12.3 us  [call(): pl.pallas_call(kernel, out_shape=outs, in_specs=specs or [VMEM] * len(ins...]
where the time goes in v9:
time: 55.9 us; the launch traced here: 55.5 us
  starting transfers between devices  16 us (29%)
  Pallas kernels  12.3 us (22%)
  waiting for transfers between devices  10.7 us (19%)
  blocking collectives  9.23 us (17%)
  local copies, waits for them, and re-layouts  5.82 us (10%)
  between operations  0.76 us (1%)
  other arithmetic  0.65 us (1%)
    ppermute x12, starting transfers between devices, swapped(): lax.ppermute(value, 'shot', [(d, partner(d) % count) for d in range(count)])  16 us
    pallas_call x8, Pallas kernels, call(): pl.pallas_call(kernel, out_shape=outs, in_specs=specs or [VMEM] * len(ins...  12.3 us
    ppermute x12, waiting for transfers between devices, swapped(): lax.ppermute(value, 'shot', [(d, partner(d) % count) for d in range(count)])  10.7 us
    all_to_all x1, blocking collectives, per_device(): lax.all_to_all(observed, 'shot', split_axis=0, concat_axis=0, tiled=True)  9.23 us
    unnamed x14, local copies, waits for them, and re-layouts  5.82 us
  transfers between devices with their start and end apart: 12, of which 4 were waited for; matrix products, arithmetic and copies ran while one was open for 0% of the time, Pallas kernels for 5%

profile of v9, /device:TPU:0, one launch (start us, length us, event | category | flops | bytes accessed | tf_op | source)
XLA Modules:
  0.0 55.5 jit_solution(10095688232488747360)
XLA Ops:
  0.0 0.5 collective-permute-start.1
  0.5 5.7 %collective-permute-start = (f32[16,32,128]{2,1,0:T(8,128)}, f32[16,32,128]{2,1,0:T(8,128)S(1)}, u32[]{:S(2)}, u32[]{:S(2)}) collective-permute-start(f32[16,32,128]{2,1,0:T(8,128)} %now.1), channel_id=1, source_target_pairs={{0,15},{1,2},{2,1},{3,4},{4,3},{5,6},{6,5},{7,8},{8,7},{9,10},{10,... | collective-permute-start | bytes 786440 | tf_op jit(solution)/shard_map/ppermute | solution.py:422
  6.8 0.9 %copy-done.1 = f32[16,32,128]{2,1,0:T(8,128)S(1)} copy-done((f32[16,32,128]{2,1,0:T(8,128)S(1)}, f32[16,32,128]{2,1,0:T(8,128)}, u32[]{:S(2)}) %copy-start.1) | copy-done | bytes 262168
  7.7 0.7 %copy-done.6 = f32[1,8]{1,0:T(1,128)S(1)} copy-done((f32[1,8]{1,0:T(1,128)S(1)}, f32[1,8]{1,0:T(1,128)}, u32[]{:S(2)}) %copy-start.6) | copy-done | bytes 56
  8.4 0.6 %message.1 = (f32[400,128]{1,0:T(8,128)S(1)}, f32[400,128]{1,0:T(8,128)S(1)}, f32[16,128]{1,0:T(8,128)S(1)}, f32[16,32,128]{2,1,0:T(8,128)S(1)}) custom-call(f32[16,32,128]{2,1,0:T(8,128)S(1)} %copy-done.1, f32[1,8]{1,0:T(1,128)S(1)} %copy-done.6, s32[1]{0:T(128)S(6)} %copy.10.source), custom_call_target="tpu_custom_call" | custom-call | flops 1000000 | bytes 1000000 | tf_op jit(solution)/shard_map/message/pallas_call | solution.py:408
  9.0 0.1 collective-permute-start.2
  9.1 0.1 collective-permute-start.3
  9.1 0.0 copy-start
  9.1 1.2 %copy-done = f32[64,32,128]{2,1,0:T(8,128)S(1)} copy-done((f32[64,32,128]{2,1,0:T(8,128)S(1)}, f32[64,32,128]{2,1,0:T(8,128)}, u32[]{:S(2)}) %copy-start) | copy-done | bytes 1048600
  10.4 0.9 %copy-done.2 = f32[16,32,128]{2,1,0:T(8,128)S(1)} copy-done((f32[16,32,128]{2,1,0:T(8,128)S(1)}, f32[16,32,128]{2,1,0:T(8,128)}, u32[]{:S(2)}) %copy-start.2) | copy-done | bytes 262168
  11.3 0.7 %copy-done.3 = f32[16,128]{1,0:T(8,128)S(1)} copy-done((f32[16,128]{1,0:T(8,128)S(1)}, f32[16,128]{1,0:T(8,128)}, u32[]{:S(2)}) %copy-start.3) | copy-done | bytes 8216
  12.0 0.7 %copy-done.4 = s32[256]{0:T(256)S(1)} copy-done((s32[256]{0:T(256)S(1)}, s32[256]{0:T(256)}, u32[]{:S(2)}) %copy-start.4) | copy-done | bytes 1048
  12.7 0.7 %copy-done.5 = s32[256]{0:T(256)S(1)} copy-done((s32[256]{0:T(256)S(1)}, s32[256]{0:T(256)}, u32[]{:S(2)}) %copy-start.5) | copy-done | bytes 1048
  13.4 0.7 %prepare.1 = (f32[72,32,128]{2,1,0:T(8,128)S(1)}, f32[8,256]{1,0:T(8,128)S(1)}, f32[16,128]{1,0:T(8,128)S(1)}, f32[16,32,128]{2,1,0:T(8,128)S(1)}, bf16[256,256]...) custom-call(f32[64,32,128]{2,1,0:T(8,128)S(1)} %copy-done, s32[1,256]{1,0:T(1,128)S(1)} %bitcast.8, s32[1,256]{1,0:T(1,128)S(1)} %bitcast.9, ...), custom_call_target="tpu_custom_call" | custom-call | flops 1000000 | bytes 1000000 | tf_op jit(solution)/shard_map/prepare/pallas_call | solution.py:408
  14.1 2.9 %collective-permute-done.2.refs_4_ = f32[400,128]{1,0:T(8,128)S(1)} collective-permute-done((f32[400,128]{1,0:T(8,128)S(1)}, f32[400,128]{1,0:T(8,128)S(1)}, u32[]{:S(2)}, u32[]{:S(2)}) %collective-permute-start.2) | collective-permute-done | bytes 204832 | tf_op jit(solution)/shard_map/ppermute | solution.py:422
  16.9 2.1 %forward.1 = (f32[4,16,32,128]{3,2,1,0:T(8,128)S(1)}, f32[2,4,32,128]{3,2,1,0:T(8,128)S(1)}, f32[24,32,128]{2,1,0:T(8,128)S(1)}, f32[3,16,128]{2,1,0:T(8,128)S(1)}) custom-call(f32[16,32,128]{2,1,0:T(8,128)S(1)} %get-tuple-element.29.refs_0_, f32[16,32,128]{2,1,0:T(8,128)S(1)} %get-tuple-element.30.refs_1_, f32[16,32,128]{2,1,0:T(8,128)S(1)} %collective-permute-done.refs_2_, ...), custom_call_target="tpu_custom_call" | custom-call | flops 1000000 | bytes 1000000 | tf_op jit(solution)/shard_map/forward/pallas_call | solution.py:408
  19.0 0.1 collective-permute-start.5
  19.1 2.9 %collective-permute-start.4 = (f32[24,32,128]{2,1,0:T(8,128)S(1)}, f32[24,32,128]{2,1,0:T(8,128)S(1)}, u32[]{:S(2)}, u32[]{:S(2)}) collective-permute-start(f32[24,32,128]{2,1,0:T(8,128)S(1)} %get-tuple-element.38), channel_id=1, source_target_pairs={{0,15},{1,2},{2,1},{3,4},{4,3},{5,6},{6,5},{7,8},{8,7},{9,10},{10,... | collective-permute-start | bytes 1179656 | tf_op jit(solution)/shard_map/ppermute | solution.py:422
  22.0 9.2 %all_to_all.11 = f32[16,1,128]{2,1,0:T(1,128)S(1)} all-to-all(f32[16,1,128]{2,1,0:T(1,128)S(1)} %bitcast.7), channel_id=1, replica_groups=mesh['groups'=2,'shot'=16] {'shot'}, dimensions={0} | all-to-all | bytes 16384 | tf_op jit(solution)/shard_map/all_to_all | solution.py:475
  31.2 0.8 %traces.1 = (bf16[256,512]{1,0:T(8,128)(2,1)S(1)}, f32[256,256]{1,0:T(8,128)S(1)}, f32[8,256]{1,0:T(8,128)S(1)}) custom-call(f32[8,256]{1,0:T(8,128)S(1)} %get-tuple-element.40.refs_0_.refs_8_, f32[16,128]{1,0:T(8,128)S(1)} %bitcast.6, f32[4,16,32,128]{3,2,1,0:T(8,128)S(1)} %get-tuple-element.36.refs_2_.refs_0_), custom_call_target="tpu_custom_call" | custom-call | flops 1000000 | bytes 1000000 | tf_op jit(solution)/shard_map/traces/pallas_call | solution.py:408
  32.1 2.9 %forward_last.1 = (f32[4,16,32,128]{3,2,1,0:T(8,128)S(1)}, f32[16,256]{1,0:T(8,128)S(1)}) custom-call(f32[4,16,32,128]{3,2,1,0:T(8,128)S(1)} %get-tuple-element.36.refs_2_.refs_0_, f32[2,4,32,128]{3,2,1,0:T(8,128)S(1)} %get-tuple-element.37.refs_1_, f32[24,32,128]{2,1,0:T(8,128)S(1)} %collective-permute-done.4.refs_2_, ...), custom_call_target="tpu_custom_call" | custom-call | flops 1000000 | bytes 1000000 | tf_op jit(solution)/shard_map/forward_last/pallas_call | solution.py:408
  35.0 0.1 collective-permute-start.6
  35.1 1.1 %collective-permute-done.6.mate = f32[16,256]{1,0:T(8,128)S(1)} collective-permute-done((f32[16,256]{1,0:T(8,128)S(1)}, f32[16,256]{1,0:T(8,128)S(1)}, u32[]{:S(2)}, u32[]{:S(2)}) %collective-permute-start.6) | collective-permute-done | bytes 16416 | tf_op jit(solution)/shard_map/ppermute | solution.py:422
  36.2 2.3 %collective-permute-start.8 = (f32[2,16,256]{2,1,0:T(8,128)S(1)}, f32[2,16,256]{2,1,0:T(8,128)S(1)}, u32[]{:S(2)}, u32[]{:S(2)}) collective-permute-start(f32[2,16,256]{2,1,0:T(8,128)S(1)} %pair.1.refs_6_), channel_id=1, source_target_pairs={{0,14},{1,15},{2,4},{3,5},{4,2},{5,3},{6,8},{7,9},{8,6},{9,7},{10,... | collective-permute-start | bytes 98312 | tf_op jit(solution)/shard_map/ppermute | solution.py:422
  38.5 0.8 %own_sources.1.refs_5_ = f32[8,16,32,128]{3,2,1,0:T(8,128)S(1)} custom-call(f32[16,256]{1,0:T(8,128)S(1)} %get-tuple-element.46.adj), custom_call_target="tpu_custom_call" | custom-call | flops 1000000 | bytes 1000000 | tf_op jit(solution)/shard_map/own_sources/pallas_call | solution.py:408
  39.3 3.6 %collective-permute-done.8.refs_8_ = f32[2,16,256]{2,1,0:T(8,128)S(1)} collective-permute-done((f32[2,16,256]{2,1,0:T(8,128)S(1)}, f32[2,16,256]{2,1,0:T(8,128)S(1)}, u32[]{:S(2)}, u32[]{:S(2)}) %collective-permute-start.8) | collective-permute-done | bytes 32800 | tf_op jit(solution)/shard_map/ppermute | solution.py:422
  42.8 4.5 %adjoint.1 = (f32[4,32,128]{2,1,0:T(8,128)S(1)}, f32[4,32,128]{2,1,0:T(8,128)S(1)}, f32[4,32,128]{2,1,0:T(8,128)S(1)}, f32[4,32,128]{2,1,0:T(8,128)S(1)}) custom-call(f32[4,16,32,128]{3,2,1,0:T(8,128)S(1)} %get-tuple-element.36.refs_2_.refs_0_, f32[4,16,32,128]{3,2,1,0:T(8,128)S(1)} %get-tuple-element.45.refs_1_, ...), custom_call_target="tpu_custom_call" | custom-call | flops 1000000 | bytes 1000000 | tf_op jit(solution)/shard_map/adjoint/pallas_call | solution.py:408
  47.3 0.1 collective-permute-start.9
  47.4 1.1 %collective-permute-start.10 = (f32[4,32,128]{2,1,0:T(8,128)S(1)}, f32[4,32,128]{2,1,0:T(8,128)S(1)}, u32[]{:S(2)}, u32[]{:S(2)}) collective-permute-start(f32[4,32,128]{2,1,0:T(8,128)S(1)} %get-tuple-element.49), channel_id=1, source_target_pairs={{0,8},{1,9},{2,10},{3,11},{4,12},{5,13},{6,14},{7,15},{8,0},{9,1},... | collective-permute-start | bytes 196616 | tf_op jit(solution)/shard_map/ppermute | solution.py:422
  48.5 3.3 %collective-permute-start.11 = (f32[4,32,128]{2,1,0:T(8,128)S(1)}, f32[4,32,128]{2,1,0:T(8,128)S(1)}, u32[]{:S(2)}, u32[]{:S(2)}) collective-permute-start(f32[4,32,128]{2,1,0:T(8,128)S(1)} %get-tuple-element.50), channel_id=1, source_target_pairs={{0,12},{1,13},{2,14},{3,15},{4,8},{5,9},{6,10},{7,11},{8,4},{9,5},... | collective-permute-start | bytes 196616 | tf_op jit(solution)/shard_map/ppermute | solution.py:422
  51.7 3.1 %collective-permute-done.10 = f32[4,32,128]{2,1,0:T(8,128)S(1)} collective-permute-done((f32[4,32,128]{2,1,0:T(8,128)S(1)}, f32[4,32,128]{2,1,0:T(8,128)S(1)}, u32[]{:S(2)}, u32[]{:S(2)}) %collective-permute-start.10) | collective-permute-done | bytes 65568 | tf_op jit(solution)/shard_map/ppermute | solution.py:422
  54.9 0.6 %add_add_fusion = f32[4,32,128]{2,1,0:T(8,128)} fusion(f32[4,32,128]{2,1,0:T(8,128)S(1)} %collective-permute-done.11, f32[4,32,128]{2,1,0:T(8,128)S(1)} %collective-permute-done.10, f32[4,32,128]{2,1,0:T(8,128)S(1)} %get-tuple-element.47, f32[4,32,128]{2,1,0:T(8,128)S(1)} %collective-permute-done.9), kind=kLoop, calls=%fused_computation | loop fusion | flops 49152 | bytes 327680 | tf_op jit(solution)/shard_map/add | solution.py:544
  (16 shorter events, 0.0 us)
Async XLA Ops:
  0.0 16.9 %collective-permute-start.1 = (f32[16,32,128]{2,1,0:T(8,128)}, f32[16,32,128]{2,1,0:T(8,128)S(1)}, u32[]{:S(2)}, u32[]{:S(2)}) collective-permute-start(f32[16,32,128]{2,1,0:T(8,128)} %now.1), channel_id=1, source_target_pairs={{0,1},{1,0},{2,3},{3,2},{4,5},{5,4},{6,7},{7,6},{8,9},{9,8},{10,11... | collective-permute-start | bytes 786440 | tf_op jit(solution)/shard_map/ppermute | solution.py:422
  0.5 16.5 %collective-permute-start = (f32[16,32,128]{2,1,0:T(8,128)}, f32[16,32,128]{2,1,0:T(8,128)S(1)}, u32[]{:S(2)}, u32[]{:S(2)}) collective-permute-start(f32[16,32,128]{2,1,0:T(8,128)} %now.1), channel_id=1, source_target_pairs={{0,15},{1,2},{2,1},{3,4},{4,3},{5,6},{6,5},{7,8},{8,7},{9,10},{10,... | collective-permute-start | bytes 786440 | tf_op jit(solution)/shard_map/ppermute | solution.py:422
  6.8 1.0 %copy-start.1 = (f32[16,32,128]{2,1,0:T(8,128)S(1)}, f32[16,32,128]{2,1,0:T(8,128)}, u32[]{:S(2)}) copy-start(f32[16,32,128]{2,1,0:T(8,128)} %before.1) | copy-start | bytes 786436
  7.7 0.7 %copy-start.6 = (f32[1,8]{1,0:T(1,128)S(1)}, f32[1,8]{1,0:T(1,128)}, u32[]{:S(2)}) copy-start(f32[1,8]{1,0:T(1,128)} %wavelet.1) | copy-start | bytes 100
  9.0 7.9 %collective-permute-start.2 = (f32[400,128]{1,0:T(8,128)S(1)}, f32[400,128]{1,0:T(8,128)S(1)}, u32[]{:S(2)}, u32[]{:S(2)}) collective-permute-start(f32[400,128]{1,0:T(8,128)S(1)} %get-tuple-element.31), channel_id=1, source_target_pairs={{0,15},{1,2},{2,1},{3,4},{4,3},{5,6},{6,5},{7,8},{8,7},{9,10},{10,... | collective-permute-start | bytes 614408 | tf_op jit(solution)/shard_map/ppermute | solution.py:422
  9.1 7.9 %collective-permute-start.3 = (f32[400,128]{1,0:T(8,128)S(1)}, f32[400,128]{1,0:T(8,128)S(1)}, u32[]{:S(2)}, u32[]{:S(2)}) collective-permute-start(f32[400,128]{1,0:T(8,128)S(1)} %get-tuple-element.32), channel_id=1, source_target_pairs={{0,1},{1,0},{2,3},{3,2},{4,5},{5,4},{6,7},{7,6},{8,9},{9,8},{10,11... | collective-permute-start | bytes 614408 | tf_op jit(solution)/shard_map/ppermute | solution.py:422
  9.1 1.2 %copy-start = (f32[64,32,128]{2,1,0:T(8,128)S(1)}, f32[64,32,128]{2,1,0:T(8,128)}, u32[]{:S(2)}) copy-start(f32[64,32,128]{2,1,0:T(8,128)} %courant.1) | copy-start | bytes 3145732
  10.4 0.9 %copy-start.2 = (f32[16,32,128]{2,1,0:T(8,128)S(1)}, f32[16,32,128]{2,1,0:T(8,128)}, u32[]{:S(2)}) copy-start(f32[16,32,128]{2,1,0:T(8,128)} %now.1) | copy-start | bytes 786436
  11.3 0.7 %copy-start.3 = (f32[16,128]{1,0:T(8,128)S(1)}, f32[16,128]{1,0:T(8,128)}, u32[]{:S(2)}) copy-start(f32[16,128]{1,0:T(8,128)} %observed.1) | copy-start | bytes 24580
  12.0 0.7 %copy-start.4 = (s32[256]{0:T(256)S(1)}, s32[256]{0:T(256)}, u32[]{:S(2)}) copy-start(s32[256]{0:T(256)} %param.13) | copy-start | bytes 3076
  12.7 0.7 %copy-start.5 = (s32[256]{0:T(256)S(1)}, s32[256]{0:T(256)}, u32[]{:S(2)}) copy-start(s32[256]{0:T(256)} %param.14) | copy-start | bytes 3076
  19.0 13.1 %collective-permute-start.5 = (f32[24,32,128]{2,1,0:T(8,128)S(1)}, f32[24,32,128]{2,1,0:T(8,128)S(1)}, u32[]{:S(2)}, u32[]{:S(2)}) collective-permute-start(f32[24,32,128]{2,1,0:T(8,128)S(1)} %get-tuple-element.38), channel_id=1, source_target_pairs={{0,1},{1,0},{2,3},{3,2},{4,5},{5,4},{6,7},{7,6},{8,9},{9,8},{10,11... | collective-permute-start | bytes 1179656 | tf_op jit(solution)/shard_map/ppermute | solution.py:422
  19.1 13.0 %collective-permute-start.4 = (f32[24,32,128]{2,1,0:T(8,128)S(1)}, f32[24,32,128]{2,1,0:T(8,128)S(1)}, u32[]{:S(2)}, u32[]{:S(2)}) collective-permute-start(f32[24,32,128]{2,1,0:T(8,128)S(1)} %get-tuple-element.38), channel_id=1, source_target_pairs={{0,15},{1,2},{2,1},{3,4},{4,3},{5,6},{6,5},{7,8},{8,7},{9,10},{10,... | collective-permute-start | bytes 1179656 | tf_op jit(solution)/shard_map/ppermute | solution.py:422
  35.0 1.2 %collective-permute-start.6 = (f32[16,256]{1,0:T(8,128)S(1)}, f32[16,256]{1,0:T(8,128)S(1)}, u32[]{:S(2)}, u32[]{:S(2)}) collective-permute-start(f32[16,256]{1,0:T(8,128)S(1)} %get-tuple-element.46.adj), channel_id=1, source_target_pairs={{0,1},{1,0},{2,3},{3,2},{4,5},{5,4},{6,7},{7,6},{8,9},{9,8},{10,11... | collective-permute-start | bytes 49160 | tf_op jit(solution)/shard_map/ppermute | solution.py:422
  36.2 6.6 %collective-permute-start.8 = (f32[2,16,256]{2,1,0:T(8,128)S(1)}, f32[2,16,256]{2,1,0:T(8,128)S(1)}, u32[]{:S(2)}, u32[]{:S(2)}) collective-permute-start(f32[2,16,256]{2,1,0:T(8,128)S(1)} %pair.1.refs_6_), channel_id=1, source_target_pairs={{0,14},{1,15},{2,4},{3,5},{4,2},{5,3},{6,8},{7,9},{8,6},{9,7},{10,... | collective-permute-start | bytes 98312 | tf_op jit(solution)/shard_map/ppermute | solution.py:422
  38.5 4.3 %collective-permute-start.7 = (f32[2,16,256]{2,1,0:T(8,128)S(1)}, f32[2,16,256]{2,1,0:T(8,128)S(1)}, u32[]{:S(2)}, u32[]{:S(2)}) collective-permute-start(f32[2,16,256]{2,1,0:T(8,128)S(1)} %pair.1.refs_6_), channel_id=1, source_target_pairs={{0,2},{1,3},{2,0},{3,1},{4,6},{5,7},{6,4},{7,5},{8,10},{9,11},{10,... | collective-permute-start | bytes 98312 | tf_op jit(solution)/shard_map/ppermute | solution.py:422
  47.3 4.5 %collective-permute-start.9 = (f32[4,32,128]{2,1,0:T(8,128)S(1)}, f32[4,32,128]{2,1,0:T(8,128)S(1)}, u32[]{:S(2)}, u32[]{:S(2)}) collective-permute-start(f32[4,32,128]{2,1,0:T(8,128)S(1)} %get-tuple-element.48), channel_id=1, source_target_pairs={{0,4},{1,5},{2,6},{3,7},{4,0},{5,1},{6,2},{7,3},{8,12},{9,13},{10,... | collective-permute-start | bytes 196616 | tf_op jit(solution)/shard_map/ppermute | solution.py:422
  47.4 7.5 %collective-permute-start.10 = (f32[4,32,128]{2,1,0:T(8,128)S(1)}, f32[4,32,128]{2,1,0:T(8,128)S(1)}, u32[]{:S(2)}, u32[]{:S(2)}) collective-permute-start(f32[4,32,128]{2,1,0:T(8,128)S(1)} %get-tuple-element.49), channel_id=1, source_target_pairs={{0,8},{1,9},{2,10},{3,11},{4,12},{5,13},{6,14},{7,15},{8,0},{9,1},... | collective-permute-start | bytes 196616 | tf_op jit(solution)/shard_map/ppermute | solution.py:422
  48.5 6.4 %collective-permute-start.11 = (f32[4,32,128]{2,1,0:T(8,128)S(1)}, f32[4,32,128]{2,1,0:T(8,128)S(1)}, u32[]{:S(2)}, u32[]{:S(2)}) collective-permute-start(f32[4,32,128]{2,1,0:T(8,128)S(1)} %get-tuple-element.50), channel_id=1, source_target_pairs={{0,12},{1,13},{2,14},{3,15},{4,8},{5,9},{6,10},{7,11},{8,4},{9,5},... | collective-permute-start | bytes 196616 | tf_op jit(solution)/shard_map/ppermute | solution.py:422

commit v10 on v9

--- a/solution.py
+++ b/solution.py
@@ -117,9 +117,7 @@
     mate_out[size:] = pack
 
 
-def prepare_kernel(
-    courant, cells, order, observed, pack, now, model_out, cells_out, observed_out, now_out, ymat_out, zmat_out
-):
+def prepare_kernel(courant, table, observed, pack, now, model_out, cells_out, observed_out, now_out, ymat_out, zmat_out):
     rows, span_y, span_z = now.shape
     now_out[...] = now[...]
     build_bands(span_y, span_z, ymat_out, zmat_out)
@@ -129,9 +127,9 @@
     for chunk in range(0, window, RAD):
         source = lax.rem(piece * rows - HALO + chunk + period, period)
         model_out[chunk : chunk + RAD] = courant[pl.ds(source, RAD)] * (1.0 / SCALE)
-    count = cells.shape[1]
-    wanted = order[...]
-    cell = cells[...]
+    count = cells_out.shape[1]
+    cell = table[:, :count]
+    wanted = table[:, count:]
     which = lax.broadcasted_iota(jnp.int32, (16, count), 0)
     digits = jnp.where(which == 0, cell // 256, jnp.where(which == 1, cell % 256, 0)).astype(F32).astype(BF)
     for j in range(0, count, 256):
@@ -459,6 +457,7 @@
     )
     before_outer, before_mate = with_outer(to_outer), with_mate(to_mate)
 
+    table = jnp.concatenate([receiver_cell, send_order]).reshape(1, 2 * count)
     model, cells, observed, now, ymat, zmat = call(
         prepare_kernel,
         (
@@ -469,7 +468,7 @@
             jax.ShapeDtypeStruct((GROUP * span_y, GROUP * span_y), BF),
             jax.ShapeDtypeStruct((2 * span_z, 2 * span_z), BF),
         ),
-        (courant_sq, receiver_cell.reshape(1, count), send_order.reshape(1, count), observed, pack, wave_now),
+        (courant_sq, table, observed, pack, wave_now),
         name="prepare",
     )
     recorded = lax.all_to_all(observed, "shot", split_axis=0, concat_axis=0, tiled=True)
@@ -540,7 +539,7 @@
         name="adjoint",
     )
     total = parts[0]
-    for i in range(1, slabs):
+    for i in [*range(2, slabs), 1]:
         total = total + swapped(parts[i], lambda d: d ^ (i * PIECES))
     return total
 

time: 55.9 us -> 55.3 us (0.989)
  local copies, waits for them, and re-layouts: 5.82 us -> 4.47 us
  waiting for transfers between devices: 10.7 us -> 11.7 us
  starting transfers between devices: 16 us -> 15.2 us
  other arithmetic: 0.65 us -> 1.35 us
    unnamed x14 -> x10, local copies, waits for them, and re-layouts: 5.82 us -> 4.47 us
    ppermute x12, waiting for transfers between devices: 10.7 us -> 11.7 us  [swapped(): lax.ppermute(value, 'shot', [(d, partner(d) % count) for d in range(count)])]
    ppermute x12, starting transfers between devices: 16 us -> 15.2 us  [swapped(): lax.ppermute(value, 'shot', [(d, partner(d) % count) for d in range(count)])]
    concatenate x0 -> x1, other arithmetic: none -> 0.7 us  [per_device(): table = jnp.concatenate([receiver_cell, send_order]).reshape(1, 2 * count)]
  transfers between devices with their start and end apart: 12 -> 12, of which waited for: 4 -> 5; matrix products, arithmetic and copies ran while one was open for 0% -> 1% of each run, Pallas kernels for 5% -> 5%
where the time goes in v10:
time: 55.3 us; the launch traced here: 55 us
  starting transfers between devices  15.2 us (27%)
  Pallas kernels  12.3 us (22%)
  waiting for transfers between devices  11.7 us (21%)
  blocking collectives  9.23 us (17%)
  local copies, waits for them, and re-layouts  4.47 us (8%)
  other arithmetic  1.35 us (2%)
  between operations  0.75 us (1%)
    ppermute x12, starting transfers between devices, swapped(): lax.ppermute(value, 'shot', [(d, partner(d) % count) for d in range(count)])  15.2 us
    pallas_call x8, Pallas kernels, call(): pl.pallas_call(kernel, out_shape=outs, in_specs=specs or [VMEM] * len(ins...  12.3 us
    ppermute x12, waiting for transfers between devices, swapped(): lax.ppermute(value, 'shot', [(d, partner(d) % count) for d in range(count)])  11.7 us
    all_to_all x1, blocking collectives, per_device(): lax.all_to_all(observed, 'shot', split_axis=0, concat_axis=0, tiled=True)  9.23 us
    unnamed x10, local copies, waits for them, and re-layouts  4.47 us
  transfers between devices with their start and end apart: 12, of which 5 were waited for; matrix products, arithmetic and copies ran while one was open for 1% of the time, Pallas kernels for 5%

profile of v10, /device:TPU:0, one launch (start us, length us, event | category | flops | bytes accessed | tf_op | source)
XLA Modules:
  0.0 55.0 jit_solution(11989941322654505249)
XLA Ops:
  0.0 0.5 collective-permute-start.1
  0.5 5.7 %collective-permute-start = (f32[16,32,128]{2,1,0:T(8,128)}, f32[16,32,128]{2,1,0:T(8,128)S(1)}, u32[]{:S(2)}, u32[]{:S(2)}) collective-permute-start(f32[16,32,128]{2,1,0:T(8,128)} %now.1), channel_id=1, source_target_pairs={{0,15},{1,2},{2,1},{3,4},{4,3},{5,6},{6,5},{7,8},{8,7},{9,10},{10,... | collective-permute-start | bytes 786440 | tf_op jit(solution)/shard_map/ppermute | solution.py:420
  6.8 0.9 %copy-done.1 = f32[16,32,128]{2,1,0:T(8,128)S(1)} copy-done((f32[16,32,128]{2,1,0:T(8,128)S(1)}, f32[16,32,128]{2,1,0:T(8,128)}, u32[]{:S(2)}) %copy-start.1) | copy-done | bytes 262168
  7.7 0.7 %copy-done.4 = f32[1,8]{1,0:T(1,128)S(1)} copy-done((f32[1,8]{1,0:T(1,128)S(1)}, f32[1,8]{1,0:T(1,128)}, u32[]{:S(2)}) %copy-start.4) | copy-done | bytes 56
  8.4 0.6 %message.1 = (f32[400,128]{1,0:T(8,128)S(1)}, f32[400,128]{1,0:T(8,128)S(1)}, f32[16,128]{1,0:T(8,128)S(1)}, f32[16,32,128]{2,1,0:T(8,128)S(1)}) custom-call(f32[16,32,128]{2,1,0:T(8,128)S(1)} %copy-done.1, f32[1,8]{1,0:T(1,128)S(1)} %copy-done.4, s32[1]{0:T(128)S(6)} %copy.10.source), custom_call_target="tpu_custom_call" | custom-call | flops 1000000 | bytes 1000000 | tf_op jit(solution)/shard_map/message/pallas_call | solution.py:406
  9.0 0.1 collective-permute-start.2
  9.1 0.1 collective-permute-start.3
  9.1 0.7 %pad_add_fusion = s32[512]{0:T(512)S(1)} fusion(s32[256]{0:T(256)} %param.14, s32[256]{0:T(256)} %param.13), kind=kLoop, calls=%fused_computation.1 | loop fusion | flops 512 | bytes 4096 | tf_op jit(solution)/shard_map/concatenate | solution.py:460
  9.8 1.2 %copy-done = f32[64,32,128]{2,1,0:T(8,128)S(1)} copy-done((f32[64,32,128]{2,1,0:T(8,128)S(1)}, f32[64,32,128]{2,1,0:T(8,128)}, u32[]{:S(2)}) %copy-start) | copy-done | bytes 1048600
  11.1 0.9 %copy-done.2 = f32[16,32,128]{2,1,0:T(8,128)S(1)} copy-done((f32[16,32,128]{2,1,0:T(8,128)S(1)}, f32[16,32,128]{2,1,0:T(8,128)}, u32[]{:S(2)}) %copy-start.2) | copy-done | bytes 262168
  12.0 0.7 %copy-done.3 = f32[16,128]{1,0:T(8,128)S(1)} copy-done((f32[16,128]{1,0:T(8,128)S(1)}, f32[16,128]{1,0:T(8,128)}, u32[]{:S(2)}) %copy-start.3) | copy-done | bytes 8216
  12.7 0.7 %prepare.1 = (f32[72,32,128]{2,1,0:T(8,128)S(1)}, f32[8,256]{1,0:T(8,128)S(1)}, f32[16,128]{1,0:T(8,128)S(1)}, f32[16,32,128]{2,1,0:T(8,128)S(1)}, bf16[256,256]...) custom-call(f32[64,32,128]{2,1,0:T(8,128)S(1)} %copy-done, s32[1,512]{1,0:T(1,128)S(1)} %bitcast.6, ...), custom_call_target="tpu_custom_call" | custom-call | flops 1000000 | bytes 1000000 | tf_op jit(solution)/shard_map/prepare/pallas_call | solution.py:406
  13.4 3.5 %collective-permute-done.2.refs_4_ = f32[400,128]{1,0:T(8,128)S(1)} collective-permute-done((f32[400,128]{1,0:T(8,128)S(1)}, f32[400,128]{1,0:T(8,128)S(1)}, u32[]{:S(2)}, u32[]{:S(2)}) %collective-permute-start.2) | collective-permute-done | bytes 204832 | tf_op jit(solution)/shard_map/ppermute | solution.py:420
  16.9 0.0 collective-permute-done.1.refs_3_
  16.9 2.1 %forward.1 = (f32[4,16,32,128]{3,2,1,0:T(8,128)S(1)}, f32[2,4,32,128]{3,2,1,0:T(8,128)S(1)}, f32[24,32,128]{2,1,0:T(8,128)S(1)}, f32[3,16,128]{2,1,0:T(8,128)S(1)}) custom-call(f32[16,32,128]{2,1,0:T(8,128)S(1)} %get-tuple-element.29.refs_0_, f32[16,32,128]{2,1,0:T(8,128)S(1)} %get-tuple-element.30.refs_1_, f32[16,32,128]{2,1,0:T(8,128)S(1)} %collective-permute-done.refs_2_, ...), custom_call_target="tpu_custom_call" | custom-call | flops 1000000 | bytes 1000000 | tf_op jit(solution)/shard_map/forward/pallas_call | solution.py:406
  19.0 0.1 collective-permute-start.5
  19.1 2.9 %collective-permute-start.4 = (f32[24,32,128]{2,1,0:T(8,128)S(1)}, f32[24,32,128]{2,1,0:T(8,128)S(1)}, u32[]{:S(2)}, u32[]{:S(2)}) collective-permute-start(f32[24,32,128]{2,1,0:T(8,128)S(1)} %get-tuple-element.38), channel_id=1, source_target_pairs={{0,15},{1,2},{2,1},{3,4},{4,3},{5,6},{6,5},{7,8},{8,7},{9,10},{10,... | collective-permute-start | bytes 1179656 | tf_op jit(solution)/shard_map/ppermute | solution.py:420
  22.0 9.2 %all_to_all.11 = f32[16,1,128]{2,1,0:T(1,128)S(1)} all-to-all(f32[16,1,128]{2,1,0:T(1,128)S(1)} %bitcast.7), channel_id=1, replica_groups=mesh['groups'=2,'shot'=16] {'shot'}, dimensions={0} | all-to-all | bytes 16384 | tf_op jit(solution)/shard_map/all_to_all | solution.py:474
  31.2 0.8 %traces.1 = (bf16[256,512]{1,0:T(8,128)(2,1)S(1)}, f32[256,256]{1,0:T(8,128)S(1)}, f32[8,256]{1,0:T(8,128)S(1)}) custom-call(f32[8,256]{1,0:T(8,128)S(1)} %get-tuple-element.40.refs_0_.refs_8_, f32[16,128]{1,0:T(8,128)S(1)} %bitcast.5, f32[4,16,32,128]{3,2,1,0:T(8,128)S(1)} %get-tuple-element.36.refs_2_.refs_0_), custom_call_target="tpu_custom_call" | custom-call | flops 1000000 | bytes 1000000 | tf_op jit(solution)/shard_map/traces/pallas_call | solution.py:406
  32.1 2.9 %forward_last.1 = (f32[4,16,32,128]{3,2,1,0:T(8,128)S(1)}, f32[16,256]{1,0:T(8,128)S(1)}) custom-call(f32[4,16,32,128]{3,2,1,0:T(8,128)S(1)} %get-tuple-element.36.refs_2_.refs_0_, f32[2,4,32,128]{3,2,1,0:T(8,128)S(1)} %get-tuple-element.37.refs_1_, f32[24,32,128]{2,1,0:T(8,128)S(1)} %collective-permute-done.4.refs_2_, ...), custom_call_target="tpu_custom_call" | custom-call | flops 1000000 | bytes 1000000 | tf_op jit(solution)/shard_map/forward_last/pallas_call | solution.py:406
  35.0 0.1 collective-permute-start.6
  35.1 1.1 %collective-permute-done.6.mate = f32[16,256]{1,0:T(8,128)S(1)} collective-permute-done((f32[16,256]{1,0:T(8,128)S(1)}, f32[16,256]{1,0:T(8,128)S(1)}, u32[]{:S(2)}, u32[]{:S(2)}) %collective-permute-start.6) | collective-permute-done | bytes 16416 | tf_op jit(solution)/shard_map/ppermute | solution.py:420
  36.2 2.3 %collective-permute-start.8 = (f32[2,16,256]{2,1,0:T(8,128)S(1)}, f32[2,16,256]{2,1,0:T(8,128)S(1)}, u32[]{:S(2)}, u32[]{:S(2)}) collective-permute-start(f32[2,16,256]{2,1,0:T(8,128)S(1)} %pair.1.refs_6_), channel_id=1, source_target_pairs={{0,14},{1,15},{2,4},{3,5},{4,2},{5,3},{6,8},{7,9},{8,6},{9,7},{10,... | collective-permute-start | bytes 98312 | tf_op jit(solution)/shard_map/ppermute | solution.py:420
  38.5 0.8 %own_sources.1.refs_5_ = f32[8,16,32,128]{3,2,1,0:T(8,128)S(1)} custom-call(f32[16,256]{1,0:T(8,128)S(1)} %get-tuple-element.46.adj), custom_call_target="tpu_custom_call" | custom-call | flops 1000000 | bytes 1000000 | tf_op jit(solution)/shard_map/own_sources/pallas_call | solution.py:406
  39.3 3.6 %collective-permute-done.8.refs_8_ = f32[2,16,256]{2,1,0:T(8,128)S(1)} collective-permute-done((f32[2,16,256]{2,1,0:T(8,128)S(1)}, f32[2,16,256]{2,1,0:T(8,128)S(1)}, u32[]{:S(2)}, u32[]{:S(2)}) %collective-permute-start.8) | collective-permute-done | bytes 32800 | tf_op jit(solution)/shard_map/ppermute | solution.py:420
  42.8 4.5 %adjoint.1 = (f32[4,32,128]{2,1,0:T(8,128)S(1)}, f32[4,32,128]{2,1,0:T(8,128)S(1)}, f32[4,32,128]{2,1,0:T(8,128)S(1)}, f32[4,32,128]{2,1,0:T(8,128)S(1)}) custom-call(f32[4,16,32,128]{3,2,1,0:T(8,128)S(1)} %get-tuple-element.36.refs_2_.refs_0_, f32[4,16,32,128]{3,2,1,0:T(8,128)S(1)} %get-tuple-element.45.refs_1_, ...), custom_call_target="tpu_custom_call" | custom-call | flops 1000000 | bytes 1000000 | tf_op jit(solution)/shard_map/adjoint/pallas_call | solution.py:406
  47.3 0.1 collective-permute-start.9
  47.4 1.5 %collective-permute-start.10 = (f32[4,32,128]{2,1,0:T(8,128)S(1)}, f32[4,32,128]{2,1,0:T(8,128)S(1)}, u32[]{:S(2)}, u32[]{:S(2)}) collective-permute-start(f32[4,32,128]{2,1,0:T(8,128)S(1)} %get-tuple-element.49), channel_id=1, source_target_pairs={{0,12},{1,13},{2,14},{3,15},{4,8},{5,9},{6,10},{7,11},{8,4},{9,5},... | collective-permute-start | bytes 196616 | tf_op jit(solution)/shard_map/ppermute | solution.py:420
  48.9 1.9 %collective-permute-start.11 = (f32[4,32,128]{2,1,0:T(8,128)S(1)}, f32[4,32,128]{2,1,0:T(8,128)S(1)}, u32[]{:S(2)}, u32[]{:S(2)}) collective-permute-start(f32[4,32,128]{2,1,0:T(8,128)S(1)} %get-tuple-element.50), channel_id=1, source_target_pairs={{0,4},{1,5},{2,6},{3,7},{4,0},{5,1},{6,2},{7,3},{8,12},{9,13},{10,... | collective-permute-start | bytes 196616 | tf_op jit(solution)/shard_map/ppermute | solution.py:420
  50.9 3.2 %collective-permute-done.9 = f32[4,32,128]{2,1,0:T(8,128)S(1)} collective-permute-done((f32[4,32,128]{2,1,0:T(8,128)S(1)}, f32[4,32,128]{2,1,0:T(8,128)S(1)}, u32[]{:S(2)}, u32[]{:S(2)}) %collective-permute-start.9) | collective-permute-done | bytes 65568 | tf_op jit(solution)/shard_map/ppermute | solution.py:420
  54.1 0.3 collective-permute-done.11
  54.4 0.6 %add_add_fusion = f32[4,32,128]{2,1,0:T(8,128)} fusion(f32[4,32,128]{2,1,0:T(8,128)S(1)} %collective-permute-done.11, f32[4,32,128]{2,1,0:T(8,128)S(1)} %collective-permute-done.10, f32[4,32,128]{2,1,0:T(8,128)S(1)} %get-tuple-element.47, f32[4,32,128]{2,1,0:T(8,128)S(1)} %collective-permute-done.9), kind=kLoop, calls=%fused_computation | loop fusion | flops 49152 | bytes 327680 | tf_op jit(solution)/shard_map/add | solution.py:543
  (13 shorter events, 0.0 us)
Async XLA Ops:
  0.0 16.9 %collective-permute-start.1 = (f32[16,32,128]{2,1,0:T(8,128)}, f32[16,32,128]{2,1,0:T(8,128)S(1)}, u32[]{:S(2)}, u32[]{:S(2)}) collective-permute-start(f32[16,32,128]{2,1,0:T(8,128)} %now.1), channel_id=1, source_target_pairs={{0,1},{1,0},{2,3},{3,2},{4,5},{5,4},{6,7},{7,6},{8,9},{9,8},{10,11... | collective-permute-start | bytes 786440 | tf_op jit(solution)/shard_map/ppermute | solution.py:420
  0.5 16.5 %collective-permute-start = (f32[16,32,128]{2,1,0:T(8,128)}, f32[16,32,128]{2,1,0:T(8,128)S(1)}, u32[]{:S(2)}, u32[]{:S(2)}) collective-permute-start(f32[16,32,128]{2,1,0:T(8,128)} %now.1), channel_id=1, source_target_pairs={{0,15},{1,2},{2,1},{3,4},{4,3},{5,6},{6,5},{7,8},{8,7},{9,10},{10,... | collective-permute-start | bytes 786440 | tf_op jit(solution)/shard_map/ppermute | solution.py:420
  6.8 1.0 %copy-start.1 = (f32[16,32,128]{2,1,0:T(8,128)S(1)}, f32[16,32,128]{2,1,0:T(8,128)}, u32[]{:S(2)}) copy-start(f32[16,32,128]{2,1,0:T(8,128)} %before.1) | copy-start | bytes 786436
  7.7 0.7 %copy-start.4 = (f32[1,8]{1,0:T(1,128)S(1)}, f32[1,8]{1,0:T(1,128)}, u32[]{:S(2)}) copy-start(f32[1,8]{1,0:T(1,128)} %wavelet.1) | copy-start | bytes 100
  9.0 7.9 %collective-permute-start.2 = (f32[400,128]{1,0:T(8,128)S(1)}, f32[400,128]{1,0:T(8,128)S(1)}, u32[]{:S(2)}, u32[]{:S(2)}) collective-permute-start(f32[400,128]{1,0:T(8,128)S(1)} %get-tuple-element.31), channel_id=1, source_target_pairs={{0,15},{1,2},{2,1},{3,4},{4,3},{5,6},{6,5},{7,8},{8,7},{9,10},{10,... | collective-permute-start | bytes 614408 | tf_op jit(solution)/shard_map/ppermute | solution.py:420
  9.1 7.9 %collective-permute-start.3 = (f32[400,128]{1,0:T(8,128)S(1)}, f32[400,128]{1,0:T(8,128)S(1)}, u32[]{:S(2)}, u32[]{:S(2)}) collective-permute-start(f32[400,128]{1,0:T(8,128)S(1)} %get-tuple-element.32), channel_id=1, source_target_pairs={{0,1},{1,0},{2,3},{3,2},{4,5},{5,4},{6,7},{7,6},{8,9},{9,8},{10,11... | collective-permute-start | bytes 614408 | tf_op jit(solution)/shard_map/ppermute | solution.py:420
  9.8 1.2 %copy-start = (f32[64,32,128]{2,1,0:T(8,128)S(1)}, f32[64,32,128]{2,1,0:T(8,128)}, u32[]{:S(2)}) copy-start(f32[64,32,128]{2,1,0:T(8,128)} %courant.1) | copy-start | bytes 3145732
  11.1 0.9 %copy-start.2 = (f32[16,32,128]{2,1,0:T(8,128)S(1)}, f32[16,32,128]{2,1,0:T(8,128)}, u32[]{:S(2)}) copy-start(f32[16,32,128]{2,1,0:T(8,128)} %now.1) | copy-start | bytes 786436
  12.0 0.7 %copy-start.3 = (f32[16,128]{1,0:T(8,128)S(1)}, f32[16,128]{1,0:T(8,128)}, u32[]{:S(2)}) copy-start(f32[16,128]{1,0:T(8,128)} %observed.1) | copy-start | bytes 24580
  19.0 13.1 %collective-permute-start.5 = (f32[24,32,128]{2,1,0:T(8,128)S(1)}, f32[24,32,128]{2,1,0:T(8,128)S(1)}, u32[]{:S(2)}, u32[]{:S(2)}) collective-permute-start(f32[24,32,128]{2,1,0:T(8,128)S(1)} %get-tuple-element.38), channel_id=1, source_target_pairs={{0,1},{1,0},{2,3},{3,2},{4,5},{5,4},{6,7},{7,6},{8,9},{9,8},{10,11... | collective-permute-start | bytes 1179656 | tf_op jit(solution)/shard_map/ppermute | solution.py:420
  19.1 13.0 %collective-permute-start.4 = (f32[24,32,128]{2,1,0:T(8,128)S(1)}, f32[24,32,128]{2,1,0:T(8,128)S(1)}, u32[]{:S(2)}, u32[]{:S(2)}) collective-permute-start(f32[24,32,128]{2,1,0:T(8,128)S(1)} %get-tuple-element.38), channel_id=1, source_target_pairs={{0,15},{1,2},{2,1},{3,4},{4,3},{5,6},{6,5},{7,8},{8,7},{9,10},{10,... | collective-permute-start | bytes 1179656 | tf_op jit(solution)/shard_map/ppermute | solution.py:420
  35.0 1.2 %collective-permute-start.6 = (f32[16,256]{1,0:T(8,128)S(1)}, f32[16,256]{1,0:T(8,128)S(1)}, u32[]{:S(2)}, u32[]{:S(2)}) collective-permute-start(f32[16,256]{1,0:T(8,128)S(1)} %get-tuple-element.46.adj), channel_id=1, source_target_pairs={{0,1},{1,0},{2,3},{3,2},{4,5},{5,4},{6,7},{7,6},{8,9},{9,8},{10,11... | collective-permute-start | bytes 49160 | tf_op jit(solution)/shard_map/ppermute | solution.py:420
  36.2 6.6 %collective-permute-start.8 = (f32[2,16,256]{2,1,0:T(8,128)S(1)}, f32[2,16,256]{2,1,0:T(8,128)S(1)}, u32[]{:S(2)}, u32[]{:S(2)}) collective-permute-start(f32[2,16,256]{2,1,0:T(8,128)S(1)} %pair.1.refs_6_), channel_id=1, source_target_pairs={{0,14},{1,15},{2,4},{3,5},{4,2},{5,3},{6,8},{7,9},{8,6},{9,7},{10,... | collective-permute-start | bytes 98312 | tf_op jit(solution)/shard_map/ppermute | solution.py:420
  38.5 4.3 %collective-permute-start.7 = (f32[2,16,256]{2,1,0:T(8,128)S(1)}, f32[2,16,256]{2,1,0:T(8,128)S(1)}, u32[]{:S(2)}, u32[]{:S(2)}) collective-permute-start(f32[2,16,256]{2,1,0:T(8,128)S(1)} %pair.1.refs_6_), channel_id=1, source_target_pairs={{0,2},{1,3},{2,0},{3,1},{4,6},{5,7},{6,4},{7,5},{8,10},{9,11},{10,... | collective-permute-start | bytes 98312 | tf_op jit(solution)/shard_map/ppermute | solution.py:420
  47.3 6.8 %collective-permute-start.9 = (f32[4,32,128]{2,1,0:T(8,128)S(1)}, f32[4,32,128]{2,1,0:T(8,128)S(1)}, u32[]{:S(2)}, u32[]{:S(2)}) collective-permute-start(f32[4,32,128]{2,1,0:T(8,128)S(1)} %get-tuple-element.48), channel_id=1, source_target_pairs={{0,8},{1,9},{2,10},{3,11},{4,12},{5,13},{6,14},{7,15},{8,0},{9,1},... | collective-permute-start | bytes 196616 | tf_op jit(solution)/shard_map/ppermute | solution.py:420
  47.4 6.7 %collective-permute-start.10 = (f32[4,32,128]{2,1,0:T(8,128)S(1)}, f32[4,32,128]{2,1,0:T(8,128)S(1)}, u32[]{:S(2)}, u32[]{:S(2)}) collective-permute-start(f32[4,32,128]{2,1,0:T(8,128)S(1)} %get-tuple-element.49), channel_id=1, source_target_pairs={{0,12},{1,13},{2,14},{3,15},{4,8},{5,9},{6,10},{7,11},{8,4},{9,5},... | collective-permute-start | bytes 196616 | tf_op jit(solution)/shard_map/ppermute | solution.py:420
  48.9 5.4 %collective-permute-start.11 = (f32[4,32,128]{2,1,0:T(8,128)S(1)}, f32[4,32,128]{2,1,0:T(8,128)S(1)}, u32[]{:S(2)}, u32[]{:S(2)}) collective-permute-start(f32[4,32,128]{2,1,0:T(8,128)S(1)} %get-tuple-element.50), channel_id=1, source_target_pairs={{0,4},{1,5},{2,6},{3,7},{4,0},{5,1},{6,2},{7,3},{8,12},{9,13},{10,... | collective-permute-start | bytes 196616 | tf_op jit(solution)/shard_map/ppermute | solution.py:420

commit v11 on v10

--- a/solution.py
+++ b/solution.py
@@ -182,7 +182,7 @@
     cur_outer = jnp.where(odd == 0, low, high)
     cur_mate = jnp.where(odd == 0, high, low)
     if index == 0:
-        now, before, now_outer, now_mate, before_outer, before_mate = refs_in
+        now, before, now_mate, now_outer, before_outer, before_mate = refs_in
         cur[own : own + rows] = now[...]
         old[own : own + rows] = before[...]
         cur[pl.ds(cur_outer, wide)] = now_outer[...]
@@ -192,7 +192,7 @@
         old[pl.ds(jnp.where(odd == 0, low, high), narrow)] = before_outer[:size].reshape((narrow,) + shape)
         old[pl.ds(jnp.where(odd == 0, high, low), narrow)] = before_mate[:size].reshape((narrow,) + shape)
     else:
-        earlier, known, got_outer, got_mate = refs_in
+        earlier, known, got_mate, got_outer = refs_in
         cur[own : own + rows] = earlier[earlier.shape[0] - 1]
         old[own : own + rows] = earlier[earlier.shape[0] - 2]
         cur[pl.ds(cur_outer, wide)] = got_outer[0:wide]
@@ -446,7 +446,7 @@
     plane = (span_y, span_z)
 
     narrow = RAD * (ROUNDS[0] - 1)
-    now_outer, now_mate = with_outer(wave_now), with_mate(wave_now)
+    now_mate, now_outer = with_mate(wave_now), with_outer(wave_now)
     message = jax.ShapeDtypeStruct((narrow * span_y + 16, span_z), F32)
     to_outer, to_mate, pack, before = call(
         message_kernel,
@@ -475,7 +475,7 @@
 
     common = (zmat, ymat, model)
     field_list = []
-    ins = (now, before, now_outer, now_mate, before_outer, before_mate)
+    ins = (now, before, now_mate, now_outer, before_outer, before_mate)
     for index in range(len(ROUNDS) - 1):
         window = rows + 2 * RAD * ROUNDS[index]
         sent = 2 * rows - 2 * RAD
@@ -494,7 +494,8 @@
         )
         field_list.append(fields)
         pack = made[0] if made else pack
-        ins = (fields, known, with_outer(send), with_mate(send))
+        got_mate, got_outer = with_mate(send), with_outer(send)
+        ins = (fields, known, got_mate, got_outer)
 
     rows_table, lane_table, traces = call(
         functools.partial(tables_kernel, count),

time: 55.3 us -> 55.1 us (level)
  starting transfers between devices: 15.2 us -> 12.6 us
  blocking collectives: 9.23 us -> 11.7 us
    ppermute x12, starting transfers between devices: 15.2 us -> 12.6 us  [swapped(): lax.ppermute(value, 'shot', [(d, partner(d) % count) for d in range(count)])]
    all_to_all x1, blocking collectives: 9.23 us -> 11.7 us  [per_device(): lax.all_to_all(observed, 'shot', split_axis=0, concat_axis=0, tiled=True)]
where the time goes in v11:
time: 55.1 us; the launch traced here: 54.8 us
  starting transfers between devices  12.6 us (23%)
  Pallas kernels  12.3 us (22%)
  waiting for transfers between devices  11.7 us (21%)
  blocking collectives  11.7 us (21%)
  local copies, waits for them, and re-layouts  4.47 us (8%)
  other arithmetic  1.35 us (2%)
  between operations  0.73 us (1%)
    ppermute x12, starting transfers between devices, swapped(): lax.ppermute(value, 'shot', [(d, partner(d) % count) for d in range(count)])  12.6 us
    pallas_call x8, Pallas kernels, call(): pl.pallas_call(kernel, out_shape=outs, in_specs=specs or [VMEM] * len(ins...  12.3 us
    ppermute x12, waiting for transfers between devices, swapped(): lax.ppermute(value, 'shot', [(d, partner(d) % count) for d in range(count)])  11.7 us
    all_to_all x1, blocking collectives, per_device(): lax.all_to_all(observed, 'shot', split_axis=0, concat_axis=0, tiled=True)  11.7 us
    unnamed x10, local copies, waits for them, and re-layouts  4.47 us
  transfers between devices with their start and end apart: 12, of which 5 were waited for; matrix products, arithmetic and copies ran while one was open for 1% of the time, Pallas kernels for 5%

profile of v11, /device:TPU:0, one launch (start us, length us, event | category | flops | bytes accessed | tf_op | source)
XLA Modules:
  0.0 54.8 jit_solution(16727005645235412493)
XLA Ops:
  0.0 5.4 %collective-permute-start.1 = (f32[16,32,128]{2,1,0:T(8,128)}, f32[16,32,128]{2,1,0:T(8,128)S(1)}, u32[]{:S(2)}, u32[]{:S(2)}) collective-permute-start(f32[16,32,128]{2,1,0:T(8,128)} %now.1), channel_id=1, source_target_pairs={{0,15},{1,2},{2,1},{3,4},{4,3},{5,6},{6,5},{7,8},{8,7},{9,10},{10,... | collective-permute-start | bytes 786440 | tf_op jit(solution)/shard_map/ppermute | solution.py:420
  6.1 0.9 %copy-done.1 = f32[16,32,128]{2,1,0:T(8,128)S(1)} copy-done((f32[16,32,128]{2,1,0:T(8,128)S(1)}, f32[16,32,128]{2,1,0:T(8,128)}, u32[]{:S(2)}) %copy-start.1) | copy-done | bytes 262168
  7.1 0.7 %copy-done.4 = f32[1,8]{1,0:T(1,128)S(1)} copy-done((f32[1,8]{1,0:T(1,128)S(1)}, f32[1,8]{1,0:T(1,128)}, u32[]{:S(2)}) %copy-start.4) | copy-done | bytes 56
  7.7 0.6 %message.1 = (f32[400,128]{1,0:T(8,128)S(1)}, f32[400,128]{1,0:T(8,128)S(1)}, f32[16,128]{1,0:T(8,128)S(1)}, f32[16,32,128]{2,1,0:T(8,128)S(1)}) custom-call(f32[16,32,128]{2,1,0:T(8,128)S(1)} %copy-done.1, f32[1,8]{1,0:T(1,128)S(1)} %copy-done.4, s32[1]{0:T(128)S(6)} %copy.10.source), custom_call_target="tpu_custom_call" | custom-call | flops 1000000 | bytes 1000000 | tf_op jit(solution)/shard_map/message/pallas_call | solution.py:406
  8.3 0.7 %collective-permute-start.2 = (f32[400,128]{1,0:T(8,128)S(1)}, f32[400,128]{1,0:T(8,128)S(1)}, u32[]{:S(2)}, u32[]{:S(2)}) collective-permute-start(f32[400,128]{1,0:T(8,128)S(1)} %get-tuple-element.31), channel_id=1, source_target_pairs={{0,15},{1,2},{2,1},{3,4},{4,3},{5,6},{6,5},{7,8},{8,7},{9,10},{10,... | collective-permute-start | bytes 614408 | tf_op jit(solution)/shard_map/ppermute | solution.py:420
  9.0 0.0 collective-permute-start.3
  9.0 0.7 %pad_add_fusion = s32[512]{0:T(512)S(1)} fusion(s32[256]{0:T(256)} %param.14, s32[256]{0:T(256)} %param.13), kind=kLoop, calls=%fused_computation.1 | loop fusion | flops 512 | bytes 4096 | tf_op jit(solution)/shard_map/concatenate | solution.py:460
  9.7 1.2 %copy-done = f32[64,32,128]{2,1,0:T(8,128)S(1)} copy-done((f32[64,32,128]{2,1,0:T(8,128)S(1)}, f32[64,32,128]{2,1,0:T(8,128)}, u32[]{:S(2)}) %copy-start) | copy-done | bytes 1048600
  11.0 0.9 %copy-done.2 = f32[16,32,128]{2,1,0:T(8,128)S(1)} copy-done((f32[16,32,128]{2,1,0:T(8,128)S(1)}, f32[16,32,128]{2,1,0:T(8,128)}, u32[]{:S(2)}) %copy-start.2) | copy-done | bytes 262168
  11.9 0.7 %copy-done.3 = f32[16,128]{1,0:T(8,128)S(1)} copy-done((f32[16,128]{1,0:T(8,128)S(1)}, f32[16,128]{1,0:T(8,128)}, u32[]{:S(2)}) %copy-start.3) | copy-done | bytes 8216
  12.6 0.7 %prepare.1 = (f32[72,32,128]{2,1,0:T(8,128)S(1)}, f32[8,256]{1,0:T(8,128)S(1)}, f32[16,128]{1,0:T(8,128)S(1)}, f32[16,32,128]{2,1,0:T(8,128)S(1)}, bf16[256,256]...) custom-call(f32[64,32,128]{2,1,0:T(8,128)S(1)} %copy-done, s32[1,512]{1,0:T(1,128)S(1)} %bitcast.6, ...), custom_call_target="tpu_custom_call" | custom-call | flops 1000000 | bytes 1000000 | tf_op jit(solution)/shard_map/prepare/pallas_call | solution.py:406
  13.3 3.0 %collective-permute-done.2.refs_4_ = f32[400,128]{1,0:T(8,128)S(1)} collective-permute-done((f32[400,128]{1,0:T(8,128)S(1)}, f32[400,128]{1,0:T(8,128)S(1)}, u32[]{:S(2)}, u32[]{:S(2)}) %collective-permute-start.2) | collective-permute-done | bytes 204832 | tf_op jit(solution)/shard_map/ppermute | solution.py:420
  16.4 0.0 collective-permute-done.3.refs_5_
  16.4 0.0 collective-permute-done.1.refs_3_
  16.4 0.0 collective-permute-done.refs_2_
  16.4 2.1 %forward.1 = (f32[4,16,32,128]{3,2,1,0:T(8,128)S(1)}, f32[2,4,32,128]{3,2,1,0:T(8,128)S(1)}, f32[24,32,128]{2,1,0:T(8,128)S(1)}, f32[3,16,128]{2,1,0:T(8,128)S(1)}) custom-call(f32[16,32,128]{2,1,0:T(8,128)S(1)} %get-tuple-element.29.refs_0_, f32[16,32,128]{2,1,0:T(8,128)S(1)} %get-tuple-element.30.refs_1_, f32[16,32,128]{2,1,0:T(8,128)S(1)} %collective-permute-done.refs_2_, ...), custom_call_target="tpu_custom_call" | custom-call | flops 1000000 | bytes 1000000 | tf_op jit(solution)/shard_map/forward/pallas_call | solution.py:406
  18.4 0.8 %collective-permute-start.5 = (f32[24,32,128]{2,1,0:T(8,128)S(1)}, f32[24,32,128]{2,1,0:T(8,128)S(1)}, u32[]{:S(2)}, u32[]{:S(2)}) collective-permute-start(f32[24,32,128]{2,1,0:T(8,128)S(1)} %get-tuple-element.38), channel_id=1, source_target_pairs={{0,15},{1,2},{2,1},{3,4},{4,3},{5,6},{6,5},{7,8},{8,7},{9,10},{10,... | collective-permute-start | bytes 1179656 | tf_op jit(solution)/shard_map/ppermute | solution.py:420
  19.2 0.0 collective-permute-start.4
  19.2 11.7 %all_to_all.11 = f32[16,1,128]{2,1,0:T(1,128)S(1)} all-to-all(f32[16,1,128]{2,1,0:T(1,128)S(1)} %bitcast.7), channel_id=1, replica_groups=mesh['groups'=2,'shot'=16] {'shot'}, dimensions={0} | all-to-all | bytes 16384 | tf_op jit(solution)/shard_map/all_to_all | solution.py:474
  30.9 0.8 %traces.1 = (bf16[256,512]{1,0:T(8,128)(2,1)S(1)}, f32[256,256]{1,0:T(8,128)S(1)}, f32[8,256]{1,0:T(8,128)S(1)}) custom-call(f32[8,256]{1,0:T(8,128)S(1)} %get-tuple-element.40.refs_0_.refs_8_, f32[16,128]{1,0:T(8,128)S(1)} %bitcast.5, f32[4,16,32,128]{3,2,1,0:T(8,128)S(1)} %get-tuple-element.36.refs_2_.refs_0_), custom_call_target="tpu_custom_call" | custom-call | flops 1000000 | bytes 1000000 | tf_op jit(solution)/shard_map/traces/pallas_call | solution.py:406
  31.8 2.9 %forward_last.1 = (f32[4,16,32,128]{3,2,1,0:T(8,128)S(1)}, f32[16,256]{1,0:T(8,128)S(1)}) custom-call(f32[4,16,32,128]{3,2,1,0:T(8,128)S(1)} %get-tuple-element.36.refs_2_.refs_0_, f32[2,4,32,128]{3,2,1,0:T(8,128)S(1)} %get-tuple-element.37.refs_1_, f32[24,32,128]{2,1,0:T(8,128)S(1)} %collective-permute-done.4.refs_2_, ...), custom_call_target="tpu_custom_call" | custom-call | flops 1000000 | bytes 1000000 | tf_op jit(solution)/shard_map/forward_last/pallas_call | solution.py:406
  34.7 1.2 %collective-permute-done.6.mate = f32[16,256]{1,0:T(8,128)S(1)} collective-permute-done((f32[16,256]{1,0:T(8,128)S(1)}, f32[16,256]{1,0:T(8,128)S(1)}, u32[]{:S(2)}, u32[]{:S(2)}) %collective-permute-start.6) | collective-permute-done | bytes 16416 | tf_op jit(solution)/shard_map/ppermute | solution.py:420
  35.9 2.0 %collective-permute-start.8 = (f32[2,16,256]{2,1,0:T(8,128)S(1)}, f32[2,16,256]{2,1,0:T(8,128)S(1)}, u32[]{:S(2)}, u32[]{:S(2)}) collective-permute-start(f32[2,16,256]{2,1,0:T(8,128)S(1)} %pair.1.refs_6_), channel_id=1, source_target_pairs={{0,14},{1,15},{2,4},{3,5},{4,2},{5,3},{6,8},{7,9},{8,6},{9,7},{10,... | collective-permute-start | bytes 98312 | tf_op jit(solution)/shard_map/ppermute | solution.py:420
  37.9 0.8 %own_sources.1.refs_5_ = f32[8,16,32,128]{3,2,1,0:T(8,128)S(1)} custom-call(f32[16,256]{1,0:T(8,128)S(1)} %get-tuple-element.46.adj), custom_call_target="tpu_custom_call" | custom-call | flops 1000000 | bytes 1000000 | tf_op jit(solution)/shard_map/own_sources/pallas_call | solution.py:406
  38.7 3.9 %collective-permute-done.8.refs_8_ = f32[2,16,256]{2,1,0:T(8,128)S(1)} collective-permute-done((f32[2,16,256]{2,1,0:T(8,128)S(1)}, f32[2,16,256]{2,1,0:T(8,128)S(1)}, u32[]{:S(2)}, u32[]{:S(2)}) %collective-permute-start.8) | collective-permute-done | bytes 32800 | tf_op jit(solution)/shard_map/ppermute | solution.py:420
  42.5 4.5 %adjoint.1 = (f32[4,32,128]{2,1,0:T(8,128)S(1)}, f32[4,32,128]{2,1,0:T(8,128)S(1)}, f32[4,32,128]{2,1,0:T(8,128)S(1)}, f32[4,32,128]{2,1,0:T(8,128)S(1)}) custom-call(f32[4,16,32,128]{3,2,1,0:T(8,128)S(1)} %get-tuple-element.36.refs_2_.refs_0_, f32[4,16,32,128]{3,2,1,0:T(8,128)S(1)} %get-tuple-element.45.refs_1_, ...), custom_call_target="tpu_custom_call" | custom-call | flops 1000000 | bytes 1000000 | tf_op jit(solution)/shard_map/adjoint/pallas_call | solution.py:406
  47.0 0.1 collective-permute-start.9
  47.1 1.6 %collective-permute-start.10 = (f32[4,32,128]{2,1,0:T(8,128)S(1)}, f32[4,32,128]{2,1,0:T(8,128)S(1)}, u32[]{:S(2)}, u32[]{:S(2)}) collective-permute-start(f32[4,32,128]{2,1,0:T(8,128)S(1)} %get-tuple-element.49), channel_id=1, source_target_pairs={{0,12},{1,13},{2,14},{3,15},{4,8},{5,9},{6,10},{7,11},{8,4},{9,5},... | collective-permute-start | bytes 196616 | tf_op jit(solution)/shard_map/ppermute | solution.py:420
  48.7 1.9 %collective-permute-start.11 = (f32[4,32,128]{2,1,0:T(8,128)S(1)}, f32[4,32,128]{2,1,0:T(8,128)S(1)}, u32[]{:S(2)}, u32[]{:S(2)}) collective-permute-start(f32[4,32,128]{2,1,0:T(8,128)S(1)} %get-tuple-element.50), channel_id=1, source_target_pairs={{0,4},{1,5},{2,6},{3,7},{4,0},{5,1},{6,2},{7,3},{8,12},{9,13},{10,... | collective-permute-start | bytes 196616 | tf_op jit(solution)/shard_map/ppermute | solution.py:420
  50.5 3.3 %collective-permute-done.9 = f32[4,32,128]{2,1,0:T(8,128)S(1)} collective-permute-done((f32[4,32,128]{2,1,0:T(8,128)S(1)}, f32[4,32,128]{2,1,0:T(8,128)S(1)}, u32[]{:S(2)}, u32[]{:S(2)}) %collective-permute-start.9) | collective-permute-done | bytes 65568 | tf_op jit(solution)/shard_map/ppermute | solution.py:420
  53.8 0.3 collective-permute-done.11
  54.1 0.6 %add_add_fusion = f32[4,32,128]{2,1,0:T(8,128)} fusion(f32[4,32,128]{2,1,0:T(8,128)S(1)} %collective-permute-done.11, f32[4,32,128]{2,1,0:T(8,128)S(1)} %collective-permute-done.10, f32[4,32,128]{2,1,0:T(8,128)S(1)} %get-tuple-element.47, f32[4,32,128]{2,1,0:T(8,128)S(1)} %collective-permute-done.9), kind=kLoop, calls=%fused_computation | loop fusion | flops 49152 | bytes 327680 | tf_op jit(solution)/shard_map/add | solution.py:544
  (13 shorter events, 0.0 us)
Async XLA Ops:
  0.0 16.4 %collective-permute-start.1 = (f32[16,32,128]{2,1,0:T(8,128)}, f32[16,32,128]{2,1,0:T(8,128)S(1)}, u32[]{:S(2)}, u32[]{:S(2)}) collective-permute-start(f32[16,32,128]{2,1,0:T(8,128)} %now.1), channel_id=1, source_target_pairs={{0,15},{1,2},{2,1},{3,4},{4,3},{5,6},{6,5},{7,8},{8,7},{9,10},{10,... | collective-permute-start | bytes 786440 | tf_op jit(solution)/shard_map/ppermute | solution.py:420
  5.4 10.9 %collective-permute-start = (f32[16,32,128]{2,1,0:T(8,128)}, f32[16,32,128]{2,1,0:T(8,128)S(1)}, u32[]{:S(2)}, u32[]{:S(2)}) collective-permute-start(f32[16,32,128]{2,1,0:T(8,128)} %now.1), channel_id=1, source_target_pairs={{0,1},{1,0},{2,3},{3,2},{4,5},{5,4},{6,7},{7,6},{8,9},{9,8},{10,11... | collective-permute-start | bytes 786440 | tf_op jit(solution)/shard_map/ppermute | solution.py:420
  6.1 1.0 %copy-start.1 = (f32[16,32,128]{2,1,0:T(8,128)S(1)}, f32[16,32,128]{2,1,0:T(8,128)}, u32[]{:S(2)}) copy-start(f32[16,32,128]{2,1,0:T(8,128)} %before.1) | copy-start | bytes 786436
  7.1 0.7 %copy-start.4 = (f32[1,8]{1,0:T(1,128)S(1)}, f32[1,8]{1,0:T(1,128)}, u32[]{:S(2)}) copy-start(f32[1,8]{1,0:T(1,128)} %wavelet.1) | copy-start | bytes 100
  8.3 8.1 %collective-permute-start.2 = (f32[400,128]{1,0:T(8,128)S(1)}, f32[400,128]{1,0:T(8,128)S(1)}, u32[]{:S(2)}, u32[]{:S(2)}) collective-permute-start(f32[400,128]{1,0:T(8,128)S(1)} %get-tuple-element.31), channel_id=1, source_target_pairs={{0,15},{1,2},{2,1},{3,4},{4,3},{5,6},{6,5},{7,8},{8,7},{9,10},{10,... | collective-permute-start | bytes 614408 | tf_op jit(solution)/shard_map/ppermute | solution.py:420
  9.0 7.3 %collective-permute-start.3 = (f32[400,128]{1,0:T(8,128)S(1)}, f32[400,128]{1,0:T(8,128)S(1)}, u32[]{:S(2)}, u32[]{:S(2)}) collective-permute-start(f32[400,128]{1,0:T(8,128)S(1)} %get-tuple-element.32), channel_id=1, source_target_pairs={{0,1},{1,0},{2,3},{3,2},{4,5},{5,4},{6,7},{7,6},{8,9},{9,8},{10,11... | collective-permute-start | bytes 614408 | tf_op jit(solution)/shard_map/ppermute | solution.py:420
  9.7 1.2 %copy-start = (f32[64,32,128]{2,1,0:T(8,128)S(1)}, f32[64,32,128]{2,1,0:T(8,128)}, u32[]{:S(2)}) copy-start(f32[64,32,128]{2,1,0:T(8,128)} %courant.1) | copy-start | bytes 3145732
  11.0 0.9 %copy-start.2 = (f32[16,32,128]{2,1,0:T(8,128)S(1)}, f32[16,32,128]{2,1,0:T(8,128)}, u32[]{:S(2)}) copy-start(f32[16,32,128]{2,1,0:T(8,128)} %now.1) | copy-start | bytes 786436
  11.9 0.7 %copy-start.3 = (f32[16,128]{1,0:T(8,128)S(1)}, f32[16,128]{1,0:T(8,128)}, u32[]{:S(2)}) copy-start(f32[16,128]{1,0:T(8,128)} %observed.1) | copy-start | bytes 24580
  18.4 13.3 %collective-permute-start.5 = (f32[24,32,128]{2,1,0:T(8,128)S(1)}, f32[24,32,128]{2,1,0:T(8,128)S(1)}, u32[]{:S(2)}, u32[]{:S(2)}) collective-permute-start(f32[24,32,128]{2,1,0:T(8,128)S(1)} %get-tuple-element.38), channel_id=1, source_target_pairs={{0,15},{1,2},{2,1},{3,4},{4,3},{5,6},{6,5},{7,8},{8,7},{9,10},{10,... | collective-permute-start | bytes 1179656 | tf_op jit(solution)/shard_map/ppermute | solution.py:420
  19.2 12.5 %collective-permute-start.4 = (f32[24,32,128]{2,1,0:T(8,128)S(1)}, f32[24,32,128]{2,1,0:T(8,128)S(1)}, u32[]{:S(2)}, u32[]{:S(2)}) collective-permute-start(f32[24,32,128]{2,1,0:T(8,128)S(1)} %get-tuple-element.38), channel_id=1, source_target_pairs={{0,1},{1,0},{2,3},{3,2},{4,5},{5,4},{6,7},{7,6},{8,9},{9,8},{10,11... | collective-permute-start | bytes 1179656 | tf_op jit(solution)/shard_map/ppermute | solution.py:420
  34.7 1.2 %collective-permute-start.6 = (f32[16,256]{1,0:T(8,128)S(1)}, f32[16,256]{1,0:T(8,128)S(1)}, u32[]{:S(2)}, u32[]{:S(2)}) collective-permute-start(f32[16,256]{1,0:T(8,128)S(1)} %get-tuple-element.46.adj), channel_id=1, source_target_pairs={{0,1},{1,0},{2,3},{3,2},{4,5},{5,4},{6,7},{7,6},{8,9},{9,8},{10,11... | collective-permute-start | bytes 49160 | tf_op jit(solution)/shard_map/ppermute | solution.py:420
  35.9 6.6 %collective-permute-start.8 = (f32[2,16,256]{2,1,0:T(8,128)S(1)}, f32[2,16,256]{2,1,0:T(8,128)S(1)}, u32[]{:S(2)}, u32[]{:S(2)}) collective-permute-start(f32[2,16,256]{2,1,0:T(8,128)S(1)} %pair.1.refs_6_), channel_id=1, source_target_pairs={{0,14},{1,15},{2,4},{3,5},{4,2},{5,3},{6,8},{7,9},{8,6},{9,7},{10,... | collective-permute-start | bytes 98312 | tf_op jit(solution)/shard_map/ppermute | solution.py:420
  37.9 4.6 %collective-permute-start.7 = (f32[2,16,256]{2,1,0:T(8,128)S(1)}, f32[2,16,256]{2,1,0:T(8,128)S(1)}, u32[]{:S(2)}, u32[]{:S(2)}) collective-permute-start(f32[2,16,256]{2,1,0:T(8,128)S(1)} %pair.1.refs_6_), channel_id=1, source_target_pairs={{0,2},{1,3},{2,0},{3,1},{4,6},{5,7},{6,4},{7,5},{8,10},{9,11},{10,... | collective-permute-start | bytes 98312 | tf_op jit(solution)/shard_map/ppermute | solution.py:420
  47.0 6.8 %collective-permute-start.9 = (f32[4,32,128]{2,1,0:T(8,128)S(1)}, f32[4,32,128]{2,1,0:T(8,128)S(1)}, u32[]{:S(2)}, u32[]{:S(2)}) collective-permute-start(f32[4,32,128]{2,1,0:T(8,128)S(1)} %get-tuple-element.48), channel_id=1, source_target_pairs={{0,8},{1,9},{2,10},{3,11},{4,12},{5,13},{6,14},{7,15},{8,0},{9,1},... | collective-permute-start | bytes 196616 | tf_op jit(solution)/shard_map/ppermute | solution.py:420
  47.1 6.7 %collective-permute-start.10 = (f32[4,32,128]{2,1,0:T(8,128)S(1)}, f32[4,32,128]{2,1,0:T(8,128)S(1)}, u32[]{:S(2)}, u32[]{:S(2)}) collective-permute-start(f32[4,32,128]{2,1,0:T(8,128)S(1)} %get-tuple-element.49), channel_id=1, source_target_pairs={{0,12},{1,13},{2,14},{3,15},{4,8},{5,9},{6,10},{7,11},{8,4},{9,5},... | collective-permute-start | bytes 196616 | tf_op jit(solution)/shard_map/ppermute | solution.py:420
  48.7 5.4 %collective-permute-start.11 = (f32[4,32,128]{2,1,0:T(8,128)S(1)}, f32[4,32,128]{2,1,0:T(8,128)S(1)}, u32[]{:S(2)}, u32[]{:S(2)}) collective-permute-start(f32[4,32,128]{2,1,0:T(8,128)S(1)} %get-tuple-element.50), channel_id=1, source_target_pairs={{0,4},{1,5},{2,6},{3,7},{4,0},{5,1},{6,2},{7,3},{8,12},{9,13},{10,... | collective-permute-start | bytes 196616 | tf_op jit(solution)/shard_map/ppermute | solution.py:420

commit v12 on v11

--- a/solution.py
+++ b/solution.py
@@ -117,7 +117,7 @@
     mate_out[size:] = pack
 
 
-def prepare_kernel(courant, table, observed, pack, now, model_out, cells_out, observed_out, now_out, ymat_out, zmat_out):
+def prepare_kernel(courant, table, pack, now, model_out, cells_out, now_out, ymat_out, zmat_out):
     rows, span_y, span_z = now.shape
     now_out[...] = now[...]
     build_bands(span_y, span_z, ymat_out, zmat_out)
@@ -138,7 +138,6 @@
         found = dot(digits, chosen)
         ordered = found[0:1] * 256.0 + found[1:2]
         cells_out[:, j : j + 256] = jnp.broadcast_to(ordered, (8, 256))
-    observed_out[...] = observed[...] + 0.0 * pack[0:1, :]
 
 
 def pick_tables(cells, table_rows):
@@ -458,17 +457,16 @@
     before_outer, before_mate = with_outer(to_outer), with_mate(to_mate)
 
     table = jnp.concatenate([receiver_cell, send_order]).reshape(1, 2 * count)
-    model, cells, observed, now, ymat, zmat = call(
+    model, cells, now, ymat, zmat = call(
         prepare_kernel,
         (
             jax.ShapeDtypeStruct((rows + 2 * HALO,) + plane, F32),
             jax.ShapeDtypeStruct((8, count), F32),
-            jax.ShapeDtypeStruct(observed.shape, F32),
             jax.ShapeDtypeStruct(wave_now.shape, F32),
             jax.ShapeDtypeStruct((GROUP * span_y, GROUP * span_y), BF),
             jax.ShapeDtypeStruct((2 * span_z, 2 * span_z), BF),
         ),
-        (courant_sq, table, observed, pack, wave_now),
+        (courant_sq, table, pack, wave_now),
         name="prepare",
     )
     recorded = lax.all_to_all(observed, "shot", split_axis=0, concat_axis=0, tiled=True)

time: 55.1 us -> 55 us (level)
  waiting for transfers between devices: 11.7 us -> 12.4 us
  local copies, waits for them, and re-layouts: 4.47 us -> 3.78 us
    ppermute x12, waiting for transfers between devices: 11.7 us -> 12.4 us  [swapped(): lax.ppermute(value, 'shot', [(d, partner(d) % count) for d in range(count)])]
    unnamed x10, local copies, waits for them, and re-layouts: 4.47 us -> 3.78 us
where the time goes in v12:
time: 55 us; the launch traced here: 54.8 us
  starting transfers between devices  12.5 us (23%)
  waiting for transfers between devices  12.4 us (23%)
  Pallas kernels  12.3 us (22%)
  blocking collectives  11.7 us (21%)
  local copies, waits for them, and re-layouts  3.78 us (7%)
  other arithmetic  1.35 us (2%)
  between operations  0.73 us (1%)
    ppermute x12, starting transfers between devices, swapped(): lax.ppermute(value, 'shot', [(d, partner(d) % count) for d in range(count)])  12.5 us
    ppermute x12, waiting for transfers between devices, swapped(): lax.ppermute(value, 'shot', [(d, partner(d) % count) for d in range(count)])  12.4 us
    pallas_call x8, Pallas kernels, call(): pl.pallas_call(kernel, out_shape=outs, in_specs=specs or [VMEM] * len(ins...  12.3 us
    all_to_all x1, blocking collectives, per_device(): lax.all_to_all(observed, 'shot', split_axis=0, concat_axis=0, tiled=True)  11.7 us
    unnamed x10, local copies, waits for them, and re-layouts  3.78 us
  transfers between devices with their start and end apart: 12, of which 5 were waited for; matrix products, arithmetic and copies ran while one was open for 1% of the time, Pallas kernels for 5%

profile of v12, /device:TPU:0, one launch (start us, length us, event | category | flops | bytes accessed | tf_op | source)
XLA Modules:
  0.0 54.8 jit_solution(12820111470364751334)
XLA Ops:
  0.0 5.4 %collective-permute-start.1 = (f32[16,32,128]{2,1,0:T(8,128)}, f32[16,32,128]{2,1,0:T(8,128)S(1)}, u32[]{:S(2)}, u32[]{:S(2)}) collective-permute-start(f32[16,32,128]{2,1,0:T(8,128)} %now.1), channel_id=1, source_target_pairs={{0,15},{1,2},{2,1},{3,4},{4,3},{5,6},{6,5},{7,8},{8,7},{9,10},{10,... | collective-permute-start | bytes 786440 | tf_op jit(solution)/shard_map/ppermute | solution.py:419
  6.1 0.9 %copy-done.2 = f32[16,32,128]{2,1,0:T(8,128)S(1)} copy-done((f32[16,32,128]{2,1,0:T(8,128)S(1)}, f32[16,32,128]{2,1,0:T(8,128)}, u32[]{:S(2)}) %copy-start.2) | copy-done | bytes 262168
  7.1 0.7 %copy-done.3 = f32[1,8]{1,0:T(1,128)S(1)} copy-done((f32[1,8]{1,0:T(1,128)S(1)}, f32[1,8]{1,0:T(1,128)}, u32[]{:S(2)}) %copy-start.3) | copy-done | bytes 56
  7.7 0.6 %message.1 = (f32[400,128]{1,0:T(8,128)S(1)}, f32[400,128]{1,0:T(8,128)S(1)}, f32[16,128]{1,0:T(8,128)S(1)}, f32[16,32,128]{2,1,0:T(8,128)S(1)}) custom-call(f32[16,32,128]{2,1,0:T(8,128)S(1)} %copy-done.2, f32[1,8]{1,0:T(1,128)S(1)} %copy-done.3, s32[1]{0:T(128)S(6)} %copy.9.source), custom_call_target="tpu_custom_call" | custom-call | flops 1000000 | bytes 1000000 | tf_op jit(solution)/shard_map/message/pallas_call | solution.py:405
  8.3 0.7 %collective-permute-start.2 = (f32[400,128]{1,0:T(8,128)S(1)}, f32[400,128]{1,0:T(8,128)S(1)}, u32[]{:S(2)}, u32[]{:S(2)}) collective-permute-start(f32[400,128]{1,0:T(8,128)S(1)} %get-tuple-element.30), channel_id=1, source_target_pairs={{0,15},{1,2},{2,1},{3,4},{4,3},{5,6},{6,5},{7,8},{8,7},{9,10},{10,... | collective-permute-start | bytes 614408 | tf_op jit(solution)/shard_map/ppermute | solution.py:419
  9.0 0.7 %pad_add_fusion = s32[512]{0:T(512)S(1)} fusion(s32[256]{0:T(256)} %param.14, s32[256]{0:T(256)} %param.13), kind=kLoop, calls=%fused_computation.1 | loop fusion | flops 512 | bytes 4096 | tf_op jit(solution)/shard_map/concatenate | solution.py:459
  9.7 1.2 %copy-done = f32[64,32,128]{2,1,0:T(8,128)S(1)} copy-done((f32[64,32,128]{2,1,0:T(8,128)S(1)}, f32[64,32,128]{2,1,0:T(8,128)}, u32[]{:S(2)}) %copy-start) | copy-done | bytes 1048600
  11.0 0.9 %copy-done.1 = f32[16,32,128]{2,1,0:T(8,128)S(1)} copy-done((f32[16,32,128]{2,1,0:T(8,128)S(1)}, f32[16,32,128]{2,1,0:T(8,128)}, u32[]{:S(2)}) %copy-start.1) | copy-done | bytes 262168
  11.9 0.7 %prepare.1 = (f32[72,32,128]{2,1,0:T(8,128)S(1)}, f32[8,256]{1,0:T(8,128)S(1)}, f32[16,32,128]{2,1,0:T(8,128)S(1)}, bf16[256,256]{1,0:T(8,128)(2,1)S(1)}, bf16[256,256]{1,0:T(8,128)(2,1)S(1)}) custom-call(f32[64,32,128]{2,1,0:T(8,128)S(1)} %copy-done, s32[1,512]{1,0:T(1,128)S(1)} %bitcast.4, f32[16,128]{1,0:T(8,128)S(1)} %get-tuple-element.27.pack.refs_9_, ...), custom_call_target="tpu_custom_call" | custom-call | flops 1000000 | bytes 1000000 | tf_op jit(solution)/shard_map/prepare/pallas_call | solution.py:405
  12.6 3.7 %collective-permute-done.2.refs_4_ = f32[400,128]{1,0:T(8,128)S(1)} collective-permute-done((f32[400,128]{1,0:T(8,128)S(1)}, f32[400,128]{1,0:T(8,128)S(1)}, u32[]{:S(2)}, u32[]{:S(2)}) %collective-permute-start.2) | collective-permute-done | bytes 204832 | tf_op jit(solution)/shard_map/ppermute | solution.py:419
  16.4 0.0 collective-permute-done.3.refs_5_
  16.4 0.0 collective-permute-done.1.refs_3_
  16.4 0.0 collective-permute-done.refs_2_
  16.4 2.1 %forward.1 = (f32[4,16,32,128]{3,2,1,0:T(8,128)S(1)}, f32[2,4,32,128]{3,2,1,0:T(8,128)S(1)}, f32[24,32,128]{2,1,0:T(8,128)S(1)}, f32[3,16,128]{2,1,0:T(8,128)S(1)}) custom-call(f32[16,32,128]{2,1,0:T(8,128)S(1)} %get-tuple-element.28.refs_0_, f32[16,32,128]{2,1,0:T(8,128)S(1)} %get-tuple-element.29.refs_1_, f32[16,32,128]{2,1,0:T(8,128)S(1)} %collective-permute-done.refs_2_, ...), custom_call_target="tpu_custom_call" | custom-call | flops 1000000 | bytes 1000000 | tf_op jit(solution)/shard_map/forward/pallas_call | solution.py:405
  18.4 0.7 %collective-permute-start.5 = (f32[24,32,128]{2,1,0:T(8,128)S(1)}, f32[24,32,128]{2,1,0:T(8,128)S(1)}, u32[]{:S(2)}, u32[]{:S(2)}) collective-permute-start(f32[24,32,128]{2,1,0:T(8,128)S(1)} %get-tuple-element.37), channel_id=1, source_target_pairs={{0,15},{1,2},{2,1},{3,4},{4,3},{5,6},{6,5},{7,8},{8,7},{9,10},{10,... | collective-permute-start | bytes 1179656 | tf_op jit(solution)/shard_map/ppermute | solution.py:419
  19.2 0.0 collective-permute-start.4
  19.2 11.7 %all_to_all.11 = f32[16,1,128]{2,1,0:T(1,128)S(1)} all-to-all(f32[16,1,128]{2,1,0:T(1,128)S(1)} %bitcast.5), channel_id=1, replica_groups=mesh['groups'=2,'shot'=16] {'shot'}, dimensions={0} | all-to-all | bytes 16384 | tf_op jit(solution)/shard_map/all_to_all | solution.py:472
  30.9 0.8 %traces.1 = (bf16[256,512]{1,0:T(8,128)(2,1)S(1)}, f32[256,256]{1,0:T(8,128)S(1)}, f32[8,256]{1,0:T(8,128)S(1)}) custom-call(f32[8,256]{1,0:T(8,128)S(1)} %get-tuple-element.39.refs_0_.refs_8_, f32[16,128]{1,0:T(8,128)S(1)} %bitcast.3, f32[4,16,32,128]{3,2,1,0:T(8,128)S(1)} %get-tuple-element.35.refs_2_.refs_0_), custom_call_target="tpu_custom_call" | custom-call | flops 1000000 | bytes 1000000 | tf_op jit(solution)/shard_map/traces/pallas_call | solution.py:405
  31.8 0.0 collective-permute-done.4.refs_2_
  31.8 2.9 %forward_last.1 = (f32[4,16,32,128]{3,2,1,0:T(8,128)S(1)}, f32[16,256]{1,0:T(8,128)S(1)}) custom-call(f32[4,16,32,128]{3,2,1,0:T(8,128)S(1)} %get-tuple-element.35.refs_2_.refs_0_, f32[2,4,32,128]{3,2,1,0:T(8,128)S(1)} %get-tuple-element.36.refs_1_, f32[24,32,128]{2,1,0:T(8,128)S(1)} %collective-permute-done.4.refs_2_, ...), custom_call_target="tpu_custom_call" | custom-call | flops 1000000 | bytes 1000000 | tf_op jit(solution)/shard_map/forward_last/pallas_call | solution.py:405
  34.7 0.0 collective-permute-start.6
  34.7 1.2 %collective-permute-done.6.mate = f32[16,256]{1,0:T(8,128)S(1)} collective-permute-done((f32[16,256]{1,0:T(8,128)S(1)}, f32[16,256]{1,0:T(8,128)S(1)}, u32[]{:S(2)}, u32[]{:S(2)}) %collective-permute-start.6) | collective-permute-done | bytes 16416 | tf_op jit(solution)/shard_map/ppermute | solution.py:419
  35.9 2.0 %collective-permute-start.8 = (f32[2,16,256]{2,1,0:T(8,128)S(1)}, f32[2,16,256]{2,1,0:T(8,128)S(1)}, u32[]{:S(2)}, u32[]{:S(2)}) collective-permute-start(f32[2,16,256]{2,1,0:T(8,128)S(1)} %pair.1.refs_6_), channel_id=1, source_target_pairs={{0,14},{1,15},{2,4},{3,5},{4,2},{5,3},{6,8},{7,9},{8,6},{9,7},{10,... | collective-permute-start | bytes 98312 | tf_op jit(solution)/shard_map/ppermute | solution.py:419
  37.9 0.8 %own_sources.1.refs_5_ = f32[8,16,32,128]{3,2,1,0:T(8,128)S(1)} custom-call(f32[16,256]{1,0:T(8,128)S(1)} %get-tuple-element.44.adj), custom_call_target="tpu_custom_call" | custom-call | flops 1000000 | bytes 1000000 | tf_op jit(solution)/shard_map/own_sources/pallas_call | solution.py:405
  38.7 3.9 %collective-permute-done.8.refs_8_ = f32[2,16,256]{2,1,0:T(8,128)S(1)} collective-permute-done((f32[2,16,256]{2,1,0:T(8,128)S(1)}, f32[2,16,256]{2,1,0:T(8,128)S(1)}, u32[]{:S(2)}, u32[]{:S(2)}) %collective-permute-start.8) | collective-permute-done | bytes 32800 | tf_op jit(solution)/shard_map/ppermute | solution.py:419
  42.5 4.5 %adjoint.1 = (f32[4,32,128]{2,1,0:T(8,128)S(1)}, f32[4,32,128]{2,1,0:T(8,128)S(1)}, f32[4,32,128]{2,1,0:T(8,128)S(1)}, f32[4,32,128]{2,1,0:T(8,128)S(1)}) custom-call(f32[4,16,32,128]{3,2,1,0:T(8,128)S(1)} %get-tuple-element.35.refs_2_.refs_0_, f32[4,16,32,128]{3,2,1,0:T(8,128)S(1)} %get-tuple-element.43.refs_1_, ...), custom_call_target="tpu_custom_call" | custom-call | flops 1000000 | bytes 1000000 | tf_op jit(solution)/shard_map/adjoint/pallas_call | solution.py:405
  47.0 0.1 collective-permute-start.9
  47.1 1.6 %collective-permute-start.10 = (f32[4,32,128]{2,1,0:T(8,128)S(1)}, f32[4,32,128]{2,1,0:T(8,128)S(1)}, u32[]{:S(2)}, u32[]{:S(2)}) collective-permute-start(f32[4,32,128]{2,1,0:T(8,128)S(1)} %get-tuple-element.47), channel_id=1, source_target_pairs={{0,12},{1,13},{2,14},{3,15},{4,8},{5,9},{6,10},{7,11},{8,4},{9,5},... | collective-permute-start | bytes 196616 | tf_op jit(solution)/shard_map/ppermute | solution.py:419
  48.7 1.9 %collective-permute-start.11 = (f32[4,32,128]{2,1,0:T(8,128)S(1)}, f32[4,32,128]{2,1,0:T(8,128)S(1)}, u32[]{:S(2)}, u32[]{:S(2)}) collective-permute-start(f32[4,32,128]{2,1,0:T(8,128)S(1)} %get-tuple-element.48), channel_id=1, source_target_pairs={{0,4},{1,5},{2,6},{3,7},{4,0},{5,1},{6,2},{7,3},{8,12},{9,13},{10,... | collective-permute-start | bytes 196616 | tf_op jit(solution)/shard_map/ppermute | solution.py:419
  50.5 3.3 %collective-permute-done.9 = f32[4,32,128]{2,1,0:T(8,128)S(1)} collective-permute-done((f32[4,32,128]{2,1,0:T(8,128)S(1)}, f32[4,32,128]{2,1,0:T(8,128)S(1)}, u32[]{:S(2)}, u32[]{:S(2)}) %collective-permute-start.9) | collective-permute-done | bytes 65568 | tf_op jit(solution)/shard_map/ppermute | solution.py:419
  53.8 0.3 collective-permute-done.11
  54.1 0.6 %add_add_fusion = f32[4,32,128]{2,1,0:T(8,128)} fusion(f32[4,32,128]{2,1,0:T(8,128)S(1)} %collective-permute-done.11, f32[4,32,128]{2,1,0:T(8,128)S(1)} %collective-permute-done.10, f32[4,32,128]{2,1,0:T(8,128)S(1)} %get-tuple-element.45, f32[4,32,128]{2,1,0:T(8,128)S(1)} %collective-permute-done.9), kind=kLoop, calls=%fused_computation | loop fusion | flops 49152 | bytes 327680 | tf_op jit(solution)/shard_map/add | solution.py:542
  (13 shorter events, 0.0 us)
Async XLA Ops:
  0.0 16.4 %collective-permute-start.1 = (f32[16,32,128]{2,1,0:T(8,128)}, f32[16,32,128]{2,1,0:T(8,128)S(1)}, u32[]{:S(2)}, u32[]{:S(2)}) collective-permute-start(f32[16,32,128]{2,1,0:T(8,128)} %now.1), channel_id=1, source_target_pairs={{0,15},{1,2},{2,1},{3,4},{4,3},{5,6},{6,5},{7,8},{8,7},{9,10},{10,... | collective-permute-start | bytes 786440 | tf_op jit(solution)/shard_map/ppermute | solution.py:419
  5.4 10.9 %collective-permute-start = (f32[16,32,128]{2,1,0:T(8,128)}, f32[16,32,128]{2,1,0:T(8,128)S(1)}, u32[]{:S(2)}, u32[]{:S(2)}) collective-permute-start(f32[16,32,128]{2,1,0:T(8,128)} %now.1), channel_id=1, source_target_pairs={{0,1},{1,0},{2,3},{3,2},{4,5},{5,4},{6,7},{7,6},{8,9},{9,8},{10,11... | collective-permute-start | bytes 786440 | tf_op jit(solution)/shard_map/ppermute | solution.py:419
  6.1 1.0 %copy-start.2 = (f32[16,32,128]{2,1,0:T(8,128)S(1)}, f32[16,32,128]{2,1,0:T(8,128)}, u32[]{:S(2)}) copy-start(f32[16,32,128]{2,1,0:T(8,128)} %before.1) | copy-start | bytes 786436
  7.1 0.7 %copy-start.3 = (f32[1,8]{1,0:T(1,128)S(1)}, f32[1,8]{1,0:T(1,128)}, u32[]{:S(2)}) copy-start(f32[1,8]{1,0:T(1,128)} %wavelet.1) | copy-start | bytes 100
  8.3 8.1 %collective-permute-start.2 = (f32[400,128]{1,0:T(8,128)S(1)}, f32[400,128]{1,0:T(8,128)S(1)}, u32[]{:S(2)}, u32[]{:S(2)}) collective-permute-start(f32[400,128]{1,0:T(8,128)S(1)} %get-tuple-element.30), channel_id=1, source_target_pairs={{0,15},{1,2},{2,1},{3,4},{4,3},{5,6},{6,5},{7,8},{8,7},{9,10},{10,... | collective-permute-start | bytes 614408 | tf_op jit(solution)/shard_map/ppermute | solution.py:419
  9.0 7.3 %collective-permute-start.3 = (f32[400,128]{1,0:T(8,128)S(1)}, f32[400,128]{1,0:T(8,128)S(1)}, u32[]{:S(2)}, u32[]{:S(2)}) collective-permute-start(f32[400,128]{1,0:T(8,128)S(1)} %get-tuple-element.31), channel_id=1, source_target_pairs={{0,1},{1,0},{2,3},{3,2},{4,5},{5,4},{6,7},{7,6},{8,9},{9,8},{10,11... | collective-permute-start | bytes 614408 | tf_op jit(solution)/shard_map/ppermute | solution.py:419
  9.7 1.2 %copy-start = (f32[64,32,128]{2,1,0:T(8,128)S(1)}, f32[64,32,128]{2,1,0:T(8,128)}, u32[]{:S(2)}) copy-start(f32[64,32,128]{2,1,0:T(8,128)} %courant.1) | copy-start | bytes 3145732
  11.0 0.9 %copy-start.1 = (f32[16,32,128]{2,1,0:T(8,128)S(1)}, f32[16,32,128]{2,1,0:T(8,128)}, u32[]{:S(2)}) copy-start(f32[16,32,128]{2,1,0:T(8,128)} %now.1) | copy-start | bytes 786436
  11.9 7.2 %copy-start.4 = (f32[16,128]{1,0:T(8,128)S(1)}, f32[16,128]{1,0:T(8,128)}, u32[]{:S(2)}) copy-start(f32[16,128]{1,0:T(8,128)} %param.15) | copy-start | bytes 24580
  18.4 13.3 %collective-permute-start.5 = (f32[24,32,128]{2,1,0:T(8,128)S(1)}, f32[24,32,128]{2,1,0:T(8,128)S(1)}, u32[]{:S(2)}, u32[]{:S(2)}) collective-permute-start(f32[24,32,128]{2,1,0:T(8,128)S(1)} %get-tuple-element.37), channel_id=1, source_target_pairs={{0,15},{1,2},{2,1},{3,4},{4,3},{5,6},{6,5},{7,8},{8,7},{9,10},{10,... | collective-permute-start | bytes 1179656 | tf_op jit(solution)/shard_map/ppermute | solution.py:419
  19.2 12.6 %collective-permute-start.4 = (f32[24,32,128]{2,1,0:T(8,128)S(1)}, f32[24,32,128]{2,1,0:T(8,128)S(1)}, u32[]{:S(2)}, u32[]{:S(2)}) collective-permute-start(f32[24,32,128]{2,1,0:T(8,128)S(1)} %get-tuple-element.37), channel_id=1, source_target_pairs={{0,1},{1,0},{2,3},{3,2},{4,5},{5,4},{6,7},{7,6},{8,9},{9,8},{10,11... | collective-permute-start | bytes 1179656 | tf_op jit(solution)/shard_map/ppermute | solution.py:419
  34.7 1.2 %collective-permute-start.6 = (f32[16,256]{1,0:T(8,128)S(1)}, f32[16,256]{1,0:T(8,128)S(1)}, u32[]{:S(2)}, u32[]{:S(2)}) collective-permute-start(f32[16,256]{1,0:T(8,128)S(1)} %get-tuple-element.44.adj), channel_id=1, source_target_pairs={{0,1},{1,0},{2,3},{3,2},{4,5},{5,4},{6,7},{7,6},{8,9},{9,8},{10,11... | collective-permute-start | bytes 49160 | tf_op jit(solution)/shard_map/ppermute | solution.py:419
  35.9 6.6 %collective-permute-start.8 = (f32[2,16,256]{2,1,0:T(8,128)S(1)}, f32[2,16,256]{2,1,0:T(8,128)S(1)}, u32[]{:S(2)}, u32[]{:S(2)}) collective-permute-start(f32[2,16,256]{2,1,0:T(8,128)S(1)} %pair.1.refs_6_), channel_id=1, source_target_pairs={{0,14},{1,15},{2,4},{3,5},{4,2},{5,3},{6,8},{7,9},{8,6},{9,7},{10,... | collective-permute-start | bytes 98312 | tf_op jit(solution)/shard_map/ppermute | solution.py:419
  37.9 4.6 %collective-permute-start.7 = (f32[2,16,256]{2,1,0:T(8,128)S(1)}, f32[2,16,256]{2,1,0:T(8,128)S(1)}, u32[]{:S(2)}, u32[]{:S(2)}) collective-permute-start(f32[2,16,256]{2,1,0:T(8,128)S(1)} %pair.1.refs_6_), channel_id=1, source_target_pairs={{0,2},{1,3},{2,0},{3,1},{4,6},{5,7},{6,4},{7,5},{8,10},{9,11},{10,... | collective-permute-start | bytes 98312 | tf_op jit(solution)/shard_map/ppermute | solution.py:419
  47.0 6.8 %collective-permute-start.9 = (f32[4,32,128]{2,1,0:T(8,128)S(1)}, f32[4,32,128]{2,1,0:T(8,128)S(1)}, u32[]{:S(2)}, u32[]{:S(2)}) collective-permute-start(f32[4,32,128]{2,1,0:T(8,128)S(1)} %get-tuple-element.46), channel_id=1, source_target_pairs={{0,8},{1,9},{2,10},{3,11},{4,12},{5,13},{6,14},{7,15},{8,0},{9,1},... | collective-permute-start | bytes 196616 | tf_op jit(solution)/shard_map/ppermute | solution.py:419
  47.1 6.7 %collective-permute-start.10 = (f32[4,32,128]{2,1,0:T(8,128)S(1)}, f32[4,32,128]{2,1,0:T(8,128)S(1)}, u32[]{:S(2)}, u32[]{:S(2)}) collective-permute-start(f32[4,32,128]{2,1,0:T(8,128)S(1)} %get-tuple-element.47), channel_id=1, source_target_pairs={{0,12},{1,13},{2,14},{3,15},{4,8},{5,9},{6,10},{7,11},{8,4},{9,5},... | collective-permute-start | bytes 196616 | tf_op jit(solution)/shard_map/ppermute | solution.py:419
  48.7 5.4 %collective-permute-start.11 = (f32[4,32,128]{2,1,0:T(8,128)S(1)}, f32[4,32,128]{2,1,0:T(8,128)S(1)}, u32[]{:S(2)}, u32[]{:S(2)}) collective-permute-start(f32[4,32,128]{2,1,0:T(8,128)S(1)} %get-tuple-element.48), channel_id=1, source_target_pairs={{0,4},{1,5},{2,6},{3,7},{4,0},{5,1},{6,2},{7,3},{8,12},{9,13},{10,... | collective-permute-start | bytes 196616 | tf_op jit(solution)/shard_map/ppermute | solution.py:419

commit v13 on v12

--- a/solution.py
+++ b/solution.py
@@ -149,7 +149,7 @@
     lanes = lax.broadcasted_iota(jnp.int32, (count, table_rows), 1)
     rows_table = jnp.where(row_of == lanes, 1.0, 0.0).astype(BF)
     lanes2 = lax.broadcasted_iota(jnp.int32, (count, 256), 1) % 128
-    lane_table = jnp.where(lane_of == lanes2, 1.0, 0.0)
+    lane_table = jnp.where(lane_of == lanes2, 1.0, 0.0).astype(BF)
     return rows_table, lane_table
 
 
@@ -161,7 +161,7 @@
     out = []
     for j in range(0, rows_table.shape[0], 256):
         found = dot(rows_table[j : j + 256], pair)
-        kept = (found * lane_table[j : j + 256]).astype(BF)
+        kept = found.astype(BF) * lane_table[j : j + 256]
         out.append(dot(ones, kept, (((1,), (1,)), ((), ()))))
     return jnp.concatenate(out, axis=1)
 
@@ -499,7 +499,7 @@
         functools.partial(tables_kernel, count),
         (
             jax.ShapeDtypeStruct((count, table_rows), BF),
-            jax.ShapeDtypeStruct((count, 256), F32),
+            jax.ShapeDtypeStruct((count, 256), BF),
             jax.ShapeDtypeStruct((NT, count), F32),
         ),
         (cells, recorded, *field_list),

time: 55 us -> 55.1 us (level)
  no operation moved by 1% of the time
where the time goes in v13:
time: 55.1 us; the launch traced here: 54.8 us
  starting transfers between devices  12.5 us (23%)
  waiting for transfers between devices  12.4 us (23%)
  Pallas kernels  12.3 us (22%)
  blocking collectives  11.7 us (21%)
  local copies, waits for them, and re-layouts  3.78 us (7%)
  other arithmetic  1.35 us (2%)
  between operations  0.73 us (1%)
    ppermute x12, starting transfers between devices, swapped(): lax.ppermute(value, 'shot', [(d, partner(d) % count) for d in range(count)])  12.5 us
    ppermute x12, waiting for transfers between devices, swapped(): lax.ppermute(value, 'shot', [(d, partner(d) % count) for d in range(count)])  12.4 us
    pallas_call x8, Pallas kernels, call(): pl.pallas_call(kernel, out_shape=outs, in_specs=specs or [VMEM] * len(ins...  12.3 us
    all_to_all x1, blocking collectives, per_device(): lax.all_to_all(observed, 'shot', split_axis=0, concat_axis=0, tiled=True)  11.7 us
    unnamed x10, local copies, waits for them, and re-layouts  3.78 us
  transfers between devices with their start and end apart: 12, of which 5 were waited for; matrix products, arithmetic and copies ran while one was open for 1% of the time, Pallas kernels for 5%

profile of v13, /device:TPU:0, one launch (start us, length us, event | category | flops | bytes accessed | tf_op | source)
XLA Modules:
  0.0 54.8 jit_solution(10433134270483772580)
XLA Ops:
  0.0 5.4 %collective-permute-start.1 = (f32[16,32,128]{2,1,0:T(8,128)}, f32[16,32,128]{2,1,0:T(8,128)S(1)}, u32[]{:S(2)}, u32[]{:S(2)}) collective-permute-start(f32[16,32,128]{2,1,0:T(8,128)} %now.1), channel_id=1, source_target_pairs={{0,15},{1,2},{2,1},{3,4},{4,3},{5,6},{6,5},{7,8},{8,7},{9,10},{10,... | collective-permute-start | bytes 786440 | tf_op jit(solution)/shard_map/ppermute | solution.py:419
  6.1 0.9 %copy-done.2 = f32[16,32,128]{2,1,0:T(8,128)S(1)} copy-done((f32[16,32,128]{2,1,0:T(8,128)S(1)}, f32[16,32,128]{2,1,0:T(8,128)}, u32[]{:S(2)}) %copy-start.2) | copy-done | bytes 262168
  7.1 0.7 %copy-done.3 = f32[1,8]{1,0:T(1,128)S(1)} copy-done((f32[1,8]{1,0:T(1,128)S(1)}, f32[1,8]{1,0:T(1,128)}, u32[]{:S(2)}) %copy-start.3) | copy-done | bytes 56
  7.7 0.6 %message.1 = (f32[400,128]{1,0:T(8,128)S(1)}, f32[400,128]{1,0:T(8,128)S(1)}, f32[16,128]{1,0:T(8,128)S(1)}, f32[16,32,128]{2,1,0:T(8,128)S(1)}) custom-call(f32[16,32,128]{2,1,0:T(8,128)S(1)} %copy-done.2, f32[1,8]{1,0:T(1,128)S(1)} %copy-done.3, s32[1]{0:T(128)S(6)} %copy.9.source), custom_call_target="tpu_custom_call" | custom-call | flops 1000000 | bytes 1000000 | tf_op jit(solution)/shard_map/message/pallas_call | solution.py:405
  8.3 0.7 %collective-permute-start.2 = (f32[400,128]{1,0:T(8,128)S(1)}, f32[400,128]{1,0:T(8,128)S(1)}, u32[]{:S(2)}, u32[]{:S(2)}) collective-permute-start(f32[400,128]{1,0:T(8,128)S(1)} %get-tuple-element.30), channel_id=1, source_target_pairs={{0,15},{1,2},{2,1},{3,4},{4,3},{5,6},{6,5},{7,8},{8,7},{9,10},{10,... | collective-permute-start | bytes 614408 | tf_op jit(solution)/shard_map/ppermute | solution.py:419
  9.0 0.7 %pad_add_fusion = s32[512]{0:T(512)S(1)} fusion(s32[256]{0:T(256)} %param.14, s32[256]{0:T(256)} %param.13), kind=kLoop, calls=%fused_computation.1 | loop fusion | flops 512 | bytes 4096 | tf_op jit(solution)/shard_map/concatenate | solution.py:459
  9.7 1.2 %copy-done = f32[64,32,128]{2,1,0:T(8,128)S(1)} copy-done((f32[64,32,128]{2,1,0:T(8,128)S(1)}, f32[64,32,128]{2,1,0:T(8,128)}, u32[]{:S(2)}) %copy-start) | copy-done | bytes 1048600
  11.0 0.9 %copy-done.1 = f32[16,32,128]{2,1,0:T(8,128)S(1)} copy-done((f32[16,32,128]{2,1,0:T(8,128)S(1)}, f32[16,32,128]{2,1,0:T(8,128)}, u32[]{:S(2)}) %copy-start.1) | copy-done | bytes 262168
  11.9 0.7 %prepare.1 = (f32[72,32,128]{2,1,0:T(8,128)S(1)}, f32[8,256]{1,0:T(8,128)S(1)}, f32[16,32,128]{2,1,0:T(8,128)S(1)}, bf16[256,256]{1,0:T(8,128)(2,1)S(1)}, bf16[256,256]{1,0:T(8,128)(2,1)S(1)}) custom-call(f32[64,32,128]{2,1,0:T(8,128)S(1)} %copy-done, s32[1,512]{1,0:T(1,128)S(1)} %bitcast.4, f32[16,128]{1,0:T(8,128)S(1)} %get-tuple-element.27.pack.refs_9_, ...), custom_call_target="tpu_custom_call" | custom-call | flops 1000000 | bytes 1000000 | tf_op jit(solution)/shard_map/prepare/pallas_call | solution.py:405
  12.6 3.7 %collective-permute-done.2.refs_4_ = f32[400,128]{1,0:T(8,128)S(1)} collective-permute-done((f32[400,128]{1,0:T(8,128)S(1)}, f32[400,128]{1,0:T(8,128)S(1)}, u32[]{:S(2)}, u32[]{:S(2)}) %collective-permute-start.2) | collective-permute-done | bytes 204832 | tf_op jit(solution)/shard_map/ppermute | solution.py:419
  16.4 0.0 collective-permute-done.3.refs_5_
  16.4 2.1 %forward.1 = (f32[4,16,32,128]{3,2,1,0:T(8,128)S(1)}, f32[2,4,32,128]{3,2,1,0:T(8,128)S(1)}, f32[24,32,128]{2,1,0:T(8,128)S(1)}, f32[3,16,128]{2,1,0:T(8,128)S(1)}) custom-call(f32[16,32,128]{2,1,0:T(8,128)S(1)} %get-tuple-element.28.refs_0_, f32[16,32,128]{2,1,0:T(8,128)S(1)} %get-tuple-element.29.refs_1_, f32[16,32,128]{2,1,0:T(8,128)S(1)} %collective-permute-done.refs_2_, ...), custom_call_target="tpu_custom_call" | custom-call | flops 1000000 | bytes 1000000 | tf_op jit(solution)/shard_map/forward/pallas_call | solution.py:405
  18.4 0.7 %collective-permute-start.5 = (f32[24,32,128]{2,1,0:T(8,128)S(1)}, f32[24,32,128]{2,1,0:T(8,128)S(1)}, u32[]{:S(2)}, u32[]{:S(2)}) collective-permute-start(f32[24,32,128]{2,1,0:T(8,128)S(1)} %get-tuple-element.37), channel_id=1, source_target_pairs={{0,15},{1,2},{2,1},{3,4},{4,3},{5,6},{6,5},{7,8},{8,7},{9,10},{10,... | collective-permute-start | bytes 1179656 | tf_op jit(solution)/shard_map/ppermute | solution.py:419
  19.2 0.0 collective-permute-start.4
  19.2 11.7 %all_to_all.11 = f32[16,1,128]{2,1,0:T(1,128)S(1)} all-to-all(f32[16,1,128]{2,1,0:T(1,128)S(1)} %bitcast.5), channel_id=1, replica_groups=mesh['groups'=2,'shot'=16] {'shot'}, dimensions={0} | all-to-all | bytes 16384 | tf_op jit(solution)/shard_map/all_to_all | solution.py:472
  30.9 0.8 %traces.1 = (bf16[256,512]{1,0:T(8,128)(2,1)S(1)}, bf16[256,256]{1,0:T(8,128)(2,1)S(1)}, f32[8,256]{1,0:T(8,128)S(1)}) custom-call(f32[8,256]{1,0:T(8,128)S(1)} %get-tuple-element.39.refs_0_.refs_8_, f32[16,128]{1,0:T(8,128)S(1)} %bitcast.3, f32[4,16,32,128]{3,2,1,0:T(8,128)S(1)} %get-tuple-element.35.refs_2_.refs_0_), custom_call_target="tpu_custom_call" | custom-call | flops 1000000 | bytes 1000000 | tf_op jit(solution)/shard_map/traces/pallas_call | solution.py:405
  31.8 0.0 collective-permute-done.5.refs_3_
  31.8 0.0 collective-permute-done.4.refs_2_
  31.8 3.0 %forward_last.1 = (f32[4,16,32,128]{3,2,1,0:T(8,128)S(1)}, f32[16,256]{1,0:T(8,128)S(1)}) custom-call(f32[4,16,32,128]{3,2,1,0:T(8,128)S(1)} %get-tuple-element.35.refs_2_.refs_0_, f32[2,4,32,128]{3,2,1,0:T(8,128)S(1)} %get-tuple-element.36.refs_1_, f32[24,32,128]{2,1,0:T(8,128)S(1)} %collective-permute-done.4.refs_2_, ...), custom_call_target="tpu_custom_call" | custom-call | flops 1000000 | bytes 1000000 | tf_op jit(solution)/shard_map/forward_last/pallas_call | solution.py:405
  34.7 0.0 collective-permute-start.6
  34.7 1.2 %collective-permute-done.6.mate = f32[16,256]{1,0:T(8,128)S(1)} collective-permute-done((f32[16,256]{1,0:T(8,128)S(1)}, f32[16,256]{1,0:T(8,128)S(1)}, u32[]{:S(2)}, u32[]{:S(2)}) %collective-permute-start.6) | collective-permute-done | bytes 16416 | tf_op jit(solution)/shard_map/ppermute | solution.py:419
  35.9 2.0 %collective-permute-start.8 = (f32[2,16,256]{2,1,0:T(8,128)S(1)}, f32[2,16,256]{2,1,0:T(8,128)S(1)}, u32[]{:S(2)}, u32[]{:S(2)}) collective-permute-start(f32[2,16,256]{2,1,0:T(8,128)S(1)} %pair.1.refs_6_), channel_id=1, source_target_pairs={{0,14},{1,15},{2,4},{3,5},{4,2},{5,3},{6,8},{7,9},{8,6},{9,7},{10,... | collective-permute-start | bytes 98312 | tf_op jit(solution)/shard_map/ppermute | solution.py:419
  37.9 0.0 collective-permute-start.7
  37.9 0.7 %own_sources.1.refs_5_ = f32[8,16,32,128]{3,2,1,0:T(8,128)S(1)} custom-call(f32[16,256]{1,0:T(8,128)S(1)} %get-tuple-element.44.adj), custom_call_target="tpu_custom_call" | custom-call | flops 1000000 | bytes 1000000 | tf_op jit(solution)/shard_map/own_sources/pallas_call | solution.py:405
  38.7 3.9 %collective-permute-done.8.refs_8_ = f32[2,16,256]{2,1,0:T(8,128)S(1)} collective-permute-done((f32[2,16,256]{2,1,0:T(8,128)S(1)}, f32[2,16,256]{2,1,0:T(8,128)S(1)}, u32[]{:S(2)}, u32[]{:S(2)}) %collective-permute-start.8) | collective-permute-done | bytes 32800 | tf_op jit(solution)/shard_map/ppermute | solution.py:419
  42.5 4.5 %adjoint.1 = (f32[4,32,128]{2,1,0:T(8,128)S(1)}, f32[4,32,128]{2,1,0:T(8,128)S(1)}, f32[4,32,128]{2,1,0:T(8,128)S(1)}, f32[4,32,128]{2,1,0:T(8,128)S(1)}) custom-call(f32[4,16,32,128]{3,2,1,0:T(8,128)S(1)} %get-tuple-element.35.refs_2_.refs_0_, f32[4,16,32,128]{3,2,1,0:T(8,128)S(1)} %get-tuple-element.43.refs_1_, ...), custom_call_target="tpu_custom_call" | custom-call | flops 1000000 | bytes 1000000 | tf_op jit(solution)/shard_map/adjoint/pallas_call | solution.py:405
  47.0 0.1 collective-permute-start.9
  47.1 1.6 %collective-permute-start.10 = (f32[4,32,128]{2,1,0:T(8,128)S(1)}, f32[4,32,128]{2,1,0:T(8,128)S(1)}, u32[]{:S(2)}, u32[]{:S(2)}) collective-permute-start(f32[4,32,128]{2,1,0:T(8,128)S(1)} %get-tuple-element.47), channel_id=1, source_target_pairs={{0,12},{1,13},{2,14},{3,15},{4,8},{5,9},{6,10},{7,11},{8,4},{9,5},... | collective-permute-start | bytes 196616 | tf_op jit(solution)/shard_map/ppermute | solution.py:419
  48.7 1.9 %collective-permute-start.11 = (f32[4,32,128]{2,1,0:T(8,128)S(1)}, f32[4,32,128]{2,1,0:T(8,128)S(1)}, u32[]{:S(2)}, u32[]{:S(2)}) collective-permute-start(f32[4,32,128]{2,1,0:T(8,128)S(1)} %get-tuple-element.48), channel_id=1, source_target_pairs={{0,4},{1,5},{2,6},{3,7},{4,0},{5,1},{6,2},{7,3},{8,12},{9,13},{10,... | collective-permute-start | bytes 196616 | tf_op jit(solution)/shard_map/ppermute | solution.py:419
  50.5 3.3 %collective-permute-done.9 = f32[4,32,128]{2,1,0:T(8,128)S(1)} collective-permute-done((f32[4,32,128]{2,1,0:T(8,128)S(1)}, f32[4,32,128]{2,1,0:T(8,128)S(1)}, u32[]{:S(2)}, u32[]{:S(2)}) %collective-permute-start.9) | collective-permute-done | bytes 65568 | tf_op jit(solution)/shard_map/ppermute | solution.py:419
  53.8 0.3 collective-permute-done.11
  54.1 0.6 %add_add_fusion = f32[4,32,128]{2,1,0:T(8,128)} fusion(f32[4,32,128]{2,1,0:T(8,128)S(1)} %collective-permute-done.11, f32[4,32,128]{2,1,0:T(8,128)S(1)} %collective-permute-done.10, f32[4,32,128]{2,1,0:T(8,128)S(1)} %get-tuple-element.45, f32[4,32,128]{2,1,0:T(8,128)S(1)} %collective-permute-done.9), kind=kLoop, calls=%fused_computation | loop fusion | flops 49152 | bytes 327680 | tf_op jit(solution)/shard_map/add | solution.py:542
  (13 shorter events, 0.0 us)
Async XLA Ops:
  0.0 16.4 %collective-permute-start.1 = (f32[16,32,128]{2,1,0:T(8,128)}, f32[16,32,128]{2,1,0:T(8,128)S(1)}, u32[]{:S(2)}, u32[]{:S(2)}) collective-permute-start(f32[16,32,128]{2,1,0:T(8,128)} %now.1), channel_id=1, source_target_pairs={{0,15},{1,2},{2,1},{3,4},{4,3},{5,6},{6,5},{7,8},{8,7},{9,10},{10,... | collective-permute-start | bytes 786440 | tf_op jit(solution)/shard_map/ppermute | solution.py:419
  5.4 10.9 %collective-permute-start = (f32[16,32,128]{2,1,0:T(8,128)}, f32[16,32,128]{2,1,0:T(8,128)S(1)}, u32[]{:S(2)}, u32[]{:S(2)}) collective-permute-start(f32[16,32,128]{2,1,0:T(8,128)} %now.1), channel_id=1, source_target_pairs={{0,1},{1,0},{2,3},{3,2},{4,5},{5,4},{6,7},{7,6},{8,9},{9,8},{10,11... | collective-permute-start | bytes 786440 | tf_op jit(solution)/shard_map/ppermute | solution.py:419
  6.1 1.0 %copy-start.2 = (f32[16,32,128]{2,1,0:T(8,128)S(1)}, f32[16,32,128]{2,1,0:T(8,128)}, u32[]{:S(2)}) copy-start(f32[16,32,128]{2,1,0:T(8,128)} %before.1) | copy-start | bytes 786436
  7.1 0.7 %copy-start.3 = (f32[1,8]{1,0:T(1,128)S(1)}, f32[1,8]{1,0:T(1,128)}, u32[]{:S(2)}) copy-start(f32[1,8]{1,0:T(1,128)} %wavelet.1) | copy-start | bytes 100
  8.3 8.1 %collective-permute-start.2 = (f32[400,128]{1,0:T(8,128)S(1)}, f32[400,128]{1,0:T(8,128)S(1)}, u32[]{:S(2)}, u32[]{:S(2)}) collective-permute-start(f32[400,128]{1,0:T(8,128)S(1)} %get-tuple-element.30), channel_id=1, source_target_pairs={{0,15},{1,2},{2,1},{3,4},{4,3},{5,6},{6,5},{7,8},{8,7},{9,10},{10,... | collective-permute-start | bytes 614408 | tf_op jit(solution)/shard_map/ppermute | solution.py:419
  9.0 7.3 %collective-permute-start.3 = (f32[400,128]{1,0:T(8,128)S(1)}, f32[400,128]{1,0:T(8,128)S(1)}, u32[]{:S(2)}, u32[]{:S(2)}) collective-permute-start(f32[400,128]{1,0:T(8,128)S(1)} %get-tuple-element.31), channel_id=1, source_target_pairs={{0,1},{1,0},{2,3},{3,2},{4,5},{5,4},{6,7},{7,6},{8,9},{9,8},{10,11... | collective-permute-start | bytes 614408 | tf_op jit(solution)/shard_map/ppermute | solution.py:419
  9.7 1.2 %copy-start = (f32[64,32,128]{2,1,0:T(8,128)S(1)}, f32[64,32,128]{2,1,0:T(8,128)}, u32[]{:S(2)}) copy-start(f32[64,32,128]{2,1,0:T(8,128)} %courant.1) | copy-start | bytes 3145732
  11.0 0.9 %copy-start.1 = (f32[16,32,128]{2,1,0:T(8,128)S(1)}, f32[16,32,128]{2,1,0:T(8,128)}, u32[]{:S(2)}) copy-start(f32[16,32,128]{2,1,0:T(8,128)} %now.1) | copy-start | bytes 786436
  11.9 7.2 %copy-start.4 = (f32[16,128]{1,0:T(8,128)S(1)}, f32[16,128]{1,0:T(8,128)}, u32[]{:S(2)}) copy-start(f32[16,128]{1,0:T(8,128)} %param.15) | copy-start | bytes 24580
  18.4 13.3 %collective-permute-start.5 = (f32[24,32,128]{2,1,0:T(8,128)S(1)}, f32[24,32,128]{2,1,0:T(8,128)S(1)}, u32[]{:S(2)}, u32[]{:S(2)}) collective-permute-start(f32[24,32,128]{2,1,0:T(8,128)S(1)} %get-tuple-element.37), channel_id=1, source_target_pairs={{0,15},{1,2},{2,1},{3,4},{4,3},{5,6},{6,5},{7,8},{8,7},{9,10},{10,... | collective-permute-start | bytes 1179656 | tf_op jit(solution)/shard_map/ppermute | solution.py:419
  19.2 12.6 %collective-permute-start.4 = (f32[24,32,128]{2,1,0:T(8,128)S(1)}, f32[24,32,128]{2,1,0:T(8,128)S(1)}, u32[]{:S(2)}, u32[]{:S(2)}) collective-permute-start(f32[24,32,128]{2,1,0:T(8,128)S(1)} %get-tuple-element.37), channel_id=1, source_target_pairs={{0,1},{1,0},{2,3},{3,2},{4,5},{5,4},{6,7},{7,6},{8,9},{9,8},{10,11... | collective-permute-start | bytes 1179656 | tf_op jit(solution)/shard_map/ppermute | solution.py:419
  34.7 1.2 %collective-permute-start.6 = (f32[16,256]{1,0:T(8,128)S(1)}, f32[16,256]{1,0:T(8,128)S(1)}, u32[]{:S(2)}, u32[]{:S(2)}) collective-permute-start(f32[16,256]{1,0:T(8,128)S(1)} %get-tuple-element.44.adj), channel_id=1, source_target_pairs={{0,1},{1,0},{2,3},{3,2},{4,5},{5,4},{6,7},{7,6},{8,9},{9,8},{10,11... | collective-permute-start | bytes 49160 | tf_op jit(solution)/shard_map/ppermute | solution.py:419
  35.9 6.6 %collective-permute-start.8 = (f32[2,16,256]{2,1,0:T(8,128)S(1)}, f32[2,16,256]{2,1,0:T(8,128)S(1)}, u32[]{:S(2)}, u32[]{:S(2)}) collective-permute-start(f32[2,16,256]{2,1,0:T(8,128)S(1)} %pair.1.refs_6_), channel_id=1, source_target_pairs={{0,14},{1,15},{2,4},{3,5},{4,2},{5,3},{6,8},{7,9},{8,6},{9,7},{10,... | collective-permute-start | bytes 98312 | tf_op jit(solution)/shard_map/ppermute | solution.py:419
  37.9 4.6 %collective-permute-start.7 = (f32[2,16,256]{2,1,0:T(8,128)S(1)}, f32[2,16,256]{2,1,0:T(8,128)S(1)}, u32[]{:S(2)}, u32[]{:S(2)}) collective-permute-start(f32[2,16,256]{2,1,0:T(8,128)S(1)} %pair.1.refs_6_), channel_id=1, source_target_pairs={{0,2},{1,3},{2,0},{3,1},{4,6},{5,7},{6,4},{7,5},{8,10},{9,11},{10,... | collective-permute-start | bytes 98312 | tf_op jit(solution)/shard_map/ppermute | solution.py:419
  47.0 6.8 %collective-permute-start.9 = (f32[4,32,128]{2,1,0:T(8,128)S(1)}, f32[4,32,128]{2,1,0:T(8,128)S(1)}, u32[]{:S(2)}, u32[]{:S(2)}) collective-permute-start(f32[4,32,128]{2,1,0:T(8,128)S(1)} %get-tuple-element.46), channel_id=1, source_target_pairs={{0,8},{1,9},{2,10},{3,11},{4,12},{5,13},{6,14},{7,15},{8,0},{9,1},... | collective-permute-start | bytes 196616 | tf_op jit(solution)/shard_map/ppermute | solution.py:419
  47.1 6.7 %collective-permute-start.10 = (f32[4,32,128]{2,1,0:T(8,128)S(1)}, f32[4,32,128]{2,1,0:T(8,128)S(1)}, u32[]{:S(2)}, u32[]{:S(2)}) collective-permute-start(f32[4,32,128]{2,1,0:T(8,128)S(1)} %get-tuple-element.47), channel_id=1, source_target_pairs={{0,12},{1,13},{2,14},{3,15},{4,8},{5,9},{6,10},{7,11},{8,4},{9,5},... | collective-permute-start | bytes 196616 | tf_op jit(solution)/shard_map/ppermute | solution.py:419
  48.7 5.4 %collective-permute-start.11 = (f32[4,32,128]{2,1,0:T(8,128)S(1)}, f32[4,32,128]{2,1,0:T(8,128)S(1)}, u32[]{:S(2)}, u32[]{:S(2)}) collective-permute-start(f32[4,32,128]{2,1,0:T(8,128)S(1)} %get-tuple-element.48), channel_id=1, source_target_pairs={{0,4},{1,5},{2,6},{3,7},{4,0},{5,1},{6,2},{7,3},{8,12},{9,13},{10,... | collective-permute-start | bytes 196616 | tf_op jit(solution)/shard_map/ppermute | solution.py:419
